TPU v7x, 128 devices: a whole 4x4x4 slice. The times are simulated.
128 devices in a mesh: gz: 8 (over y, z_hi), gy: 16 (over x, z_lo, core).
Axes of the slice: x: 4, y: 4, z: 4 (z_hi: 2, z_lo: 2; z = z_hi * 2 + z_lo), core: 2. Of those that a mesh axis runs over, the one named last changes fastest.
Arguments:
- activations: bfloat16 [16, 256, 12288], P('gz', 'gy'), may hold values from -6 to 6
- grad_out: bfloat16 [16, 256, 12288], P('gz', 'gy'), may hold values from -6 to 6
- relu_mask: int32 [16, 256, 12288], P('gz', 'gy'), may hold values 0 or 1
- kernel: bfloat16 [3, 3, 3, 32, 32], replicated, may hold values from -0.21875 to 0.21875
- bias: float32 [32], replicated, may hold values from -3 to 3
Outputs:
- output: bfloat16 [16, 256, 12288], P('gz', 'gy')
- grad_input: bfloat16 [16, 256, 12288], P('gz', 'gy')
- grad_kernel: float32 [3, 3, 3, 32, 32], replicated
- grad_bias: float32 [32], replicated
All inputs are finite; a program needn't handle non-finite values. No bound on the sum of `relu_mask` on one device may be relied on, other than what follows from the above.
Results may differ from a plain program's by a relative error of at most 0.001.
Values may be sent and summed in bfloat16 or wider, within the bound.
No kernel may reach another device: no remote copies, remote signals or barrier semaphores. Data moves between devices by JAX's collectives and lax.ppermute only.
A program may use at most 192 MiB of HBM per device.

v0:
```python
import functools
import math

import jax
import jax.numpy as jnp
from jax import lax
from jax.experimental import pallas as pl
from jax.experimental.pallas import tpu as pltpu
from jax.sharding import PartitionSpec as P

F32 = jnp.float32
BF16 = jnp.bfloat16
LANES = 128
MIB = 1024 * 1024


def call(body, outs, scratch, args):
    return pl.pallas_call(
        body,
        out_shape=outs,
        scratch_shapes=scratch,
        compiler_params=pltpu.CompilerParams(vmem_limit_bytes=20 * MIB),
    )(*args)


def blocked(body, grid, outs, out_specs, scratch, args, in_specs, aliases=None):
    return pl.pallas_call(
        body,
        grid=(grid,),
        out_shape=outs,
        in_specs=in_specs,
        out_specs=out_specs,
        scratch_shapes=scratch,
        input_output_aliases=aliases or {},
        compiler_params=pltpu.CompilerParams(vmem_limit_bytes=56 * MIB),
    )(*args)


def part_of(shape, *index):
    return pl.BlockSpec(shape, lambda step: index)


def spread_rows(scratch, groups, group, block):
    pitch = groups + 1
    for half in range(2):
        scratch[pl.ds(half * 8 * pitch + group, 8, stride=pitch), :] = block[half * 8 : half * 8 + 8]


def group_body(act_in, grad_in, mask_in, low, high, firsts, lasts, scratch, act, grad, mask, arrived):
    rows, groups = act.shape[1], low.shape[1]
    copies = [
        [
            pltpu.make_async_copy(source.at[plane], target.at[plane], arrived.at[plane, place])
            for place, (source, target) in enumerate(((act_in, act), (mask_in, mask), (grad_in, grad)))
        ]
        for plane in range(2)
    ]
    for plane in (1, 0):
        for copy in copies[plane]:
            copy.start()
    for plane, out in ((1, high), (0, low)):
        for kind in range(2):
            for copy in copies[plane][:1] if kind == 0 else copies[plane][1:]:
                copy.wait()
            for group in range(groups):
                span = slice(group * LANES, (group + 1) * LANES)
                if kind == 0:
                    block = act[plane, :, span].astype(F32)
                else:
                    block = grad[plane, :, span].astype(F32) * mask[plane, :, span].astype(F32)
                spread_rows(scratch, groups, group, block)
            for row in range(rows):
                at = row * (groups + 1)
                out[kind * rows + row] = scratch[at : at + groups, :].astype(BF16)
            firsts[plane * 2 + kind] = out[kind * rows]
            lasts[plane * 2 + kind] = out[kind * rows + rows - 1]


def with_edges(cells):
    groups = cells.shape[0]
    wide = cells.astype(F32)
    lane = lax.broadcasted_iota(jnp.int32, wide.shape, 1)
    row = lax.broadcasted_iota(jnp.int32, wide.shape, 0)
    before = jnp.where(row == 0, 0.0, pltpu.roll(wide, 1, 0))
    after = jnp.where(row == groups - 1, 0.0, pltpu.roll(wide, groups - 1, 0))
    return jnp.concatenate([cells, jnp.where(lane < 64, after, before).astype(BF16)], axis=1)


def fill_plane(taps, place, source, first, last):
    rows = source.shape[0]
    taps[place, 0] = with_edges(first)
    taps[place, rows + 1] = with_edges(last)

    def step(row, carry):
        taps[place, row + 1] = with_edges(source[row])
        return carry

    lax.fori_loop(0, rows, step, 0, unroll=2)


def build_weights(kernel, flip, out):
    lane = lax.broadcasted_iota(jnp.int32, (32, LANES), 1) // 32
    for tap_z in range(3):
        for tap_y in range(3):
            blocks = []
            for tap_x in range(3):
                at = (tap_z * 3 + tap_y) * 3 + tap_x
                at = 26 - at if flip else at
                block = kernel[at * 32 : at * 32 + 32, :].astype(F32)
                block = block.T if flip else block
                blocks.append(jnp.concatenate([block] * 4, axis=1))
            for place in range(8):
                voxel = place if place < 6 else place - 8
                total = jnp.zeros((32, LANES), F32)
                for tap_x in range(3):
                    total = jnp.where(lane == voxel - tap_x + 1, blocks[tap_x], total)
                out[tap_z, tap_y, place * 32 : place * 32 + 32, :] = total.astype(BF16)


CHUNK = 4


def fold(term):
    total = None
    for voxel in range(4):
        part = term[voxel * 32 : voxel * 32 + 32]
        shift = (-(voxel - 1) * 32) % 256
        if shift:
            part = pltpu.roll(part, shift, 1)
        total = part if total is None else total + part
    return total[:, :LANES]


def local_terms_body(low, high, edges, folded, bias_terms, turned, taps):
    rows, groups = low.shape[0] // 2, low.shape[1]
    sums = jnp.zeros((8, LANES), F32)
    blank = jnp.zeros((groups, LANES), BF16)
    for plane, source in enumerate((low, high)):
        span = slice(plane * LANES, (plane + 1) * LANES)
        flat = source[rows:].reshape(rows * groups, LANES)
        turned[span, :] = flat.T
        edges[0, span, :] = source[rows].T
        edges[1, span, :] = source[2 * rows - 1].T
        sums = sums + jnp.sum(flat.astype(F32).reshape(-1, 8, LANES), axis=0)
        fill_plane(taps, plane, source.at[:rows], blank, blank)
    bias_terms[...] = sums
    for tap_y in range(3):
        both = []
        for plane in range(2):
            rhs = taps[plane, tap_y : tap_y + rows].reshape(rows * groups, 256)
            both.append(jnp.dot(turned[...], rhs, preferred_element_type=F32))
        folded[1, tap_y] = fold(both[0][:LANES] + both[1][LANES:])
        folded[0, tap_y] = fold(both[0][LANES:])
        folded[2, tap_y] = fold(both[1][:LANES])


def kernel_grad_body(
    below, low, from_left, from_right, edges, folded, bias_terms, flag, keep, send, packed, taps, sums
):
    rows, groups = below.shape[0] // 2, below.shape[1]
    blank = jnp.zeros((groups, LANES), BF16)
    fill_plane(taps, 0, below.at[:rows], blank, blank)
    fill_plane(taps, 1, low.at[:rows], blank, blank)
    below_turned = below[rows:].reshape(rows * groups, LANES).T
    low_turned = low[rows:].reshape(rows * groups, LANES).T
    sums[1] = jnp.zeros(sums.shape[1:], F32)
    for tap_y in range(3):
        rhs = taps[0, tap_y : tap_y + rows].reshape(rows * groups, 256)
        sums[0, tap_y] = jnp.dot(low_turned, rhs, preferred_element_type=F32)
        rhs = taps[1, tap_y : tap_y + rows].reshape(rows * groups, 256)
        sums[2, tap_y] = jnp.dot(below_turned, rhs, preferred_element_type=F32)
    for side, lines in enumerate((from_left, from_right)):
        tap_y, end = 2 * side, side * (rows - 1)
        lhs = jnp.concatenate([edges[side], below[rows + end].T], axis=0)
        term = jnp.dot(lhs, with_edges(lines[0]), preferred_element_type=F32)
        sums[1, tap_y] += term[:LANES]
        sums[0, tap_y] += term[LANES : 2 * LANES]
        sums[2, tap_y] += term[2 * LANES :]
        term = jnp.dot(edges[side], with_edges(lines[2]), preferred_element_type=F32)
        sums[2, tap_y] += term[:LANES]
        sums[1, tap_y] += term[LANES:]
        sums[0, 2 - tap_y] += jnp.dot(lines[1].T, taps[0, 1 + end], preferred_element_type=F32)
    lane = lax.broadcasted_iota(jnp.int32, (32, LANES), 1)
    parts = [folded[at // 3, at % 3] + fold(sums[at // 3, at % 3]) for at in range(9)]
    row = jnp.sum(bias_terms[...], axis=0, keepdims=True)
    row = row + pltpu.roll(row, 64, 1)
    row = row + pltpu.roll(row, 32, 1)
    first = lax.broadcasted_iota(jnp.int32, (32, LANES), 0) == 0
    for place in range(7):
        if place < 6:
            extra = pltpu.roll(parts[7 + place // 3], 96 - 32 * (place % 3), 1)
        else:
            extra = jnp.where(first, jnp.broadcast_to(row, (32, LANES)), 0.0)
        packed[place * 32 : place * 32 + 32, :] = jnp.where(lane < 96, parts[place], extra)
    upper = flag[...] > 0.5
    keep[...] = jnp.where(upper, packed[HALF : 2 * HALF], packed[:HALF])
    send[...] = jnp.where(upper, packed[:HALF], packed[HALF : 2 * HALF])


def inner_sum(taps, weights, chunk, groups):
    total = None
    for plane in range(2):
        for tap_y in range(3):
            lhs = taps[plane, pl.ds(chunk * CHUNK + tap_y, CHUNK)].reshape(CHUNK * groups, 256)
            matrix = jnp.concatenate([weights[plane + 1, tap_y], weights[plane, tap_y]], axis=1)
            term = jnp.dot(lhs, matrix, preferred_element_type=F32)
            total = term if total is None else total + term
    return total


def inner_body(flip, low, high, from_left, from_right, kernel, partial, weights, taps):
    groups = low.shape[1]
    kind = 1 if flip else 0
    chunk = pl.program_id(0)

    @pl.when(chunk == 0)
    def _():
        build_weights(kernel, flip, weights)
        fill_plane(taps, 0, low, from_left[kind], from_right[kind])
        fill_plane(taps, 1, high, from_left[2 + kind], from_right[2 + kind])

    total = inner_sum(taps, weights, chunk, groups)
    for plane in range(2):
        part = total[:, plane * LANES : (plane + 1) * LANES]
        partial[plane] = part.reshape(CHUNK, groups, LANES)


def outer_body(turn, plane, source, left, right, weights, partial, line, *rest):
    out, taps, scratch = rest[-3:]
    rows, groups, _ = source.shape
    fill_plane(taps, 0, source, left[0], right[0])
    for chunk in range(rows // CHUNK):
        start = chunk * CHUNK
        total = partial[0, start : start + CHUNK].reshape(CHUNK * groups, LANES)
        for tap_y in range(3):
            lhs = taps[0, start + tap_y : start + tap_y + CHUNK].reshape(CHUNK * groups, 256)
            total = total + jnp.dot(lhs, weights[0, tap_y], preferred_element_type=F32)
        put_rows(scratch, turn(total, line), chunk, groups)
    lay_out(scratch, out, 0, rows, groups)


def rectified(total, line):
    return jnp.maximum(total + line[...], 0.0)


def kept(total, line):
    return total


def lay_out(scratch, out, plane, rows, groups):
    pitch = groups + 1
    for group in range(groups):
        halves = [scratch[pl.ds(half * 8 * pitch + group, 8, stride=pitch), :] for half in range(2)]
        block = jnp.concatenate(halves, axis=0).astype(BF16)
        out[plane, :, group * LANES : (group + 1) * LANES] = block


def put_rows(scratch, total, chunk, groups):
    for row in range(CHUNK):
        at = (chunk * CHUNK + row) * (groups + 1)
        scratch[at : at + groups, :] = total[row * groups : (row + 1) * groups]


HALF = 112


def unpack_body(scaling, part, other, flag, grad_kernel, grad_bias, packed):
    upper = flag[...] > 0.5
    packed[:HALF] = jnp.where(upper, other[...], part[...])
    packed[HALF : 2 * HALF] = jnp.where(upper, part[...], other[...])
    for place in range(7):
        block = packed[place * 32 : place * 32 + 32, :] * scaling
        turned = block.T
        grad_kernel[place * 96 : place * 96 + 96, :] = turned[:96]
        if place < 6:
            grad_kernel[(21 + place) * 32 : (22 + place) * 32, :] = turned[96:]
        else:
            grad_bias[...] = pltpu.roll(block, 32, 1)[:1, :32]


def shifted(value, axis, step):
    count = lax.axis_size(axis)
    pairs = [(i, i + step) for i in range(count) if 0 <= i + step < count]
    return lax.ppermute(value, axis, pairs)


def swapped(value, bit):
    count = lax.axis_size("gz") * lax.axis_size("gy")
    return lax.ppermute(value, ("gz", "gy"), [(i, i ^ bit) for i in range(count)])


def sum_of_four(value, low, high):
    one, two, three = (swapped(value, bit) for bit in (low, high, low + high))
    return (value + one) + (two + three)


def local(activations, grad_out, relu_mask, kernel, bias):
    planes, rows, width = activations.shape
    groups = width // LANES
    block = activations.shape
    shape = jax.ShapeDtypeStruct
    pair = shape((2 * rows, groups, LANES), BF16)
    lines = shape((4, groups, LANES), BF16)
    spread = pltpu.VMEM((rows * (groups + 1) + 8, LANES), F32)
    two_taps = pltpu.VMEM((2, rows + 2, groups, 2 * LANES), BF16)
    half = shape((HALF, LANES), F32)
    packed = pltpu.VMEM((2 * HALF, LANES), F32)
    flag = jnp.full((1, LANES), lax.axis_index("gy") % 2, F32)

    low, high, firsts, lasts = pl.pallas_call(
        group_body,
        in_specs=[pl.BlockSpec(memory_space=pl.ANY)] * 3,
        out_shape=(pair, pair, lines, lines),
        scratch_shapes=[
            spread, pltpu.VMEM(block, BF16), pltpu.VMEM(block, BF16), pltpu.VMEM(block, jnp.int32),
            pltpu.SemaphoreType.DMA((2, 3)),
        ],
        compiler_params=pltpu.CompilerParams(vmem_limit_bytes=56 * MIB),
    )(activations, grad_out, relu_mask)
    below = shifted(high, "gz", 1)
    from_left = shifted(lasts, "gy", 1)
    from_right = shifted(firsts, "gy", -1)
    corner = shifted(jnp.concatenate([from_left[2:], from_right[2:]]), "gz", 1)

    edges, folded, bias_terms = blocked(
        local_terms_body,
        1,
        (shape((2, 2 * LANES, groups), BF16), shape((3, 3, 32, LANES), F32), shape((8, LANES), F32)),
        (
            part_of((2, 2 * LANES, groups), 0, 0, 0), part_of((3, 3, 32, LANES), 0, 0, 0, 0),
            part_of((8, LANES), 0, 0),
        ),
        [pltpu.VMEM((2 * LANES, rows * groups), BF16), two_taps],
        (low, high),
        [part_of(pair.shape, 0, 0, 0)] * 2,
    )

    plane = (rows, groups, LANES)
    line = jnp.tile(bias, 4).reshape(1, LANES)
    flat_kernel = kernel.reshape(27 * 32, 32)

    def inner(kind):
        return blocked(
            functools.partial(inner_body, kind == 1),
            rows // CHUNK,
            (shape((2, *plane), F32), shape((3, 3, 256, LANES), BF16)),
            (
                pl.BlockSpec((2, CHUNK, groups, LANES), lambda step: (0, step, 0, 0)),
                part_of((3, 3, 256, LANES), 0, 0, 0, 0),
            ),
            [two_taps],
            (low, high, from_left, from_right, flat_kernel),
            [part_of(plane, kind, 0, 0)] * 2
            + [part_of(lines.shape, 0, 0, 0)] * 2
            + [part_of(flat_kernel.shape, 0, 0)],
        )

    def outer(kind, side, source, edge, weights, partial, done=None):
        row = (1, groups, LANES)
        args = [source, edge, edge, weights, partial, line]
        first = 2 * rows if edge is source else 0
        specs = [
            part_of(plane, kind, 0, 0), part_of(row, first + kind, 0, 0), part_of(row, first + 2 + kind, 0, 0),
            part_of((1, 3, 256, LANES), 2 * side, 0, 0, 0), part_of((1, *plane), side, 0, 0, 0),
            part_of((1, LANES), 0, 0),
        ]
        if done is not None:
            args.append(done)
            specs.append(pl.BlockSpec(memory_space=pl.ANY))
        return blocked(
            functools.partial(outer_body, kept if kind else rectified, side),
            1,
            shape(block, BF16),
            part_of((1, *block[1:]), side, 0, 0),
            [pltpu.VMEM((1, rows + 2, groups, 2 * LANES), BF16), spread],
            args,
            specs,
            None if done is None else {6: 0},
        )

    partial_f, weights_f = inner(0)
    partial_g, weights_g = inner(1)

    ends = (from_left[:2], from_right[:2])
    ends, folded, partial_f, partial_g = lax.optimization_barrier((ends, folded, partial_f, partial_g))
    down = jnp.concatenate([low, *ends])
    down, below, corner = lax.optimization_barrier((down, below, corner))
    above = shifted(down, "gz", -1)

    part, send = call(
        kernel_grad_body,
        (half, half),
        [packed, two_taps, pltpu.VMEM((3, 3, LANES, 256), F32)],
        (below, low, from_left, from_right, edges, folded, bias_terms, flag),
    )
    output = outer(0, 0, below, corner, weights_f, partial_f)
    grad_input = outer(1, 0, below, corner, weights_g, partial_g)

    part = part + swapped(send, 1)
    part = sum_of_four(part, 4, 8)
    part = sum_of_four(part, 32, 64)
    part, above, output, grad_input = lax.optimization_barrier((part, above, output, grad_input))
    part = sum_of_four(part, 2, 16)
    output = outer(0, 1, above, above, weights_f, partial_f, output)
    grad_input = outer(1, 1, above, above, weights_g, partial_g, grad_input)
    part, output, grad_input = lax.optimization_barrier((part, output, grad_input))
    other = swapped(part, 1)

    voxels = planes * lax.axis_size("gz") * rows * lax.axis_size("gy") * (width // 32)
    grad_kernel, grad_bias = call(
        functools.partial(unpack_body, 1.0 / math.sqrt(voxels)),
        (shape((27 * 32, 32), F32), shape((1, 32), F32)),
        [packed],
        (part, other, flag),
    )
    return output, grad_input, grad_kernel.reshape(3, 3, 3, 32, 32), grad_bias.reshape(32)


def solution(mesh):
    block = P("gz", "gy", None)
    return jax.shard_map(
        local,
        mesh=mesh,
        in_specs=(block, block, block, P(), P()),
        out_specs=(block, block, P(), P()),
        check_vma=False,
    )
```

profile of v0, /device:TPU:1, one launch (start us, length us, event | category | flops | bytes accessed | tf_op | source)
XLA Modules:
  0.0 88.4 jit_solution(10730086688778783926)
XLA Ops:
  0.6 3.1 %shard_map.84 = (bf16[32,96,128]{2,1,0:T(8,128)(2,1)}, bf16[32,96,128]{2,1,0:T(8,128)(2,1)}, bf16[4,96,128]{2,1,0:T(8,128)(2,1)}, bf16[4,96,128]{2,1,0:T(8,128)(2,1)}) custom-call(bf16[2,16,12288]{2,1,0:T(8,128)(2,1)} %act_in.1, bf16[2,16,12288]{2,1,0:T(8,128)(2,1)} %grad_in.1, s32[2,16,12288]{2,1,0:T(8,128)} %mask_in.1), custom_call_target="tpu_custom_call" | custom-call | tf_op jit(solution)/shard_map/pallas_call | solution.py:310
  3.7 4.9 %collective-permute-start = (bf16[4,96,128]{2,1,0:T(8,128)(2,1)}, bf16[4,96,128]{2,1,0:T(8,128)(2,1)S(1)}, u32[]{:S(2)}, u32[]{:S(2)}) collective-permute-start(bf16[4,96,128]{2,1,0:T(8,128)(2,1)} %get-tuple-element.35), channel_id=1, source_target_pairs={{0,1},{1,2},{2,3},{3,4},{4,5},{5,6},{6,7},{7,8},{8,9},{9,10},{10,1... | collective-permute-start | bytes 294920 | tf_op jit(solution)/shard_map/ppermute | solution.py:284
  8.6 5.3 %collective-permute-start.2 = (bf16[32,96,128]{2,1,0:T(8,128)(2,1)}, bf16[32,96,128]{2,1,0:T(8,128)(2,1)S(1)}, u32[]{:S(2)}, u32[]{:S(2)}) collective-permute-start(bf16[32,96,128]{2,1,0:T(8,128)(2,1)} %get-tuple-element.37.high), channel_id=1, source_target_pairs={{0,16},{16,32},{32,48},{48,64},{64,80},{80,96},{96,112},{1,17},{17... | collective-permute-start | bytes 2359304 | tf_op jit(solution)/shard_map/ppermute | solution.py:284
  13.9 1.9 %collective-permute-start.1 = (bf16[4,96,128]{2,1,0:T(8,128)(2,1)}, bf16[4,96,128]{2,1,0:T(8,128)(2,1)S(1)}, u32[]{:S(2)}, u32[]{:S(2)}) collective-permute-start(bf16[4,96,128]{2,1,0:T(8,128)(2,1)} %get-tuple-element.36), channel_id=1, source_target_pairs={{1,0},{2,1},{3,2},{4,3},{5,4},{6,5},{7,6},{8,7},{9,8},{10,9},{11,1... | collective-permute-start | bytes 294920 | tf_op jit(solution)/shard_map/ppermute | solution.py:284
  15.8 4.4 %shard_map.85 = (bf16[2,256,96]{2,1,0:T(8,128)(2,1)}, f32[3,3,32,128]{3,2,1,0:T(8,128)}, f32[8,128]{1,0:T(8,128)}) custom-call(bf16[32,96,128]{2,1,0:T(8,128)(2,1)} %get-tuple-element.34.low, bf16[32,96,128]{2,1,0:T(8,128)(2,1)} %get-tuple-element.37.high), custom_call_target="tpu_custom_call" | custom-call | tf_op jit(solution)/shard_map/pallas_call | solution.py:27
  20.2 0.0 collective-permute-done.from_left
  20.2 13.3 %collective-permute-done.1.from_right = bf16[4,96,128]{2,1,0:T(8,128)(2,1)S(1)} collective-permute-done((bf16[4,96,128]{2,1,0:T(8,128)(2,1)}, bf16[4,96,128]{2,1,0:T(8,128)(2,1)S(1)}, u32[]{:S(2)}, u32[]{:S(2)}) %collective-permute-start.1) | collective-permute-done | bytes 98336 | tf_op jit(solution)/shard_map/ppermute | solution.py:284
  33.5 0.0 copy-start.4
  33.6 1.3 %collective-permute-start.3 = (bf16[4,96,128]{2,1,0:T(8,128)(2,1)S(1)}, bf16[4,96,128]{2,1,0:T(8,128)(2,1)S(1)}, u32[]{:S(2)}, u32[]{:S(2)}) collective-permute-start(bf16[4,96,128]{2,1,0:T(8,128)(2,1)S(1)} %pad_maximum_fusion.1), channel_id=1, source_target_pairs={{0,16},{16,32},{32,48},{48,64},{64,80},{80,96},{96,112},{1,17},{17... | collective-permute-start | bytes 294920 | tf_op jit(solution)/shard_map/ppermute | solution.py:284
  34.9 0.0 copy-done.2
  34.9 0.0 copy-done.4
  34.9 0.0 copy-start
  34.9 5.4 %shard_map.87 = (f32[2,16,96,128]{3,2,1,0:T(8,128)}, bf16[3,3,256,128]{3,2,1,0:T(8,128)(2,1)}) custom-call(bf16[32,96,128]{2,1,0:T(8,128)(2,1)} %get-tuple-element.34.low, bf16[32,96,128]{2,1,0:T(8,128)(2,1)} %get-tuple-element.37.high, bf16[4,96,128]{2,1,0:T(8,128)(2,1)} %copy-done.2, bf16[4,96,128]{2,1,0:T(8,128)(2,1)} %copy-done.4, bf16[864,32]{1,0:T(8,128)(2,1)} %bitcast.3), custom_call_target="tpu_custom_call" | custom-call | tf_op jit(solution)/shard_map/pallas_call | solution.py:27
  40.3 0.0 copy-start.3
  40.4 0.0 copy-start.6
  40.4 0.0 copy-start.7
  40.4 0.0 copy-start.8
  40.4 5.6 %shard_map.86 = (f32[2,16,96,128]{3,2,1,0:T(8,128)}, bf16[3,3,256,128]{3,2,1,0:T(8,128)(2,1)}) custom-call(bf16[32,96,128]{2,1,0:T(8,128)(2,1)} %get-tuple-element.34.low, bf16[32,96,128]{2,1,0:T(8,128)(2,1)} %get-tuple-element.37.high, bf16[4,96,128]{2,1,0:T(8,128)(2,1)} %copy-done.2, bf16[4,96,128]{2,1,0:T(8,128)(2,1)} %copy-done.4, bf16[864,32]{1,0:T(8,128)(2,1)} %bitcast.4), custom_call_target="tpu_custom_call" | custom-call | tf_op jit(solution)/shard_map/pallas_call | solution.py:27
  46.0 0.0 copy-done
  46.0 1.0 %pad_maximum_fusion = bf16[36,96,128]{2,1,0:T(8,128)(2,1)} fusion(bf16[2,96,128]{2,1,0:T(8,128)(2,1)S(1)} %get-tuple-element.42, bf16[2,96,128]{2,1,0:T(8,128)(2,1)S(1)} %get-tuple-element.41, bf16[32,96,128]{2,1,0:T(8,128)(2,1)S(1)} %copy-done), kind=kLoop, calls=%fused_computation | loop fusion | flops 884736 | bytes 1769472 | tf_op jit(solution)/shard_map/concatenate | solution.py:386
  47.0 0.0 collective-permute-done.3.left.right
  47.0 0.0 collective-permute-done.2.below.source
  47.1 0.0 copy-start.1
  47.1 1.3 %collective-permute-start.11 = (bf16[36,96,128]{2,1,0:T(8,128)(2,1)}, bf16[36,96,128]{2,1,0:T(8,128)(2,1)S(1)}, u32[]{:S(2)}, u32[]{:S(2)}) collective-permute-start(bf16[36,96,128]{2,1,0:T(8,128)(2,1)} %pad_maximum_fusion), channel_id=1, source_target_pairs={{16,0},{32,16},{48,32},{64,48},{80,64},{96,80},{112,96},{17,1},{33... | collective-permute-start | bytes 2654216 | tf_op jit(solution)/shard_map/ppermute | solution.py:284
  48.4 0.0 copy-done.3
  48.4 0.0 copy-done.5
  48.4 0.0 copy-done.6
  48.4 0.0 copy-done.7
  48.4 0.0 copy-done.8
  48.4 1.6 %shard_map.88 = (f32[112,128]{1,0:T(8,128)S(1)}, f32[112,128]{1,0:T(8,128)S(1)}) custom-call(bf16[32,96,128]{2,1,0:T(8,128)(2,1)S(1)} %collective-permute-done.2.below.source, bf16[32,96,128]{2,1,0:T(8,128)(2,1)S(1)} %copy-done, bf16[4,96,128]{2,1,0:T(8,128)(2,1)S(1)} %copy-done.3, bf16[4,96,128]{2,1,0:T(8,128)(2,1)S(1)} %copy-done.5, ...), custom_call_target="tpu_custom_call" | custom-call | tf_op jit(solution)/shard_map/pallas_call | solution.py:18
  50.1 0.1 collective-permute-start.4
  50.2 1.2 %collective-permute-done.4 = f32[112,128]{1,0:T(8,128)S(1)} collective-permute-done((f32[112,128]{1,0:T(8,128)S(1)}, f32[112,128]{1,0:T(8,128)S(1)}, u32[]{:S(2)}, u32[]{:S(2)}) %collective-permute-start.4) | collective-permute-done | bytes 57376 | tf_op jit(solution)/shard_map/ppermute | solution.py:289
  51.4 1.2 %collective-permute-start.7 = (f32[112,128]{1,0:T(8,128)S(1)}, f32[112,128]{1,0:T(8,128)S(1)}, u32[]{:S(2)}, u32[]{:S(2)}) collective-permute-start(f32[112,128]{1,0:T(8,128)S(1)} %add.35), channel_id=1, source_target_pairs={{0,12},{1,13},{2,14},{3,15},{4,8},{5,9},{6,10},{7,11},{8,4},{9,5},... | collective-permute-start | bytes 172040 | tf_op jit(solution)/shard_map/ppermute | solution.py:289
  52.6 1.9 %collective-permute-start.6 = (f32[112,128]{1,0:T(8,128)S(1)}, f32[112,128]{1,0:T(8,128)S(1)}, u32[]{:S(2)}, u32[]{:S(2)}) collective-permute-start(f32[112,128]{1,0:T(8,128)S(1)} %add.35), channel_id=1, source_target_pairs={{0,8},{1,9},{2,10},{3,11},{4,12},{5,13},{6,14},{7,15},{8,0},{9,1},... | collective-permute-start | bytes 172040 | tf_op jit(solution)/shard_map/ppermute | solution.py:289
  54.6 0.2 collective-permute-start.5
  54.8 1.4 %collective-permute-done.7 = f32[112,128]{1,0:T(8,128)S(1)} collective-permute-done((f32[112,128]{1,0:T(8,128)S(1)}, f32[112,128]{1,0:T(8,128)S(1)}, u32[]{:S(2)}, u32[]{:S(2)}) %collective-permute-start.7) | collective-permute-done | bytes 57376 | tf_op jit(solution)/shard_map/ppermute | solution.py:289
  56.2 1.0 %collective-permute-done.6 = f32[112,128]{1,0:T(8,128)S(1)} collective-permute-done((f32[112,128]{1,0:T(8,128)S(1)}, f32[112,128]{1,0:T(8,128)S(1)}, u32[]{:S(2)}, u32[]{:S(2)}) %collective-permute-start.6) | collective-permute-done | bytes 57376 | tf_op jit(solution)/shard_map/ppermute | solution.py:289
  57.2 0.9 %collective-permute-done.5 = f32[112,128]{1,0:T(8,128)S(1)} collective-permute-done((f32[112,128]{1,0:T(8,128)S(1)}, f32[112,128]{1,0:T(8,128)S(1)}, u32[]{:S(2)}, u32[]{:S(2)}) %collective-permute-start.5) | collective-permute-done | bytes 57376 | tf_op jit(solution)/shard_map/ppermute | solution.py:289
  58.1 7.9 %collective-permute-start.10 = (f32[112,128]{1,0:T(8,128)S(1)}, f32[112,128]{1,0:T(8,128)S(1)}, u32[]{:S(2)}, u32[]{:S(2)}) collective-permute-start(f32[112,128]{1,0:T(8,128)S(1)} %add_add_fusion.2), channel_id=1, source_target_pairs={{0,96},{1,97},{2,98},{3,99},{4,100},{5,101},{6,102},{7,103},{8,104... | collective-permute-start | bytes 172040 | tf_op jit(solution)/shard_map/ppermute | solution.py:289
  66.0 0.3 collective-permute-start.9
  66.4 0.3 collective-permute-start.8
  66.7 0.0 copy-done.11
  66.7 0.6 reshape_tile.3.line
  67.3 0.0 copy-done.10
  67.3 0.0 copy-done.1
  67.3 3.2 %shard_map.90.rest_0_ = bf16[2,16,12288]{2,1,0:T(8,128)(2,1)} custom-call(bf16[32,96,128]{2,1,0:T(8,128)(2,1)} %copy-done.1, bf16[4,96,128]{2,1,0:T(8,128)(2,1)} %copy-done.10, bf16[4,96,128]{2,1,0:T(8,128)(2,1)} %copy-done.10, bf16[3,3,256,128]{3,2,1,0:T(8,128)(2,1)} %get-tuple-element.53.weights, f32[2,16,96,128]{3,2,1,0:T(8,128)} %get-tuple-element.54.partial, ...), custom_call_target="tpu_custom_call" | custom-call | tf_op jit(solution)/shard_map/pallas_call | solution.py:27
  70.5 3.2 %shard_map.89.rest_0_ = bf16[2,16,12288]{2,1,0:T(8,128)(2,1)} custom-call(bf16[32,96,128]{2,1,0:T(8,128)(2,1)} %copy-done.1, bf16[4,96,128]{2,1,0:T(8,128)(2,1)} %copy-done.10, bf16[4,96,128]{2,1,0:T(8,128)(2,1)} %copy-done.10, bf16[3,3,256,128]{3,2,1,0:T(8,128)(2,1)} %get-tuple-element.51.weights, f32[2,16,96,128]{3,2,1,0:T(8,128)} %get-tuple-element.52.partial, ...), custom_call_target="tpu_custom_call" | custom-call | tf_op jit(solution)/shard_map/pallas_call | solution.py:27
  73.8 0.0 collective-permute-done.10
  73.8 0.0 collective-permute-done.9
  73.8 0.0 collective-permute-done.8
  73.8 0.0 collective-permute-done.11.source.left.right
  73.8 0.0 copy-start.9
  73.8 0.7 collective-permute-start.14
  74.5 1.7 %collective-permute-start.13 = (f32[112,128]{1,0:T(8,128)S(1)}, f32[112,128]{1,0:T(8,128)S(1)}, u32[]{:S(2)}, u32[]{:S(2)}) collective-permute-start(f32[112,128]{1,0:T(8,128)S(1)} %add_add_fusion.1), channel_id=1, source_target_pairs={{0,16},{1,17},{2,18},{3,19},{4,20},{5,21},{6,22},{7,23},{8,24},{9,... | collective-permute-start | bytes 172040 | tf_op jit(solution)/shard_map/ppermute | solution.py:289
  76.2 1.0 %collective-permute-start.12 = (f32[112,128]{1,0:T(8,128)S(1)}, f32[112,128]{1,0:T(8,128)S(1)}, u32[]{:S(2)}, u32[]{:S(2)}) collective-permute-start(f32[112,128]{1,0:T(8,128)S(1)} %add_add_fusion.1), channel_id=1, source_target_pairs={{0,2},{1,3},{2,0},{3,1},{4,6},{5,7},{6,4},{7,5},{8,10},{9,11},{10,... | collective-permute-start | bytes 172040 | tf_op jit(solution)/shard_map/ppermute | solution.py:289
  77.1 0.0 copy-done.9
  77.2 3.2 %shard_map.92 = bf16[2,16,12288]{2,1,0:T(8,128)(2,1)} custom-call(bf16[36,96,128]{2,1,0:T(8,128)(2,1)} %copy-done.9, bf16[36,96,128]{2,1,0:T(8,128)(2,1)} %copy-done.9, bf16[36,96,128]{2,1,0:T(8,128)(2,1)} %copy-done.9, bf16[3,3,256,128]{3,2,1,0:T(8,128)(2,1)} %get-tuple-element.53.weights, ...), custom_call_target="tpu_custom_call", output_to_operand_aliasing={{}: (6, {})} | custom-call | tf_op jit(solution)/shard_map/pallas_call | solution.py:27
  80.4 3.2 %shard_map.91 = bf16[2,16,12288]{2,1,0:T(8,128)(2,1)} custom-call(bf16[36,96,128]{2,1,0:T(8,128)(2,1)} %copy-done.9, bf16[36,96,128]{2,1,0:T(8,128)(2,1)} %copy-done.9, bf16[36,96,128]{2,1,0:T(8,128)(2,1)} %copy-done.9, bf16[3,3,256,128]{3,2,1,0:T(8,128)(2,1)} %get-tuple-element.51.weights, ...), custom_call_target="tpu_custom_call", output_to_operand_aliasing={{}: (6, {})} | custom-call | tf_op jit(solution)/shard_map/pallas_call | solution.py:27
  83.6 0.0 collective-permute-done.14
  83.6 0.0 collective-permute-done.13
  83.6 0.0 collective-permute-done.12
  83.7 2.9 %collective-permute-start.15 = (f32[112,128]{1,0:T(8,128)S(1)}, f32[112,128]{1,0:T(8,128)S(1)}, u32[]{:S(2)}, u32[]{:S(2)}) collective-permute-start(f32[112,128]{1,0:T(8,128)S(1)} %add_add_fusion.part), channel_id=1, source_target_pairs={{0,1},{1,0},{2,3},{3,2},{4,5},{5,4},{6,7},{7,6},{8,9},{9,8},{10,11... | collective-permute-start | bytes 172040 | tf_op jit(solution)/shard_map/ppermute | solution.py:289
  86.6 0.9 %collective-permute-done.15.other = f32[112,128]{1,0:T(8,128)S(1)} collective-permute-done((f32[112,128]{1,0:T(8,128)S(1)}, f32[112,128]{1,0:T(8,128)S(1)}, u32[]{:S(2)}, u32[]{:S(2)}) %collective-permute-start.15) | collective-permute-done | bytes 57376 | tf_op jit(solution)/shard_map/ppermute | solution.py:289
  87.5 1.0 %shard_map.93 = (f32[864,32]{1,0:T(8,128)}, f32[1,32]{1,0:T(1,128)}) custom-call(f32[112,128]{1,0:T(8,128)S(1)} %add_add_fusion.part, f32[112,128]{1,0:T(8,128)S(1)} %collective-permute-done.15.other, f32[1,128]{1,0:T(1,128)S(1)} %broadcast_in_dim.3.flag), custom_call_target="tpu_custom_call" | custom-call | tf_op jit(solution)/shard_map/pallas_call | solution.py:18
  (13 shorter events, 0.1 us)
Async XLA Ops:
  3.7 16.5 %collective-permute-start = (bf16[4,96,128]{2,1,0:T(8,128)(2,1)}, bf16[4,96,128]{2,1,0:T(8,128)(2,1)S(1)}, u32[]{:S(2)}, u32[]{:S(2)}) collective-permute-start(bf16[4,96,128]{2,1,0:T(8,128)(2,1)} %get-tuple-element.35), channel_id=1, source_target_pairs={{0,1},{1,2},{2,3},{3,4},{4,5},{5,6},{6,7},{7,8},{8,9},{9,10},{10,1... | collective-permute-start | bytes 294920 | tf_op jit(solution)/shard_map/ppermute | solution.py:284
  8.6 38.4 %collective-permute-start.2 = (bf16[32,96,128]{2,1,0:T(8,128)(2,1)}, bf16[32,96,128]{2,1,0:T(8,128)(2,1)S(1)}, u32[]{:S(2)}, u32[]{:S(2)}) collective-permute-start(bf16[32,96,128]{2,1,0:T(8,128)(2,1)} %get-tuple-element.37.high), channel_id=1, source_target_pairs={{0,16},{16,32},{32,48},{48,64},{64,80},{80,96},{96,112},{1,17},{17... | collective-permute-start | bytes 2359304 | tf_op jit(solution)/shard_map/ppermute | solution.py:284
  13.9 19.6 %collective-permute-start.1 = (bf16[4,96,128]{2,1,0:T(8,128)(2,1)}, bf16[4,96,128]{2,1,0:T(8,128)(2,1)S(1)}, u32[]{:S(2)}, u32[]{:S(2)}) collective-permute-start(bf16[4,96,128]{2,1,0:T(8,128)(2,1)} %get-tuple-element.36), channel_id=1, source_target_pairs={{1,0},{2,1},{3,2},{4,3},{5,4},{6,5},{7,6},{8,7},{9,8},{10,9},{11,1... | collective-permute-start | bytes 294920 | tf_op jit(solution)/shard_map/ppermute | solution.py:284
  20.2 14.7 %copy-start.2 = (bf16[4,96,128]{2,1,0:T(8,128)(2,1)}, bf16[4,96,128]{2,1,0:T(8,128)(2,1)S(1)}, u32[]{:S(2)}) copy-start(bf16[4,96,128]{2,1,0:T(8,128)(2,1)S(1)} %collective-permute-done.from_left) | copy-start | bytes 294916
  33.5 1.3 %copy-start.4 = (bf16[4,96,128]{2,1,0:T(8,128)(2,1)}, bf16[4,96,128]{2,1,0:T(8,128)(2,1)S(1)}, u32[]{:S(2)}) copy-start(bf16[4,96,128]{2,1,0:T(8,128)(2,1)S(1)} %collective-permute-done.1.from_right) | copy-start | bytes 294916
  33.6 13.5 %collective-permute-start.3 = (bf16[4,96,128]{2,1,0:T(8,128)(2,1)S(1)}, bf16[4,96,128]{2,1,0:T(8,128)(2,1)S(1)}, u32[]{:S(2)}, u32[]{:S(2)}) collective-permute-start(bf16[4,96,128]{2,1,0:T(8,128)(2,1)S(1)} %pad_maximum_fusion.1), channel_id=1, source_target_pairs={{0,16},{16,32},{32,48},{48,64},{64,80},{80,96},{96,112},{1,17},{17... | collective-permute-start | bytes 294920 | tf_op jit(solution)/shard_map/ppermute | solution.py:284
  34.9 11.1 %copy-start = (bf16[32,96,128]{2,1,0:T(8,128)(2,1)S(1)}, bf16[32,96,128]{2,1,0:T(8,128)(2,1)}, u32[]{:S(2)}) copy-start(bf16[32,96,128]{2,1,0:T(8,128)(2,1)} %get-tuple-element.34.low) | copy-start | bytes 2359300
  40.3 8.0 %copy-start.3 = (bf16[4,96,128]{2,1,0:T(8,128)(2,1)S(1)}, bf16[4,96,128]{2,1,0:T(8,128)(2,1)}, u32[]{:S(2)}) copy-start(bf16[4,96,128]{2,1,0:T(8,128)(2,1)} %copy-done.2) | copy-start | bytes 294916
  40.3 8.1 %copy-start.5 = (bf16[4,96,128]{2,1,0:T(8,128)(2,1)S(1)}, bf16[4,96,128]{2,1,0:T(8,128)(2,1)}, u32[]{:S(2)}) copy-start(bf16[4,96,128]{2,1,0:T(8,128)(2,1)} %copy-done.4) | copy-start | bytes 294916
  40.4 8.1 %copy-start.6 = (f32[3,3,32,128]{3,2,1,0:T(8,128)S(1)}, f32[3,3,32,128]{3,2,1,0:T(8,128)}, u32[]{:S(2)}) copy-start(f32[3,3,32,128]{3,2,1,0:T(8,128)} %get-tuple-element.45.folded) | copy-start | bytes 442372
  40.4 8.1 %copy-start.7 = (bf16[2,256,96]{2,1,0:T(8,128)(2,1)S(1)}, bf16[2,256,96]{2,1,0:T(8,128)(2,1)}, u32[]{:S(2)}) copy-start(bf16[2,256,96]{2,1,0:T(8,128)(2,1)} %get-tuple-element.44.edges) | copy-start | bytes 294916
  40.4 8.1 %copy-start.8 = (f32[8,128]{1,0:T(8,128)S(1)}, f32[8,128]{1,0:T(8,128)}, u32[]{:S(2)}) copy-start(f32[8,128]{1,0:T(8,128)} %get-tuple-element.46.bias_terms) | copy-start | bytes 12292
  47.0 19.6 %copy-start.11 = (f32[32]{0:T(128)S(1)}, f32[32]{0:T(128)}, u32[]{:S(2)}) copy-start(f32[32]{0:T(128)} %param.9) | copy-start | bytes 388
  47.0 20.2 %copy-start.10 = (bf16[4,96,128]{2,1,0:T(8,128)(2,1)}, bf16[4,96,128]{2,1,0:T(8,128)(2,1)S(1)}, u32[]{:S(2)}) copy-start(bf16[4,96,128]{2,1,0:T(8,128)(2,1)S(1)} %collective-permute-done.3.left.right) | copy-start | bytes 294916
  47.1 20.2 %copy-start.1 = (bf16[32,96,128]{2,1,0:T(8,128)(2,1)}, bf16[32,96,128]{2,1,0:T(8,128)(2,1)S(1)}, u32[]{:S(2)}) copy-start(bf16[32,96,128]{2,1,0:T(8,128)(2,1)S(1)} %collective-permute-done.2.below.source) | copy-start | bytes 2359300
  47.1 26.7 %collective-permute-start.11 = (bf16[36,96,128]{2,1,0:T(8,128)(2,1)}, bf16[36,96,128]{2,1,0:T(8,128)(2,1)S(1)}, u32[]{:S(2)}, u32[]{:S(2)}) collective-permute-start(bf16[36,96,128]{2,1,0:T(8,128)(2,1)} %pad_maximum_fusion), channel_id=1, source_target_pairs={{16,0},{32,16},{48,32},{64,48},{80,64},{96,80},{112,96},{17,1},{33... | collective-permute-start | bytes 2654216 | tf_op jit(solution)/shard_map/ppermute | solution.py:284
  50.1 1.3 %collective-permute-start.4 = (f32[112,128]{1,0:T(8,128)S(1)}, f32[112,128]{1,0:T(8,128)S(1)}, u32[]{:S(2)}, u32[]{:S(2)}) collective-permute-start(f32[112,128]{1,0:T(8,128)S(1)} %get-tuple-element.48), channel_id=1, source_target_pairs={{0,1},{1,0},{2,3},{3,2},{4,5},{5,4},{6,7},{7,6},{8,9},{9,8},{10,11... | collective-permute-start | bytes 172040 | tf_op jit(solution)/shard_map/ppermute | solution.py:289
  51.4 4.8 %collective-permute-start.7 = (f32[112,128]{1,0:T(8,128)S(1)}, f32[112,128]{1,0:T(8,128)S(1)}, u32[]{:S(2)}, u32[]{:S(2)}) collective-permute-start(f32[112,128]{1,0:T(8,128)S(1)} %add.35), channel_id=1, source_target_pairs={{0,12},{1,13},{2,14},{3,15},{4,8},{5,9},{6,10},{7,11},{8,4},{9,5},... | collective-permute-start | bytes 172040 | tf_op jit(solution)/shard_map/ppermute | solution.py:289
  52.6 4.5 %collective-permute-start.6 = (f32[112,128]{1,0:T(8,128)S(1)}, f32[112,128]{1,0:T(8,128)S(1)}, u32[]{:S(2)}, u32[]{:S(2)}) collective-permute-start(f32[112,128]{1,0:T(8,128)S(1)} %add.35), channel_id=1, source_target_pairs={{0,8},{1,9},{2,10},{3,11},{4,12},{5,13},{6,14},{7,15},{8,0},{9,1},... | collective-permute-start | bytes 172040 | tf_op jit(solution)/shard_map/ppermute | solution.py:289
  54.6 3.5 %collective-permute-start.5 = (f32[112,128]{1,0:T(8,128)S(1)}, f32[112,128]{1,0:T(8,128)S(1)}, u32[]{:S(2)}, u32[]{:S(2)}) collective-permute-start(f32[112,128]{1,0:T(8,128)S(1)} %add.35), channel_id=1, source_target_pairs={{0,4},{1,5},{2,6},{3,7},{4,0},{5,1},{6,2},{7,3},{8,12},{9,13},{10,... | collective-permute-start | bytes 172040 | tf_op jit(solution)/shard_map/ppermute | solution.py:289
  58.1 15.6 %collective-permute-start.10 = (f32[112,128]{1,0:T(8,128)S(1)}, f32[112,128]{1,0:T(8,128)S(1)}, u32[]{:S(2)}, u32[]{:S(2)}) collective-permute-start(f32[112,128]{1,0:T(8,128)S(1)} %add_add_fusion.2), channel_id=1, source_target_pairs={{0,96},{1,97},{2,98},{3,99},{4,100},{5,101},{6,102},{7,103},{8,104... | collective-permute-start | bytes 172040 | tf_op jit(solution)/shard_map/ppermute | solution.py:289
  66.0 7.7 %collective-permute-start.9 = (f32[112,128]{1,0:T(8,128)S(1)}, f32[112,128]{1,0:T(8,128)S(1)}, u32[]{:S(2)}, u32[]{:S(2)}) collective-permute-start(f32[112,128]{1,0:T(8,128)S(1)} %add_add_fusion.2), channel_id=1, source_target_pairs={{0,64},{1,65},{2,66},{3,67},{4,68},{5,69},{6,70},{7,71},{8,72},{9,... | collective-permute-start | bytes 172040 | tf_op jit(solution)/shard_map/ppermute | solution.py:289
  66.4 7.4 %collective-permute-start.8 = (f32[112,128]{1,0:T(8,128)S(1)}, f32[112,128]{1,0:T(8,128)S(1)}, u32[]{:S(2)}, u32[]{:S(2)}) collective-permute-start(f32[112,128]{1,0:T(8,128)S(1)} %add_add_fusion.2), channel_id=1, source_target_pairs={{0,32},{1,33},{2,34},{3,35},{4,36},{5,37},{6,38},{7,39},{8,40},{9,... | collective-permute-start | bytes 172040 | tf_op jit(solution)/shard_map/ppermute | solution.py:289
  73.8 3.3 %copy-start.9 = (bf16[36,96,128]{2,1,0:T(8,128)(2,1)}, bf16[36,96,128]{2,1,0:T(8,128)(2,1)S(1)}, u32[]{:S(2)}) copy-start(bf16[36,96,128]{2,1,0:T(8,128)(2,1)S(1)} %collective-permute-done.11.source.left.right) | copy-start | bytes 2654212
  73.8 9.8 %collective-permute-start.14 = (f32[112,128]{1,0:T(8,128)S(1)}, f32[112,128]{1,0:T(8,128)S(1)}, u32[]{:S(2)}, u32[]{:S(2)}) collective-permute-start(f32[112,128]{1,0:T(8,128)S(1)} %add_add_fusion.1), channel_id=1, source_target_pairs={{0,18},{1,19},{2,16},{3,17},{4,22},{5,23},{6,20},{7,21},{8,26},{9,... | collective-permute-start | bytes 172040 | tf_op jit(solution)/shard_map/ppermute | solution.py:289
  74.5 9.1 %collective-permute-start.13 = (f32[112,128]{1,0:T(8,128)S(1)}, f32[112,128]{1,0:T(8,128)S(1)}, u32[]{:S(2)}, u32[]{:S(2)}) collective-permute-start(f32[112,128]{1,0:T(8,128)S(1)} %add_add_fusion.1), channel_id=1, source_target_pairs={{0,16},{1,17},{2,18},{3,19},{4,20},{5,21},{6,22},{7,23},{8,24},{9,... | collective-permute-start | bytes 172040 | tf_op jit(solution)/shard_map/ppermute | solution.py:289
  76.2 7.4 %collective-permute-start.12 = (f32[112,128]{1,0:T(8,128)S(1)}, f32[112,128]{1,0:T(8,128)S(1)}, u32[]{:S(2)}, u32[]{:S(2)}) collective-permute-start(f32[112,128]{1,0:T(8,128)S(1)} %add_add_fusion.1), channel_id=1, source_target_pairs={{0,2},{1,3},{2,0},{3,1},{4,6},{5,7},{6,4},{7,5},{8,10},{9,11},{10,... | collective-permute-start | bytes 172040 | tf_op jit(solution)/shard_map/ppermute | solution.py:289
  83.7 3.8 %collective-permute-start.15 = (f32[112,128]{1,0:T(8,128)S(1)}, f32[112,128]{1,0:T(8,128)S(1)}, u32[]{:S(2)}, u32[]{:S(2)}) collective-permute-start(f32[112,128]{1,0:T(8,128)S(1)} %add_add_fusion.part), channel_id=1, source_target_pairs={{0,1},{1,0},{2,3},{3,2},{4,5},{5,4},{6,7},{7,6},{8,9},{9,8},{10,11... | collective-permute-start | bytes 172040 | tf_op jit(solution)/shard_map/ppermute | solution.py:289
where the time goes:
time: 88.8 us; the launch traced here: 88.4 us
  Pallas kernels  34 us (38%)
  starting transfers between devices  33 us (37%)
  waiting for transfers between devices  18.7 us (21%)
  other arithmetic  1.1 us (1%)
  between operations  0.9 us (1%)
    pallas_call x7, Pallas kernels, blocked(): pl.pallas_call(body, grid=(grid,), out_shape=outs, in_specs=in_specs, out...  28.4 us
    ppermute x11, starting transfers between devices, swapped(): lax.ppermute(value, ('gz', 'gy'), [(i, i ^ bit) for i in range(count)])  18.3 us
    ppermute x5, starting transfers between devices, shifted(): return lax.ppermute(value, axis, pairs)  14.7 us
    ppermute x5, waiting for transfers between devices, shifted(): return lax.ppermute(value, axis, pairs)  13.3 us
    ppermute x11, waiting for transfers between devices, swapped(): lax.ppermute(value, ('gz', 'gy'), [(i, i ^ bit) for i in range(count)])  5.43 us
    pallas_call x1, Pallas kernels, local(): pl.pallas_call(group_body, in_specs=[pl.BlockSpec(memory_space=pl.ANY)] *...  3.05 us
    pallas_call x2, Pallas kernels, call(): pl.pallas_call(body, out_shape=outs, scratch_shapes=scratch, compiler_par...  2.61 us
  transfers between devices with their start and end apart: 16, of which 6 were waited for; matrix products, arithmetic and copies ran while one was open for 2% of the time, Pallas kernels for 34%

commit v1 on v0

--- a/solution.py
+++ b/solution.py
@@ -157,11 +157,11 @@
 def kernel_grad_body(
     below, low, from_left, from_right, edges, folded, bias_terms, flag, keep, send, packed, taps, sums
 ):
-    rows, groups = below.shape[0] // 2, below.shape[1]
+    rows, groups = low.shape[0] // 2, low.shape[1]
     blank = jnp.zeros((groups, LANES), BF16)
     fill_plane(taps, 0, below.at[:rows], blank, blank)
     fill_plane(taps, 1, low.at[:rows], blank, blank)
-    below_turned = below[rows:].reshape(rows * groups, LANES).T
+    below_turned = below[rows : 2 * rows].reshape(rows * groups, LANES).T
     low_turned = low[rows:].reshape(rows * groups, LANES).T
     sums[1] = jnp.zeros(sums.shape[1:], F32)
     for tap_y in range(3):
@@ -317,10 +317,9 @@
         ],
         compiler_params=pltpu.CompilerParams(vmem_limit_bytes=56 * MIB),
     )(activations, grad_out, relu_mask)
-    below = shifted(high, "gz", 1)
     from_left = shifted(lasts, "gy", 1)
     from_right = shifted(firsts, "gy", -1)
-    corner = shifted(jnp.concatenate([from_left[2:], from_right[2:]]), "gz", 1)
+    below = shifted(jnp.concatenate([high, from_left[2:], from_right[2:]]), "gz", 1)
 
     edges, folded, bias_terms = blocked(
         local_terms_body,
@@ -384,7 +383,7 @@
     ends = (from_left[:2], from_right[:2])
     ends, folded, partial_f, partial_g = lax.optimization_barrier((ends, folded, partial_f, partial_g))
     down = jnp.concatenate([low, *ends])
-    down, below, corner = lax.optimization_barrier((down, below, corner))
+    down, below = lax.optimization_barrier((down, below))
     above = shifted(down, "gz", -1)
 
     part, send = call(
@@ -393,18 +392,18 @@
         [packed, two_taps, pltpu.VMEM((3, 3, LANES, 256), F32)],
         (below, low, from_left, from_right, edges, folded, bias_terms, flag),
     )
-    output = outer(0, 0, below, corner, weights_f, partial_f)
-    grad_input = outer(1, 0, below, corner, weights_g, partial_g)
-
     part = part + swapped(send, 1)
     part = sum_of_four(part, 4, 8)
+    output = outer(0, 0, below, below, weights_f, partial_f)
+    part, output = lax.optimization_barrier((part, output))
     part = sum_of_four(part, 32, 64)
-    part, above, output, grad_input = lax.optimization_barrier((part, above, output, grad_input))
+    grad_input = outer(1, 0, below, below, weights_g, partial_g)
+    part, above, grad_input = lax.optimization_barrier((part, above, grad_input))
     part = sum_of_four(part, 2, 16)
     output = outer(0, 1, above, above, weights_f, partial_f, output)
+    part, output = lax.optimization_barrier((part, output))
+    other = swapped(part, 1)
     grad_input = outer(1, 1, above, above, weights_g, partial_g, grad_input)
-    part, output, grad_input = lax.optimization_barrier((part, output, grad_input))
-    other = swapped(part, 1)
 
     voxels = planes * lax.axis_size("gz") * rows * lax.axis_size("gy") * (width // 32)
     grad_kernel, grad_bias = call(

time: 88.8 us -> 82.4 us (0.928); the launches traced: 88.4 us -> 80.9 us
  waiting for transfers between devices: 18.7 us -> 8.93 us
  other arithmetic: 1.1 us -> 2.37 us
  starting transfers between devices: 33 us -> 34 us
    ppermute x5 -> x4, waiting for transfers between devices: 13.3 us -> 4.72 us  [shifted(): return lax.ppermute(value, axis, pairs)]
    ppermute x11, starting transfers between devices: 18.3 us -> 20.6 us  [swapped(): lax.ppermute(value, ('gz', 'gy'), [(i, i ^ bit) for i in range(count)])]
    ppermute x5 -> x4, starting transfers between devices: 14.7 us -> 13.4 us  [shifted(): return lax.ppermute(value, axis, pairs)]
    concatenate x1, other arithmetic: 0.01 us -> 1.29 us  [local(): jnp.concatenate([high, from_left[2:], from_right[2:]])]
    ppermute x11, waiting for transfers between devices: 5.43 us -> 4.21 us  [swapped(): lax.ppermute(value, ('gz', 'gy'), [(i, i ^ bit) for i in range(count)])]
  transfers between devices with their start and end apart: 16 -> 15, of which waited for: 6 -> 7; matrix products, arithmetic and copies ran while one was open for 2% -> 2% of each run, Pallas kernels for 34% -> 37%
where the time goes in v1:
time: 82.4 us; the launch traced here: 80.9 us
  Pallas kernels  34.1 us (41%)
  starting transfers between devices  34 us (41%)
  waiting for transfers between devices  8.93 us (11%)
  other arithmetic  2.37 us (3%)
  between operations  0.85 us (1%)
    pallas_call x7, Pallas kernels, blocked(): pl.pallas_call(body, grid=(grid,), out_shape=outs, in_specs=in_specs, out...  28.4 us
    ppermute x11, starting transfers between devices, swapped(): lax.ppermute(value, ('gz', 'gy'), [(i, i ^ bit) for i in range(count)])  20.6 us
    ppermute x4, starting transfers between devices, shifted(): return lax.ppermute(value, axis, pairs)  13.4 us
    ppermute x4, waiting for transfers between devices, shifted(): return lax.ppermute(value, axis, pairs)  4.72 us
    ppermute x11, waiting for transfers between devices, swapped(): lax.ppermute(value, ('gz', 'gy'), [(i, i ^ bit) for i in range(count)])  4.21 us
    pallas_call x1, Pallas kernels, local(): pl.pallas_call(group_body, in_specs=[pl.BlockSpec(memory_space=pl.ANY)] *...  3.06 us
    pallas_call x2, Pallas kernels, call(): pl.pallas_call(body, out_shape=outs, scratch_shapes=scratch, compiler_par...  2.62 us
  transfers between devices with their start and end apart: 15, of which 7 were waited for; matrix products, arithmetic and copies ran while one was open for 2% of the time, Pallas kernels for 37%

profile of v1, /device:TPU:1, one launch (start us, length us, event | category | flops | bytes accessed | tf_op | source)
XLA Modules:
  0.0 80.9 jit_solution(7891068963179855524)
XLA Ops:
  0.6 3.1 %shard_map.84 = (bf16[32,96,128]{2,1,0:T(8,128)(2,1)}, bf16[32,96,128]{2,1,0:T(8,128)(2,1)}, bf16[4,96,128]{2,1,0:T(8,128)(2,1)}, bf16[4,96,128]{2,1,0:T(8,128)(2,1)}) custom-call(bf16[2,16,12288]{2,1,0:T(8,128)(2,1)} %act_in.1, bf16[2,16,12288]{2,1,0:T(8,128)(2,1)} %grad_in.1, s32[2,16,12288]{2,1,0:T(8,128)} %mask_in.1), custom_call_target="tpu_custom_call" | custom-call | tf_op jit(solution)/shard_map/pallas_call | solution.py:310
  3.7 4.9 %collective-permute-start = (bf16[4,96,128]{2,1,0:T(8,128)(2,1)}, bf16[4,96,128]{2,1,0:T(8,128)(2,1)S(1)}, u32[]{:S(2)}, u32[]{:S(2)}) collective-permute-start(bf16[4,96,128]{2,1,0:T(8,128)(2,1)} %get-tuple-element.34), channel_id=1, source_target_pairs={{0,1},{1,2},{2,3},{3,4},{4,5},{5,6},{6,7},{7,8},{8,9},{9,10},{10,1... | collective-permute-start | bytes 294920 | tf_op jit(solution)/shard_map/ppermute | solution.py:284
  8.6 1.9 %collective-permute-start.1 = (bf16[4,96,128]{2,1,0:T(8,128)(2,1)}, bf16[4,96,128]{2,1,0:T(8,128)(2,1)S(1)}, u32[]{:S(2)}, u32[]{:S(2)}) collective-permute-start(bf16[4,96,128]{2,1,0:T(8,128)(2,1)} %get-tuple-element.35), channel_id=1, source_target_pairs={{1,0},{2,1},{3,2},{4,3},{5,4},{6,5},{7,6},{8,7},{9,8},{10,9},{11,1... | collective-permute-start | bytes 294920 | tf_op jit(solution)/shard_map/ppermute | solution.py:284
  10.6 0.0 collective-permute-done.from_left
  10.6 0.0 copy-start.2
  10.6 4.2 %collective-permute-done.1.from_right = bf16[4,96,128]{2,1,0:T(8,128)(2,1)S(1)} collective-permute-done((bf16[4,96,128]{2,1,0:T(8,128)(2,1)}, bf16[4,96,128]{2,1,0:T(8,128)(2,1)S(1)}, u32[]{:S(2)}, u32[]{:S(2)}) %collective-permute-start.1) | collective-permute-done | bytes 98336 | tf_op jit(solution)/shard_map/ppermute | solution.py:284
  14.8 0.0 copy-start.4
  14.8 1.3 %pad_maximum_fusion.1 = bf16[36,96,128]{2,1,0:T(8,128)(2,1)S(1)} fusion(bf16[2,96,128]{2,1,0:T(8,128)(2,1)S(1)} %get-tuple-element.64, bf16[2,96,128]{2,1,0:T(8,128)(2,1)S(1)} %get-tuple-element.62, bf16[32,96,128]{2,1,0:T(8,128)(2,1)} %get-tuple-element.36.high), kind=kLoop, calls=%fused_computation.1 | loop fusion | flops 884736 | bytes 1769472 | tf_op jit(solution)/shard_map/concatenate | solution.py:322
  16.1 5.3 %collective-permute-start.2 = (bf16[36,96,128]{2,1,0:T(8,128)(2,1)S(1)}, bf16[36,96,128]{2,1,0:T(8,128)(2,1)S(1)}, u32[]{:S(2)}, u32[]{:S(2)}) collective-permute-start(bf16[36,96,128]{2,1,0:T(8,128)(2,1)S(1)} %pad_maximum_fusion.1), channel_id=1, source_target_pairs={{0,16},{16,32},{32,48},{48,64},{64,80},{80,96},{96,112},{1,17},{17... | collective-permute-start | bytes 2654216 | tf_op jit(solution)/shard_map/ppermute | solution.py:284
  21.4 4.4 %shard_map.85 = (bf16[2,256,96]{2,1,0:T(8,128)(2,1)}, f32[3,3,32,128]{3,2,1,0:T(8,128)}, f32[8,128]{1,0:T(8,128)}) custom-call(bf16[32,96,128]{2,1,0:T(8,128)(2,1)} %get-tuple-element.33.low, bf16[32,96,128]{2,1,0:T(8,128)(2,1)} %get-tuple-element.36.high), custom_call_target="tpu_custom_call" | custom-call | tf_op jit(solution)/shard_map/pallas_call | solution.py:27
  25.7 0.0 copy-done.2
  25.8 0.0 copy-done.4
  25.8 0.0 copy-start.1
  25.8 5.5 %shard_map.87 = (f32[2,16,96,128]{3,2,1,0:T(8,128)}, bf16[3,3,256,128]{3,2,1,0:T(8,128)(2,1)}) custom-call(bf16[32,96,128]{2,1,0:T(8,128)(2,1)} %get-tuple-element.33.low, bf16[32,96,128]{2,1,0:T(8,128)(2,1)} %get-tuple-element.36.high, bf16[4,96,128]{2,1,0:T(8,128)(2,1)} %copy-done.2, bf16[4,96,128]{2,1,0:T(8,128)(2,1)} %copy-done.4, bf16[864,32]{1,0:T(8,128)(2,1)} %bitcast.3), custom_call_target="tpu_custom_call" | custom-call | tf_op jit(solution)/shard_map/pallas_call | solution.py:27
  31.2 0.0 copy-start.3
  31.2 0.0 copy-start.5
  31.3 0.0 copy-start.6
  31.3 0.0 copy-start.7
  31.3 0.0 copy-start.8
  31.3 5.6 %shard_map.86 = (f32[2,16,96,128]{3,2,1,0:T(8,128)}, bf16[3,3,256,128]{3,2,1,0:T(8,128)(2,1)}) custom-call(bf16[32,96,128]{2,1,0:T(8,128)(2,1)} %get-tuple-element.33.low, bf16[32,96,128]{2,1,0:T(8,128)(2,1)} %get-tuple-element.36.high, bf16[4,96,128]{2,1,0:T(8,128)(2,1)} %copy-done.2, bf16[4,96,128]{2,1,0:T(8,128)(2,1)} %copy-done.4, bf16[864,32]{1,0:T(8,128)(2,1)} %bitcast.4), custom_call_target="tpu_custom_call" | custom-call | tf_op jit(solution)/shard_map/pallas_call | solution.py:27
  36.9 0.0 copy-done.1
  36.9 1.0 %pad_maximum_fusion = bf16[36,96,128]{2,1,0:T(8,128)(2,1)} fusion(bf16[2,96,128]{2,1,0:T(8,128)(2,1)S(1)} %get-tuple-element.41, bf16[2,96,128]{2,1,0:T(8,128)(2,1)S(1)} %get-tuple-element.40, bf16[32,96,128]{2,1,0:T(8,128)(2,1)S(1)} %copy-done.1), kind=kLoop, calls=%fused_computation | loop fusion | flops 884736 | bytes 1769472 | tf_op jit(solution)/shard_map/concatenate | solution.py:385
  38.0 0.0 copy-start.10
  38.0 0.5 collective-permute-done.2.below.source.left.right
  38.5 1.3 %collective-permute-start.10 = (bf16[36,96,128]{2,1,0:T(8,128)(2,1)}, bf16[36,96,128]{2,1,0:T(8,128)(2,1)S(1)}, u32[]{:S(2)}, u32[]{:S(2)}) collective-permute-start(bf16[36,96,128]{2,1,0:T(8,128)(2,1)} %pad_maximum_fusion), channel_id=1, source_target_pairs={{16,0},{32,16},{48,32},{64,48},{80,64},{96,80},{112,96},{17,1},{33... | collective-permute-start | bytes 2654216 | tf_op jit(solution)/shard_map/ppermute | solution.py:284
  39.8 0.0 copy-done.3
  39.8 0.0 copy-done.5
  39.8 0.0 copy-done.6
  39.8 0.0 copy-done.7
  39.8 0.0 copy-done.8
  39.8 1.6 %shard_map.88 = (f32[112,128]{1,0:T(8,128)S(1)}, f32[112,128]{1,0:T(8,128)S(1)}) custom-call(bf16[36,96,128]{2,1,0:T(8,128)(2,1)S(1)} %collective-permute-done.2.below.source.left.right, bf16[32,96,128]{2,1,0:T(8,128)(2,1)S(1)} %copy-done.1, bf16[4,96,128]{2,1,0:T(8,128)(2,1)S(1)} %copy-done.3, bf16[4,96,128]{2,1,0:T(8,128)(2,1)S(1)} %copy-done.5, ...), custom_call_target="tpu_custom_call" | custom-call | tf_op jit(solution)/shard_map/pallas_call | solution.py:18
  41.5 0.1 collective-permute-start.3
  41.6 1.2 %collective-permute-done.3 = f32[112,128]{1,0:T(8,128)S(1)} collective-permute-done((f32[112,128]{1,0:T(8,128)S(1)}, f32[112,128]{1,0:T(8,128)S(1)}, u32[]{:S(2)}, u32[]{:S(2)}) %collective-permute-start.3) | collective-permute-done | bytes 57376 | tf_op jit(solution)/shard_map/ppermute | solution.py:289
  42.8 4.8 %collective-permute-start.6 = (f32[112,128]{1,0:T(8,128)S(1)}, f32[112,128]{1,0:T(8,128)S(1)}, u32[]{:S(2)}, u32[]{:S(2)}) collective-permute-start(f32[112,128]{1,0:T(8,128)S(1)} %add.35), channel_id=1, source_target_pairs={{0,12},{1,13},{2,14},{3,15},{4,8},{5,9},{6,10},{7,11},{8,4},{9,5},... | collective-permute-start | bytes 172040 | tf_op jit(solution)/shard_map/ppermute | solution.py:289
  47.7 0.5 collective-permute-start.5
  48.2 0.1 collective-permute-start.4
  48.3 0.0 copy-done.10
  48.3 0.6 reshape_tile.3.line
  48.9 0.0 copy-done
  48.9 3.2 %shard_map.89.rest_0_ = bf16[2,16,12288]{2,1,0:T(8,128)(2,1)} custom-call(bf16[36,96,128]{2,1,0:T(8,128)(2,1)} %copy-done, bf16[36,96,128]{2,1,0:T(8,128)(2,1)} %copy-done, bf16[36,96,128]{2,1,0:T(8,128)(2,1)} %copy-done, bf16[3,3,256,128]{3,2,1,0:T(8,128)(2,1)} %get-tuple-element.48.weights, f32[2,16,96,128]{3,2,1,0:T(8,128)} %get-tuple-element.49.partial, ...), custom_call_target="tpu_custom_call" | custom-call | tf_op jit(solution)/shard_map/pallas_call | solution.py:27
  52.2 0.0 collective-permute-done.6
  52.2 0.3 collective-permute-done.5
  52.5 0.0 collective-permute-done.4
  52.5 7.6 %collective-permute-start.9 = (f32[112,128]{1,0:T(8,128)S(1)}, f32[112,128]{1,0:T(8,128)S(1)}, u32[]{:S(2)}, u32[]{:S(2)}) collective-permute-start(f32[112,128]{1,0:T(8,128)S(1)} %add_add_fusion.2), channel_id=1, source_target_pairs={{0,96},{1,97},{2,98},{3,99},{4,100},{5,101},{6,102},{7,103},{8,104... | collective-permute-start | bytes 172040 | tf_op jit(solution)/shard_map/ppermute | solution.py:289
  60.1 0.1 collective-permute-start.8
  60.2 0.6 collective-permute-start.7
  60.8 3.2 %shard_map.90.rest_0_ = bf16[2,16,12288]{2,1,0:T(8,128)(2,1)} custom-call(bf16[36,96,128]{2,1,0:T(8,128)(2,1)} %copy-done, bf16[36,96,128]{2,1,0:T(8,128)(2,1)} %copy-done, bf16[36,96,128]{2,1,0:T(8,128)(2,1)} %copy-done, bf16[3,3,256,128]{3,2,1,0:T(8,128)(2,1)} %get-tuple-element.52.weights, f32[2,16,96,128]{3,2,1,0:T(8,128)} %get-tuple-element.53.partial, ...), custom_call_target="tpu_custom_call" | custom-call | tf_op jit(solution)/shard_map/pallas_call | solution.py:27
  64.0 0.0 collective-permute-done.9
  64.0 0.6 collective-permute-done.8
  64.6 1.9 %collective-permute-done.7 = f32[112,128]{1,0:T(8,128)S(1)} collective-permute-done((f32[112,128]{1,0:T(8,128)S(1)}, f32[112,128]{1,0:T(8,128)S(1)}, u32[]{:S(2)}, u32[]{:S(2)}) %collective-permute-start.7) | collective-permute-done | bytes 57376 | tf_op jit(solution)/shard_map/ppermute | solution.py:289
  66.6 0.0 collective-permute-done.10.source.left.right
  66.6 0.0 copy-start.9
  66.6 2.8 %collective-permute-start.13 = (f32[112,128]{1,0:T(8,128)S(1)}, f32[112,128]{1,0:T(8,128)S(1)}, u32[]{:S(2)}, u32[]{:S(2)}) collective-permute-start(f32[112,128]{1,0:T(8,128)S(1)} %add_add_fusion.1), channel_id=1, source_target_pairs={{0,18},{1,19},{2,16},{3,17},{4,22},{5,23},{6,20},{7,21},{8,26},{9,... | collective-permute-start | bytes 172040 | tf_op jit(solution)/shard_map/ppermute | solution.py:289
  69.5 2.0 %collective-permute-start.12 = (f32[112,128]{1,0:T(8,128)S(1)}, f32[112,128]{1,0:T(8,128)S(1)}, u32[]{:S(2)}, u32[]{:S(2)}) collective-permute-start(f32[112,128]{1,0:T(8,128)S(1)} %add_add_fusion.1), channel_id=1, source_target_pairs={{0,16},{1,17},{2,18},{3,19},{4,20},{5,21},{6,22},{7,23},{8,24},{9,... | collective-permute-start | bytes 172040 | tf_op jit(solution)/shard_map/ppermute | solution.py:289
  71.5 0.0 collective-permute-start.11
  71.5 0.0 copy-done.9
  71.5 3.2 %shard_map.91 = bf16[2,16,12288]{2,1,0:T(8,128)(2,1)} custom-call(bf16[36,96,128]{2,1,0:T(8,128)(2,1)} %copy-done.9, bf16[36,96,128]{2,1,0:T(8,128)(2,1)} %copy-done.9, bf16[36,96,128]{2,1,0:T(8,128)(2,1)} %copy-done.9, bf16[3,3,256,128]{3,2,1,0:T(8,128)(2,1)} %get-tuple-element.48.weights, ...), custom_call_target="tpu_custom_call", output_to_operand_aliasing={{}: (6, {})} | custom-call | tf_op jit(solution)/shard_map/pallas_call | solution.py:27
  74.7 0.0 collective-permute-done.13
  74.7 0.0 collective-permute-done.12
  74.7 0.1 collective-permute-done.11
  74.8 1.9 %collective-permute-start.14 = (f32[112,128]{1,0:T(8,128)S(1)}, f32[112,128]{1,0:T(8,128)S(1)}, u32[]{:S(2)}, u32[]{:S(2)}) collective-permute-start(f32[112,128]{1,0:T(8,128)S(1)} %add_add_fusion.part), channel_id=1, source_target_pairs={{0,1},{1,0},{2,3},{3,2},{4,5},{5,4},{6,7},{7,6},{8,9},{9,8},{10,11... | collective-permute-start | bytes 172040 | tf_op jit(solution)/shard_map/ppermute | solution.py:289
  76.7 3.2 %shard_map.92 = bf16[2,16,12288]{2,1,0:T(8,128)(2,1)} custom-call(bf16[36,96,128]{2,1,0:T(8,128)(2,1)} %copy-done.9, bf16[36,96,128]{2,1,0:T(8,128)(2,1)} %copy-done.9, bf16[36,96,128]{2,1,0:T(8,128)(2,1)} %copy-done.9, bf16[3,3,256,128]{3,2,1,0:T(8,128)(2,1)} %get-tuple-element.52.weights, ...), custom_call_target="tpu_custom_call", output_to_operand_aliasing={{}: (6, {})} | custom-call | tf_op jit(solution)/shard_map/pallas_call | solution.py:27
  79.9 0.0 collective-permute-done.14.other
  79.9 1.0 %shard_map.93 = (f32[864,32]{1,0:T(8,128)}, f32[1,32]{1,0:T(1,128)}) custom-call(f32[112,128]{1,0:T(8,128)S(1)} %add_add_fusion.part, f32[112,128]{1,0:T(8,128)S(1)} %collective-permute-done.14.other, f32[1,128]{1,0:T(1,128)S(1)} %broadcast_in_dim.3.flag), custom_call_target="tpu_custom_call" | custom-call | tf_op jit(solution)/shard_map/pallas_call | solution.py:18
  (9 shorter events, 0.1 us)
Async XLA Ops:
  3.7 6.9 %collective-permute-start = (bf16[4,96,128]{2,1,0:T(8,128)(2,1)}, bf16[4,96,128]{2,1,0:T(8,128)(2,1)S(1)}, u32[]{:S(2)}, u32[]{:S(2)}) collective-permute-start(bf16[4,96,128]{2,1,0:T(8,128)(2,1)} %get-tuple-element.34), channel_id=1, source_target_pairs={{0,1},{1,2},{2,3},{3,4},{4,5},{5,6},{6,7},{7,8},{8,9},{9,10},{10,1... | collective-permute-start | bytes 294920 | tf_op jit(solution)/shard_map/ppermute | solution.py:284
  8.6 6.1 %collective-permute-start.1 = (bf16[4,96,128]{2,1,0:T(8,128)(2,1)}, bf16[4,96,128]{2,1,0:T(8,128)(2,1)S(1)}, u32[]{:S(2)}, u32[]{:S(2)}) collective-permute-start(bf16[4,96,128]{2,1,0:T(8,128)(2,1)} %get-tuple-element.35), channel_id=1, source_target_pairs={{1,0},{2,1},{3,2},{4,3},{5,4},{6,5},{7,6},{8,7},{9,8},{10,9},{11,1... | collective-permute-start | bytes 294920 | tf_op jit(solution)/shard_map/ppermute | solution.py:284
  10.6 15.2 %copy-start.2 = (bf16[4,96,128]{2,1,0:T(8,128)(2,1)}, bf16[4,96,128]{2,1,0:T(8,128)(2,1)S(1)}, u32[]{:S(2)}) copy-start(bf16[4,96,128]{2,1,0:T(8,128)(2,1)S(1)} %collective-permute-done.from_left) | copy-start | bytes 294916
  14.8 11.0 %copy-start.4 = (bf16[4,96,128]{2,1,0:T(8,128)(2,1)}, bf16[4,96,128]{2,1,0:T(8,128)(2,1)S(1)}, u32[]{:S(2)}) copy-start(bf16[4,96,128]{2,1,0:T(8,128)(2,1)S(1)} %collective-permute-done.1.from_right) | copy-start | bytes 294916
  16.1 22.4 %collective-permute-start.2 = (bf16[36,96,128]{2,1,0:T(8,128)(2,1)S(1)}, bf16[36,96,128]{2,1,0:T(8,128)(2,1)S(1)}, u32[]{:S(2)}, u32[]{:S(2)}) collective-permute-start(bf16[36,96,128]{2,1,0:T(8,128)(2,1)S(1)} %pad_maximum_fusion.1), channel_id=1, source_target_pairs={{0,16},{16,32},{32,48},{48,64},{64,80},{80,96},{96,112},{1,17},{17... | collective-permute-start | bytes 2654216 | tf_op jit(solution)/shard_map/ppermute | solution.py:284
  25.8 11.2 %copy-start.1 = (bf16[32,96,128]{2,1,0:T(8,128)(2,1)S(1)}, bf16[32,96,128]{2,1,0:T(8,128)(2,1)}, u32[]{:S(2)}) copy-start(bf16[32,96,128]{2,1,0:T(8,128)(2,1)} %get-tuple-element.33.low) | copy-start | bytes 2359300
  31.2 8.6 %copy-start.3 = (bf16[4,96,128]{2,1,0:T(8,128)(2,1)S(1)}, bf16[4,96,128]{2,1,0:T(8,128)(2,1)}, u32[]{:S(2)}) copy-start(bf16[4,96,128]{2,1,0:T(8,128)(2,1)} %copy-done.2) | copy-start | bytes 294916
  31.2 8.6 %copy-start.5 = (bf16[4,96,128]{2,1,0:T(8,128)(2,1)S(1)}, bf16[4,96,128]{2,1,0:T(8,128)(2,1)}, u32[]{:S(2)}) copy-start(bf16[4,96,128]{2,1,0:T(8,128)(2,1)} %copy-done.4) | copy-start | bytes 294916
  31.3 8.6 %copy-start.6 = (f32[3,3,32,128]{3,2,1,0:T(8,128)S(1)}, f32[3,3,32,128]{3,2,1,0:T(8,128)}, u32[]{:S(2)}) copy-start(f32[3,3,32,128]{3,2,1,0:T(8,128)} %get-tuple-element.44.folded) | copy-start | bytes 442372
  31.3 8.6 %copy-start.7 = (bf16[2,256,96]{2,1,0:T(8,128)(2,1)S(1)}, bf16[2,256,96]{2,1,0:T(8,128)(2,1)}, u32[]{:S(2)}) copy-start(bf16[2,256,96]{2,1,0:T(8,128)(2,1)} %get-tuple-element.43.edges) | copy-start | bytes 294916
  31.3 8.6 %copy-start.8 = (f32[8,128]{1,0:T(8,128)S(1)}, f32[8,128]{1,0:T(8,128)}, u32[]{:S(2)}) copy-start(f32[8,128]{1,0:T(8,128)} %get-tuple-element.45.bias_terms) | copy-start | bytes 12292
  38.0 10.4 %copy-start.10 = (f32[32]{0:T(128)S(1)}, f32[32]{0:T(128)}, u32[]{:S(2)}) copy-start(f32[32]{0:T(128)} %param.9) | copy-start | bytes 388
  38.5 10.4 %copy-start = (bf16[36,96,128]{2,1,0:T(8,128)(2,1)}, bf16[36,96,128]{2,1,0:T(8,128)(2,1)S(1)}, u32[]{:S(2)}) copy-start(bf16[36,96,128]{2,1,0:T(8,128)(2,1)S(1)} %collective-permute-done.2.below.source.left.right) | copy-start | bytes 2654212
  38.5 28.1 %collective-permute-start.10 = (bf16[36,96,128]{2,1,0:T(8,128)(2,1)}, bf16[36,96,128]{2,1,0:T(8,128)(2,1)S(1)}, u32[]{:S(2)}, u32[]{:S(2)}) collective-permute-start(bf16[36,96,128]{2,1,0:T(8,128)(2,1)} %pad_maximum_fusion), channel_id=1, source_target_pairs={{16,0},{32,16},{48,32},{64,48},{80,64},{96,80},{112,96},{17,1},{33... | collective-permute-start | bytes 2654216 | tf_op jit(solution)/shard_map/ppermute | solution.py:284
  41.5 1.3 %collective-permute-start.3 = (f32[112,128]{1,0:T(8,128)S(1)}, f32[112,128]{1,0:T(8,128)S(1)}, u32[]{:S(2)}, u32[]{:S(2)}) collective-permute-start(f32[112,128]{1,0:T(8,128)S(1)} %get-tuple-element.47), channel_id=1, source_target_pairs={{0,1},{1,0},{2,3},{3,2},{4,5},{5,4},{6,7},{7,6},{8,9},{9,8},{10,11... | collective-permute-start | bytes 172040 | tf_op jit(solution)/shard_map/ppermute | solution.py:289
  42.8 9.3 %collective-permute-start.6 = (f32[112,128]{1,0:T(8,128)S(1)}, f32[112,128]{1,0:T(8,128)S(1)}, u32[]{:S(2)}, u32[]{:S(2)}) collective-permute-start(f32[112,128]{1,0:T(8,128)S(1)} %add.35), channel_id=1, source_target_pairs={{0,12},{1,13},{2,14},{3,15},{4,8},{5,9},{6,10},{7,11},{8,4},{9,5},... | collective-permute-start | bytes 172040 | tf_op jit(solution)/shard_map/ppermute | solution.py:289
  47.7 4.8 %collective-permute-start.5 = (f32[112,128]{1,0:T(8,128)S(1)}, f32[112,128]{1,0:T(8,128)S(1)}, u32[]{:S(2)}, u32[]{:S(2)}) collective-permute-start(f32[112,128]{1,0:T(8,128)S(1)} %add.35), channel_id=1, source_target_pairs={{0,8},{1,9},{2,10},{3,11},{4,12},{5,13},{6,14},{7,15},{8,0},{9,1},... | collective-permute-start | bytes 172040 | tf_op jit(solution)/shard_map/ppermute | solution.py:289
  48.2 4.3 %collective-permute-start.4 = (f32[112,128]{1,0:T(8,128)S(1)}, f32[112,128]{1,0:T(8,128)S(1)}, u32[]{:S(2)}, u32[]{:S(2)}) collective-permute-start(f32[112,128]{1,0:T(8,128)S(1)} %add.35), channel_id=1, source_target_pairs={{0,4},{1,5},{2,6},{3,7},{4,0},{5,1},{6,2},{7,3},{8,12},{9,13},{10,... | collective-permute-start | bytes 172040 | tf_op jit(solution)/shard_map/ppermute | solution.py:289
  52.5 11.5 %collective-permute-start.9 = (f32[112,128]{1,0:T(8,128)S(1)}, f32[112,128]{1,0:T(8,128)S(1)}, u32[]{:S(2)}, u32[]{:S(2)}) collective-permute-start(f32[112,128]{1,0:T(8,128)S(1)} %add_add_fusion.2), channel_id=1, source_target_pairs={{0,96},{1,97},{2,98},{3,99},{4,100},{5,101},{6,102},{7,103},{8,104... | collective-permute-start | bytes 172040 | tf_op jit(solution)/shard_map/ppermute | solution.py:289
  60.1 4.5 %collective-permute-start.8 = (f32[112,128]{1,0:T(8,128)S(1)}, f32[112,128]{1,0:T(8,128)S(1)}, u32[]{:S(2)}, u32[]{:S(2)}) collective-permute-start(f32[112,128]{1,0:T(8,128)S(1)} %add_add_fusion.2), channel_id=1, source_target_pairs={{0,64},{1,65},{2,66},{3,67},{4,68},{5,69},{6,70},{7,71},{8,72},{9,... | collective-permute-start | bytes 172040 | tf_op jit(solution)/shard_map/ppermute | solution.py:289
  60.2 6.4 %collective-permute-start.7 = (f32[112,128]{1,0:T(8,128)S(1)}, f32[112,128]{1,0:T(8,128)S(1)}, u32[]{:S(2)}, u32[]{:S(2)}) collective-permute-start(f32[112,128]{1,0:T(8,128)S(1)} %add_add_fusion.2), channel_id=1, source_target_pairs={{0,32},{1,33},{2,34},{3,35},{4,36},{5,37},{6,38},{7,39},{8,40},{9,... | collective-permute-start | bytes 172040 | tf_op jit(solution)/shard_map/ppermute | solution.py:289
  66.6 4.9 %copy-start.9 = (bf16[36,96,128]{2,1,0:T(8,128)(2,1)}, bf16[36,96,128]{2,1,0:T(8,128)(2,1)S(1)}, u32[]{:S(2)}) copy-start(bf16[36,96,128]{2,1,0:T(8,128)(2,1)S(1)} %collective-permute-done.10.source.left.right) | copy-start | bytes 2654212
  66.6 8.1 %collective-permute-start.13 = (f32[112,128]{1,0:T(8,128)S(1)}, f32[112,128]{1,0:T(8,128)S(1)}, u32[]{:S(2)}, u32[]{:S(2)}) collective-permute-start(f32[112,128]{1,0:T(8,128)S(1)} %add_add_fusion.1), channel_id=1, source_target_pairs={{0,18},{1,19},{2,16},{3,17},{4,22},{5,23},{6,20},{7,21},{8,26},{9,... | collective-permute-start | bytes 172040 | tf_op jit(solution)/shard_map/ppermute | solution.py:289
  69.5 5.3 %collective-permute-start.12 = (f32[112,128]{1,0:T(8,128)S(1)}, f32[112,128]{1,0:T(8,128)S(1)}, u32[]{:S(2)}, u32[]{:S(2)}) collective-permute-start(f32[112,128]{1,0:T(8,128)S(1)} %add_add_fusion.1), channel_id=1, source_target_pairs={{0,16},{1,17},{2,18},{3,19},{4,20},{5,21},{6,22},{7,23},{8,24},{9,... | collective-permute-start | bytes 172040 | tf_op jit(solution)/shard_map/ppermute | solution.py:289
  71.5 3.3 %collective-permute-start.11 = (f32[112,128]{1,0:T(8,128)S(1)}, f32[112,128]{1,0:T(8,128)S(1)}, u32[]{:S(2)}, u32[]{:S(2)}) collective-permute-start(f32[112,128]{1,0:T(8,128)S(1)} %add_add_fusion.1), channel_id=1, source_target_pairs={{0,2},{1,3},{2,0},{3,1},{4,6},{5,7},{6,4},{7,5},{8,10},{9,11},{10,... | collective-permute-start | bytes 172040 | tf_op jit(solution)/shard_map/ppermute | solution.py:289
  74.8 5.1 %collective-permute-start.14 = (f32[112,128]{1,0:T(8,128)S(1)}, f32[112,128]{1,0:T(8,128)S(1)}, u32[]{:S(2)}, u32[]{:S(2)}) collective-permute-start(f32[112,128]{1,0:T(8,128)S(1)} %add_add_fusion.part), channel_id=1, source_target_pairs={{0,1},{1,0},{2,3},{3,2},{4,5},{5,4},{6,7},{7,6},{8,9},{9,8},{10,11... | collective-permute-start | bytes 172040 | tf_op jit(solution)/shard_map/ppermute | solution.py:289

commit v2 on v1

--- a/solution.py
+++ b/solution.py
@@ -23,7 +23,7 @@
     )(*args)
 
 
-def blocked(body, grid, outs, out_specs, scratch, args, in_specs, aliases=None):
+def blocked(body, grid, outs, out_specs, scratch, args, in_specs, aliases=None, flops=0):
     return pl.pallas_call(
         body,
         grid=(grid,),
@@ -32,6 +32,7 @@
         out_specs=out_specs,
         scratch_shapes=scratch,
         input_output_aliases=aliases or {},
+        cost_estimate=pl.CostEstimate(flops=flops, bytes_accessed=0, transcendentals=0),
         compiler_params=pltpu.CompilerParams(vmem_limit_bytes=56 * MIB),
     )(*args)
 
@@ -157,11 +158,11 @@
 def kernel_grad_body(
     below, low, from_left, from_right, edges, folded, bias_terms, flag, keep, send, packed, taps, sums
 ):
-    rows, groups = low.shape[0] // 2, low.shape[1]
+    rows, groups = below.shape[0] // 2, below.shape[1]
     blank = jnp.zeros((groups, LANES), BF16)
     fill_plane(taps, 0, below.at[:rows], blank, blank)
     fill_plane(taps, 1, low.at[:rows], blank, blank)
-    below_turned = below[rows : 2 * rows].reshape(rows * groups, LANES).T
+    below_turned = below[rows:].reshape(rows * groups, LANES).T
     low_turned = low[rows:].reshape(rows * groups, LANES).T
     sums[1] = jnp.zeros(sums.shape[1:], F32)
     for tap_y in range(3):
@@ -319,7 +320,8 @@
     )(activations, grad_out, relu_mask)
     from_left = shifted(lasts, "gy", 1)
     from_right = shifted(firsts, "gy", -1)
-    below = shifted(jnp.concatenate([high, from_left[2:], from_right[2:]]), "gz", 1)
+    below = shifted(high, "gz", 1)
+    corner = shifted(jnp.concatenate([from_left[2:], from_right[2:]]), "gz", 1)
 
     edges, folded, bias_terms = blocked(
         local_terms_body,
@@ -332,6 +334,7 @@
         [pltpu.VMEM((2 * LANES, rows * groups), BF16), two_taps],
         (low, high),
         [part_of(pair.shape, 0, 0, 0)] * 2,
+        flops=0,
     )
 
     plane = (rows, groups, LANES)
@@ -383,7 +386,7 @@
     ends = (from_left[:2], from_right[:2])
     ends, folded, partial_f, partial_g = lax.optimization_barrier((ends, folded, partial_f, partial_g))
     down = jnp.concatenate([low, *ends])
-    down, below = lax.optimization_barrier((down, below))
+    down, corner = lax.optimization_barrier((down, corner))
     above = shifted(down, "gz", -1)
 
     part, send = call(
@@ -394,10 +397,10 @@
     )
     part = part + swapped(send, 1)
     part = sum_of_four(part, 4, 8)
-    output = outer(0, 0, below, below, weights_f, partial_f)
+    output = outer(0, 0, below, corner, weights_f, partial_f)
     part, output = lax.optimization_barrier((part, output))
     part = sum_of_four(part, 32, 64)
-    grad_input = outer(1, 0, below, below, weights_g, partial_g)
+    grad_input = outer(1, 0, below, corner, weights_g, partial_g)
     part, above, grad_input = lax.optimization_barrier((part, above, grad_input))
     part = sum_of_four(part, 2, 16)
     output = outer(0, 1, above, above, weights_f, partial_f, output)

time: 82.4 us -> 76.8 us (0.932); the launches traced: 80.9 us -> 76.4 us
  waiting for transfers between devices: 8.93 us -> 5.37 us
  other arithmetic: 2.37 us -> 1.09 us
    ppermute x4 -> x5, waiting for transfers between devices: 4.72 us -> 0.01 us  [shifted(): return lax.ppermute(value, axis, pairs)]
    ppermute x4 -> x5, starting transfers between devices: 13.4 us -> 16.1 us  [shifted(): return lax.ppermute(value, axis, pairs)]
    ppermute x11, starting transfers between devices: 20.6 us -> 18.2 us  [swapped(): lax.ppermute(value, ('gz', 'gy'), [(i, i ^ bit) for i in range(count)])]
    concatenate x1, other arithmetic: 1.29 us -> 0.01 us  [local(): corner = shifted(jnp.concatenate([from_left[2:], from_right[2:]]), 'gz', 1)]
    ppermute x11, waiting for transfers between devices: 4.21 us -> 5.36 us  [swapped(): lax.ppermute(value, ('gz', 'gy'), [(i, i ^ bit) for i in range(count)])]
  transfers between devices with their start and end apart: 15 -> 16, of which waited for: 7 -> 4; matrix products, arithmetic and copies ran while one was open for 2% -> 2% of each run, Pallas kernels for 37% -> 39%
where the time goes in v2:
time: 76.8 us; the launch traced here: 76.4 us
  starting transfers between devices  34.3 us (45%)
  Pallas kernels  34 us (44%)
  waiting for transfers between devices  5.37 us (7%)
  other arithmetic  1.09 us (1%)
  between operations  0.92 us (1%)
    pallas_call x7, Pallas kernels, blocked(): pl.pallas_call(body, grid=(grid,), out_shape=outs, in_specs=in_specs, out...  28.4 us
    ppermute x11, starting transfers between devices, swapped(): lax.ppermute(value, ('gz', 'gy'), [(i, i ^ bit) for i in range(count)])  18.2 us
    ppermute x5, starting transfers between devices, shifted(): return lax.ppermute(value, axis, pairs)  16.1 us
    ppermute x11, waiting for transfers between devices, swapped(): lax.ppermute(value, ('gz', 'gy'), [(i, i ^ bit) for i in range(count)])  5.36 us
    pallas_call x1, Pallas kernels, local(): pl.pallas_call(group_body, in_specs=[pl.BlockSpec(memory_space=pl.ANY)] *...  3.05 us
    pallas_call x2, Pallas kernels, call(): pl.pallas_call(body, out_shape=outs, scratch_shapes=scratch, compiler_par...  2.62 us
  transfers between devices with their start and end apart: 16, of which 4 were waited for; matrix products, arithmetic and copies ran while one was open for 2% of the time, Pallas kernels for 39%

profile of v2, /device:TPU:1, one launch (start us, length us, event | category | flops | bytes accessed | tf_op | source)
XLA Modules:
  0.0 76.4 jit_solution(1199068396876317272)
XLA Ops:
  0.6 3.1 %shard_map.84 = (bf16[32,96,128]{2,1,0:T(8,128)(2,1)}, bf16[32,96,128]{2,1,0:T(8,128)(2,1)}, bf16[4,96,128]{2,1,0:T(8,128)(2,1)}, bf16[4,96,128]{2,1,0:T(8,128)(2,1)}) custom-call(bf16[2,16,12288]{2,1,0:T(8,128)(2,1)} %act_in.1, bf16[2,16,12288]{2,1,0:T(8,128)(2,1)} %grad_in.1, s32[2,16,12288]{2,1,0:T(8,128)} %mask_in.1), custom_call_target="tpu_custom_call" | custom-call | tf_op jit(solution)/shard_map/pallas_call | solution.py:311
  3.7 4.9 %collective-permute-start.1 = (bf16[4,96,128]{2,1,0:T(8,128)(2,1)}, bf16[4,96,128]{2,1,0:T(8,128)(2,1)S(1)}, u32[]{:S(2)}, u32[]{:S(2)}) collective-permute-start(bf16[4,96,128]{2,1,0:T(8,128)(2,1)} %get-tuple-element.35), channel_id=1, source_target_pairs={{0,1},{1,2},{2,3},{3,4},{4,5},{5,6},{6,7},{7,8},{8,9},{9,10},{10,1... | collective-permute-start | bytes 294920 | tf_op jit(solution)/shard_map/ppermute | solution.py:285
  8.6 1.9 %collective-permute-start.2 = (bf16[4,96,128]{2,1,0:T(8,128)(2,1)}, bf16[4,96,128]{2,1,0:T(8,128)(2,1)S(1)}, u32[]{:S(2)}, u32[]{:S(2)}) collective-permute-start(bf16[4,96,128]{2,1,0:T(8,128)(2,1)} %get-tuple-element.36), channel_id=1, source_target_pairs={{1,0},{2,1},{3,2},{4,3},{5,4},{6,5},{7,6},{8,7},{9,8},{10,9},{11,1... | collective-permute-start | bytes 294920 | tf_op jit(solution)/shard_map/ppermute | solution.py:285
  10.6 5.3 %collective-permute-start = (bf16[32,96,128]{2,1,0:T(8,128)(2,1)}, bf16[32,96,128]{2,1,0:T(8,128)(2,1)S(1)}, u32[]{:S(2)}, u32[]{:S(2)}) collective-permute-start(bf16[32,96,128]{2,1,0:T(8,128)(2,1)} %get-tuple-element.33.high), channel_id=1, source_target_pairs={{0,16},{16,32},{32,48},{48,64},{64,80},{80,96},{96,112},{1,17},{17... | collective-permute-start | bytes 2359304 | tf_op jit(solution)/shard_map/ppermute | solution.py:285
  15.8 4.4 %shard_map.85 = (bf16[2,256,96]{2,1,0:T(8,128)(2,1)}, f32[3,3,32,128]{3,2,1,0:T(8,128)}, f32[8,128]{1,0:T(8,128)}) custom-call(bf16[32,96,128]{2,1,0:T(8,128)(2,1)} %get-tuple-element.34.low, bf16[32,96,128]{2,1,0:T(8,128)(2,1)} %get-tuple-element.33.high), custom_call_target="tpu_custom_call" | custom-call | tf_op jit(solution)/shard_map/pallas_call | solution.py:27
  20.2 0.0 collective-permute-done.1.from_left
  20.2 0.0 copy-start.2
  20.2 0.0 collective-permute-done.2.from_right
  20.2 0.0 copy-start.4
  20.3 2.5 %collective-permute-start.7 = (bf16[4,96,128]{2,1,0:T(8,128)(2,1)S(1)}, bf16[4,96,128]{2,1,0:T(8,128)(2,1)S(1)}, u32[]{:S(2)}, u32[]{:S(2)}) collective-permute-start(bf16[4,96,128]{2,1,0:T(8,128)(2,1)S(1)} %pad_maximum_fusion.1), channel_id=1, source_target_pairs={{0,16},{16,32},{32,48},{48,64},{64,80},{80,96},{96,112},{1,17},{17... | collective-permute-start | bytes 294920 | tf_op jit(solution)/shard_map/ppermute | solution.py:285
  22.8 0.0 copy-done.2
  22.9 0.0 copy-done.4
  22.9 0.0 copy-start
  22.9 5.4 %shard_map.87 = (f32[2,16,96,128]{3,2,1,0:T(8,128)}, bf16[3,3,256,128]{3,2,1,0:T(8,128)(2,1)}) custom-call(bf16[32,96,128]{2,1,0:T(8,128)(2,1)} %get-tuple-element.34.low, bf16[32,96,128]{2,1,0:T(8,128)(2,1)} %get-tuple-element.33.high, bf16[4,96,128]{2,1,0:T(8,128)(2,1)} %copy-done.2, bf16[4,96,128]{2,1,0:T(8,128)(2,1)} %copy-done.4, bf16[864,32]{1,0:T(8,128)(2,1)} %bitcast.3), custom_call_target="tpu_custom_call" | custom-call | tf_op jit(solution)/shard_map/pallas_call | solution.py:27
  28.3 0.0 copy-start.6
  28.3 0.0 copy-start.7
  28.3 0.0 copy-start.8
  28.4 5.6 %shard_map.86 = (f32[2,16,96,128]{3,2,1,0:T(8,128)}, bf16[3,3,256,128]{3,2,1,0:T(8,128)(2,1)}) custom-call(bf16[32,96,128]{2,1,0:T(8,128)(2,1)} %get-tuple-element.34.low, bf16[32,96,128]{2,1,0:T(8,128)(2,1)} %get-tuple-element.33.high, bf16[4,96,128]{2,1,0:T(8,128)(2,1)} %copy-done.2, bf16[4,96,128]{2,1,0:T(8,128)(2,1)} %copy-done.4, bf16[864,32]{1,0:T(8,128)(2,1)} %bitcast.4), custom_call_target="tpu_custom_call" | custom-call | tf_op jit(solution)/shard_map/pallas_call | solution.py:27
  34.0 0.0 copy-done
  34.0 1.0 %pad_maximum_fusion = bf16[36,96,128]{2,1,0:T(8,128)(2,1)} fusion(bf16[2,96,128]{2,1,0:T(8,128)(2,1)S(1)} %get-tuple-element.46, bf16[2,96,128]{2,1,0:T(8,128)(2,1)S(1)} %get-tuple-element.45, bf16[32,96,128]{2,1,0:T(8,128)(2,1)S(1)} %copy-done), kind=kLoop, calls=%fused_computation | loop fusion | flops 884736 | bytes 1769472 | tf_op jit(solution)/shard_map/concatenate | solution.py:388
  35.0 0.0 collective-permute-done.7.left.right
  35.0 1.4 %collective-permute-start.11 = (bf16[36,96,128]{2,1,0:T(8,128)(2,1)}, bf16[36,96,128]{2,1,0:T(8,128)(2,1)S(1)}, u32[]{:S(2)}, u32[]{:S(2)}) collective-permute-start(bf16[36,96,128]{2,1,0:T(8,128)(2,1)} %pad_maximum_fusion), channel_id=1, source_target_pairs={{16,0},{32,16},{48,32},{64,48},{80,64},{96,80},{112,96},{17,1},{33... | collective-permute-start | bytes 2654216 | tf_op jit(solution)/shard_map/ppermute | solution.py:285
  36.4 0.0 collective-permute-done.below.source
  36.5 0.0 copy-start.1
  36.5 0.0 copy-done.3
  36.5 0.0 copy-done.5
  36.5 0.0 copy-done.6
  36.5 0.0 copy-done.7
  36.5 0.0 copy-done.8
  36.5 1.6 %shard_map.88 = (f32[112,128]{1,0:T(8,128)S(1)}, f32[112,128]{1,0:T(8,128)S(1)}) custom-call(bf16[32,96,128]{2,1,0:T(8,128)(2,1)S(1)} %collective-permute-done.below.source, bf16[32,96,128]{2,1,0:T(8,128)(2,1)S(1)} %copy-done, bf16[4,96,128]{2,1,0:T(8,128)(2,1)S(1)} %copy-done.3, bf16[4,96,128]{2,1,0:T(8,128)(2,1)S(1)} %copy-done.5, ...), custom_call_target="tpu_custom_call" | custom-call | tf_op jit(solution)/shard_map/pallas_call | solution.py:18
  38.2 0.1 collective-permute-start.3
  38.3 1.2 %collective-permute-done.3 = f32[112,128]{1,0:T(8,128)S(1)} collective-permute-done((f32[112,128]{1,0:T(8,128)S(1)}, f32[112,128]{1,0:T(8,128)S(1)}, u32[]{:S(2)}, u32[]{:S(2)}) %collective-permute-start.3) | collective-permute-done | bytes 57376 | tf_op jit(solution)/shard_map/ppermute | solution.py:290
  39.5 3.8 %collective-permute-start.6 = (f32[112,128]{1,0:T(8,128)S(1)}, f32[112,128]{1,0:T(8,128)S(1)}, u32[]{:S(2)}, u32[]{:S(2)}) collective-permute-start(f32[112,128]{1,0:T(8,128)S(1)} %add.35), channel_id=1, source_target_pairs={{0,12},{1,13},{2,14},{3,15},{4,8},{5,9},{6,10},{7,11},{8,4},{9,5},... | collective-permute-start | bytes 172040 | tf_op jit(solution)/shard_map/ppermute | solution.py:290
  43.3 0.5 collective-permute-start.5
  43.9 0.2 collective-permute-start.4
  44.0 0.0 copy-done.11
  44.0 0.6 reshape_tile.3.line
  44.6 0.0 copy-done.10
  44.6 0.0 copy-done.1
  44.6 3.2 %shard_map.89.rest_0_ = bf16[2,16,12288]{2,1,0:T(8,128)(2,1)} custom-call(bf16[32,96,128]{2,1,0:T(8,128)(2,1)} %copy-done.1, bf16[4,96,128]{2,1,0:T(8,128)(2,1)} %copy-done.10, bf16[4,96,128]{2,1,0:T(8,128)(2,1)} %copy-done.10, bf16[3,3,256,128]{3,2,1,0:T(8,128)(2,1)} %get-tuple-element.48.weights, f32[2,16,96,128]{3,2,1,0:T(8,128)} %get-tuple-element.49.partial, ...), custom_call_target="tpu_custom_call" | custom-call | tf_op jit(solution)/shard_map/pallas_call | solution.py:27
  47.9 0.0 collective-permute-done.6
  47.9 0.3 collective-permute-done.5
  48.2 0.0 collective-permute-done.4
  48.2 7.2 %collective-permute-start.10 = (f32[112,128]{1,0:T(8,128)S(1)}, f32[112,128]{1,0:T(8,128)S(1)}, u32[]{:S(2)}, u32[]{:S(2)}) collective-permute-start(f32[112,128]{1,0:T(8,128)S(1)} %add_add_fusion.2), channel_id=1, source_target_pairs={{0,96},{1,97},{2,98},{3,99},{4,100},{5,101},{6,102},{7,103},{8,104... | collective-permute-start | bytes 172040 | tf_op jit(solution)/shard_map/ppermute | solution.py:290
  55.4 0.3 collective-permute-start.9
  55.7 0.3 collective-permute-start.8
  56.1 3.2 %shard_map.90.rest_0_ = bf16[2,16,12288]{2,1,0:T(8,128)(2,1)} custom-call(bf16[32,96,128]{2,1,0:T(8,128)(2,1)} %copy-done.1, bf16[4,96,128]{2,1,0:T(8,128)(2,1)} %copy-done.10, bf16[4,96,128]{2,1,0:T(8,128)(2,1)} %copy-done.10, bf16[3,3,256,128]{3,2,1,0:T(8,128)(2,1)} %get-tuple-element.52.weights, f32[2,16,96,128]{3,2,1,0:T(8,128)} %get-tuple-element.53.partial, ...), custom_call_target="tpu_custom_call" | custom-call | tf_op jit(solution)/shard_map/pallas_call | solution.py:27
  59.3 0.0 collective-permute-done.10
  59.3 0.6 collective-permute-done.9
  59.9 3.2 %collective-permute-done.8 = f32[112,128]{1,0:T(8,128)S(1)} collective-permute-done((f32[112,128]{1,0:T(8,128)S(1)}, f32[112,128]{1,0:T(8,128)S(1)}, u32[]{:S(2)}, u32[]{:S(2)}) %collective-permute-start.8) | collective-permute-done | bytes 57376 | tf_op jit(solution)/shard_map/ppermute | solution.py:290
  63.1 0.0 collective-permute-done.11.source.left.right
  63.1 0.0 copy-start.9
  63.1 0.1 collective-permute-start.14
  63.2 1.3 %collective-permute-start.13 = (f32[112,128]{1,0:T(8,128)S(1)}, f32[112,128]{1,0:T(8,128)S(1)}, u32[]{:S(2)}, u32[]{:S(2)}) collective-permute-start(f32[112,128]{1,0:T(8,128)S(1)} %add_add_fusion.1), channel_id=1, source_target_pairs={{0,16},{1,17},{2,18},{3,19},{4,20},{5,21},{6,22},{7,23},{8,24},{9,... | collective-permute-start | bytes 172040 | tf_op jit(solution)/shard_map/ppermute | solution.py:290
  64.5 1.9 %collective-permute-start.12 = (f32[112,128]{1,0:T(8,128)S(1)}, f32[112,128]{1,0:T(8,128)S(1)}, u32[]{:S(2)}, u32[]{:S(2)}) collective-permute-start(f32[112,128]{1,0:T(8,128)S(1)} %add_add_fusion.1), channel_id=1, source_target_pairs={{0,2},{1,3},{2,0},{3,1},{4,6},{5,7},{6,4},{7,5},{8,10},{9,11},{10,... | collective-permute-start | bytes 172040 | tf_op jit(solution)/shard_map/ppermute | solution.py:290
  66.5 0.0 copy-done.9
  66.5 3.2 %shard_map.91 = bf16[2,16,12288]{2,1,0:T(8,128)(2,1)} custom-call(bf16[36,96,128]{2,1,0:T(8,128)(2,1)} %copy-done.9, bf16[36,96,128]{2,1,0:T(8,128)(2,1)} %copy-done.9, bf16[36,96,128]{2,1,0:T(8,128)(2,1)} %copy-done.9, bf16[3,3,256,128]{3,2,1,0:T(8,128)(2,1)} %get-tuple-element.48.weights, ...), custom_call_target="tpu_custom_call", output_to_operand_aliasing={{}: (6, {})} | custom-call | tf_op jit(solution)/shard_map/pallas_call | solution.py:27
  69.7 0.0 collective-permute-done.14
  69.7 0.0 collective-permute-done.13
  69.7 0.0 collective-permute-done.12
  69.7 2.4 %collective-permute-start.15 = (f32[112,128]{1,0:T(8,128)S(1)}, f32[112,128]{1,0:T(8,128)S(1)}, u32[]{:S(2)}, u32[]{:S(2)}) collective-permute-start(f32[112,128]{1,0:T(8,128)S(1)} %add_add_fusion.part), channel_id=1, source_target_pairs={{0,1},{1,0},{2,3},{3,2},{4,5},{5,4},{6,7},{7,6},{8,9},{9,8},{10,11... | collective-permute-start | bytes 172040 | tf_op jit(solution)/shard_map/ppermute | solution.py:290
  72.2 3.2 %shard_map.92 = bf16[2,16,12288]{2,1,0:T(8,128)(2,1)} custom-call(bf16[36,96,128]{2,1,0:T(8,128)(2,1)} %copy-done.9, bf16[36,96,128]{2,1,0:T(8,128)(2,1)} %copy-done.9, bf16[36,96,128]{2,1,0:T(8,128)(2,1)} %copy-done.9, bf16[3,3,256,128]{3,2,1,0:T(8,128)(2,1)} %get-tuple-element.52.weights, ...), custom_call_target="tpu_custom_call", output_to_operand_aliasing={{}: (6, {})} | custom-call | tf_op jit(solution)/shard_map/pallas_call | solution.py:27
  75.4 0.0 collective-permute-done.15.other
  75.4 1.0 %shard_map.93 = (f32[864,32]{1,0:T(8,128)}, f32[1,32]{1,0:T(1,128)}) custom-call(f32[112,128]{1,0:T(8,128)S(1)} %add_add_fusion.part, f32[112,128]{1,0:T(8,128)S(1)} %collective-permute-done.15.other, f32[1,128]{1,0:T(1,128)S(1)} %broadcast_in_dim.3.flag), custom_call_target="tpu_custom_call" | custom-call | tf_op jit(solution)/shard_map/pallas_call | solution.py:18
  (13 shorter events, 0.1 us)
Async XLA Ops:
  3.7 16.5 %collective-permute-start.1 = (bf16[4,96,128]{2,1,0:T(8,128)(2,1)}, bf16[4,96,128]{2,1,0:T(8,128)(2,1)S(1)}, u32[]{:S(2)}, u32[]{:S(2)}) collective-permute-start(bf16[4,96,128]{2,1,0:T(8,128)(2,1)} %get-tuple-element.35), channel_id=1, source_target_pairs={{0,1},{1,2},{2,3},{3,4},{4,5},{5,6},{6,7},{7,8},{8,9},{9,10},{10,1... | collective-permute-start | bytes 294920 | tf_op jit(solution)/shard_map/ppermute | solution.py:285
  8.6 11.6 %collective-permute-start.2 = (bf16[4,96,128]{2,1,0:T(8,128)(2,1)}, bf16[4,96,128]{2,1,0:T(8,128)(2,1)S(1)}, u32[]{:S(2)}, u32[]{:S(2)}) collective-permute-start(bf16[4,96,128]{2,1,0:T(8,128)(2,1)} %get-tuple-element.36), channel_id=1, source_target_pairs={{1,0},{2,1},{3,2},{4,3},{5,4},{6,5},{7,6},{8,7},{9,8},{10,9},{11,1... | collective-permute-start | bytes 294920 | tf_op jit(solution)/shard_map/ppermute | solution.py:285
  10.6 25.9 %collective-permute-start = (bf16[32,96,128]{2,1,0:T(8,128)(2,1)}, bf16[32,96,128]{2,1,0:T(8,128)(2,1)S(1)}, u32[]{:S(2)}, u32[]{:S(2)}) collective-permute-start(bf16[32,96,128]{2,1,0:T(8,128)(2,1)} %get-tuple-element.33.high), channel_id=1, source_target_pairs={{0,16},{16,32},{32,48},{48,64},{64,80},{80,96},{96,112},{1,17},{17... | collective-permute-start | bytes 2359304 | tf_op jit(solution)/shard_map/ppermute | solution.py:285
  20.2 2.6 %copy-start.2 = (bf16[4,96,128]{2,1,0:T(8,128)(2,1)}, bf16[4,96,128]{2,1,0:T(8,128)(2,1)S(1)}, u32[]{:S(2)}) copy-start(bf16[4,96,128]{2,1,0:T(8,128)(2,1)S(1)} %collective-permute-done.1.from_left) | copy-start | bytes 294916
  20.2 2.6 %copy-start.4 = (bf16[4,96,128]{2,1,0:T(8,128)(2,1)}, bf16[4,96,128]{2,1,0:T(8,128)(2,1)S(1)}, u32[]{:S(2)}) copy-start(bf16[4,96,128]{2,1,0:T(8,128)(2,1)S(1)} %collective-permute-done.2.from_right) | copy-start | bytes 294916
  20.3 14.7 %collective-permute-start.7 = (bf16[4,96,128]{2,1,0:T(8,128)(2,1)S(1)}, bf16[4,96,128]{2,1,0:T(8,128)(2,1)S(1)}, u32[]{:S(2)}, u32[]{:S(2)}) collective-permute-start(bf16[4,96,128]{2,1,0:T(8,128)(2,1)S(1)} %pad_maximum_fusion.1), channel_id=1, source_target_pairs={{0,16},{16,32},{32,48},{48,64},{64,80},{80,96},{96,112},{1,17},{17... | collective-permute-start | bytes 294920 | tf_op jit(solution)/shard_map/ppermute | solution.py:285
  22.9 11.1 %copy-start = (bf16[32,96,128]{2,1,0:T(8,128)(2,1)S(1)}, bf16[32,96,128]{2,1,0:T(8,128)(2,1)}, u32[]{:S(2)}) copy-start(bf16[32,96,128]{2,1,0:T(8,128)(2,1)} %get-tuple-element.34.low) | copy-start | bytes 2359300
  28.3 8.2 %copy-start.3 = (bf16[4,96,128]{2,1,0:T(8,128)(2,1)S(1)}, bf16[4,96,128]{2,1,0:T(8,128)(2,1)}, u32[]{:S(2)}) copy-start(bf16[4,96,128]{2,1,0:T(8,128)(2,1)} %copy-done.2) | copy-start | bytes 294916
  28.3 8.2 %copy-start.5 = (bf16[4,96,128]{2,1,0:T(8,128)(2,1)S(1)}, bf16[4,96,128]{2,1,0:T(8,128)(2,1)}, u32[]{:S(2)}) copy-start(bf16[4,96,128]{2,1,0:T(8,128)(2,1)} %copy-done.4) | copy-start | bytes 294916
  28.3 8.2 %copy-start.6 = (f32[3,3,32,128]{3,2,1,0:T(8,128)S(1)}, f32[3,3,32,128]{3,2,1,0:T(8,128)}, u32[]{:S(2)}) copy-start(f32[3,3,32,128]{3,2,1,0:T(8,128)} %get-tuple-element.41.folded) | copy-start | bytes 442372
  28.3 8.2 %copy-start.7 = (bf16[2,256,96]{2,1,0:T(8,128)(2,1)S(1)}, bf16[2,256,96]{2,1,0:T(8,128)(2,1)}, u32[]{:S(2)}) copy-start(bf16[2,256,96]{2,1,0:T(8,128)(2,1)} %get-tuple-element.37.edges) | copy-start | bytes 294916
  28.3 8.2 %copy-start.8 = (f32[8,128]{1,0:T(8,128)S(1)}, f32[8,128]{1,0:T(8,128)}, u32[]{:S(2)}) copy-start(f32[8,128]{1,0:T(8,128)} %get-tuple-element.42.bias_terms) | copy-start | bytes 12292
  35.0 9.0 %copy-start.11 = (f32[32]{0:T(128)S(1)}, f32[32]{0:T(128)}, u32[]{:S(2)}) copy-start(f32[32]{0:T(128)} %param.9) | copy-start | bytes 388
  35.0 9.6 %copy-start.10 = (bf16[4,96,128]{2,1,0:T(8,128)(2,1)}, bf16[4,96,128]{2,1,0:T(8,128)(2,1)S(1)}, u32[]{:S(2)}) copy-start(bf16[4,96,128]{2,1,0:T(8,128)(2,1)S(1)} %collective-permute-done.7.left.right) | copy-start | bytes 294916
  35.0 28.1 %collective-permute-start.11 = (bf16[36,96,128]{2,1,0:T(8,128)(2,1)}, bf16[36,96,128]{2,1,0:T(8,128)(2,1)S(1)}, u32[]{:S(2)}, u32[]{:S(2)}) collective-permute-start(bf16[36,96,128]{2,1,0:T(8,128)(2,1)} %pad_maximum_fusion), channel_id=1, source_target_pairs={{16,0},{32,16},{48,32},{64,48},{80,64},{96,80},{112,96},{17,1},{33... | collective-permute-start | bytes 2654216 | tf_op jit(solution)/shard_map/ppermute | solution.py:285
  36.5 8.2 %copy-start.1 = (bf16[32,96,128]{2,1,0:T(8,128)(2,1)}, bf16[32,96,128]{2,1,0:T(8,128)(2,1)S(1)}, u32[]{:S(2)}) copy-start(bf16[32,96,128]{2,1,0:T(8,128)(2,1)S(1)} %collective-permute-done.below.source) | copy-start | bytes 2359300
  38.2 1.3 %collective-permute-start.3 = (f32[112,128]{1,0:T(8,128)S(1)}, f32[112,128]{1,0:T(8,128)S(1)}, u32[]{:S(2)}, u32[]{:S(2)}) collective-permute-start(f32[112,128]{1,0:T(8,128)S(1)} %get-tuple-element.44), channel_id=1, source_target_pairs={{0,1},{1,0},{2,3},{3,2},{4,5},{5,4},{6,7},{7,6},{8,9},{9,8},{10,11... | collective-permute-start | bytes 172040 | tf_op jit(solution)/shard_map/ppermute | solution.py:290
  39.5 8.4 %collective-permute-start.6 = (f32[112,128]{1,0:T(8,128)S(1)}, f32[112,128]{1,0:T(8,128)S(1)}, u32[]{:S(2)}, u32[]{:S(2)}) collective-permute-start(f32[112,128]{1,0:T(8,128)S(1)} %add.35), channel_id=1, source_target_pairs={{0,12},{1,13},{2,14},{3,15},{4,8},{5,9},{6,10},{7,11},{8,4},{9,5},... | collective-permute-start | bytes 172040 | tf_op jit(solution)/shard_map/ppermute | solution.py:290
  43.3 4.8 %collective-permute-start.5 = (f32[112,128]{1,0:T(8,128)S(1)}, f32[112,128]{1,0:T(8,128)S(1)}, u32[]{:S(2)}, u32[]{:S(2)}) collective-permute-start(f32[112,128]{1,0:T(8,128)S(1)} %add.35), channel_id=1, source_target_pairs={{0,8},{1,9},{2,10},{3,11},{4,12},{5,13},{6,14},{7,15},{8,0},{9,1},... | collective-permute-start | bytes 172040 | tf_op jit(solution)/shard_map/ppermute | solution.py:290
  43.9 4.3 %collective-permute-start.4 = (f32[112,128]{1,0:T(8,128)S(1)}, f32[112,128]{1,0:T(8,128)S(1)}, u32[]{:S(2)}, u32[]{:S(2)}) collective-permute-start(f32[112,128]{1,0:T(8,128)S(1)} %add.35), channel_id=1, source_target_pairs={{0,4},{1,5},{2,6},{3,7},{4,0},{5,1},{6,2},{7,3},{8,12},{9,13},{10,... | collective-permute-start | bytes 172040 | tf_op jit(solution)/shard_map/ppermute | solution.py:290
  48.2 11.1 %collective-permute-start.10 = (f32[112,128]{1,0:T(8,128)S(1)}, f32[112,128]{1,0:T(8,128)S(1)}, u32[]{:S(2)}, u32[]{:S(2)}) collective-permute-start(f32[112,128]{1,0:T(8,128)S(1)} %add_add_fusion.2), channel_id=1, source_target_pairs={{0,96},{1,97},{2,98},{3,99},{4,100},{5,101},{6,102},{7,103},{8,104... | collective-permute-start | bytes 172040 | tf_op jit(solution)/shard_map/ppermute | solution.py:290
  55.4 4.5 %collective-permute-start.9 = (f32[112,128]{1,0:T(8,128)S(1)}, f32[112,128]{1,0:T(8,128)S(1)}, u32[]{:S(2)}, u32[]{:S(2)}) collective-permute-start(f32[112,128]{1,0:T(8,128)S(1)} %add_add_fusion.2), channel_id=1, source_target_pairs={{0,64},{1,65},{2,66},{3,67},{4,68},{5,69},{6,70},{7,71},{8,72},{9,... | collective-permute-start | bytes 172040 | tf_op jit(solution)/shard_map/ppermute | solution.py:290
  55.7 7.3 %collective-permute-start.8 = (f32[112,128]{1,0:T(8,128)S(1)}, f32[112,128]{1,0:T(8,128)S(1)}, u32[]{:S(2)}, u32[]{:S(2)}) collective-permute-start(f32[112,128]{1,0:T(8,128)S(1)} %add_add_fusion.2), channel_id=1, source_target_pairs={{0,32},{1,33},{2,34},{3,35},{4,36},{5,37},{6,38},{7,39},{8,40},{9,... | collective-permute-start | bytes 172040 | tf_op jit(solution)/shard_map/ppermute | solution.py:290
  63.1 3.3 %copy-start.9 = (bf16[36,96,128]{2,1,0:T(8,128)(2,1)}, bf16[36,96,128]{2,1,0:T(8,128)(2,1)S(1)}, u32[]{:S(2)}) copy-start(bf16[36,96,128]{2,1,0:T(8,128)(2,1)S(1)} %collective-permute-done.11.source.left.right) | copy-start | bytes 2654212
  63.1 6.6 %collective-permute-start.14 = (f32[112,128]{1,0:T(8,128)S(1)}, f32[112,128]{1,0:T(8,128)S(1)}, u32[]{:S(2)}, u32[]{:S(2)}) collective-permute-start(f32[112,128]{1,0:T(8,128)S(1)} %add_add_fusion.1), channel_id=1, source_target_pairs={{0,18},{1,19},{2,16},{3,17},{4,22},{5,23},{6,20},{7,21},{8,26},{9,... | collective-permute-start | bytes 172040 | tf_op jit(solution)/shard_map/ppermute | solution.py:290
  63.2 6.5 %collective-permute-start.13 = (f32[112,128]{1,0:T(8,128)S(1)}, f32[112,128]{1,0:T(8,128)S(1)}, u32[]{:S(2)}, u32[]{:S(2)}) collective-permute-start(f32[112,128]{1,0:T(8,128)S(1)} %add_add_fusion.1), channel_id=1, source_target_pairs={{0,16},{1,17},{2,18},{3,19},{4,20},{5,21},{6,22},{7,23},{8,24},{9,... | collective-permute-start | bytes 172040 | tf_op jit(solution)/shard_map/ppermute | solution.py:290
  64.5 5.2 %collective-permute-start.12 = (f32[112,128]{1,0:T(8,128)S(1)}, f32[112,128]{1,0:T(8,128)S(1)}, u32[]{:S(2)}, u32[]{:S(2)}) collective-permute-start(f32[112,128]{1,0:T(8,128)S(1)} %add_add_fusion.1), channel_id=1, source_target_pairs={{0,2},{1,3},{2,0},{3,1},{4,6},{5,7},{6,4},{7,5},{8,10},{9,11},{10,... | collective-permute-start | bytes 172040 | tf_op jit(solution)/shard_map/ppermute | solution.py:290
  69.7 5.7 %collective-permute-start.15 = (f32[112,128]{1,0:T(8,128)S(1)}, f32[112,128]{1,0:T(8,128)S(1)}, u32[]{:S(2)}, u32[]{:S(2)}) collective-permute-start(f32[112,128]{1,0:T(8,128)S(1)} %add_add_fusion.part), channel_id=1, source_target_pairs={{0,1},{1,0},{2,3},{3,2},{4,5},{5,4},{6,7},{7,6},{8,9},{9,8},{10,11... | collective-permute-start | bytes 172040 | tf_op jit(solution)/shard_map/ppermute | solution.py:290

commit v3 on v2

--- a/solution.py
+++ b/solution.py
@@ -132,57 +132,77 @@
     return total[:, :LANES]
 
 
-def local_terms_body(low, high, edges, folded, bias_terms, turned, taps):
+def own_body(
+    low, high, from_left, from_right, kernel,
+    folded, bias_terms, partial_f, weights_f, partial_g, weights_g, turned, taps,
+):
     rows, groups = low.shape[0] // 2, low.shape[1]
-    sums = jnp.zeros((8, LANES), F32)
-    blank = jnp.zeros((groups, LANES), BF16)
-    for plane, source in enumerate((low, high)):
-        span = slice(plane * LANES, (plane + 1) * LANES)
-        flat = source[rows:].reshape(rows * groups, LANES)
-        turned[span, :] = flat.T
-        edges[0, span, :] = source[rows].T
-        edges[1, span, :] = source[2 * rows - 1].T
-        sums = sums + jnp.sum(flat.astype(F32).reshape(-1, 8, LANES), axis=0)
-        fill_plane(taps, plane, source.at[:rows], blank, blank)
-    bias_terms[...] = sums
-    for tap_y in range(3):
-        both = []
+    chunks = rows // CHUNK
+    step = pl.program_id(0)
+
+    def fill(kind):
+        for plane, source in enumerate((low, high)):
+            at = 2 * plane + kind
+            fill_plane(taps, plane, source.at[kind * rows : kind * rows + rows], from_left[at], from_right[at])
+
+    @pl.when(step == 0)
+    def _():
+        sums = jnp.zeros((8, LANES), F32)
+        for plane, source in enumerate((low, high)):
+            flat = source[rows:].reshape(rows * groups, LANES)
+            turned[plane * LANES : (plane + 1) * LANES, :] = flat.T
+            sums = sums + jnp.sum(flat.astype(F32).reshape(-1, 8, LANES), axis=0)
+        bias_terms[...] = sums
+        build_weights(kernel, False, weights_f)
+        build_weights(kernel, True, weights_g)
+        fill(0)
+        for tap_y in range(3):
+            both = []
+            for plane in range(2):
+                rhs = taps[plane, tap_y : tap_y + rows].reshape(rows * groups, 256)
+                both.append(jnp.dot(turned[...], rhs, preferred_element_type=F32))
+            folded[1, tap_y] = fold(both[0][:LANES] + both[1][LANES:])
+            folded[0, tap_y] = fold(both[0][LANES:])
+            folded[2, tap_y] = fold(both[1][:LANES])
+
+    @pl.when(step == chunks)
+    def _():
+        fill(1)
+
+    def add(weights, partial, chunk):
+        total = inner_sum(taps, weights, chunk, groups)
         for plane in range(2):
-            rhs = taps[plane, tap_y : tap_y + rows].reshape(rows * groups, 256)
-            both.append(jnp.dot(turned[...], rhs, preferred_element_type=F32))
-        folded[1, tap_y] = fold(both[0][:LANES] + both[1][LANES:])
-        folded[0, tap_y] = fold(both[0][LANES:])
-        folded[2, tap_y] = fold(both[1][:LANES])
-
-
-def kernel_grad_body(
-    below, low, from_left, from_right, edges, folded, bias_terms, flag, keep, send, packed, taps, sums
-):
-    rows, groups = below.shape[0] // 2, below.shape[1]
+            part = total[:, plane * LANES : (plane + 1) * LANES]
+            partial[plane] = part.reshape(CHUNK, groups, LANES)
+
+    @pl.when(step < chunks)
+    def _():
+        add(weights_f, partial_f, step)
+
+    @pl.when(step >= chunks)
+    def _():
+        add(weights_g, partial_g, step - chunks)
+
+
+def kernel_grad_body(below, low, from_left, from_right, folded, bias_terms, flag, keep, send, packed, taps, sums):
+    rows, groups = low.shape[0] // 2, low.shape[1]
     blank = jnp.zeros((groups, LANES), BF16)
     fill_plane(taps, 0, below.at[:rows], blank, blank)
-    fill_plane(taps, 1, low.at[:rows], blank, blank)
-    below_turned = below[rows:].reshape(rows * groups, LANES).T
+    fill_plane(taps, 1, low.at[:rows], from_left[0], from_right[0])
+    below_turned = below[rows : 2 * rows].reshape(rows * groups, LANES).T
     low_turned = low[rows:].reshape(rows * groups, LANES).T
-    sums[1] = jnp.zeros(sums.shape[1:], F32)
     for tap_y in range(3):
         rhs = taps[0, tap_y : tap_y + rows].reshape(rows * groups, 256)
         sums[0, tap_y] = jnp.dot(low_turned, rhs, preferred_element_type=F32)
         rhs = taps[1, tap_y : tap_y + rows].reshape(rows * groups, 256)
-        sums[2, tap_y] = jnp.dot(below_turned, rhs, preferred_element_type=F32)
-    for side, lines in enumerate((from_left, from_right)):
-        tap_y, end = 2 * side, side * (rows - 1)
-        lhs = jnp.concatenate([edges[side], below[rows + end].T], axis=0)
-        term = jnp.dot(lhs, with_edges(lines[0]), preferred_element_type=F32)
-        sums[1, tap_y] += term[:LANES]
-        sums[0, tap_y] += term[LANES : 2 * LANES]
-        sums[2, tap_y] += term[2 * LANES :]
-        term = jnp.dot(edges[side], with_edges(lines[2]), preferred_element_type=F32)
-        sums[2, tap_y] += term[:LANES]
-        sums[1, tap_y] += term[LANES:]
-        sums[0, 2 - tap_y] += jnp.dot(lines[1].T, taps[0, 1 + end], preferred_element_type=F32)
+        sums[1, tap_y] = jnp.dot(below_turned, rhs, preferred_element_type=F32)
+    sums[0, 2] += jnp.dot(from_left[1].T, taps[0, 1], preferred_element_type=F32)
+    sums[0, 0] += jnp.dot(from_right[1].T, taps[0, rows], preferred_element_type=F32)
     lane = lax.broadcasted_iota(jnp.int32, (32, LANES), 1)
-    parts = [folded[at // 3, at % 3] + fold(sums[at // 3, at % 3]) for at in range(9)]
+    parts = [folded[at // 3, at % 3] for at in range(9)]
+    for tap_y in range(3):
+        parts[tap_y] += fold(sums[0, tap_y])
+        parts[6 + tap_y] += fold(sums[1, tap_y])
     row = jnp.sum(bias_terms[...], axis=0, keepdims=True)
     row = row + pltpu.roll(row, 64, 1)
     row = row + pltpu.roll(row, 32, 1)
@@ -209,35 +229,24 @@
     return total
 
 
-def inner_body(flip, low, high, from_left, from_right, kernel, partial, weights, taps):
-    groups = low.shape[1]
-    kind = 1 if flip else 0
-    chunk = pl.program_id(0)
-
-    @pl.when(chunk == 0)
-    def _():
-        build_weights(kernel, flip, weights)
-        fill_plane(taps, 0, low, from_left[kind], from_right[kind])
-        fill_plane(taps, 1, high, from_left[2 + kind], from_right[2 + kind])
-
-    total = inner_sum(taps, weights, chunk, groups)
-    for plane in range(2):
-        part = total[:, plane * LANES : (plane + 1) * LANES]
-        partial[plane] = part.reshape(CHUNK, groups, LANES)
-
-
-def outer_body(turn, plane, source, left, right, weights, partial, line, *rest):
-    out, taps, scratch = rest[-3:]
-    rows, groups, _ = source.shape
-    fill_plane(taps, 0, source, left[0], right[0])
-    for chunk in range(rows // CHUNK):
-        start = chunk * CHUNK
-        total = partial[0, start : start + CHUNK].reshape(CHUNK * groups, LANES)
-        for tap_y in range(3):
-            lhs = taps[0, start + tap_y : start + tap_y + CHUNK].reshape(CHUNK * groups, 256)
-            total = total + jnp.dot(lhs, weights[0, tap_y], preferred_element_type=F32)
-        put_rows(scratch, turn(total, line), chunk, groups)
-    lay_out(scratch, out, 0, rows, groups)
+def outer_body(plane, source, edge, weights_f, weights_g, partial_f, partial_g, line, *rest):
+    output, grad_input, taps, scratch = rest[-4:]
+    rows, groups = partial_f.shape[1:3]
+    first = edge.shape[0] - 4
+    for kind, (weights, partial, out, turn) in enumerate(
+        ((weights_f, partial_f, output, rectified), (weights_g, partial_g, grad_input, kept))
+    ):
+        span = source.at[kind * rows : kind * rows + rows]
+        fill_plane(taps, kind, span, edge[first + kind], edge[first + 2 + kind])
+        for chunk in range(rows // CHUNK):
+            start = chunk * CHUNK
+            total = partial[0, start : start + CHUNK].reshape(CHUNK * groups, LANES)
+            for tap_y in range(3):
+                at = start + tap_y
+                lhs = taps[kind, at : at + CHUNK].reshape(CHUNK * groups, 256)
+                total = total + jnp.dot(lhs, weights[0, tap_y], preferred_element_type=F32)
+            put_rows(scratch, turn(total, line), chunk, groups)
+        lay_out(scratch, out, 0, rows, groups)
 
 
 def rectified(total, line):
@@ -265,12 +274,16 @@
 HALF = 112
 
 
-def unpack_body(scaling, part, other, flag, grad_kernel, grad_bias, packed):
+def join_body(part, other, flag, packed):
     upper = flag[...] > 0.5
     packed[:HALF] = jnp.where(upper, other[...], part[...])
     packed[HALF : 2 * HALF] = jnp.where(upper, part[...], other[...])
+
+
+def unpack_body(scaling, part, one, two, three, grad_kernel, grad_bias):
     for place in range(7):
-        block = packed[place * 32 : place * 32 + 32, :] * scaling
+        span = slice(place * 32, place * 32 + 32)
+        block = ((part[span, :] + one[span, :]) + (two[span, :] + three[span, :])) * scaling
         turned = block.T
         grad_kernel[place * 96 : place * 96 + 96, :] = turned[:96]
         if place < 6:
@@ -323,68 +336,51 @@
     below = shifted(high, "gz", 1)
     corner = shifted(jnp.concatenate([from_left[2:], from_right[2:]]), "gz", 1)
 
-    edges, folded, bias_terms = blocked(
-        local_terms_body,
-        1,
-        (shape((2, 2 * LANES, groups), BF16), shape((3, 3, 32, LANES), F32), shape((8, LANES), F32)),
+    line = jnp.tile(bias, 4).reshape(1, LANES)
+    flat_kernel = kernel.reshape(27 * 32, 32)
+    chunks = rows // CHUNK
+    plane = (rows, groups, LANES)
+    folded_shape, bias_shape, weights_shape = (3, 3, 32, LANES), (8, LANES), (3, 3, 256, LANES)
+    piece = (2, CHUNK, groups, LANES)
+    folded, bias_terms, partial_f, weights_f, partial_g, weights_g = blocked(
+        own_body,
+        2 * chunks,
         (
-            part_of((2, 2 * LANES, groups), 0, 0, 0), part_of((3, 3, 32, LANES), 0, 0, 0, 0),
-            part_of((8, LANES), 0, 0),
+            shape(folded_shape, F32), shape(bias_shape, F32),
+            shape((2, *plane), F32), shape(weights_shape, BF16),
+            shape((2, *plane), F32), shape(weights_shape, BF16),
+        ),
+        (
+            part_of(folded_shape, 0, 0, 0, 0), part_of(bias_shape, 0, 0),
+            pl.BlockSpec(piece, lambda step: (0, jnp.minimum(step, chunks - 1), 0, 0)),
+            part_of(weights_shape, 0, 0, 0, 0),
+            pl.BlockSpec(piece, lambda step: (0, jnp.maximum(step - chunks, 0), 0, 0)),
+            part_of(weights_shape, 0, 0, 0, 0),
         ),
         [pltpu.VMEM((2 * LANES, rows * groups), BF16), two_taps],
-        (low, high),
-        [part_of(pair.shape, 0, 0, 0)] * 2,
-        flops=0,
+        (low, high, from_left, from_right, flat_kernel),
+        [part_of(pair.shape, 0, 0, 0)] * 2 + [part_of(lines.shape, 0, 0, 0)] * 2 + [part_of(flat_kernel.shape, 0, 0)],
     )
 
-    plane = (rows, groups, LANES)
-    line = jnp.tile(bias, 4).reshape(1, LANES)
-    flat_kernel = kernel.reshape(27 * 32, 32)
-
-    def inner(kind):
+    def outer(side, source, edge, done=()):
+        weights, partial = part_of((1, 3, 256, LANES), 2 * side, 0, 0, 0), part_of((1, *plane), side, 0, 0, 0)
         return blocked(
-            functools.partial(inner_body, kind == 1),
-            rows // CHUNK,
-            (shape((2, *plane), F32), shape((3, 3, 256, LANES), BF16)),
-            (
-                pl.BlockSpec((2, CHUNK, groups, LANES), lambda step: (0, step, 0, 0)),
-                part_of((3, 3, 256, LANES), 0, 0, 0, 0),
-            ),
-            [two_taps],
-            (low, high, from_left, from_right, flat_kernel),
-            [part_of(plane, kind, 0, 0)] * 2
-            + [part_of(lines.shape, 0, 0, 0)] * 2
-            + [part_of(flat_kernel.shape, 0, 0)],
+            functools.partial(outer_body, side),
+            1,
+            (shape(block, BF16), shape(block, BF16)),
+            (part_of((1, *block[1:]), side, 0, 0),) * 2,
+            [two_taps, spread],
+            (source, edge, weights_f, weights_g, partial_f, partial_g, line, *done),
+            [
+                part_of(source.shape, 0, 0, 0), part_of(edge.shape, 0, 0, 0),
+                weights, weights, partial, partial, part_of((1, LANES), 0, 0),
+                *[pl.BlockSpec(memory_space=pl.ANY)] * len(done),
+            ],
+            {7: 0, 8: 1} if done else None,
         )
 
-    def outer(kind, side, source, edge, weights, partial, done=None):
-        row = (1, groups, LANES)
-        args = [source, edge, edge, weights, partial, line]
-        first = 2 * rows if edge is source else 0
-        specs = [
-            part_of(plane, kind, 0, 0), part_of(row, first + kind, 0, 0), part_of(row, first + 2 + kind, 0, 0),
-            part_of((1, 3, 256, LANES), 2 * side, 0, 0, 0), part_of((1, *plane), side, 0, 0, 0),
-            part_of((1, LANES), 0, 0),
-        ]
-        if done is not None:
-            args.append(done)
-            specs.append(pl.BlockSpec(memory_space=pl.ANY))
-        return blocked(
-            functools.partial(outer_body, kept if kind else rectified, side),
-            1,
-            shape(block, BF16),
-            part_of((1, *block[1:]), side, 0, 0),
-            [pltpu.VMEM((1, rows + 2, groups, 2 * LANES), BF16), spread],
-            args,
-            specs,
-            None if done is None else {6: 0},
-        )
-
-    partial_f, weights_f = inner(0)
-    partial_g, weights_g = inner(1)
-
     ends = (from_left[:2], from_right[:2])
-    ends, folded, partial_f, partial_g = lax.optimization_barrier((ends, folded, partial_f, partial_g))
+    ends, folded, partial_g = lax.optimization_barrier((ends, folded, partial_g))
     down = jnp.concatenate([low, *ends])
     down, corner = lax.optimization_barrier((down, corner))
     above = shifted(down, "gz", -1)
@@ -392,30 +388,27 @@
     part, send = call(
         kernel_grad_body,
         (half, half),
-        [packed, two_taps, pltpu.VMEM((3, 3, LANES, 256), F32)],
-        (below, low, from_left, from_right, edges, folded, bias_terms, flag),
+        [packed, two_taps, pltpu.VMEM((2, 3, LANES, 256), F32)],
+        (below, low, from_left, from_right, folded, bias_terms, flag),
     )
     part = part + swapped(send, 1)
     part = sum_of_four(part, 4, 8)
-    output = outer(0, 0, below, corner, weights_f, partial_f)
-    part, output = lax.optimization_barrier((part, output))
     part = sum_of_four(part, 32, 64)
-    grad_input = outer(1, 0, below, corner, weights_g, partial_g)
-    part, above, grad_input = lax.optimization_barrier((part, above, grad_input))
-    part = sum_of_four(part, 2, 16)
-    output = outer(0, 1, above, above, weights_f, partial_f, output)
-    part, output = lax.optimization_barrier((part, output))
-    other = swapped(part, 1)
-    grad_input = outer(1, 1, above, above, weights_g, partial_g, grad_input)
+    results = outer(0, below, corner)
+    part, results = lax.optimization_barrier((part, results))
+    part = call(join_body, shape((2 * HALF, LANES), F32), [], (part, swapped(part, 1), flag))
+    part, above = lax.optimization_barrier((part, above))
+    others = [swapped(part, bit) for bit in (2, 16, 18)]
+    results = outer(1, above, above, results)
 
     voxels = planes * lax.axis_size("gz") * rows * lax.axis_size("gy") * (width // 32)
     grad_kernel, grad_bias = call(
         functools.partial(unpack_body, 1.0 / math.sqrt(voxels)),
         (shape((27 * 32, 32), F32), shape((1, 32), F32)),
-        [packed],
-        (part, other, flag),
+        [],
+        (part, *others),
     )
-    return output, grad_input, grad_kernel.reshape(3, 3, 3, 32, 32), grad_bias.reshape(32)
+    return *results, grad_kernel.reshape(3, 3, 3, 32, 32), grad_bias.reshape(32)
 
 
 def solution(mesh):

time: 76.8 us -> 74.8 us (0.974)
  Pallas kernels: 34 us -> 26.3 us
  waiting for transfers between devices: 5.37 us -> 9.96 us
    pallas_call x7 -> x3, Pallas kernels: 28.4 us -> 20.7 us  [blocked(): pl.pallas_call(body, grid=(grid,), out_shape=outs, in_specs=in_specs, out...]
    ppermute x11, waiting for transfers between devices: 5.36 us -> 8.23 us  [swapped(): lax.ppermute(value, ('gz', 'gy'), [(i, i ^ bit) for i in range(count)])]
    ppermute x5, waiting for transfers between devices: 0.01 us -> 1.72 us  [shifted(): return lax.ppermute(value, axis, pairs)]
    ppermute x5, starting transfers between devices: 16.1 us -> 17.6 us  [shifted(): return lax.ppermute(value, axis, pairs)]
    ppermute x11, starting transfers between devices: 18.2 us -> 17.3 us  [swapped(): lax.ppermute(value, ('gz', 'gy'), [(i, i ^ bit) for i in range(count)])]
    pallas_call x2 -> x3, Pallas kernels: 2.62 us -> 2.5 us  [call(): pl.pallas_call(body, out_shape=outs, scratch_shapes=scratch, compiler_par...]
  transfers between devices with their start and end apart: 16 -> 16, of which waited for: 4 -> 7; matrix products, arithmetic and copies ran while one was open for 2% -> 2% of each run, Pallas kernels for 39% -> 30%
where the time goes in v3:
time: 74.8 us; the launch traced here: 73.8 us
  starting transfers between devices  34.9 us (47%)
  Pallas kernels  26.3 us (35%)
  waiting for transfers between devices  9.96 us (13%)
  other arithmetic  1.08 us (1%)
  between operations  0.92 us (1%)
    pallas_call x3, Pallas kernels, blocked(): pl.pallas_call(body, grid=(grid,), out_shape=outs, in_specs=in_specs, out...  20.7 us
    ppermute x5, starting transfers between devices, shifted(): return lax.ppermute(value, axis, pairs)  17.6 us
    ppermute x11, starting transfers between devices, swapped(): lax.ppermute(value, ('gz', 'gy'), [(i, i ^ bit) for i in range(count)])  17.3 us
    ppermute x11, waiting for transfers between devices, swapped(): lax.ppermute(value, ('gz', 'gy'), [(i, i ^ bit) for i in range(count)])  8.23 us
    pallas_call x1, Pallas kernels, local(): pl.pallas_call(group_body, in_specs=[pl.BlockSpec(memory_space=pl.ANY)] *...  3.07 us
    pallas_call x3, Pallas kernels, call(): pl.pallas_call(body, out_shape=outs, scratch_shapes=scratch, compiler_par...  2.5 us
    ppermute x5, waiting for transfers between devices, shifted(): return lax.ppermute(value, axis, pairs)  1.72 us
  transfers between devices with their start and end apart: 16, of which 7 were waited for; matrix products, arithmetic and copies ran while one was open for 2% of the time, Pallas kernels for 30%

profile of v3, /device:TPU:1, one launch (start us, length us, event | category | flops | bytes accessed | tf_op | source)
XLA Modules:
  0.0 73.8 jit_solution(1012677292875546581)
XLA Ops:
  0.6 3.1 %shard_map.84 = (bf16[32,96,128]{2,1,0:T(8,128)(2,1)}, bf16[32,96,128]{2,1,0:T(8,128)(2,1)}, bf16[4,96,128]{2,1,0:T(8,128)(2,1)}, bf16[4,96,128]{2,1,0:T(8,128)(2,1)}) custom-call(bf16[2,16,12288]{2,1,0:T(8,128)(2,1)} %act_in.1, bf16[2,16,12288]{2,1,0:T(8,128)(2,1)} %grad_in.1, s32[2,16,12288]{2,1,0:T(8,128)} %mask_in.1), custom_call_target="tpu_custom_call" | custom-call | tf_op jit(solution)/shard_map/pallas_call | solution.py:324
  3.7 0.0 copy-start
  3.7 5.1 %collective-permute-start.1 = (bf16[4,96,128]{2,1,0:T(8,128)(2,1)}, bf16[4,96,128]{2,1,0:T(8,128)(2,1)S(1)}, u32[]{:S(2)}, u32[]{:S(2)}) collective-permute-start(bf16[4,96,128]{2,1,0:T(8,128)(2,1)} %get-tuple-element.35), channel_id=1, source_target_pairs={{0,1},{1,2},{2,3},{3,4},{4,5},{5,6},{6,7},{7,8},{8,9},{9,10},{10,1... | collective-permute-start | bytes 294920 | tf_op jit(solution)/shard_map/ppermute | solution.py:298
  8.8 1.9 %collective-permute-start.2 = (bf16[4,96,128]{2,1,0:T(8,128)(2,1)}, bf16[4,96,128]{2,1,0:T(8,128)(2,1)S(1)}, u32[]{:S(2)}, u32[]{:S(2)}) collective-permute-start(bf16[4,96,128]{2,1,0:T(8,128)(2,1)} %get-tuple-element.36), channel_id=1, source_target_pairs={{1,0},{2,1},{3,2},{4,3},{5,4},{6,5},{7,6},{8,7},{9,8},{10,9},{11,1... | collective-permute-start | bytes 294920 | tf_op jit(solution)/shard_map/ppermute | solution.py:298
  10.7 5.3 %collective-permute-start = (bf16[32,96,128]{2,1,0:T(8,128)(2,1)}, bf16[32,96,128]{2,1,0:T(8,128)(2,1)S(1)}, u32[]{:S(2)}, u32[]{:S(2)}) collective-permute-start(bf16[32,96,128]{2,1,0:T(8,128)(2,1)} %get-tuple-element.33.high), channel_id=1, source_target_pairs={{0,16},{16,32},{32,48},{48,64},{64,80},{80,96},{96,112},{1,17},{17... | collective-permute-start | bytes 2359304 | tf_op jit(solution)/shard_map/ppermute | solution.py:298
  16.0 0.0 collective-permute-done.1.from_left
  16.0 0.0 copy-start.2
  16.0 0.0 collective-permute-done.2.from_right
  16.0 0.0 copy-start.4
  16.1 4.1 %collective-permute-start.10 = (bf16[4,96,128]{2,1,0:T(8,128)(2,1)S(1)}, bf16[4,96,128]{2,1,0:T(8,128)(2,1)S(1)}, u32[]{:S(2)}, u32[]{:S(2)}) collective-permute-start(bf16[4,96,128]{2,1,0:T(8,128)(2,1)S(1)} %pad_maximum_fusion.1), channel_id=1, source_target_pairs={{0,16},{16,32},{32,48},{48,64},{64,80},{80,96},{96,112},{1,17},{17... | collective-permute-start | bytes 294920 | tf_op jit(solution)/shard_map/ppermute | solution.py:298
  20.2 0.0 copy-done.2
  20.2 0.0 copy-done.4
  20.2 11.0 %shard_map.85 = (f32[3,3,32,128]{3,2,1,0:T(8,128)}, f32[8,128]{1,0:T(8,128)}, f32[2,16,96,128]{3,2,1,0:T(8,128)}, bf16[3,3,256,128]{3,2,1,0:T(8,128)(2,1)}, f32[...) custom-call(bf16[32,96,128]{2,1,0:T(8,128)(2,1)} %get-tuple-element.34.low, ...), custom_call_target="tpu_custom_call" | custom-call | tf_op jit(solution)/shard_map/pallas_call | solution.py:27
  31.2 0.0 copy-start.3
  31.3 0.0 copy-start.5
  31.3 0.0 copy-start.6
  31.3 0.0 copy-start.7
  31.3 0.0 copy-done
  31.3 1.0 %pad_maximum_fusion = bf16[36,96,128]{2,1,0:T(8,128)(2,1)} fusion(bf16[2,96,128]{2,1,0:T(8,128)(2,1)S(1)} %get-tuple-element.44, bf16[2,96,128]{2,1,0:T(8,128)(2,1)S(1)} %get-tuple-element.43, bf16[32,96,128]{2,1,0:T(8,128)(2,1)S(1)} %copy-done), kind=kLoop, calls=%fused_computation | loop fusion | flops 884736 | bytes 1769472 | tf_op jit(solution)/shard_map/concatenate | solution.py:384
  32.3 0.0 copy-start.10
  32.3 1.7 %collective-permute-done.10.edge = bf16[4,96,128]{2,1,0:T(8,128)(2,1)S(1)} collective-permute-done((bf16[4,96,128]{2,1,0:T(8,128)(2,1)S(1)}, bf16[4,96,128]{2,1,0:T(8,128)(2,1)S(1)}, u32[]{:S(2)}, u32[]{:S(2)}) %collective-permute-start.10) | collective-permute-done | bytes 98336 | tf_op jit(solution)/shard_map/ppermute | solution.py:298
  34.0 0.0 copy-start.9
  34.0 1.3 %collective-permute-start.12 = (bf16[36,96,128]{2,1,0:T(8,128)(2,1)}, bf16[36,96,128]{2,1,0:T(8,128)(2,1)S(1)}, u32[]{:S(2)}, u32[]{:S(2)}) collective-permute-start(bf16[36,96,128]{2,1,0:T(8,128)(2,1)} %pad_maximum_fusion), channel_id=1, source_target_pairs={{16,0},{32,16},{48,32},{64,48},{80,64},{96,80},{112,96},{17,1},{33... | collective-permute-start | bytes 2654216 | tf_op jit(solution)/shard_map/ppermute | solution.py:298
  35.3 0.0 collective-permute-done.below.source
  35.3 0.0 copy-start.1
  35.4 0.0 copy-done.3
  35.4 0.0 copy-done.5
  35.4 0.0 copy-done.6
  35.4 0.0 copy-done.7
  35.4 1.5 %shard_map.86 = (f32[112,128]{1,0:T(8,128)S(1)}, f32[112,128]{1,0:T(8,128)S(1)}) custom-call(bf16[32,96,128]{2,1,0:T(8,128)(2,1)S(1)} %collective-permute-done.below.source, bf16[32,96,128]{2,1,0:T(8,128)(2,1)S(1)} %copy-done, bf16[4,96,128]{2,1,0:T(8,128)(2,1)S(1)} %copy-done.3, bf16[4,96,128]{2,1,0:T(8,128)(2,1)S(1)} %copy-done.5, ...), custom_call_target="tpu_custom_call" | custom-call | tf_op jit(solution)/shard_map/pallas_call | solution.py:18
  36.9 0.1 collective-permute-start.3
  37.0 1.2 %collective-permute-done.3 = f32[112,128]{1,0:T(8,128)S(1)} collective-permute-done((f32[112,128]{1,0:T(8,128)S(1)}, f32[112,128]{1,0:T(8,128)S(1)}, u32[]{:S(2)}, u32[]{:S(2)}) %collective-permute-start.3) | collective-permute-done | bytes 57376 | tf_op jit(solution)/shard_map/ppermute | solution.py:303
  38.3 4.1 %collective-permute-start.6 = (f32[112,128]{1,0:T(8,128)S(1)}, f32[112,128]{1,0:T(8,128)S(1)}, u32[]{:S(2)}, u32[]{:S(2)}) collective-permute-start(f32[112,128]{1,0:T(8,128)S(1)} %add.26), channel_id=1, source_target_pairs={{0,12},{1,13},{2,14},{3,15},{4,8},{5,9},{6,10},{7,11},{8,4},{9,5},... | collective-permute-start | bytes 172040 | tf_op jit(solution)/shard_map/ppermute | solution.py:303
  42.4 0.5 collective-permute-start.5
  42.9 0.1 collective-permute-start.4
  43.1 1.3 %collective-permute-done.6 = f32[112,128]{1,0:T(8,128)S(1)} collective-permute-done((f32[112,128]{1,0:T(8,128)S(1)}, f32[112,128]{1,0:T(8,128)S(1)}, u32[]{:S(2)}, u32[]{:S(2)}) %collective-permute-start.6) | collective-permute-done | bytes 57376 | tf_op jit(solution)/shard_map/ppermute | solution.py:303
  44.3 2.9 %collective-permute-done.5 = f32[112,128]{1,0:T(8,128)S(1)} collective-permute-done((f32[112,128]{1,0:T(8,128)S(1)}, f32[112,128]{1,0:T(8,128)S(1)}, u32[]{:S(2)}, u32[]{:S(2)}) %collective-permute-start.5) | collective-permute-done | bytes 57376 | tf_op jit(solution)/shard_map/ppermute | solution.py:303
  47.2 0.0 collective-permute-done.4
  47.2 7.6 %collective-permute-start.9 = (f32[112,128]{1,0:T(8,128)S(1)}, f32[112,128]{1,0:T(8,128)S(1)}, u32[]{:S(2)}, u32[]{:S(2)}) collective-permute-start(f32[112,128]{1,0:T(8,128)S(1)} %add_add_fusion.1), channel_id=1, source_target_pairs={{0,96},{1,97},{2,98},{3,99},{4,100},{5,101},{6,102},{7,103},{8,104... | collective-permute-start | bytes 172040 | tf_op jit(solution)/shard_map/ppermute | solution.py:303
  54.8 0.1 collective-permute-start.8
  54.9 0.6 collective-permute-start.7
  55.5 0.0 copy-done.10
  55.5 0.6 reshape_tile.3.line
  56.1 0.0 copy-done.9
  56.1 0.0 copy-done.1
  56.1 4.7 %shard_map.87 = (bf16[2,16,12288]{2,1,0:T(8,128)(2,1)}, bf16[2,16,12288]{2,1,0:T(8,128)(2,1)}) custom-call(bf16[32,96,128]{2,1,0:T(8,128)(2,1)} %copy-done.1, bf16[4,96,128]{2,1,0:T(8,128)(2,1)} %copy-done.9, bf16[3,3,256,128]{3,2,1,0:T(8,128)(2,1)} %get-tuple-element.46.weights_f, bf16[3,3,256,128]{3,2,1,0:T(8,128)(2,1)} %get-tuple-element.47.weights_g, ...), custom_call_target="tpu_custom_call" | custom-call | tf_op jit(solution)/shard_map/pallas_call | solution.py:27
  60.8 0.0 collective-permute-done.9
  60.8 0.0 collective-permute-done.8
  60.8 1.8 %collective-permute-done.7 = f32[112,128]{1,0:T(8,128)S(1)} collective-permute-done((f32[112,128]{1,0:T(8,128)S(1)}, f32[112,128]{1,0:T(8,128)S(1)}, u32[]{:S(2)}, u32[]{:S(2)}) %collective-permute-start.7) | collective-permute-done | bytes 57376 | tf_op jit(solution)/shard_map/ppermute | solution.py:303
  62.6 0.5 collective-permute-start.11
  63.1 0.9 %collective-permute-done.11.other = f32[112,128]{1,0:T(8,128)S(1)} collective-permute-done((f32[112,128]{1,0:T(8,128)S(1)}, f32[112,128]{1,0:T(8,128)S(1)}, u32[]{:S(2)}, u32[]{:S(2)}) %collective-permute-start.11) | collective-permute-done | bytes 57376 | tf_op jit(solution)/shard_map/ppermute | solution.py:303
  64.0 0.0 collective-permute-done.12.source.edge
  64.1 0.0 copy-start.8
  64.1 0.3 collective-permute-start.15
  64.4 3.3 %collective-permute-start.14 = (f32[224,128]{1,0:T(8,128)S(1)}, f32[224,128]{1,0:T(8,128)S(1)}, u32[]{:S(2)}, u32[]{:S(2)}) collective-permute-start(f32[224,128]{1,0:T(8,128)S(1)} %shard_map.88.part), channel_id=1, source_target_pairs={{0,16},{1,17},{2,18},{3,19},{4,20},{5,21},{6,22},{7,23},{8,24},{9,... | collective-permute-start | bytes 344072 | tf_op jit(solution)/shard_map/ppermute | solution.py:303
  67.7 0.0 collective-permute-start.13
  67.7 0.0 copy-done.8
  67.7 4.9 %shard_map.89 = (bf16[2,16,12288]{2,1,0:T(8,128)(2,1)}, bf16[2,16,12288]{2,1,0:T(8,128)(2,1)}) custom-call(bf16[36,96,128]{2,1,0:T(8,128)(2,1)} %copy-done.8, bf16[36,96,128]{2,1,0:T(8,128)(2,1)} %copy-done.8, bf16[3,3,256,128]{3,2,1,0:T(8,128)(2,1)} %get-tuple-element.46.weights_f, ...), custom_call_target="tpu_custom_call", output_to_operand_aliasing={{0}: (7, {}), {1}: (8, {})} | custom-call | tf_op jit(solution)/shard_map/pallas_call | solution.py:27
  72.6 0.0 collective-permute-done.15.three
  72.6 0.0 collective-permute-done.14.two
  72.6 0.2 collective-permute-done.13.one
  72.8 1.0 %shard_map.90 = (f32[864,32]{1,0:T(8,128)}, f32[1,32]{1,0:T(1,128)}) custom-call(f32[224,128]{1,0:T(8,128)S(1)} %shard_map.88.part, f32[224,128]{1,0:T(8,128)S(1)} %collective-permute-done.13.one, f32[224,128]{1,0:T(8,128)S(1)} %collective-permute-done.14.two, f32[224,128]{1,0:T(8,128)S(1)} %collective-permute-done.15.three), custom_call_target="tpu_custom_call" | custom-call | tf_op jit(solution)/shard_map/pallas_call | solution.py:18
  (9 shorter events, 0.1 us)
Async XLA Ops:
  3.7 27.6 %copy-start = (bf16[32,96,128]{2,1,0:T(8,128)(2,1)S(1)}, bf16[32,96,128]{2,1,0:T(8,128)(2,1)}, u32[]{:S(2)}) copy-start(bf16[32,96,128]{2,1,0:T(8,128)(2,1)} %get-tuple-element.34.low) | copy-start | bytes 2359300
  3.7 12.3 %collective-permute-start.1 = (bf16[4,96,128]{2,1,0:T(8,128)(2,1)}, bf16[4,96,128]{2,1,0:T(8,128)(2,1)S(1)}, u32[]{:S(2)}, u32[]{:S(2)}) collective-permute-start(bf16[4,96,128]{2,1,0:T(8,128)(2,1)} %get-tuple-element.35), channel_id=1, source_target_pairs={{0,1},{1,2},{2,3},{3,4},{4,5},{5,6},{6,7},{7,8},{8,9},{9,10},{10,1... | collective-permute-start | bytes 294920 | tf_op jit(solution)/shard_map/ppermute | solution.py:298
  8.8 7.2 %collective-permute-start.2 = (bf16[4,96,128]{2,1,0:T(8,128)(2,1)}, bf16[4,96,128]{2,1,0:T(8,128)(2,1)S(1)}, u32[]{:S(2)}, u32[]{:S(2)}) collective-permute-start(bf16[4,96,128]{2,1,0:T(8,128)(2,1)} %get-tuple-element.36), channel_id=1, source_target_pairs={{1,0},{2,1},{3,2},{4,3},{5,4},{6,5},{7,6},{8,7},{9,8},{10,9},{11,1... | collective-permute-start | bytes 294920 | tf_op jit(solution)/shard_map/ppermute | solution.py:298
  10.7 24.6 %collective-permute-start = (bf16[32,96,128]{2,1,0:T(8,128)(2,1)}, bf16[32,96,128]{2,1,0:T(8,128)(2,1)S(1)}, u32[]{:S(2)}, u32[]{:S(2)}) collective-permute-start(bf16[32,96,128]{2,1,0:T(8,128)(2,1)} %get-tuple-element.33.high), channel_id=1, source_target_pairs={{0,16},{16,32},{32,48},{48,64},{64,80},{80,96},{96,112},{1,17},{17... | collective-permute-start | bytes 2359304 | tf_op jit(solution)/shard_map/ppermute | solution.py:298
  16.0 4.2 %copy-start.2 = (bf16[4,96,128]{2,1,0:T(8,128)(2,1)}, bf16[4,96,128]{2,1,0:T(8,128)(2,1)S(1)}, u32[]{:S(2)}) copy-start(bf16[4,96,128]{2,1,0:T(8,128)(2,1)S(1)} %collective-permute-done.1.from_left) | copy-start | bytes 294916
  16.0 4.2 %copy-start.4 = (bf16[4,96,128]{2,1,0:T(8,128)(2,1)}, bf16[4,96,128]{2,1,0:T(8,128)(2,1)S(1)}, u32[]{:S(2)}) copy-start(bf16[4,96,128]{2,1,0:T(8,128)(2,1)S(1)} %collective-permute-done.2.from_right) | copy-start | bytes 294916
  16.1 18.0 %collective-permute-start.10 = (bf16[4,96,128]{2,1,0:T(8,128)(2,1)S(1)}, bf16[4,96,128]{2,1,0:T(8,128)(2,1)S(1)}, u32[]{:S(2)}, u32[]{:S(2)}) collective-permute-start(bf16[4,96,128]{2,1,0:T(8,128)(2,1)S(1)} %pad_maximum_fusion.1), channel_id=1, source_target_pairs={{0,16},{16,32},{32,48},{48,64},{64,80},{80,96},{96,112},{1,17},{17... | collective-permute-start | bytes 294920 | tf_op jit(solution)/shard_map/ppermute | solution.py:298
  31.2 4.1 %copy-start.3 = (bf16[4,96,128]{2,1,0:T(8,128)(2,1)S(1)}, bf16[4,96,128]{2,1,0:T(8,128)(2,1)}, u32[]{:S(2)}) copy-start(bf16[4,96,128]{2,1,0:T(8,128)(2,1)} %copy-done.2) | copy-start | bytes 294916
  31.3 4.1 %copy-start.5 = (bf16[4,96,128]{2,1,0:T(8,128)(2,1)S(1)}, bf16[4,96,128]{2,1,0:T(8,128)(2,1)}, u32[]{:S(2)}) copy-start(bf16[4,96,128]{2,1,0:T(8,128)(2,1)} %copy-done.4) | copy-start | bytes 294916
  31.3 4.1 %copy-start.6 = (f32[3,3,32,128]{3,2,1,0:T(8,128)S(1)}, f32[3,3,32,128]{3,2,1,0:T(8,128)}, u32[]{:S(2)}) copy-start(f32[3,3,32,128]{3,2,1,0:T(8,128)} %get-tuple-element.39.folded) | copy-start | bytes 442372
  31.3 4.1 %copy-start.7 = (f32[8,128]{1,0:T(8,128)S(1)}, f32[8,128]{1,0:T(8,128)}, u32[]{:S(2)}) copy-start(f32[8,128]{1,0:T(8,128)} %get-tuple-element.40.bias_terms) | copy-start | bytes 12292
  32.3 23.2 %copy-start.10 = (f32[32]{0:T(128)S(1)}, f32[32]{0:T(128)}, u32[]{:S(2)}) copy-start(f32[32]{0:T(128)} %param.9) | copy-start | bytes 388
  34.0 22.1 %copy-start.9 = (bf16[4,96,128]{2,1,0:T(8,128)(2,1)}, bf16[4,96,128]{2,1,0:T(8,128)(2,1)S(1)}, u32[]{:S(2)}) copy-start(bf16[4,96,128]{2,1,0:T(8,128)(2,1)S(1)} %collective-permute-done.10.edge) | copy-start | bytes 294916
  34.0 30.0 %collective-permute-start.12 = (bf16[36,96,128]{2,1,0:T(8,128)(2,1)}, bf16[36,96,128]{2,1,0:T(8,128)(2,1)S(1)}, u32[]{:S(2)}, u32[]{:S(2)}) collective-permute-start(bf16[36,96,128]{2,1,0:T(8,128)(2,1)} %pad_maximum_fusion), channel_id=1, source_target_pairs={{16,0},{32,16},{48,32},{64,48},{80,64},{96,80},{112,96},{17,1},{33... | collective-permute-start | bytes 2654216 | tf_op jit(solution)/shard_map/ppermute | solution.py:298
  35.3 20.8 %copy-start.1 = (bf16[32,96,128]{2,1,0:T(8,128)(2,1)}, bf16[32,96,128]{2,1,0:T(8,128)(2,1)S(1)}, u32[]{:S(2)}) copy-start(bf16[32,96,128]{2,1,0:T(8,128)(2,1)S(1)} %collective-permute-done.below.source) | copy-start | bytes 2359300
  36.9 1.3 %collective-permute-start.3 = (f32[112,128]{1,0:T(8,128)S(1)}, f32[112,128]{1,0:T(8,128)S(1)}, u32[]{:S(2)}, u32[]{:S(2)}) collective-permute-start(f32[112,128]{1,0:T(8,128)S(1)} %get-tuple-element.42), channel_id=1, source_target_pairs={{0,1},{1,0},{2,3},{3,2},{4,5},{5,4},{6,7},{7,6},{8,9},{9,8},{10,11... | collective-permute-start | bytes 172040 | tf_op jit(solution)/shard_map/ppermute | solution.py:303
  38.3 6.1 %collective-permute-start.6 = (f32[112,128]{1,0:T(8,128)S(1)}, f32[112,128]{1,0:T(8,128)S(1)}, u32[]{:S(2)}, u32[]{:S(2)}) collective-permute-start(f32[112,128]{1,0:T(8,128)S(1)} %add.26), channel_id=1, source_target_pairs={{0,12},{1,13},{2,14},{3,15},{4,8},{5,9},{6,10},{7,11},{8,4},{9,5},... | collective-permute-start | bytes 172040 | tf_op jit(solution)/shard_map/ppermute | solution.py:303
  42.4 4.8 %collective-permute-start.5 = (f32[112,128]{1,0:T(8,128)S(1)}, f32[112,128]{1,0:T(8,128)S(1)}, u32[]{:S(2)}, u32[]{:S(2)}) collective-permute-start(f32[112,128]{1,0:T(8,128)S(1)} %add.26), channel_id=1, source_target_pairs={{0,8},{1,9},{2,10},{3,11},{4,12},{5,13},{6,14},{7,15},{8,0},{9,1},... | collective-permute-start | bytes 172040 | tf_op jit(solution)/shard_map/ppermute | solution.py:303
  42.9 4.3 %collective-permute-start.4 = (f32[112,128]{1,0:T(8,128)S(1)}, f32[112,128]{1,0:T(8,128)S(1)}, u32[]{:S(2)}, u32[]{:S(2)}) collective-permute-start(f32[112,128]{1,0:T(8,128)S(1)} %add.26), channel_id=1, source_target_pairs={{0,4},{1,5},{2,6},{3,7},{4,0},{5,1},{6,2},{7,3},{8,12},{9,13},{10,... | collective-permute-start | bytes 172040 | tf_op jit(solution)/shard_map/ppermute | solution.py:303
  47.2 13.6 %collective-permute-start.9 = (f32[112,128]{1,0:T(8,128)S(1)}, f32[112,128]{1,0:T(8,128)S(1)}, u32[]{:S(2)}, u32[]{:S(2)}) collective-permute-start(f32[112,128]{1,0:T(8,128)S(1)} %add_add_fusion.1), channel_id=1, source_target_pairs={{0,96},{1,97},{2,98},{3,99},{4,100},{5,101},{6,102},{7,103},{8,104... | collective-permute-start | bytes 172040 | tf_op jit(solution)/shard_map/ppermute | solution.py:303
  54.8 6.0 %collective-permute-start.8 = (f32[112,128]{1,0:T(8,128)S(1)}, f32[112,128]{1,0:T(8,128)S(1)}, u32[]{:S(2)}, u32[]{:S(2)}) collective-permute-start(f32[112,128]{1,0:T(8,128)S(1)} %add_add_fusion.1), channel_id=1, source_target_pairs={{0,64},{1,65},{2,66},{3,67},{4,68},{5,69},{6,70},{7,71},{8,72},{9,... | collective-permute-start | bytes 172040 | tf_op jit(solution)/shard_map/ppermute | solution.py:303
  54.9 7.7 %collective-permute-start.7 = (f32[112,128]{1,0:T(8,128)S(1)}, f32[112,128]{1,0:T(8,128)S(1)}, u32[]{:S(2)}, u32[]{:S(2)}) collective-permute-start(f32[112,128]{1,0:T(8,128)S(1)} %add_add_fusion.1), channel_id=1, source_target_pairs={{0,32},{1,33},{2,34},{3,35},{4,36},{5,37},{6,38},{7,39},{8,40},{9,... | collective-permute-start | bytes 172040 | tf_op jit(solution)/shard_map/ppermute | solution.py:303
  62.6 1.4 %collective-permute-start.11 = (f32[112,128]{1,0:T(8,128)S(1)}, f32[112,128]{1,0:T(8,128)S(1)}, u32[]{:S(2)}, u32[]{:S(2)}) collective-permute-start(f32[112,128]{1,0:T(8,128)S(1)} %add_add_fusion.part), channel_id=1, source_target_pairs={{0,1},{1,0},{2,3},{3,2},{4,5},{5,4},{6,7},{7,6},{8,9},{9,8},{10,11... | collective-permute-start | bytes 172040 | tf_op jit(solution)/shard_map/ppermute | solution.py:303
  64.1 3.6 %copy-start.8 = (bf16[36,96,128]{2,1,0:T(8,128)(2,1)}, bf16[36,96,128]{2,1,0:T(8,128)(2,1)S(1)}, u32[]{:S(2)}) copy-start(bf16[36,96,128]{2,1,0:T(8,128)(2,1)S(1)} %collective-permute-done.12.source.edge) | copy-start | bytes 2654212
  64.1 8.5 %collective-permute-start.15 = (f32[224,128]{1,0:T(8,128)S(1)}, f32[224,128]{1,0:T(8,128)S(1)}, u32[]{:S(2)}, u32[]{:S(2)}) collective-permute-start(f32[224,128]{1,0:T(8,128)S(1)} %shard_map.88.part), channel_id=1, source_target_pairs={{0,18},{1,19},{2,16},{3,17},{4,22},{5,23},{6,20},{7,21},{8,26},{9,... | collective-permute-start | bytes 344072 | tf_op jit(solution)/shard_map/ppermute | solution.py:303
  64.4 8.2 %collective-permute-start.14 = (f32[224,128]{1,0:T(8,128)S(1)}, f32[224,128]{1,0:T(8,128)S(1)}, u32[]{:S(2)}, u32[]{:S(2)}) collective-permute-start(f32[224,128]{1,0:T(8,128)S(1)} %shard_map.88.part), channel_id=1, source_target_pairs={{0,16},{1,17},{2,18},{3,19},{4,20},{5,21},{6,22},{7,23},{8,24},{9,... | collective-permute-start | bytes 344072 | tf_op jit(solution)/shard_map/ppermute | solution.py:303
  67.7 5.1 %collective-permute-start.13 = (f32[224,128]{1,0:T(8,128)S(1)}, f32[224,128]{1,0:T(8,128)S(1)}, u32[]{:S(2)}, u32[]{:S(2)}) collective-permute-start(f32[224,128]{1,0:T(8,128)S(1)} %shard_map.88.part), channel_id=1, source_target_pairs={{0,2},{1,3},{2,0},{3,1},{4,6},{5,7},{6,4},{7,5},{8,10},{9,11},{10,... | collective-permute-start | bytes 344072 | tf_op jit(solution)/shard_map/ppermute | solution.py:303

commit v4 on v3

--- a/solution.py
+++ b/solution.py
@@ -47,7 +47,7 @@
         scratch[pl.ds(half * 8 * pitch + group, 8, stride=pitch), :] = block[half * 8 : half * 8 + 8]
 
 
-def group_body(act_in, grad_in, mask_in, low, high, firsts, lasts, scratch, act, grad, mask, arrived):
+def group_body(act_in, grad_in, mask_in, low, high_first, high_rest, firsts, lasts, scratch, act, grad, mask, arrived):
     rows, groups = act.shape[1], low.shape[1]
     copies = [
         [
@@ -59,8 +59,9 @@
     for plane in (1, 0):
         for copy in copies[plane]:
             copy.start()
-    for plane, out in ((1, high), (0, low)):
+    for plane in (1, 0):
         for kind in range(2):
+            out = high_first if plane else low
             for copy in copies[plane][:1] if kind == 0 else copies[plane][1:]:
                 copy.wait()
             for group in range(groups):
@@ -72,9 +73,15 @@
                 spread_rows(scratch, groups, group, block)
             for row in range(rows):
                 at = row * (groups + 1)
-                out[kind * rows + row] = scratch[at : at + groups, :].astype(BF16)
-            firsts[plane * 2 + kind] = out[kind * rows]
-            lasts[plane * 2 + kind] = out[kind * rows + rows - 1]
+                cells = scratch[at : at + groups, :].astype(BF16)
+                if plane and kind and row >= EARLY:
+                    high_rest[row - EARLY] = cells
+                else:
+                    out[kind * rows + row] = cells
+                if row == 0:
+                    firsts[plane * 2 + kind] = cells
+                if row == rows - 1:
+                    lasts[plane * 2 + kind] = cells
 
 
 def with_edges(cells):
@@ -119,6 +126,7 @@
 
 
 CHUNK = 4
+EARLY = 8
 
 
 def fold(term):
@@ -132,24 +140,34 @@
     return total[:, :LANES]
 
 
+def gather_grad(first, rest, grad):
+    rows = grad.shape[0]
+    if first.shape == rest.shape:
+        grad[...] = first[rows : 2 * rows]
+    else:
+        grad[:EARLY] = first[rows:]
+        grad[EARLY:] = rest[: rows - EARLY]
+
+
 def own_body(
-    low, high, from_left, from_right, kernel,
-    folded, bias_terms, partial_f, weights_f, partial_g, weights_g, turned, taps,
+    low, high_first, high_rest, from_left, from_right, kernel,
+    folded, bias_terms, partial_f, weights_f, partial_g, weights_g, turned, taps, high_grad,
 ):
     rows, groups = low.shape[0] // 2, low.shape[1]
     chunks = rows // CHUNK
     step = pl.program_id(0)
 
     def fill(kind):
-        for plane, source in enumerate((low, high)):
+        for plane, source in enumerate((low.at[kind * rows : kind * rows + rows], (high_first.at[:rows], high_grad)[kind])):
             at = 2 * plane + kind
-            fill_plane(taps, plane, source.at[kind * rows : kind * rows + rows], from_left[at], from_right[at])
+            fill_plane(taps, plane, source, from_left[at], from_right[at])
 
     @pl.when(step == 0)
     def _():
+        gather_grad(high_first, high_rest, high_grad)
         sums = jnp.zeros((8, LANES), F32)
-        for plane, source in enumerate((low, high)):
-            flat = source[rows:].reshape(rows * groups, LANES)
+        for plane, source in enumerate((low.at[rows:], high_grad)):
+            flat = source[...].reshape(rows * groups, LANES)
             turned[plane * LANES : (plane + 1) * LANES, :] = flat.T
             sums = sums + jnp.sum(flat.astype(F32).reshape(-1, 8, LANES), axis=0)
         bias_terms[...] = sums
@@ -184,12 +202,16 @@
         add(weights_g, partial_g, step - chunks)
 
 
-def kernel_grad_body(below, low, from_left, from_right, folded, bias_terms, flag, keep, send, packed, taps, sums):
+def kernel_grad_body(
+    below_first, below_rest, low, from_left, from_right, folded, bias_terms, flag,
+    keep, send, packed, taps, sums, below_grad,
+):
     rows, groups = low.shape[0] // 2, low.shape[1]
     blank = jnp.zeros((groups, LANES), BF16)
-    fill_plane(taps, 0, below.at[:rows], blank, blank)
+    gather_grad(below_first, below_rest, below_grad)
+    fill_plane(taps, 0, below_first.at[:rows], blank, blank)
     fill_plane(taps, 1, low.at[:rows], from_left[0], from_right[0])
-    below_turned = below[rows : 2 * rows].reshape(rows * groups, LANES).T
+    below_turned = below_grad[...].reshape(rows * groups, LANES).T
     low_turned = low[rows:].reshape(rows * groups, LANES).T
     for tap_y in range(3):
         rhs = taps[0, tap_y : tap_y + rows].reshape(rows * groups, 256)
@@ -229,15 +251,18 @@
     return total
 
 
-def outer_body(plane, source, edge, weights_f, weights_g, partial_f, partial_g, line, *rest):
-    output, grad_input, taps, scratch = rest[-4:]
+def outer_body(first, rest, weights_f, weights_g, partial_f, partial_g, line, *more):
+    output, grad_input, taps, scratch, grad = more[-5:]
     rows, groups = partial_f.shape[1:3]
-    first = edge.shape[0] - 4
-    for kind, (weights, partial, out, turn) in enumerate(
-        ((weights_f, partial_f, output, rectified), (weights_g, partial_g, grad_input, kept))
+    act, edge = first.at[:rows], rest.at[rest.shape[0] - 4 :]
+    gather_grad(first, rest, grad)
+    for kind, (source, weights, partial, out, turn) in enumerate(
+        (
+            (act, weights_f, partial_f, output, rectified),
+            (grad, weights_g, partial_g, grad_input, kept),
+        )
     ):
-        span = source.at[kind * rows : kind * rows + rows]
-        fill_plane(taps, kind, span, edge[first + kind], edge[first + 2 + kind])
+        fill_plane(taps, kind, source, edge[kind], edge[2 + kind])
         for chunk in range(rows // CHUNK):
             start = chunk * CHUNK
             total = partial[0, start : start + CHUNK].reshape(CHUNK * groups, LANES)
@@ -314,6 +339,7 @@
     block = activations.shape
     shape = jax.ShapeDtypeStruct
     pair = shape((2 * rows, groups, LANES), BF16)
+    one_plane = pltpu.VMEM((rows, groups, LANES), BF16)
     lines = shape((4, groups, LANES), BF16)
     spread = pltpu.VMEM((rows * (groups + 1) + 8, LANES), F32)
     two_taps = pltpu.VMEM((2, rows + 2, groups, 2 * LANES), BF16)
@@ -321,10 +347,12 @@
     packed = pltpu.VMEM((2 * HALF, LANES), F32)
     flag = jnp.full((1, LANES), lax.axis_index("gy") % 2, F32)
 
-    low, high, firsts, lasts = pl.pallas_call(
+    low, high_first, high_rest, firsts, lasts = pl.pallas_call(
         group_body,
         in_specs=[pl.BlockSpec(memory_space=pl.ANY)] * 3,
-        out_shape=(pair, pair, lines, lines),
+        out_shape=(
+            pair, shape((rows + EARLY, groups, LANES), BF16), shape((rows - EARLY, groups, LANES), BF16), lines, lines,
+        ),
         scratch_shapes=[
             spread, pltpu.VMEM(block, BF16), pltpu.VMEM(block, BF16), pltpu.VMEM(block, jnp.int32),
             pltpu.SemaphoreType.DMA((2, 3)),
@@ -333,8 +361,8 @@
     )(activations, grad_out, relu_mask)
     from_left = shifted(lasts, "gy", 1)
     from_right = shifted(firsts, "gy", -1)
-    below = shifted(high, "gz", 1)
-    corner = shifted(jnp.concatenate([from_left[2:], from_right[2:]]), "gz", 1)
+    below_first = shifted(high_first, "gz", 1)
+    below_rest = shifted(jnp.concatenate([high_rest, from_left[2:], from_right[2:]]), "gz", 1)
 
     line = jnp.tile(bias, 4).reshape(1, LANES)
     flat_kernel = kernel.reshape(27 * 32, 32)
@@ -357,22 +385,22 @@
             pl.BlockSpec(piece, lambda step: (0, jnp.maximum(step - chunks, 0), 0, 0)),
             part_of(weights_shape, 0, 0, 0, 0),
         ),
-        [pltpu.VMEM((2 * LANES, rows * groups), BF16), two_taps],
-        (low, high, from_left, from_right, flat_kernel),
-        [part_of(pair.shape, 0, 0, 0)] * 2 + [part_of(lines.shape, 0, 0, 0)] * 2 + [part_of(flat_kernel.shape, 0, 0)],
+        [pltpu.VMEM((2 * LANES, rows * groups), BF16), two_taps, one_plane],
+        (low, high_first, high_rest, from_left, from_right, flat_kernel),
+        [part_of(array.shape, 0, 0, 0) for array in (low, high_first, high_rest)] + [part_of(lines.shape, 0, 0, 0)] * 2 + [part_of(flat_kernel.shape, 0, 0)],
     )
 
-    def outer(side, source, edge, done=()):
+    def outer(side, first, rest, done=()):
         weights, partial = part_of((1, 3, 256, LANES), 2 * side, 0, 0, 0), part_of((1, *plane), side, 0, 0, 0)
         return blocked(
-            functools.partial(outer_body, side),
+            outer_body,
             1,
             (shape(block, BF16), shape(block, BF16)),
             (part_of((1, *block[1:]), side, 0, 0),) * 2,
-            [two_taps, spread],
-            (source, edge, weights_f, weights_g, partial_f, partial_g, line, *done),
+            [two_taps, spread, one_plane],
+            (first, rest, weights_f, weights_g, partial_f, partial_g, line, *done),
             [
-                part_of(source.shape, 0, 0, 0), part_of(edge.shape, 0, 0, 0),
+                part_of(first.shape, 0, 0, 0), part_of(rest.shape, 0, 0, 0),
                 weights, weights, partial, partial, part_of((1, LANES), 0, 0),
                 *[pl.BlockSpec(memory_space=pl.ANY)] * len(done),
             ],
@@ -382,19 +410,18 @@
     ends = (from_left[:2], from_right[:2])
     ends, folded, partial_g = lax.optimization_barrier((ends, folded, partial_g))
     down = jnp.concatenate([low, *ends])
-    down, corner = lax.optimization_barrier((down, corner))
     above = shifted(down, "gz", -1)
 
     part, send = call(
         kernel_grad_body,
         (half, half),
-        [packed, two_taps, pltpu.VMEM((2, 3, LANES, 256), F32)],
-        (below, low, from_left, from_right, folded, bias_terms, flag),
+        [packed, two_taps, pltpu.VMEM((2, 3, LANES, 256), F32), one_plane],
+        (below_first, below_rest, low, from_left, from_right, folded, bias_terms, flag),
     )
     part = part + swapped(send, 1)
     part = sum_of_four(part, 4, 8)
     part = sum_of_four(part, 32, 64)
-    results = outer(0, below, corner)
+    results = outer(0, below_first, below_rest)
     part, results = lax.optimization_barrier((part, results))
     part = call(join_body, shape((2 * HALF, LANES), F32), [], (part, swapped(part, 1), flag))
     part, above = lax.optimization_barrier((part, above))

time: 74.8 us -> 72.3 us (0.967)
  waiting for transfers between devices: 9.96 us -> 8.09 us
  starting transfers between devices: 34.9 us -> 33.1 us
  other arithmetic: 1.08 us -> 2.06 us
    ppermute x11, starting transfers between devices: 17.3 us -> 15.3 us  [swapped(): lax.ppermute(value, ('gz', 'gy'), [(i, i ^ bit) for i in range(count)])]
    ppermute x5, waiting for transfers between devices: 1.72 us -> 0.01 us  [shifted(): return lax.ppermute(value, axis, pairs)]
    concatenate x1, other arithmetic: 0.01 us -> 0.99 us  [local(): jnp.concatenate([high_rest, from_left[2:], from_right[2:]])]
  transfers between devices with their start and end apart: 16 -> 16, of which waited for: 7 -> 5; matrix products, arithmetic and copies ran while one was open for 2% -> 4% of each run, Pallas kernels for 30% -> 31%
where the time goes in v4:
time: 72.3 us; the launch traced here: 71.1 us
  starting transfers between devices  33.1 us (46%)
  Pallas kernels  26.3 us (36%)
  waiting for transfers between devices  8.09 us (11%)
  other arithmetic  2.06 us (3%)
  between operations  0.94 us (1%)
    pallas_call x3, Pallas kernels, blocked(): pl.pallas_call(body, grid=(grid,), out_shape=outs, in_specs=in_specs, out...  20.7 us
    ppermute x5, starting transfers between devices, shifted(): return lax.ppermute(value, axis, pairs)  17.8 us
    ppermute x11, starting transfers between devices, swapped(): lax.ppermute(value, ('gz', 'gy'), [(i, i ^ bit) for i in range(count)])  15.3 us
    ppermute x11, waiting for transfers between devices, swapped(): lax.ppermute(value, ('gz', 'gy'), [(i, i ^ bit) for i in range(count)])  8.07 us
    pallas_call x1, Pallas kernels, local(): pl.pallas_call(group_body, in_specs=[pl.BlockSpec(memory_space=pl.ANY)] *...  3.06 us
    pallas_call x3, Pallas kernels, call(): pl.pallas_call(body, out_shape=outs, scratch_shapes=scratch, compiler_par...  2.52 us
  transfers between devices with their start and end apart: 16, of which 5 were waited for; matrix products, arithmetic and copies ran while one was open for 4% of the time, Pallas kernels for 31%

profile of v4, /device:TPU:1, one launch (start us, length us, event | category | flops | bytes accessed | tf_op | source)
XLA Modules:
  0.0 71.1 jit_solution(11455183998278245449)
XLA Ops:
  0.6 3.1 %shard_map.84 = (bf16[32,96,128]{2,1,0:T(8,128)(2,1)}, bf16[24,96,128]{2,1,0:T(8,128)(2,1)}, bf16[8,96,128]{2,1,0:T(8,128)(2,1)}, bf16[4,96,128]{2,1,0:T(8,128)(2,1)}, bf16[4,96,128]{2,1,0:T(8,128)(2,1)}) custom-call(bf16[2,16,12288]{2,1,0:T(8,128)(2,1)} %act_in.1, bf16[2,16,12288]{2,1,0:T(8,128)(2,1)} %grad_in.1, s32[2,16,12288]{2,1,0:T(8,128)} %mask_in.1), custom_call_target="tpu_custom_call" | custom-call | tf_op jit(solution)/shard_map/pallas_call | solution.py:350
  3.7 0.0 copy-start
  3.7 5.1 %collective-permute-start.1 = (bf16[4,96,128]{2,1,0:T(8,128)(2,1)}, bf16[4,96,128]{2,1,0:T(8,128)(2,1)S(1)}, u32[]{:S(2)}, u32[]{:S(2)}) collective-permute-start(bf16[4,96,128]{2,1,0:T(8,128)(2,1)} %get-tuple-element.34), channel_id=1, source_target_pairs={{0,1},{1,2},{2,3},{3,4},{4,5},{5,6},{6,7},{7,8},{8,9},{9,10},{10,1... | collective-permute-start | bytes 294920 | tf_op jit(solution)/shard_map/ppermute | solution.py:323
  8.8 1.9 %collective-permute-start.2 = (bf16[4,96,128]{2,1,0:T(8,128)(2,1)}, bf16[4,96,128]{2,1,0:T(8,128)(2,1)S(1)}, u32[]{:S(2)}, u32[]{:S(2)}) collective-permute-start(bf16[4,96,128]{2,1,0:T(8,128)(2,1)} %get-tuple-element.35), channel_id=1, source_target_pairs={{1,0},{2,1},{3,2},{4,3},{5,4},{6,5},{7,6},{8,7},{9,8},{10,9},{11,1... | collective-permute-start | bytes 294920 | tf_op jit(solution)/shard_map/ppermute | solution.py:323
  10.7 5.2 %collective-permute-start = (bf16[24,96,128]{2,1,0:T(8,128)(2,1)}, bf16[24,96,128]{2,1,0:T(8,128)(2,1)S(1)}, u32[]{:S(2)}, u32[]{:S(2)}) collective-permute-start(bf16[24,96,128]{2,1,0:T(8,128)(2,1)} %get-tuple-element.32.high_first), channel_id=1, source_target_pairs={{0,16},{16,32},{32,48},{48,64},{64,80},{80,96},{96,112},{1,17},{17... | collective-permute-start | bytes 1769480 | tf_op jit(solution)/shard_map/ppermute | solution.py:323
  16.0 0.0 collective-permute-done.1.from_left
  16.0 0.0 copy-start.3
  16.0 0.0 collective-permute-done.2.from_right
  16.0 0.0 copy-start.5
  16.0 1.0 %pad_maximum_fusion.1 = bf16[12,96,128]{2,1,0:T(8,128)(2,1)S(1)} fusion(bf16[2,96,128]{2,1,0:T(8,128)(2,1)S(1)} %get-tuple-element.61, bf16[2,96,128]{2,1,0:T(8,128)(2,1)S(1)} %get-tuple-element.63, bf16[8,96,128]{2,1,0:T(8,128)(2,1)} %get-tuple-element.33.high_rest), kind=kLoop, calls=%fused_computation.1 | loop fusion | flops 294912 | bytes 589824 | tf_op jit(solution)/shard_map/concatenate | solution.py:365
  17.0 4.1 %collective-permute-start.3 = (bf16[12,96,128]{2,1,0:T(8,128)(2,1)S(1)}, bf16[12,96,128]{2,1,0:T(8,128)(2,1)S(1)}, u32[]{:S(2)}, u32[]{:S(2)}) collective-permute-start(bf16[12,96,128]{2,1,0:T(8,128)(2,1)S(1)} %pad_maximum_fusion.1), channel_id=1, source_target_pairs={{0,16},{16,32},{32,48},{48,64},{64,80},{80,96},{96,112},{1,17},{17... | collective-permute-start | bytes 884744 | tf_op jit(solution)/shard_map/ppermute | solution.py:323
  21.2 0.0 copy-done.3
  21.2 0.0 copy-done.5
  21.2 11.0 %shard_map.85 = (f32[3,3,32,128]{3,2,1,0:T(8,128)}, f32[8,128]{1,0:T(8,128)}, f32[2,16,96,128]{3,2,1,0:T(8,128)}, bf16[3,3,256,128]{3,2,1,0:T(8,128)(2,1)}, f32[...) custom-call(bf16[32,96,128]{2,1,0:T(8,128)(2,1)} %get-tuple-element.36.low, ...), custom_call_target="tpu_custom_call" | custom-call | tf_op jit(solution)/shard_map/pallas_call | solution.py:27
  32.2 0.0 copy-start.4
  32.3 0.0 copy-start.6
  32.3 0.0 copy-start.7
  32.3 0.0 copy-start.8
  32.3 0.0 copy-done
  32.3 1.0 %pad_maximum_fusion = bf16[36,96,128]{2,1,0:T(8,128)(2,1)} fusion(bf16[2,96,128]{2,1,0:T(8,128)(2,1)S(1)} %get-tuple-element.51, bf16[2,96,128]{2,1,0:T(8,128)(2,1)S(1)} %get-tuple-element.50, bf16[32,96,128]{2,1,0:T(8,128)(2,1)S(1)} %copy-done), kind=kLoop, calls=%fused_computation | loop fusion | flops 884736 | bytes 1769472 | tf_op jit(solution)/shard_map/concatenate | solution.py:412
  33.3 0.0 copy-start.10
  33.3 1.4 %collective-permute-start.12 = (bf16[36,96,128]{2,1,0:T(8,128)(2,1)}, bf16[36,96,128]{2,1,0:T(8,128)(2,1)S(1)}, u32[]{:S(2)}, u32[]{:S(2)}) collective-permute-start(bf16[36,96,128]{2,1,0:T(8,128)(2,1)} %pad_maximum_fusion), channel_id=1, source_target_pairs={{16,0},{32,16},{48,32},{64,48},{80,64},{96,80},{112,96},{17,1},{33... | collective-permute-start | bytes 2654216 | tf_op jit(solution)/shard_map/ppermute | solution.py:323
  34.7 0.0 collective-permute-done.3.below_rest.rest
  34.8 0.0 copy-start.2
  34.8 0.0 collective-permute-done.below_first.first
  34.8 0.0 copy-start.1
  34.8 0.0 copy-done.4
  34.8 0.0 copy-done.6
  34.8 0.0 copy-done.7
  34.8 0.0 copy-done.8
  34.8 1.5 %shard_map.86 = (f32[112,128]{1,0:T(8,128)S(1)}, f32[112,128]{1,0:T(8,128)S(1)}) custom-call(bf16[24,96,128]{2,1,0:T(8,128)(2,1)S(1)} %collective-permute-done.below_first.first, bf16[12,96,128]{2,1,0:T(8,128)(2,1)S(1)} %collective-permute-done.3.below_rest.rest, bf16[32,96,128]{2,1,0:T(8,128)(2,1)S(1)} %copy-done, bf16[4,96,128]{2,1,0:T(8,128)(2,1)S(1)} %copy-done.4, ...), custom_call_target="tpu_custom_call" | custom-call | tf_op jit(solution)/shard_map/pallas_call | solution.py:18
  36.4 0.1 collective-permute-start.4
  36.5 1.2 %collective-permute-done.4 = f32[112,128]{1,0:T(8,128)S(1)} collective-permute-done((f32[112,128]{1,0:T(8,128)S(1)}, f32[112,128]{1,0:T(8,128)S(1)}, u32[]{:S(2)}, u32[]{:S(2)}) %collective-permute-start.4) | collective-permute-done | bytes 57376 | tf_op jit(solution)/shard_map/ppermute | solution.py:328
  37.7 3.4 %collective-permute-start.7 = (f32[112,128]{1,0:T(8,128)S(1)}, f32[112,128]{1,0:T(8,128)S(1)}, u32[]{:S(2)}, u32[]{:S(2)}) collective-permute-start(f32[112,128]{1,0:T(8,128)S(1)} %add.26), channel_id=1, source_target_pairs={{0,12},{1,13},{2,14},{3,15},{4,8},{5,9},{6,10},{7,11},{8,4},{9,5},... | collective-permute-start | bytes 172040 | tf_op jit(solution)/shard_map/ppermute | solution.py:328
  41.1 0.5 collective-permute-start.6
  41.6 0.2 collective-permute-start.5
  41.8 1.3 %collective-permute-done.7 = f32[112,128]{1,0:T(8,128)S(1)} collective-permute-done((f32[112,128]{1,0:T(8,128)S(1)}, f32[112,128]{1,0:T(8,128)S(1)}, u32[]{:S(2)}, u32[]{:S(2)}) %collective-permute-start.7) | collective-permute-done | bytes 57376 | tf_op jit(solution)/shard_map/ppermute | solution.py:328
  43.0 2.9 %collective-permute-done.6 = f32[112,128]{1,0:T(8,128)S(1)} collective-permute-done((f32[112,128]{1,0:T(8,128)S(1)}, f32[112,128]{1,0:T(8,128)S(1)}, u32[]{:S(2)}, u32[]{:S(2)}) %collective-permute-start.6) | collective-permute-done | bytes 57376 | tf_op jit(solution)/shard_map/ppermute | solution.py:328
  45.9 0.0 collective-permute-done.5
  45.9 6.1 %collective-permute-start.10 = (f32[112,128]{1,0:T(8,128)S(1)}, f32[112,128]{1,0:T(8,128)S(1)}, u32[]{:S(2)}, u32[]{:S(2)}) collective-permute-start(f32[112,128]{1,0:T(8,128)S(1)} %add_add_fusion.1), channel_id=1, source_target_pairs={{0,96},{1,97},{2,98},{3,99},{4,100},{5,101},{6,102},{7,103},{8,104... | collective-permute-start | bytes 172040 | tf_op jit(solution)/shard_map/ppermute | solution.py:328
  52.0 0.3 collective-permute-start.9
  52.4 0.3 collective-permute-start.8
  52.7 0.0 copy-done.10
  52.7 0.6 reshape_tile.3.line
  53.3 0.0 copy-done.2
  53.3 0.0 copy-done.1
  53.3 4.7 %shard_map.87 = (bf16[2,16,12288]{2,1,0:T(8,128)(2,1)}, bf16[2,16,12288]{2,1,0:T(8,128)(2,1)}) custom-call(bf16[24,96,128]{2,1,0:T(8,128)(2,1)} %copy-done.1, bf16[12,96,128]{2,1,0:T(8,128)(2,1)} %copy-done.2, bf16[3,3,256,128]{3,2,1,0:T(8,128)(2,1)} %get-tuple-element.43.weights_f, bf16[3,3,256,128]{3,2,1,0:T(8,128)(2,1)} %get-tuple-element.44.weights_g, ...), custom_call_target="tpu_custom_call" | custom-call | tf_op jit(solution)/shard_map/pallas_call | solution.py:27
  58.0 0.0 collective-permute-done.10
  58.0 0.0 collective-permute-done.9
  58.0 1.8 %collective-permute-done.8 = f32[112,128]{1,0:T(8,128)S(1)} collective-permute-done((f32[112,128]{1,0:T(8,128)S(1)}, f32[112,128]{1,0:T(8,128)S(1)}, u32[]{:S(2)}, u32[]{:S(2)}) %collective-permute-start.8) | collective-permute-done | bytes 57376 | tf_op jit(solution)/shard_map/ppermute | solution.py:328
  59.8 0.5 collective-permute-start.11
  60.3 0.9 %collective-permute-done.11.other = f32[112,128]{1,0:T(8,128)S(1)} collective-permute-done((f32[112,128]{1,0:T(8,128)S(1)}, f32[112,128]{1,0:T(8,128)S(1)}, u32[]{:S(2)}, u32[]{:S(2)}) %collective-permute-start.11) | collective-permute-done | bytes 57376 | tf_op jit(solution)/shard_map/ppermute | solution.py:328
  61.2 0.0 collective-permute-done.12.first.rest
  61.2 0.0 copy-start.9
  61.2 0.4 collective-permute-start.15
  61.6 3.6 %collective-permute-start.14 = (f32[224,128]{1,0:T(8,128)S(1)}, f32[224,128]{1,0:T(8,128)S(1)}, u32[]{:S(2)}, u32[]{:S(2)}) collective-permute-start(f32[224,128]{1,0:T(8,128)S(1)} %shard_map.88.part), channel_id=1, source_target_pairs={{0,16},{1,17},{2,18},{3,19},{4,20},{5,21},{6,22},{7,23},{8,24},{9,... | collective-permute-start | bytes 344072 | tf_op jit(solution)/shard_map/ppermute | solution.py:328
  65.2 0.0 collective-permute-start.13
  65.2 0.0 copy-done.9
  65.2 4.9 %shard_map.89 = (bf16[2,16,12288]{2,1,0:T(8,128)(2,1)}, bf16[2,16,12288]{2,1,0:T(8,128)(2,1)}) custom-call(bf16[36,96,128]{2,1,0:T(8,128)(2,1)} %copy-done.9, bf16[36,96,128]{2,1,0:T(8,128)(2,1)} %copy-done.9, bf16[3,3,256,128]{3,2,1,0:T(8,128)(2,1)} %get-tuple-element.43.weights_f, ...), custom_call_target="tpu_custom_call", output_to_operand_aliasing={{0}: (7, {}), {1}: (8, {})} | custom-call | tf_op jit(solution)/shard_map/pallas_call | solution.py:27
  70.1 0.0 collective-permute-done.15.three
  70.1 0.0 collective-permute-done.14.two
  70.1 0.0 collective-permute-done.13.one
  70.1 1.0 %shard_map.90 = (f32[864,32]{1,0:T(8,128)}, f32[1,32]{1,0:T(1,128)}) custom-call(f32[224,128]{1,0:T(8,128)S(1)} %shard_map.88.part, f32[224,128]{1,0:T(8,128)S(1)} %collective-permute-done.13.one, f32[224,128]{1,0:T(8,128)S(1)} %collective-permute-done.14.two, f32[224,128]{1,0:T(8,128)S(1)} %collective-permute-done.15.three), custom_call_target="tpu_custom_call" | custom-call | tf_op jit(solution)/shard_map/pallas_call | solution.py:18
  (8 shorter events, 0.1 us)
Async XLA Ops:
  3.7 28.6 %copy-start = (bf16[32,96,128]{2,1,0:T(8,128)(2,1)S(1)}, bf16[32,96,128]{2,1,0:T(8,128)(2,1)}, u32[]{:S(2)}) copy-start(bf16[32,96,128]{2,1,0:T(8,128)(2,1)} %get-tuple-element.36.low) | copy-start | bytes 2359300
  3.7 12.3 %collective-permute-start.1 = (bf16[4,96,128]{2,1,0:T(8,128)(2,1)}, bf16[4,96,128]{2,1,0:T(8,128)(2,1)S(1)}, u32[]{:S(2)}, u32[]{:S(2)}) collective-permute-start(bf16[4,96,128]{2,1,0:T(8,128)(2,1)} %get-tuple-element.34), channel_id=1, source_target_pairs={{0,1},{1,2},{2,3},{3,4},{4,5},{5,6},{6,7},{7,8},{8,9},{9,10},{10,1... | collective-permute-start | bytes 294920 | tf_op jit(solution)/shard_map/ppermute | solution.py:323
  8.8 7.2 %collective-permute-start.2 = (bf16[4,96,128]{2,1,0:T(8,128)(2,1)}, bf16[4,96,128]{2,1,0:T(8,128)(2,1)S(1)}, u32[]{:S(2)}, u32[]{:S(2)}) collective-permute-start(bf16[4,96,128]{2,1,0:T(8,128)(2,1)} %get-tuple-element.35), channel_id=1, source_target_pairs={{1,0},{2,1},{3,2},{4,3},{5,4},{6,5},{7,6},{8,7},{9,8},{10,9},{11,1... | collective-permute-start | bytes 294920 | tf_op jit(solution)/shard_map/ppermute | solution.py:323
  10.7 24.1 %collective-permute-start = (bf16[24,96,128]{2,1,0:T(8,128)(2,1)}, bf16[24,96,128]{2,1,0:T(8,128)(2,1)S(1)}, u32[]{:S(2)}, u32[]{:S(2)}) collective-permute-start(bf16[24,96,128]{2,1,0:T(8,128)(2,1)} %get-tuple-element.32.high_first), channel_id=1, source_target_pairs={{0,16},{16,32},{32,48},{48,64},{64,80},{80,96},{96,112},{1,17},{17... | collective-permute-start | bytes 1769480 | tf_op jit(solution)/shard_map/ppermute | solution.py:323
  16.0 5.2 %copy-start.3 = (bf16[4,96,128]{2,1,0:T(8,128)(2,1)}, bf16[4,96,128]{2,1,0:T(8,128)(2,1)S(1)}, u32[]{:S(2)}) copy-start(bf16[4,96,128]{2,1,0:T(8,128)(2,1)S(1)} %collective-permute-done.1.from_left) | copy-start | bytes 294916
  16.0 5.2 %copy-start.5 = (bf16[4,96,128]{2,1,0:T(8,128)(2,1)}, bf16[4,96,128]{2,1,0:T(8,128)(2,1)S(1)}, u32[]{:S(2)}) copy-start(bf16[4,96,128]{2,1,0:T(8,128)(2,1)S(1)} %collective-permute-done.2.from_right) | copy-start | bytes 294916
  17.0 17.7 %collective-permute-start.3 = (bf16[12,96,128]{2,1,0:T(8,128)(2,1)S(1)}, bf16[12,96,128]{2,1,0:T(8,128)(2,1)S(1)}, u32[]{:S(2)}, u32[]{:S(2)}) collective-permute-start(bf16[12,96,128]{2,1,0:T(8,128)(2,1)S(1)} %pad_maximum_fusion.1), channel_id=1, source_target_pairs={{0,16},{16,32},{32,48},{48,64},{64,80},{80,96},{96,112},{1,17},{17... | collective-permute-start | bytes 884744 | tf_op jit(solution)/shard_map/ppermute | solution.py:323
  32.2 2.6 %copy-start.4 = (bf16[4,96,128]{2,1,0:T(8,128)(2,1)S(1)}, bf16[4,96,128]{2,1,0:T(8,128)(2,1)}, u32[]{:S(2)}) copy-start(bf16[4,96,128]{2,1,0:T(8,128)(2,1)} %copy-done.3) | copy-start | bytes 294916
  32.3 2.6 %copy-start.6 = (bf16[4,96,128]{2,1,0:T(8,128)(2,1)S(1)}, bf16[4,96,128]{2,1,0:T(8,128)(2,1)}, u32[]{:S(2)}) copy-start(bf16[4,96,128]{2,1,0:T(8,128)(2,1)} %copy-done.5) | copy-start | bytes 294916
  32.3 2.6 %copy-start.7 = (f32[3,3,32,128]{3,2,1,0:T(8,128)S(1)}, f32[3,3,32,128]{3,2,1,0:T(8,128)}, u32[]{:S(2)}) copy-start(f32[3,3,32,128]{3,2,1,0:T(8,128)} %get-tuple-element.39.folded) | copy-start | bytes 442372
  32.3 2.6 %copy-start.8 = (f32[8,128]{1,0:T(8,128)S(1)}, f32[8,128]{1,0:T(8,128)}, u32[]{:S(2)}) copy-start(f32[8,128]{1,0:T(8,128)} %get-tuple-element.40.bias_terms) | copy-start | bytes 12292
  33.3 19.4 %copy-start.10 = (f32[32]{0:T(128)S(1)}, f32[32]{0:T(128)}, u32[]{:S(2)}) copy-start(f32[32]{0:T(128)} %param.9) | copy-start | bytes 388
  33.3 27.9 %collective-permute-start.12 = (bf16[36,96,128]{2,1,0:T(8,128)(2,1)}, bf16[36,96,128]{2,1,0:T(8,128)(2,1)S(1)}, u32[]{:S(2)}, u32[]{:S(2)}) collective-permute-start(bf16[36,96,128]{2,1,0:T(8,128)(2,1)} %pad_maximum_fusion), channel_id=1, source_target_pairs={{16,0},{32,16},{48,32},{64,48},{80,64},{96,80},{112,96},{17,1},{33... | collective-permute-start | bytes 2654216 | tf_op jit(solution)/shard_map/ppermute | solution.py:323
  34.8 18.5 %copy-start.2 = (bf16[12,96,128]{2,1,0:T(8,128)(2,1)}, bf16[12,96,128]{2,1,0:T(8,128)(2,1)S(1)}, u32[]{:S(2)}) copy-start(bf16[12,96,128]{2,1,0:T(8,128)(2,1)S(1)} %collective-permute-done.3.below_rest.rest) | copy-start | bytes 884740
  34.8 18.5 %copy-start.1 = (bf16[24,96,128]{2,1,0:T(8,128)(2,1)}, bf16[24,96,128]{2,1,0:T(8,128)(2,1)S(1)}, u32[]{:S(2)}) copy-start(bf16[24,96,128]{2,1,0:T(8,128)(2,1)S(1)} %collective-permute-done.below_first.first) | copy-start | bytes 1769476
  36.4 1.3 %collective-permute-start.4 = (f32[112,128]{1,0:T(8,128)S(1)}, f32[112,128]{1,0:T(8,128)S(1)}, u32[]{:S(2)}, u32[]{:S(2)}) collective-permute-start(f32[112,128]{1,0:T(8,128)S(1)} %get-tuple-element.42), channel_id=1, source_target_pairs={{0,1},{1,0},{2,3},{3,2},{4,5},{5,4},{6,7},{7,6},{8,9},{9,8},{10,11... | collective-permute-start | bytes 172040 | tf_op jit(solution)/shard_map/ppermute | solution.py:328
  37.7 5.3 %collective-permute-start.7 = (f32[112,128]{1,0:T(8,128)S(1)}, f32[112,128]{1,0:T(8,128)S(1)}, u32[]{:S(2)}, u32[]{:S(2)}) collective-permute-start(f32[112,128]{1,0:T(8,128)S(1)} %add.26), channel_id=1, source_target_pairs={{0,12},{1,13},{2,14},{3,15},{4,8},{5,9},{6,10},{7,11},{8,4},{9,5},... | collective-permute-start | bytes 172040 | tf_op jit(solution)/shard_map/ppermute | solution.py:328
  41.1 4.8 %collective-permute-start.6 = (f32[112,128]{1,0:T(8,128)S(1)}, f32[112,128]{1,0:T(8,128)S(1)}, u32[]{:S(2)}, u32[]{:S(2)}) collective-permute-start(f32[112,128]{1,0:T(8,128)S(1)} %add.26), channel_id=1, source_target_pairs={{0,8},{1,9},{2,10},{3,11},{4,12},{5,13},{6,14},{7,15},{8,0},{9,1},... | collective-permute-start | bytes 172040 | tf_op jit(solution)/shard_map/ppermute | solution.py:328
  41.6 4.3 %collective-permute-start.5 = (f32[112,128]{1,0:T(8,128)S(1)}, f32[112,128]{1,0:T(8,128)S(1)}, u32[]{:S(2)}, u32[]{:S(2)}) collective-permute-start(f32[112,128]{1,0:T(8,128)S(1)} %add.26), channel_id=1, source_target_pairs={{0,4},{1,5},{2,6},{3,7},{4,0},{5,1},{6,2},{7,3},{8,12},{9,13},{10,... | collective-permute-start | bytes 172040 | tf_op jit(solution)/shard_map/ppermute | solution.py:328
  45.9 12.1 %collective-permute-start.10 = (f32[112,128]{1,0:T(8,128)S(1)}, f32[112,128]{1,0:T(8,128)S(1)}, u32[]{:S(2)}, u32[]{:S(2)}) collective-permute-start(f32[112,128]{1,0:T(8,128)S(1)} %add_add_fusion.1), channel_id=1, source_target_pairs={{0,96},{1,97},{2,98},{3,99},{4,100},{5,101},{6,102},{7,103},{8,104... | collective-permute-start | bytes 172040 | tf_op jit(solution)/shard_map/ppermute | solution.py:328
  52.0 6.0 %collective-permute-start.9 = (f32[112,128]{1,0:T(8,128)S(1)}, f32[112,128]{1,0:T(8,128)S(1)}, u32[]{:S(2)}, u32[]{:S(2)}) collective-permute-start(f32[112,128]{1,0:T(8,128)S(1)} %add_add_fusion.1), channel_id=1, source_target_pairs={{0,64},{1,65},{2,66},{3,67},{4,68},{5,69},{6,70},{7,71},{8,72},{9,... | collective-permute-start | bytes 172040 | tf_op jit(solution)/shard_map/ppermute | solution.py:328
  52.4 7.4 %collective-permute-start.8 = (f32[112,128]{1,0:T(8,128)S(1)}, f32[112,128]{1,0:T(8,128)S(1)}, u32[]{:S(2)}, u32[]{:S(2)}) collective-permute-start(f32[112,128]{1,0:T(8,128)S(1)} %add_add_fusion.1), channel_id=1, source_target_pairs={{0,32},{1,33},{2,34},{3,35},{4,36},{5,37},{6,38},{7,39},{8,40},{9,... | collective-permute-start | bytes 172040 | tf_op jit(solution)/shard_map/ppermute | solution.py:328
  59.8 1.4 %collective-permute-start.11 = (f32[112,128]{1,0:T(8,128)S(1)}, f32[112,128]{1,0:T(8,128)S(1)}, u32[]{:S(2)}, u32[]{:S(2)}) collective-permute-start(f32[112,128]{1,0:T(8,128)S(1)} %add_add_fusion.part), channel_id=1, source_target_pairs={{0,1},{1,0},{2,3},{3,2},{4,5},{5,4},{6,7},{7,6},{8,9},{9,8},{10,11... | collective-permute-start | bytes 172040 | tf_op jit(solution)/shard_map/ppermute | solution.py:328
  61.2 3.9 %copy-start.9 = (bf16[36,96,128]{2,1,0:T(8,128)(2,1)}, bf16[36,96,128]{2,1,0:T(8,128)(2,1)S(1)}, u32[]{:S(2)}) copy-start(bf16[36,96,128]{2,1,0:T(8,128)(2,1)S(1)} %collective-permute-done.12.first.rest) | copy-start | bytes 2654212
  61.2 8.9 %collective-permute-start.15 = (f32[224,128]{1,0:T(8,128)S(1)}, f32[224,128]{1,0:T(8,128)S(1)}, u32[]{:S(2)}, u32[]{:S(2)}) collective-permute-start(f32[224,128]{1,0:T(8,128)S(1)} %shard_map.88.part), channel_id=1, source_target_pairs={{0,18},{1,19},{2,16},{3,17},{4,22},{5,23},{6,20},{7,21},{8,26},{9,... | collective-permute-start | bytes 344072 | tf_op jit(solution)/shard_map/ppermute | solution.py:328
  61.6 8.5 %collective-permute-start.14 = (f32[224,128]{1,0:T(8,128)S(1)}, f32[224,128]{1,0:T(8,128)S(1)}, u32[]{:S(2)}, u32[]{:S(2)}) collective-permute-start(f32[224,128]{1,0:T(8,128)S(1)} %shard_map.88.part), channel_id=1, source_target_pairs={{0,16},{1,17},{2,18},{3,19},{4,20},{5,21},{6,22},{7,23},{8,24},{9,... | collective-permute-start | bytes 344072 | tf_op jit(solution)/shard_map/ppermute | solution.py:328
  65.2 5.0 %collective-permute-start.13 = (f32[224,128]{1,0:T(8,128)S(1)}, f32[224,128]{1,0:T(8,128)S(1)}, u32[]{:S(2)}, u32[]{:S(2)}) collective-permute-start(f32[224,128]{1,0:T(8,128)S(1)} %shard_map.88.part), channel_id=1, source_target_pairs={{0,2},{1,3},{2,0},{3,1},{4,6},{5,7},{6,4},{7,5},{8,10},{9,11},{10,... | collective-permute-start | bytes 344072 | tf_op jit(solution)/shard_map/ppermute | solution.py:328

commit v5 on v4

--- a/solution.py
+++ b/solution.py
@@ -126,41 +126,39 @@
 
 
 CHUNK = 4
+WIDE_CHUNK = 8
 EARLY = 8
 
 
 def fold(term):
-    total = None
-    for voxel in range(4):
-        part = term[voxel * 32 : voxel * 32 + 32]
-        shift = (-(voxel - 1) * 32) % 256
-        if shift:
-            part = pltpu.roll(part, shift, 1)
-        total = part if total is None else total + part
-    return total[:, :LANES]
+    near, far = term[:, :LANES], term[:, LANES:]
+    lane = lax.broadcasted_iota(jnp.int32, (32, LANES), 1)
+    first = pltpu.roll(jnp.where(lane < 96, near[:32], far[:32]), 32, 1)
+    third = pltpu.roll(near[64:96], 96, 1)
+    fourth = pltpu.roll(jnp.where(lane < 32, far[96:], near[96:]), 64, 1)
+    return (first + near[32:64]) + (third + fourth)
 
 
 def gather_grad(first, rest, grad):
     rows = grad.shape[0]
-    if first.shape == rest.shape:
-        grad[...] = first[rows : 2 * rows]
-    else:
-        grad[:EARLY] = first[rows:]
-        grad[EARLY:] = rest[: rows - EARLY]
+    early = first.shape[0] - rows
+    if early:
+        grad[:early] = first[rows:]
+    grad[early:] = rest[: rows - early]
 
 
 def own_body(
     low, high_first, high_rest, from_left, from_right, kernel,
-    folded, bias_terms, partial_f, weights_f, partial_g, weights_g, turned, taps, high_grad,
+    folded, bias_terms, partial, weights, turned, taps, high_grad,
 ):
     rows, groups = low.shape[0] // 2, low.shape[1]
-    chunks = rows // CHUNK
     step = pl.program_id(0)
 
     def fill(kind):
         for plane, source in enumerate((low.at[kind * rows : kind * rows + rows], (high_first.at[:rows], high_grad)[kind])):
             at = 2 * plane + kind
             fill_plane(taps, plane, source, from_left[at], from_right[at])
+        build_weights(kernel, kind == 1, weights.at[0])
 
     @pl.when(step == 0)
     def _():
@@ -171,8 +169,6 @@
             turned[plane * LANES : (plane + 1) * LANES, :] = flat.T
             sums = sums + jnp.sum(flat.astype(F32).reshape(-1, 8, LANES), axis=0)
         bias_terms[...] = sums
-        build_weights(kernel, False, weights_f)
-        build_weights(kernel, True, weights_g)
         fill(0)
         for tap_y in range(3):
             both = []
@@ -183,23 +179,18 @@
             folded[0, tap_y] = fold(both[0][LANES:])
             folded[2, tap_y] = fold(both[1][:LANES])
 
-    @pl.when(step == chunks)
+    @pl.when(step == 1)
     def _():
         fill(1)
 
-    def add(weights, partial, chunk):
-        total = inner_sum(taps, weights, chunk, groups)
+    def add(chunk, carry):
+        total = inner_sum(taps, weights.at[0], chunk, groups)
         for plane in range(2):
             part = total[:, plane * LANES : (plane + 1) * LANES]
-            partial[plane] = part.reshape(CHUNK, groups, LANES)
-
-    @pl.when(step < chunks)
-    def _():
-        add(weights_f, partial_f, step)
-
-    @pl.when(step >= chunks)
-    def _():
-        add(weights_g, partial_g, step - chunks)
+            partial[0, plane, pl.ds(chunk * WIDE_CHUNK, WIDE_CHUNK)] = part.reshape(WIDE_CHUNK, groups, LANES)
+        return carry
+
+    lax.fori_loop(0, rows // WIDE_CHUNK, add, 0)
 
 
 def kernel_grad_body(
@@ -244,32 +235,27 @@
     total = None
     for plane in range(2):
         for tap_y in range(3):
-            lhs = taps[plane, pl.ds(chunk * CHUNK + tap_y, CHUNK)].reshape(CHUNK * groups, 256)
+            lhs = taps[plane, pl.ds(chunk * WIDE_CHUNK + tap_y, WIDE_CHUNK)].reshape(WIDE_CHUNK * groups, 256)
             matrix = jnp.concatenate([weights[plane + 1, tap_y], weights[plane, tap_y]], axis=1)
             term = jnp.dot(lhs, matrix, preferred_element_type=F32)
             total = term if total is None else total + term
     return total
 
 
-def outer_body(first, rest, weights_f, weights_g, partial_f, partial_g, line, *more):
+def outer_body(first, rest, weights, partial, line, *more):
     output, grad_input, taps, scratch, grad = more[-5:]
-    rows, groups = partial_f.shape[1:3]
+    rows, groups = partial.shape[2:4]
     act, edge = first.at[:rows], rest.at[rest.shape[0] - 4 :]
     gather_grad(first, rest, grad)
-    for kind, (source, weights, partial, out, turn) in enumerate(
-        (
-            (act, weights_f, partial_f, output, rectified),
-            (grad, weights_g, partial_g, grad_input, kept),
-        )
-    ):
+    for kind, (source, out, turn) in enumerate(((act, output, rectified), (grad, grad_input, kept))):
         fill_plane(taps, kind, source, edge[kind], edge[2 + kind])
         for chunk in range(rows // CHUNK):
             start = chunk * CHUNK
-            total = partial[0, start : start + CHUNK].reshape(CHUNK * groups, LANES)
+            total = partial[kind, 0, start : start + CHUNK].reshape(CHUNK * groups, LANES)
             for tap_y in range(3):
                 at = start + tap_y
                 lhs = taps[kind, at : at + CHUNK].reshape(CHUNK * groups, 256)
-                total = total + jnp.dot(lhs, weights[0, tap_y], preferred_element_type=F32)
+                total = total + jnp.dot(lhs, weights[kind, 0, tap_y], preferred_element_type=F32)
             put_rows(scratch, turn(total, line), chunk, groups)
         lay_out(scratch, out, 0, rows, groups)
 
@@ -283,7 +269,7 @@
 
 
 def lay_out(scratch, out, plane, rows, groups):
-    pitch = groups + 1
+    pitch = groups + PITCH
     for group in range(groups):
         halves = [scratch[pl.ds(half * 8 * pitch + group, 8, stride=pitch), :] for half in range(2)]
         block = jnp.concatenate(halves, axis=0).astype(BF16)
@@ -292,23 +278,20 @@
 
 def put_rows(scratch, total, chunk, groups):
     for row in range(CHUNK):
-        at = (chunk * CHUNK + row) * (groups + 1)
+        at = (chunk * CHUNK + row) * (groups + PITCH)
         scratch[at : at + groups, :] = total[row * groups : (row + 1) * groups]
 
 
 HALF = 112
-
-
-def join_body(part, other, flag, packed):
+PITCH = 8
+
+
+def unpack_body(scaling, part, other, flag, grad_kernel, grad_bias, packed):
     upper = flag[...] > 0.5
     packed[:HALF] = jnp.where(upper, other[...], part[...])
     packed[HALF : 2 * HALF] = jnp.where(upper, part[...], other[...])
-
-
-def unpack_body(scaling, part, one, two, three, grad_kernel, grad_bias):
     for place in range(7):
-        span = slice(place * 32, place * 32 + 32)
-        block = ((part[span, :] + one[span, :]) + (two[span, :] + three[span, :])) * scaling
+        block = packed[place * 32 : place * 32 + 32, :] * scaling
         turned = block.T
         grad_kernel[place * 96 : place * 96 + 96, :] = turned[:96]
         if place < 6:
@@ -341,7 +324,7 @@
     pair = shape((2 * rows, groups, LANES), BF16)
     one_plane = pltpu.VMEM((rows, groups, LANES), BF16)
     lines = shape((4, groups, LANES), BF16)
-    spread = pltpu.VMEM((rows * (groups + 1) + 8, LANES), F32)
+    spread = pltpu.VMEM((rows * (groups + 8), LANES), F32)
     two_taps = pltpu.VMEM((2, rows + 2, groups, 2 * LANES), BF16)
     half = shape((HALF, LANES), F32)
     packed = pltpu.VMEM((2 * HALF, LANES), F32)
@@ -366,24 +349,19 @@
 
     line = jnp.tile(bias, 4).reshape(1, LANES)
     flat_kernel = kernel.reshape(27 * 32, 32)
-    chunks = rows // CHUNK
     plane = (rows, groups, LANES)
     folded_shape, bias_shape, weights_shape = (3, 3, 32, LANES), (8, LANES), (3, 3, 256, LANES)
-    piece = (2, CHUNK, groups, LANES)
-    folded, bias_terms, partial_f, weights_f, partial_g, weights_g = blocked(
+    folded, bias_terms, partial, weights = blocked(
         own_body,
-        2 * chunks,
+        2,
         (
             shape(folded_shape, F32), shape(bias_shape, F32),
-            shape((2, *plane), F32), shape(weights_shape, BF16),
-            shape((2, *plane), F32), shape(weights_shape, BF16),
+            shape((2, 2, *plane), F32), shape((2, *weights_shape), BF16),
         ),
         (
             part_of(folded_shape, 0, 0, 0, 0), part_of(bias_shape, 0, 0),
-            pl.BlockSpec(piece, lambda step: (0, jnp.minimum(step, chunks - 1), 0, 0)),
-            part_of(weights_shape, 0, 0, 0, 0),
-            pl.BlockSpec(piece, lambda step: (0, jnp.maximum(step - chunks, 0), 0, 0)),
-            part_of(weights_shape, 0, 0, 0, 0),
+            pl.BlockSpec((1, 2, *plane), lambda step: (step, 0, 0, 0, 0)),
+            pl.BlockSpec((1, *weights_shape), lambda step: (step, 0, 0, 0, 0)),
         ),
         [pltpu.VMEM((2 * LANES, rows * groups), BF16), two_taps, one_plane],
         (low, high_first, high_rest, from_left, from_right, flat_kernel),
@@ -391,26 +369,27 @@
     )
 
     def outer(side, first, rest, done=()):
-        weights, partial = part_of((1, 3, 256, LANES), 2 * side, 0, 0, 0), part_of((1, *plane), side, 0, 0, 0)
         return blocked(
             outer_body,
             1,
             (shape(block, BF16), shape(block, BF16)),
             (part_of((1, *block[1:]), side, 0, 0),) * 2,
             [two_taps, spread, one_plane],
-            (first, rest, weights_f, weights_g, partial_f, partial_g, line, *done),
+            (first, rest, weights, partial, line, *done),
             [
                 part_of(first.shape, 0, 0, 0), part_of(rest.shape, 0, 0, 0),
-                weights, weights, partial, partial, part_of((1, LANES), 0, 0),
+                part_of((2, 1, 3, 256, LANES), 0, 2 * side, 0, 0, 0), part_of((2, 1, *plane), 0, side, 0, 0, 0),
+                part_of((1, LANES), 0, 0),
                 *[pl.BlockSpec(memory_space=pl.ANY)] * len(done),
             ],
-            {7: 0, 8: 1} if done else None,
+            {5: 0, 6: 1} if done else None,
         )
 
+    split = rows + 4
     ends = (from_left[:2], from_right[:2])
-    ends, folded, partial_g = lax.optimization_barrier((ends, folded, partial_g))
-    down = jnp.concatenate([low, *ends])
-    above = shifted(down, "gz", -1)
+    ends, folded, partial, low_late = lax.optimization_barrier((ends, folded, partial, low))
+    above_first = shifted(low_late[:split], "gz", -1)
+    down_rest = jnp.concatenate([low_late[split:], *ends])
 
     part, send = call(
         kernel_grad_body,
@@ -420,20 +399,21 @@
     )
     part = part + swapped(send, 1)
     part = sum_of_four(part, 4, 8)
+    part, down_rest, above_first = lax.optimization_barrier((part, down_rest, above_first))
+    part = sum_of_four(part, 2, 16)
+    above_rest = shifted(down_rest, "gz", -1)
     part = sum_of_four(part, 32, 64)
     results = outer(0, below_first, below_rest)
-    part, results = lax.optimization_barrier((part, results))
-    part = call(join_body, shape((2 * HALF, LANES), F32), [], (part, swapped(part, 1), flag))
-    part, above = lax.optimization_barrier((part, above))
-    others = [swapped(part, bit) for bit in (2, 16, 18)]
-    results = outer(1, above, above, results)
+    part, results, above_rest = lax.optimization_barrier((part, results, above_rest))
+    other = swapped(part, 1)
+    results = outer(1, above_first, above_rest, results)
 
     voxels = planes * lax.axis_size("gz") * rows * lax.axis_size("gy") * (width // 32)
     grad_kernel, grad_bias = call(
         functools.partial(unpack_body, 1.0 / math.sqrt(voxels)),
         (shape((27 * 32, 32), F32), shape((1, 32), F32)),
-        [],
-        (part, *others),
+        [packed],
+        (part, other, flag),
     )
     return *results, grad_kernel.reshape(3, 3, 3, 32, 32), grad_bias.reshape(32)
 

time: 72.3 us -> 88.7 us (1.23)
  starting transfers between devices: 33.1 us -> 47.4 us
  local copies, waits for them, and re-layouts: 0.67 us -> 4.19 us
  waiting for transfers between devices: 8.09 us -> 10.2 us
  Pallas kernels: 26.3 us -> 24.4 us
  other arithmetic: 2.06 us -> 1.1 us
    ppermute x11, starting transfers between devices: 15.3 us -> 28.4 us  [swapped(): lax.ppermute(value, ('gz', 'gy'), [(i, i ^ bit) for i in range(count)])]
    unnamed x22 -> x24, local copies, waits for them, and re-layouts: 0.05 us -> 3.52 us
    ppermute x5 -> x6, waiting for transfers between devices: 0.01 us -> 2.3 us  [shifted(): return lax.ppermute(value, axis, pairs)]
    pallas_call x3, Pallas kernels: 20.7 us -> 18.8 us  [blocked(): pl.pallas_call(body, grid=(grid,), out_shape=outs, in_specs=in_specs, out...]
    ppermute x5 -> x6, starting transfers between devices: 17.8 us -> 18.9 us  [shifted(): return lax.ppermute(value, axis, pairs)]
    concatenate x1, other arithmetic: 1.02 us -> 0.05 us  [local(): down_rest = jnp.concatenate([low_late[split:], *ends])]
    pallas_call x3 -> x2, Pallas kernels: 2.52 us -> 2.49 us  [call(): pl.pallas_call(body, out_shape=outs, scratch_shapes=scratch, compiler_par...]
  transfers between devices with their start and end apart: 16 -> 17, of which waited for: 5 -> 6; matrix products, arithmetic and copies ran while one was open for 4% -> 2% of each run, Pallas kernels for 31% -> 23%
where the time goes in v5:
time: 88.7 us; the launch traced here: 88.2 us
  starting transfers between devices  47.4 us (53%)
  Pallas kernels  24.4 us (28%)
  waiting for transfers between devices  10.2 us (11%)
  local copies, waits for them, and re-layouts  4.19 us (5%)
  other arithmetic  1.1 us (1%)
  between operations  0.9 us (1%)
    ppermute x11, starting transfers between devices, swapped(): lax.ppermute(value, ('gz', 'gy'), [(i, i ^ bit) for i in range(count)])  28.4 us
    ppermute x6, starting transfers between devices, shifted(): return lax.ppermute(value, axis, pairs)  18.9 us
    pallas_call x3, Pallas kernels, blocked(): pl.pallas_call(body, grid=(grid,), out_shape=outs, in_specs=in_specs, out...  18.8 us
    ppermute x11, waiting for transfers between devices, swapped(): lax.ppermute(value, ('gz', 'gy'), [(i, i ^ bit) for i in range(count)])  7.91 us
    unnamed x24, local copies, waits for them, and re-layouts  3.52 us
    pallas_call x1, Pallas kernels, local(): pl.pallas_call(group_body, in_specs=[pl.BlockSpec(memory_space=pl.ANY)] *...  3.07 us
    pallas_call x2, Pallas kernels, call(): pl.pallas_call(body, out_shape=outs, scratch_shapes=scratch, compiler_par...  2.49 us
    ppermute x6, waiting for transfers between devices, shifted(): return lax.ppermute(value, axis, pairs)  2.3 us
  transfers between devices with their start and end apart: 17, of which 6 were waited for; matrix products, arithmetic and copies ran while one was open for 2% of the time, Pallas kernels for 23%

profile of v5, /device:TPU:1, one launch (start us, length us, event | category | flops | bytes accessed | tf_op | source)
XLA Modules:
  0.0 88.2 jit_solution(10108858201268304687)
XLA Ops:
  0.6 3.1 %shard_map.84 = (bf16[32,96,128]{2,1,0:T(8,128)(2,1)}, bf16[24,96,128]{2,1,0:T(8,128)(2,1)}, bf16[8,96,128]{2,1,0:T(8,128)(2,1)}, bf16[4,96,128]{2,1,0:T(8,128)(2,1)}, bf16[4,96,128]{2,1,0:T(8,128)(2,1)}) custom-call(bf16[2,16,12288]{2,1,0:T(8,128)(2,1)} %act_in.1, bf16[2,16,12288]{2,1,0:T(8,128)(2,1)} %grad_in.1, s32[2,16,12288]{2,1,0:T(8,128)} %mask_in.1), custom_call_target="tpu_custom_call" | custom-call | tf_op jit(solution)/shard_map/pallas_call | solution.py:333
  3.7 0.0 copy-start
  3.7 5.1 %collective-permute-start.1 = (bf16[4,96,128]{2,1,0:T(8,128)(2,1)}, bf16[4,96,128]{2,1,0:T(8,128)(2,1)S(1)}, u32[]{:S(2)}, u32[]{:S(2)}) collective-permute-start(bf16[4,96,128]{2,1,0:T(8,128)(2,1)} %get-tuple-element.35), channel_id=1, source_target_pairs={{0,1},{1,2},{2,3},{3,4},{4,5},{5,6},{6,7},{7,8},{8,9},{9,10},{10,1... | collective-permute-start | bytes 294920 | tf_op jit(solution)/shard_map/ppermute | solution.py:306
  8.8 1.9 %collective-permute-start.2 = (bf16[4,96,128]{2,1,0:T(8,128)(2,1)}, bf16[4,96,128]{2,1,0:T(8,128)(2,1)S(1)}, u32[]{:S(2)}, u32[]{:S(2)}) collective-permute-start(bf16[4,96,128]{2,1,0:T(8,128)(2,1)} %get-tuple-element.36), channel_id=1, source_target_pairs={{1,0},{2,1},{3,2},{4,3},{5,4},{6,5},{7,6},{8,7},{9,8},{10,9},{11,1... | collective-permute-start | bytes 294920 | tf_op jit(solution)/shard_map/ppermute | solution.py:306
  10.7 5.2 %collective-permute-start = (bf16[24,96,128]{2,1,0:T(8,128)(2,1)}, bf16[24,96,128]{2,1,0:T(8,128)(2,1)S(1)}, u32[]{:S(2)}, u32[]{:S(2)}) collective-permute-start(bf16[24,96,128]{2,1,0:T(8,128)(2,1)} %get-tuple-element.33.high_first), channel_id=1, source_target_pairs={{0,16},{16,32},{32,48},{48,64},{64,80},{80,96},{96,112},{1,17},{17... | collective-permute-start | bytes 1769480 | tf_op jit(solution)/shard_map/ppermute | solution.py:306
  16.0 0.0 collective-permute-done.1.from_left
  16.0 0.0 copy-start.3
  16.0 0.0 collective-permute-done.2.from_right
  16.0 0.0 copy-start.5
  16.0 1.0 %pad_maximum_fusion.1 = bf16[12,96,128]{2,1,0:T(8,128)(2,1)S(1)} fusion(bf16[2,96,128]{2,1,0:T(8,128)(2,1)S(1)} %get-tuple-element.63, bf16[2,96,128]{2,1,0:T(8,128)(2,1)S(1)} %get-tuple-element.65, bf16[8,96,128]{2,1,0:T(8,128)(2,1)} %get-tuple-element.34.high_rest), kind=kLoop, calls=%fused_computation.1 | loop fusion | flops 294912 | bytes 589824 | tf_op jit(solution)/shard_map/concatenate | solution.py:348
  17.0 4.1 %collective-permute-start.3 = (bf16[12,96,128]{2,1,0:T(8,128)(2,1)S(1)}, bf16[12,96,128]{2,1,0:T(8,128)(2,1)S(1)}, u32[]{:S(2)}, u32[]{:S(2)}) collective-permute-start(bf16[12,96,128]{2,1,0:T(8,128)(2,1)S(1)} %pad_maximum_fusion.1), channel_id=1, source_target_pairs={{0,16},{16,32},{32,48},{48,64},{64,80},{80,96},{96,112},{1,17},{17... | collective-permute-start | bytes 884744 | tf_op jit(solution)/shard_map/ppermute | solution.py:306
  21.2 0.0 copy-done.3
  21.2 0.0 copy-done.5
  21.2 9.2 %shard_map.85 = (f32[3,3,32,128]{3,2,1,0:T(8,128)}, f32[8,128]{1,0:T(8,128)}, f32[2,2,16,96,128]{4,3,2,1,0:T(8,128)}, bf16[2,3,3,256,128]{4,3,2,1,0:T(8,128)(2,1)}) custom-call(bf16[32,96,128]{2,1,0:T(8,128)(2,1)} %get-tuple-element.44.low, bf16[24,96,128]{2,1,0:T(8,128)(2,1)} %get-tuple-element.33.high_first, ...), custom_call_target="tpu_custom_call" | custom-call | tf_op jit(solution)/shard_map/pallas_call | solution.py:27
  30.4 0.0 copy-done
  30.4 1.3 %collective-permute-start.8 = (bf16[20,96,128]{2,1,0:T(8,128)(2,1)S(1)}, bf16[20,96,128]{2,1,0:T(8,128)(2,1)S(1)}, u32[]{:S(2)}, u32[]{:S(2)}) collective-permute-start(bf16[20,96,128]{2,1,0:T(8,128)(2,1)S(1)} %slice.23), channel_id=1, source_target_pairs={{16,0},{32,16},{48,32},{64,48},{80,64},{96,80},{112,96},{17,1},{33... | collective-permute-start | bytes 1474568 | tf_op jit(solution)/shard_map/ppermute | solution.py:306
  31.8 2.3 %collective-permute-done.3.below_rest.rest = bf16[12,96,128]{2,1,0:T(8,128)(2,1)S(1)} collective-permute-done((bf16[12,96,128]{2,1,0:T(8,128)(2,1)S(1)}, bf16[12,96,128]{2,1,0:T(8,128)(2,1)S(1)}, u32[]{:S(2)}, u32[]{:S(2)}) %collective-permute-start.3) | collective-permute-done | bytes 294944 | tf_op jit(solution)/shard_map/ppermute | solution.py:306
  34.0 0.0 copy-start.2
  34.0 0.0 collective-permute-done.below_first.first
  34.0 0.0 copy-start.1
  34.0 0.0 copy-start.4
  34.1 1.0 %copy-done.4 = bf16[4,96,128]{2,1,0:T(8,128)(2,1)S(1)} copy-done((bf16[4,96,128]{2,1,0:T(8,128)(2,1)S(1)}, bf16[4,96,128]{2,1,0:T(8,128)(2,1)}, u32[]{:S(2)}) %copy-start.4) | copy-done | bytes 98328
  35.1 0.0 copy-start.6
  35.1 0.9 %copy-done.6 = bf16[4,96,128]{2,1,0:T(8,128)(2,1)S(1)} copy-done((bf16[4,96,128]{2,1,0:T(8,128)(2,1)S(1)}, bf16[4,96,128]{2,1,0:T(8,128)(2,1)}, u32[]{:S(2)}) %copy-start.6) | copy-done | bytes 98328
  36.0 0.9 %copy-done.7 = f32[3,3,32,128]{3,2,1,0:T(8,128)S(1)} copy-done((f32[3,3,32,128]{3,2,1,0:T(8,128)S(1)}, f32[3,3,32,128]{3,2,1,0:T(8,128)}, u32[]{:S(2)}) %copy-start.7) | copy-done | bytes 147480
  36.9 0.7 copy-done.8
  37.5 1.5 %shard_map.86 = (f32[112,128]{1,0:T(8,128)S(1)}, f32[112,128]{1,0:T(8,128)S(1)}) custom-call(bf16[24,96,128]{2,1,0:T(8,128)(2,1)S(1)} %collective-permute-done.below_first.first, bf16[12,96,128]{2,1,0:T(8,128)(2,1)S(1)} %collective-permute-done.3.below_rest.rest, bf16[32,96,128]{2,1,0:T(8,128)(2,1)S(1)} %copy-done, bf16[4,96,128]{2,1,0:T(8,128)(2,1)S(1)} %copy-done.4, ...), custom_call_target="tpu_custom_call" | custom-call | tf_op jit(solution)/shard_map/pallas_call | solution.py:18
  39.1 0.1 collective-permute-start.4
  39.2 1.2 %collective-permute-done.4 = f32[112,128]{1,0:T(8,128)S(1)} collective-permute-done((f32[112,128]{1,0:T(8,128)S(1)}, f32[112,128]{1,0:T(8,128)S(1)}, u32[]{:S(2)}, u32[]{:S(2)}) %collective-permute-start.4) | collective-permute-done | bytes 57376 | tf_op jit(solution)/shard_map/ppermute | solution.py:311
  40.4 4.2 %collective-permute-start.7 = (f32[112,128]{1,0:T(8,128)S(1)}, f32[112,128]{1,0:T(8,128)S(1)}, u32[]{:S(2)}, u32[]{:S(2)}) collective-permute-start(f32[112,128]{1,0:T(8,128)S(1)} %add.35), channel_id=1, source_target_pairs={{0,12},{1,13},{2,14},{3,15},{4,8},{5,9},{6,10},{7,11},{8,4},{9,5},... | collective-permute-start | bytes 172040 | tf_op jit(solution)/shard_map/ppermute | solution.py:311
  44.6 0.5 collective-permute-start.6
  45.1 0.1 collective-permute-start.5
  45.3 0.1 pad_maximum_fusion
  45.3 0.0 copy-done.2
  45.3 0.0 copy-done.1
  45.3 1.2 %collective-permute-done.7 = f32[112,128]{1,0:T(8,128)S(1)} collective-permute-done((f32[112,128]{1,0:T(8,128)S(1)}, f32[112,128]{1,0:T(8,128)S(1)}, u32[]{:S(2)}, u32[]{:S(2)}) %collective-permute-start.7) | collective-permute-done | bytes 57376 | tf_op jit(solution)/shard_map/ppermute | solution.py:311
  46.6 2.6 %collective-permute-done.6 = f32[112,128]{1,0:T(8,128)S(1)} collective-permute-done((f32[112,128]{1,0:T(8,128)S(1)}, f32[112,128]{1,0:T(8,128)S(1)}, u32[]{:S(2)}, u32[]{:S(2)}) %collective-permute-start.6) | collective-permute-done | bytes 57376 | tf_op jit(solution)/shard_map/ppermute | solution.py:311
  49.1 0.0 collective-permute-done.5
  49.2 0.0 collective-permute-done.8.first
  49.2 0.0 copy-start.9
  49.2 13.2 %collective-permute-start.11 = (f32[112,128]{1,0:T(8,128)S(1)}, f32[112,128]{1,0:T(8,128)S(1)}, u32[]{:S(2)}, u32[]{:S(2)}) collective-permute-start(f32[112,128]{1,0:T(8,128)S(1)} %add_add_fusion.2), channel_id=1, source_target_pairs={{0,18},{1,19},{2,16},{3,17},{4,22},{5,23},{6,20},{7,21},{8,26},{9,... | collective-permute-start | bytes 172040 | tf_op jit(solution)/shard_map/ppermute | solution.py:311
  62.4 1.2 %collective-permute-start.10 = (f32[112,128]{1,0:T(8,128)S(1)}, f32[112,128]{1,0:T(8,128)S(1)}, u32[]{:S(2)}, u32[]{:S(2)}) collective-permute-start(f32[112,128]{1,0:T(8,128)S(1)} %add_add_fusion.2), channel_id=1, source_target_pairs={{0,16},{1,17},{2,18},{3,19},{4,20},{5,21},{6,22},{7,23},{8,24},{9,... | collective-permute-start | bytes 172040 | tf_op jit(solution)/shard_map/ppermute | solution.py:311
  63.5 0.0 collective-permute-start.9
  63.5 1.3 %collective-permute-start.15 = (bf16[16,96,128]{2,1,0:T(8,128)(2,1)S(1)}, bf16[16,96,128]{2,1,0:T(8,128)(2,1)S(1)}, u32[]{:S(2)}, u32[]{:S(2)}) collective-permute-start(bf16[16,96,128]{2,1,0:T(8,128)(2,1)S(1)} %pad_maximum_fusion), channel_id=1, source_target_pairs={{16,0},{32,16},{48,32},{64,48},{80,64},{96,80},{112,96},{17,1},{33... | collective-permute-start | bytes 1179656 | tf_op jit(solution)/shard_map/ppermute | solution.py:306
  64.8 0.0 collective-permute-done.11
  64.8 2.1 %collective-permute-done.10 = f32[112,128]{1,0:T(8,128)S(1)} collective-permute-done((f32[112,128]{1,0:T(8,128)S(1)}, f32[112,128]{1,0:T(8,128)S(1)}, u32[]{:S(2)}, u32[]{:S(2)}) %collective-permute-start.10) | collective-permute-done | bytes 57376 | tf_op jit(solution)/shard_map/ppermute | solution.py:311
  66.9 0.0 collective-permute-done.9
  66.9 4.7 %collective-permute-start.14 = (f32[112,128]{1,0:T(8,128)S(1)}, f32[112,128]{1,0:T(8,128)S(1)}, u32[]{:S(2)}, u32[]{:S(2)}) collective-permute-start(f32[112,128]{1,0:T(8,128)S(1)} %add_add_fusion.1), channel_id=1, source_target_pairs={{0,96},{1,97},{2,98},{3,99},{4,100},{5,101},{6,102},{7,103},{8,104... | collective-permute-start | bytes 172040 | tf_op jit(solution)/shard_map/ppermute | solution.py:311
  71.6 0.1 collective-permute-start.13
  71.7 0.6 collective-permute-start.12
  72.3 0.0 copy-done.11
  72.3 0.6 reshape_tile.3.line
  72.9 4.8 %shard_map.87 = (bf16[2,16,12288]{2,1,0:T(8,128)(2,1)}, bf16[2,16,12288]{2,1,0:T(8,128)(2,1)}) custom-call(bf16[24,96,128]{2,1,0:T(8,128)(2,1)} %copy-done.1, bf16[12,96,128]{2,1,0:T(8,128)(2,1)} %copy-done.2, bf16[2,3,3,256,128]{4,3,2,1,0:T(8,128)(2,1)} %get-tuple-element.49.weights, f32[2,2,16,96,128]{4,3,2,1,0:T(8,128)} %get-tuple-element.50.partial, ...), custom_call_target="tpu_custom_call" | custom-call | tf_op jit(solution)/shard_map/pallas_call | solution.py:27
  77.7 0.0 copy-done.9
  77.7 0.0 collective-permute-done.14
  77.7 0.0 collective-permute-done.13
  77.7 0.8 collective-permute-done.12
  78.6 0.0 collective-permute-done.15.rest
  78.6 0.0 copy-start.10
  78.6 3.8 %collective-permute-start.16 = (f32[112,128]{1,0:T(8,128)S(1)}, f32[112,128]{1,0:T(8,128)S(1)}, u32[]{:S(2)}, u32[]{:S(2)}) collective-permute-start(f32[112,128]{1,0:T(8,128)S(1)} %add_add_fusion.part), channel_id=1, source_target_pairs={{0,1},{1,0},{2,3},{3,2},{4,5},{5,4},{6,7},{7,6},{8,9},{9,8},{10,11... | collective-permute-start | bytes 172040 | tf_op jit(solution)/shard_map/ppermute | solution.py:311
  82.4 0.0 copy-done.10
  82.4 4.8 %shard_map.88 = (bf16[2,16,12288]{2,1,0:T(8,128)(2,1)}, bf16[2,16,12288]{2,1,0:T(8,128)(2,1)}) custom-call(bf16[20,96,128]{2,1,0:T(8,128)(2,1)} %copy-done.9, bf16[16,96,128]{2,1,0:T(8,128)(2,1)} %copy-done.10, bf16[2,3,3,256,128]{4,3,2,1,0:T(8,128)(2,1)} %get-tuple-element.49.weights, ...), custom_call_target="tpu_custom_call", output_to_operand_aliasing={{0}: (5, {}), {1}: (6, {})} | custom-call | tf_op jit(solution)/shard_map/pallas_call | solution.py:27
  87.2 0.0 collective-permute-done.16.other
  87.2 1.0 %shard_map.89 = (f32[864,32]{1,0:T(8,128)}, f32[1,32]{1,0:T(1,128)}) custom-call(f32[112,128]{1,0:T(8,128)S(1)} %add_add_fusion.part, f32[112,128]{1,0:T(8,128)S(1)} %collective-permute-done.16.other, f32[1,128]{1,0:T(1,128)S(1)} %broadcast_in_dim.3.flag), custom_call_target="tpu_custom_call" | custom-call | tf_op jit(solution)/shard_map/pallas_call | solution.py:18
  (13 shorter events, 0.1 us)
Async XLA Ops:
  3.7 26.7 %copy-start = (bf16[32,96,128]{2,1,0:T(8,128)(2,1)S(1)}, bf16[32,96,128]{2,1,0:T(8,128)(2,1)}, u32[]{:S(2)}) copy-start(bf16[32,96,128]{2,1,0:T(8,128)(2,1)} %get-tuple-element.44.low) | copy-start | bytes 2359300
  3.7 12.3 %collective-permute-start.1 = (bf16[4,96,128]{2,1,0:T(8,128)(2,1)}, bf16[4,96,128]{2,1,0:T(8,128)(2,1)S(1)}, u32[]{:S(2)}, u32[]{:S(2)}) collective-permute-start(bf16[4,96,128]{2,1,0:T(8,128)(2,1)} %get-tuple-element.35), channel_id=1, source_target_pairs={{0,1},{1,2},{2,3},{3,4},{4,5},{5,6},{6,7},{7,8},{8,9},{9,10},{10,1... | collective-permute-start | bytes 294920 | tf_op jit(solution)/shard_map/ppermute | solution.py:306
  8.8 7.2 %collective-permute-start.2 = (bf16[4,96,128]{2,1,0:T(8,128)(2,1)}, bf16[4,96,128]{2,1,0:T(8,128)(2,1)S(1)}, u32[]{:S(2)}, u32[]{:S(2)}) collective-permute-start(bf16[4,96,128]{2,1,0:T(8,128)(2,1)} %get-tuple-element.36), channel_id=1, source_target_pairs={{1,0},{2,1},{3,2},{4,3},{5,4},{6,5},{7,6},{8,7},{9,8},{10,9},{11,1... | collective-permute-start | bytes 294920 | tf_op jit(solution)/shard_map/ppermute | solution.py:306
  10.7 23.3 %collective-permute-start = (bf16[24,96,128]{2,1,0:T(8,128)(2,1)}, bf16[24,96,128]{2,1,0:T(8,128)(2,1)S(1)}, u32[]{:S(2)}, u32[]{:S(2)}) collective-permute-start(bf16[24,96,128]{2,1,0:T(8,128)(2,1)} %get-tuple-element.33.high_first), channel_id=1, source_target_pairs={{0,16},{16,32},{32,48},{48,64},{64,80},{80,96},{96,112},{1,17},{17... | collective-permute-start | bytes 1769480 | tf_op jit(solution)/shard_map/ppermute | solution.py:306
  16.0 5.2 %copy-start.3 = (bf16[4,96,128]{2,1,0:T(8,128)(2,1)}, bf16[4,96,128]{2,1,0:T(8,128)(2,1)S(1)}, u32[]{:S(2)}) copy-start(bf16[4,96,128]{2,1,0:T(8,128)(2,1)S(1)} %collective-permute-done.1.from_left) | copy-start | bytes 294916
  16.0 5.2 %copy-start.5 = (bf16[4,96,128]{2,1,0:T(8,128)(2,1)}, bf16[4,96,128]{2,1,0:T(8,128)(2,1)S(1)}, u32[]{:S(2)}) copy-start(bf16[4,96,128]{2,1,0:T(8,128)(2,1)S(1)} %collective-permute-done.2.from_right) | copy-start | bytes 294916
  17.0 17.0 %collective-permute-start.3 = (bf16[12,96,128]{2,1,0:T(8,128)(2,1)S(1)}, bf16[12,96,128]{2,1,0:T(8,128)(2,1)S(1)}, u32[]{:S(2)}, u32[]{:S(2)}) collective-permute-start(bf16[12,96,128]{2,1,0:T(8,128)(2,1)S(1)} %pad_maximum_fusion.1), channel_id=1, source_target_pairs={{0,16},{16,32},{32,48},{48,64},{64,80},{80,96},{96,112},{1,17},{17... | collective-permute-start | bytes 884744 | tf_op jit(solution)/shard_map/ppermute | solution.py:306
  30.4 18.7 %collective-permute-start.8 = (bf16[20,96,128]{2,1,0:T(8,128)(2,1)S(1)}, bf16[20,96,128]{2,1,0:T(8,128)(2,1)S(1)}, u32[]{:S(2)}, u32[]{:S(2)}) collective-permute-start(bf16[20,96,128]{2,1,0:T(8,128)(2,1)S(1)} %slice.23), channel_id=1, source_target_pairs={{16,0},{32,16},{48,32},{64,48},{80,64},{96,80},{112,96},{17,1},{33... | collective-permute-start | bytes 1474568 | tf_op jit(solution)/shard_map/ppermute | solution.py:306
  34.0 11.3 %copy-start.2 = (bf16[12,96,128]{2,1,0:T(8,128)(2,1)}, bf16[12,96,128]{2,1,0:T(8,128)(2,1)S(1)}, u32[]{:S(2)}) copy-start(bf16[12,96,128]{2,1,0:T(8,128)(2,1)S(1)} %collective-permute-done.3.below_rest.rest) | copy-start | bytes 884740
  34.0 11.3 %copy-start.1 = (bf16[24,96,128]{2,1,0:T(8,128)(2,1)}, bf16[24,96,128]{2,1,0:T(8,128)(2,1)S(1)}, u32[]{:S(2)}) copy-start(bf16[24,96,128]{2,1,0:T(8,128)(2,1)S(1)} %collective-permute-done.below_first.first) | copy-start | bytes 1769476
  34.0 1.0 %copy-start.4 = (bf16[4,96,128]{2,1,0:T(8,128)(2,1)S(1)}, bf16[4,96,128]{2,1,0:T(8,128)(2,1)}, u32[]{:S(2)}) copy-start(bf16[4,96,128]{2,1,0:T(8,128)(2,1)} %copy-done.3) | copy-start | bytes 294916
  35.1 0.9 %copy-start.6 = (bf16[4,96,128]{2,1,0:T(8,128)(2,1)S(1)}, bf16[4,96,128]{2,1,0:T(8,128)(2,1)}, u32[]{:S(2)}) copy-start(bf16[4,96,128]{2,1,0:T(8,128)(2,1)} %copy-done.5) | copy-start | bytes 294916
  36.0 0.9 %copy-start.7 = (f32[3,3,32,128]{3,2,1,0:T(8,128)S(1)}, f32[3,3,32,128]{3,2,1,0:T(8,128)}, u32[]{:S(2)}) copy-start(f32[3,3,32,128]{3,2,1,0:T(8,128)} %get-tuple-element.40.folded) | copy-start | bytes 442372
  36.9 0.7 copy-start.8
  37.5 34.8 %copy-start.11 = (f32[32]{0:T(128)S(1)}, f32[32]{0:T(128)}, u32[]{:S(2)}) copy-start(f32[32]{0:T(128)} %param.9) | copy-start | bytes 388
  39.1 1.3 %collective-permute-start.4 = (f32[112,128]{1,0:T(8,128)S(1)}, f32[112,128]{1,0:T(8,128)S(1)}, u32[]{:S(2)}, u32[]{:S(2)}) collective-permute-start(f32[112,128]{1,0:T(8,128)S(1)} %get-tuple-element.43), channel_id=1, source_target_pairs={{0,1},{1,0},{2,3},{3,2},{4,5},{5,4},{6,7},{7,6},{8,9},{9,8},{10,11... | collective-permute-start | bytes 172040 | tf_op jit(solution)/shard_map/ppermute | solution.py:311
  40.4 6.1 %collective-permute-start.7 = (f32[112,128]{1,0:T(8,128)S(1)}, f32[112,128]{1,0:T(8,128)S(1)}, u32[]{:S(2)}, u32[]{:S(2)}) collective-permute-start(f32[112,128]{1,0:T(8,128)S(1)} %add.35), channel_id=1, source_target_pairs={{0,12},{1,13},{2,14},{3,15},{4,8},{5,9},{6,10},{7,11},{8,4},{9,5},... | collective-permute-start | bytes 172040 | tf_op jit(solution)/shard_map/ppermute | solution.py:311
  44.6 4.5 %collective-permute-start.6 = (f32[112,128]{1,0:T(8,128)S(1)}, f32[112,128]{1,0:T(8,128)S(1)}, u32[]{:S(2)}, u32[]{:S(2)}) collective-permute-start(f32[112,128]{1,0:T(8,128)S(1)} %add.35), channel_id=1, source_target_pairs={{0,8},{1,9},{2,10},{3,11},{4,12},{5,13},{6,14},{7,15},{8,0},{9,1},... | collective-permute-start | bytes 172040 | tf_op jit(solution)/shard_map/ppermute | solution.py:311
  45.1 4.0 %collective-permute-start.5 = (f32[112,128]{1,0:T(8,128)S(1)}, f32[112,128]{1,0:T(8,128)S(1)}, u32[]{:S(2)}, u32[]{:S(2)}) collective-permute-start(f32[112,128]{1,0:T(8,128)S(1)} %add.35), channel_id=1, source_target_pairs={{0,4},{1,5},{2,6},{3,7},{4,0},{5,1},{6,2},{7,3},{8,12},{9,13},{10,... | collective-permute-start | bytes 172040 | tf_op jit(solution)/shard_map/ppermute | solution.py:311
  49.2 28.6 %copy-start.9 = (bf16[20,96,128]{2,1,0:T(8,128)(2,1)}, bf16[20,96,128]{2,1,0:T(8,128)(2,1)S(1)}, u32[]{:S(2)}) copy-start(bf16[20,96,128]{2,1,0:T(8,128)(2,1)S(1)} %collective-permute-done.8.first) | copy-start | bytes 1474564
  49.2 15.6 %collective-permute-start.11 = (f32[112,128]{1,0:T(8,128)S(1)}, f32[112,128]{1,0:T(8,128)S(1)}, u32[]{:S(2)}, u32[]{:S(2)}) collective-permute-start(f32[112,128]{1,0:T(8,128)S(1)} %add_add_fusion.2), channel_id=1, source_target_pairs={{0,18},{1,19},{2,16},{3,17},{4,22},{5,23},{6,20},{7,21},{8,26},{9,... | collective-permute-start | bytes 172040 | tf_op jit(solution)/shard_map/ppermute | solution.py:311
  62.4 4.5 %collective-permute-start.10 = (f32[112,128]{1,0:T(8,128)S(1)}, f32[112,128]{1,0:T(8,128)S(1)}, u32[]{:S(2)}, u32[]{:S(2)}) collective-permute-start(f32[112,128]{1,0:T(8,128)S(1)} %add_add_fusion.2), channel_id=1, source_target_pairs={{0,16},{1,17},{2,18},{3,19},{4,20},{5,21},{6,22},{7,23},{8,24},{9,... | collective-permute-start | bytes 172040 | tf_op jit(solution)/shard_map/ppermute | solution.py:311
  63.5 3.4 %collective-permute-start.9 = (f32[112,128]{1,0:T(8,128)S(1)}, f32[112,128]{1,0:T(8,128)S(1)}, u32[]{:S(2)}, u32[]{:S(2)}) collective-permute-start(f32[112,128]{1,0:T(8,128)S(1)} %add_add_fusion.2), channel_id=1, source_target_pairs={{0,2},{1,3},{2,0},{3,1},{4,6},{5,7},{6,4},{7,5},{8,10},{9,11},{10,... | collective-permute-start | bytes 172040 | tf_op jit(solution)/shard_map/ppermute | solution.py:311
  63.5 15.1 %collective-permute-start.15 = (bf16[16,96,128]{2,1,0:T(8,128)(2,1)S(1)}, bf16[16,96,128]{2,1,0:T(8,128)(2,1)S(1)}, u32[]{:S(2)}, u32[]{:S(2)}) collective-permute-start(bf16[16,96,128]{2,1,0:T(8,128)(2,1)S(1)} %pad_maximum_fusion), channel_id=1, source_target_pairs={{16,0},{32,16},{48,32},{64,48},{80,64},{96,80},{112,96},{17,1},{33... | collective-permute-start | bytes 1179656 | tf_op jit(solution)/shard_map/ppermute | solution.py:306
  66.9 10.8 %collective-permute-start.14 = (f32[112,128]{1,0:T(8,128)S(1)}, f32[112,128]{1,0:T(8,128)S(1)}, u32[]{:S(2)}, u32[]{:S(2)}) collective-permute-start(f32[112,128]{1,0:T(8,128)S(1)} %add_add_fusion.1), channel_id=1, source_target_pairs={{0,96},{1,97},{2,98},{3,99},{4,100},{5,101},{6,102},{7,103},{8,104... | collective-permute-start | bytes 172040 | tf_op jit(solution)/shard_map/ppermute | solution.py:311
  71.6 6.1 %collective-permute-start.13 = (f32[112,128]{1,0:T(8,128)S(1)}, f32[112,128]{1,0:T(8,128)S(1)}, u32[]{:S(2)}, u32[]{:S(2)}) collective-permute-start(f32[112,128]{1,0:T(8,128)S(1)} %add_add_fusion.1), channel_id=1, source_target_pairs={{0,64},{1,65},{2,66},{3,67},{4,68},{5,69},{6,70},{7,71},{8,72},{9,... | collective-permute-start | bytes 172040 | tf_op jit(solution)/shard_map/ppermute | solution.py:311
  71.7 6.9 %collective-permute-start.12 = (f32[112,128]{1,0:T(8,128)S(1)}, f32[112,128]{1,0:T(8,128)S(1)}, u32[]{:S(2)}, u32[]{:S(2)}) collective-permute-start(f32[112,128]{1,0:T(8,128)S(1)} %add_add_fusion.1), channel_id=1, source_target_pairs={{0,32},{1,33},{2,34},{3,35},{4,36},{5,37},{6,38},{7,39},{8,40},{9,... | collective-permute-start | bytes 172040 | tf_op jit(solution)/shard_map/ppermute | solution.py:311
  78.6 3.8 %copy-start.10 = (bf16[16,96,128]{2,1,0:T(8,128)(2,1)}, bf16[16,96,128]{2,1,0:T(8,128)(2,1)S(1)}, u32[]{:S(2)}) copy-start(bf16[16,96,128]{2,1,0:T(8,128)(2,1)S(1)} %collective-permute-done.15.rest) | copy-start | bytes 1179652
  78.6 8.6 %collective-permute-start.16 = (f32[112,128]{1,0:T(8,128)S(1)}, f32[112,128]{1,0:T(8,128)S(1)}, u32[]{:S(2)}, u32[]{:S(2)}) collective-permute-start(f32[112,128]{1,0:T(8,128)S(1)} %add_add_fusion.part), channel_id=1, source_target_pairs={{0,1},{1,0},{2,3},{3,2},{4,5},{5,4},{6,7},{7,6},{8,9},{9,8},{10,11... | collective-permute-start | bytes 172040 | tf_op jit(solution)/shard_map/ppermute | solution.py:311

commit v6 on v5

--- a/solution.py
+++ b/solution.py
@@ -141,10 +141,11 @@
 
 def gather_grad(first, rest, grad):
     rows = grad.shape[0]
-    early = first.shape[0] - rows
-    if early:
-        grad[:early] = first[rows:]
-    grad[early:] = rest[: rows - early]
+    if first.shape == rest.shape:
+        grad[...] = first[rows : 2 * rows]
+    else:
+        grad[:EARLY] = first[rows:]
+        grad[EARLY:] = rest[: rows - EARLY]
 
 
 def own_body(
@@ -242,8 +243,10 @@
     return total
 
 
-def outer_body(first, rest, weights, partial, line, *more):
-    output, grad_input, taps, scratch, grad = more[-5:]
+def outer_body(count, *refs):
+    first, rest = refs[0], refs[count - 1]
+    weights, partial, line = refs[count : count + 3]
+    output, grad_input, taps, scratch, grad = refs[-5:]
     rows, groups = partial.shape[2:4]
     act, edge = first.at[:rows], rest.at[rest.shape[0] - 4 :]
     gather_grad(first, rest, grad)
@@ -286,12 +289,16 @@
 PITCH = 8
 
 
-def unpack_body(scaling, part, other, flag, grad_kernel, grad_bias, packed):
+def join_body(part, other, flag, packed):
     upper = flag[...] > 0.5
     packed[:HALF] = jnp.where(upper, other[...], part[...])
     packed[HALF : 2 * HALF] = jnp.where(upper, part[...], other[...])
+
+
+def unpack_body(scaling, part, one, two, three, grad_kernel, grad_bias):
     for place in range(7):
-        block = packed[place * 32 : place * 32 + 32, :] * scaling
+        span = slice(place * 32, place * 32 + 32)
+        block = ((part[span, :] + one[span, :]) + (two[span, :] + three[span, :])) * scaling
         turned = block.T
         grad_kernel[place * 96 : place * 96 + 96, :] = turned[:96]
         if place < 6:
@@ -368,28 +375,29 @@
         [part_of(array.shape, 0, 0, 0) for array in (low, high_first, high_rest)] + [part_of(lines.shape, 0, 0, 0)] * 2 + [part_of(flat_kernel.shape, 0, 0)],
     )
 
-    def outer(side, first, rest, done=()):
+    def outer(side, planes_beside, done=()):
+        count = len(planes_beside)
         return blocked(
-            outer_body,
+            functools.partial(outer_body, count),
             1,
             (shape(block, BF16), shape(block, BF16)),
             (part_of((1, *block[1:]), side, 0, 0),) * 2,
             [two_taps, spread, one_plane],
-            (first, rest, weights, partial, line, *done),
+            (*planes_beside, weights, partial, line, *done),
             [
-                part_of(first.shape, 0, 0, 0), part_of(rest.shape, 0, 0, 0),
+                *[part_of(array.shape, 0, 0, 0) for array in planes_beside],
                 part_of((2, 1, 3, 256, LANES), 0, 2 * side, 0, 0, 0), part_of((2, 1, *plane), 0, side, 0, 0, 0),
                 part_of((1, LANES), 0, 0),
                 *[pl.BlockSpec(memory_space=pl.ANY)] * len(done),
             ],
-            {5: 0, 6: 1} if done else None,
+            {count + 3: 0, count + 4: 1} if done else None,
         )
 
-    split = rows + 4
     ends = (from_left[:2], from_right[:2])
-    ends, folded, partial, low_late = lax.optimization_barrier((ends, folded, partial, low))
-    above_first = shifted(low_late[:split], "gz", -1)
-    down_rest = jnp.concatenate([low_late[split:], *ends])
+    ends, folded, partial = lax.optimization_barrier((ends, folded, partial))
+    down = jnp.concatenate([low, *ends])
+    down, below_rest = lax.optimization_barrier((down, below_rest))
+    above = shifted(down, "gz", -1)
 
     part, send = call(
         kernel_grad_body,
@@ -399,21 +407,20 @@
     )
     part = part + swapped(send, 1)
     part = sum_of_four(part, 4, 8)
-    part, down_rest, above_first = lax.optimization_barrier((part, down_rest, above_first))
-    part = sum_of_four(part, 2, 16)
-    above_rest = shifted(down_rest, "gz", -1)
     part = sum_of_four(part, 32, 64)
-    results = outer(0, below_first, below_rest)
-    part, results, above_rest = lax.optimization_barrier((part, results, above_rest))
-    other = swapped(part, 1)
-    results = outer(1, above_first, above_rest, results)
+    results = outer(0, (below_first, below_rest))
+    part, results = lax.optimization_barrier((part, results))
+    part = call(join_body, shape((2 * HALF, LANES), F32), [], (part, swapped(part, 1), flag))
+    part, above = lax.optimization_barrier((part, above))
+    others = [swapped(part, bit) for bit in (2, 16, 18)]
+    results = outer(1, (above,), results)
 
     voxels = planes * lax.axis_size("gz") * rows * lax.axis_size("gy") * (width // 32)
     grad_kernel, grad_bias = call(
         functools.partial(unpack_body, 1.0 / math.sqrt(voxels)),
         (shape((27 * 32, 32), F32), shape((1, 32), F32)),
-        [packed],
-        (part, other, flag),
+        [],
+        (part, *others),
     )
     return *results, grad_kernel.reshape(3, 3, 3, 32, 32), grad_bias.reshape(32)
 

time: 88.7 us -> 74.6 us (0.84)
  starting transfers between devices: 47.4 us -> 35 us
  local copies, waits for them, and re-layouts: 4.19 us -> 0.66 us
  waiting for transfers between devices: 10.2 us -> 11.5 us
    ppermute x11, starting transfers between devices: 28.4 us -> 17.3 us  [swapped(): lax.ppermute(value, ('gz', 'gy'), [(i, i ^ bit) for i in range(count)])]
    unnamed x24 -> x20, local copies, waits for them, and re-layouts: 3.52 us -> 0.04 us
    ppermute x6 -> x5, starting transfers between devices: 18.9 us -> 17.6 us  [shifted(): return lax.ppermute(value, axis, pairs)]
    ppermute x6 -> x5, waiting for transfers between devices: 2.3 us -> 3.46 us  [shifted(): return lax.ppermute(value, axis, pairs)]
    pallas_call x2 -> x3, Pallas kernels: 2.49 us -> 2.51 us  [call(): pl.pallas_call(body, out_shape=outs, scratch_shapes=scratch, compiler_par...]
  transfers between devices with their start and end apart: 17 -> 16, of which waited for: 6 -> 7; matrix products, arithmetic and copies ran while one was open for 2% -> 2% of each run, Pallas kernels for 23% -> 28%
where the time goes in v6:
time: 74.6 us; the launch traced here: 73.6 us
  starting transfers between devices  35 us (47%)
  Pallas kernels  24.4 us (33%)
  waiting for transfers between devices  11.5 us (15%)
  other arithmetic  1.15 us (2%)
  between operations  0.91 us (1%)
    pallas_call x3, Pallas kernels, blocked(): pl.pallas_call(body, grid=(grid,), out_shape=outs, in_specs=in_specs, out...  18.9 us
    ppermute x5, starting transfers between devices, shifted(): return lax.ppermute(value, axis, pairs)  17.6 us
    ppermute x11, starting transfers between devices, swapped(): lax.ppermute(value, ('gz', 'gy'), [(i, i ^ bit) for i in range(count)])  17.3 us
    ppermute x11, waiting for transfers between devices, swapped(): lax.ppermute(value, ('gz', 'gy'), [(i, i ^ bit) for i in range(count)])  8.04 us
    ppermute x5, waiting for transfers between devices, shifted(): return lax.ppermute(value, axis, pairs)  3.46 us
    pallas_call x1, Pallas kernels, local(): pl.pallas_call(group_body, in_specs=[pl.BlockSpec(memory_space=pl.ANY)] *...  3.06 us
    pallas_call x3, Pallas kernels, call(): pl.pallas_call(body, out_shape=outs, scratch_shapes=scratch, compiler_par...  2.51 us
  transfers between devices with their start and end apart: 16, of which 7 were waited for; matrix products, arithmetic and copies ran while one was open for 2% of the time, Pallas kernels for 28%

profile of v6, /device:TPU:1, one launch (start us, length us, event | category | flops | bytes accessed | tf_op | source)
XLA Modules:
  0.0 73.6 jit_solution(12299623069215326735)
XLA Ops:
  0.6 3.1 %shard_map.84 = (bf16[32,96,128]{2,1,0:T(8,128)(2,1)}, bf16[24,96,128]{2,1,0:T(8,128)(2,1)}, bf16[8,96,128]{2,1,0:T(8,128)(2,1)}, bf16[4,96,128]{2,1,0:T(8,128)(2,1)}, bf16[4,96,128]{2,1,0:T(8,128)(2,1)}) custom-call(bf16[2,16,12288]{2,1,0:T(8,128)(2,1)} %act_in.1, bf16[2,16,12288]{2,1,0:T(8,128)(2,1)} %grad_in.1, s32[2,16,12288]{2,1,0:T(8,128)} %mask_in.1), custom_call_target="tpu_custom_call" | custom-call | tf_op jit(solution)/shard_map/pallas_call | solution.py:340
  3.7 0.0 copy-start
  3.7 5.1 %collective-permute-start.1 = (bf16[4,96,128]{2,1,0:T(8,128)(2,1)}, bf16[4,96,128]{2,1,0:T(8,128)(2,1)S(1)}, u32[]{:S(2)}, u32[]{:S(2)}) collective-permute-start(bf16[4,96,128]{2,1,0:T(8,128)(2,1)} %get-tuple-element.34), channel_id=1, source_target_pairs={{0,1},{1,2},{2,3},{3,4},{4,5},{5,6},{6,7},{7,8},{8,9},{9,10},{10,1... | collective-permute-start | bytes 294920 | tf_op jit(solution)/shard_map/ppermute | solution.py:313
  8.8 1.9 %collective-permute-start.2 = (bf16[4,96,128]{2,1,0:T(8,128)(2,1)}, bf16[4,96,128]{2,1,0:T(8,128)(2,1)S(1)}, u32[]{:S(2)}, u32[]{:S(2)}) collective-permute-start(bf16[4,96,128]{2,1,0:T(8,128)(2,1)} %get-tuple-element.35), channel_id=1, source_target_pairs={{1,0},{2,1},{3,2},{4,3},{5,4},{6,5},{7,6},{8,7},{9,8},{10,9},{11,1... | collective-permute-start | bytes 294920 | tf_op jit(solution)/shard_map/ppermute | solution.py:313
  10.7 5.2 %collective-permute-start = (bf16[24,96,128]{2,1,0:T(8,128)(2,1)}, bf16[24,96,128]{2,1,0:T(8,128)(2,1)S(1)}, u32[]{:S(2)}, u32[]{:S(2)}) collective-permute-start(bf16[24,96,128]{2,1,0:T(8,128)(2,1)} %get-tuple-element.32.high_first), channel_id=1, source_target_pairs={{0,16},{16,32},{32,48},{48,64},{64,80},{80,96},{96,112},{1,17},{17... | collective-permute-start | bytes 1769480 | tf_op jit(solution)/shard_map/ppermute | solution.py:313
  16.0 0.0 collective-permute-done.1.from_left
  16.0 0.0 copy-start.3
  16.0 0.0 collective-permute-done.2.from_right
  16.0 0.0 copy-start.5
  16.0 1.0 %pad_maximum_fusion.1 = bf16[12,96,128]{2,1,0:T(8,128)(2,1)S(1)} fusion(bf16[2,96,128]{2,1,0:T(8,128)(2,1)S(1)} %get-tuple-element.62, bf16[2,96,128]{2,1,0:T(8,128)(2,1)S(1)} %get-tuple-element.60, bf16[8,96,128]{2,1,0:T(8,128)(2,1)} %get-tuple-element.36.high_rest), kind=kLoop, calls=%fused_computation.1 | loop fusion | flops 294912 | bytes 589824 | tf_op jit(solution)/shard_map/concatenate | solution.py:355
  17.0 4.1 %collective-permute-start.3 = (bf16[12,96,128]{2,1,0:T(8,128)(2,1)S(1)}, bf16[12,96,128]{2,1,0:T(8,128)(2,1)S(1)}, u32[]{:S(2)}, u32[]{:S(2)}) collective-permute-start(bf16[12,96,128]{2,1,0:T(8,128)(2,1)S(1)} %pad_maximum_fusion.1), channel_id=1, source_target_pairs={{0,16},{16,32},{32,48},{48,64},{64,80},{80,96},{96,112},{1,17},{17... | collective-permute-start | bytes 884744 | tf_op jit(solution)/shard_map/ppermute | solution.py:313
  21.2 0.0 copy-done.3
  21.2 0.0 copy-done.5
  21.2 9.2 %shard_map.85 = (f32[3,3,32,128]{3,2,1,0:T(8,128)}, f32[8,128]{1,0:T(8,128)}, f32[2,2,16,96,128]{4,3,2,1,0:T(8,128)}, bf16[2,3,3,256,128]{4,3,2,1,0:T(8,128)(2,1)}) custom-call(bf16[32,96,128]{2,1,0:T(8,128)(2,1)} %get-tuple-element.33.low, bf16[24,96,128]{2,1,0:T(8,128)(2,1)} %get-tuple-element.32.high_first, ...), custom_call_target="tpu_custom_call" | custom-call | tf_op jit(solution)/shard_map/pallas_call | solution.py:27
  30.4 0.0 copy-start.4
  30.4 0.0 copy-start.6
  30.4 0.0 copy-start.7
  30.4 0.0 copy-start.8
  30.4 0.0 copy-done
  30.4 0.1 pad_maximum_fusion
  30.6 0.0 copy-start.9
  30.6 3.4 %collective-permute-done.3.below_rest.refs_1_ = bf16[12,96,128]{2,1,0:T(8,128)(2,1)S(1)} collective-permute-done((bf16[12,96,128]{2,1,0:T(8,128)(2,1)S(1)}, bf16[12,96,128]{2,1,0:T(8,128)(2,1)S(1)}, u32[]{:S(2)}, u32[]{:S(2)}) %collective-permute-start.3) | collective-permute-done | bytes 294944 | tf_op jit(solution)/shard_map/ppermute | solution.py:313
  34.0 0.0 copy-start.2
  34.0 1.3 %collective-permute-start.12 = (bf16[36,96,128]{2,1,0:T(8,128)(2,1)S(1)}, bf16[36,96,128]{2,1,0:T(8,128)(2,1)}, u32[]{:S(2)}, u32[]{:S(2)}) collective-permute-start(bf16[36,96,128]{2,1,0:T(8,128)(2,1)S(1)} %pad_maximum_fusion), channel_id=1, source_target_pairs={{16,0},{32,16},{48,32},{64,48},{80,64},{96,80},{112,96},{17,1},{33... | collective-permute-start | bytes 2654216 | tf_op jit(solution)/shard_map/ppermute | solution.py:313
  35.3 0.0 collective-permute-done.below_first.refs_0_
  35.3 0.0 copy-start.1
  35.4 0.0 copy-done.4
  35.4 0.0 copy-done.6
  35.4 0.0 copy-done.7
  35.4 0.0 copy-done.8
  35.4 1.5 %shard_map.86 = (f32[112,128]{1,0:T(8,128)S(1)}, f32[112,128]{1,0:T(8,128)S(1)}) custom-call(bf16[24,96,128]{2,1,0:T(8,128)(2,1)S(1)} %collective-permute-done.below_first.refs_0_, bf16[12,96,128]{2,1,0:T(8,128)(2,1)S(1)} %collective-permute-done.3.below_rest.refs_1_, bf16[32,96,128]{2,1,0:T(8,128)(2,1)S(1)} %copy-done, bf16[4,96,128]{2,1,0:T(8,128)(2,1)S(1)} %copy-done.4, ...), custom_call_target="tpu_custom_call" | custom-call | tf_op jit(solution)/shard_map/pallas_call | solution.py:18
  36.9 0.1 collective-permute-start.4
  37.0 1.2 %collective-permute-done.4 = f32[112,128]{1,0:T(8,128)S(1)} collective-permute-done((f32[112,128]{1,0:T(8,128)S(1)}, f32[112,128]{1,0:T(8,128)S(1)}, u32[]{:S(2)}, u32[]{:S(2)}) %collective-permute-start.4) | collective-permute-done | bytes 57376 | tf_op jit(solution)/shard_map/ppermute | solution.py:318
  38.3 4.1 %collective-permute-start.7 = (f32[112,128]{1,0:T(8,128)S(1)}, f32[112,128]{1,0:T(8,128)S(1)}, u32[]{:S(2)}, u32[]{:S(2)}) collective-permute-start(f32[112,128]{1,0:T(8,128)S(1)} %add.26), channel_id=1, source_target_pairs={{0,12},{1,13},{2,14},{3,15},{4,8},{5,9},{6,10},{7,11},{8,4},{9,5},... | collective-permute-start | bytes 172040 | tf_op jit(solution)/shard_map/ppermute | solution.py:318
  42.4 0.5 collective-permute-start.6
  42.9 0.2 collective-permute-start.5
  43.1 1.4 %collective-permute-done.7 = f32[112,128]{1,0:T(8,128)S(1)} collective-permute-done((f32[112,128]{1,0:T(8,128)S(1)}, f32[112,128]{1,0:T(8,128)S(1)}, u32[]{:S(2)}, u32[]{:S(2)}) %collective-permute-start.7) | collective-permute-done | bytes 57376 | tf_op jit(solution)/shard_map/ppermute | solution.py:318
  44.5 2.9 %collective-permute-done.6 = f32[112,128]{1,0:T(8,128)S(1)} collective-permute-done((f32[112,128]{1,0:T(8,128)S(1)}, f32[112,128]{1,0:T(8,128)S(1)}, u32[]{:S(2)}, u32[]{:S(2)}) %collective-permute-start.6) | collective-permute-done | bytes 57376 | tf_op jit(solution)/shard_map/ppermute | solution.py:318
  47.3 0.0 collective-permute-done.5
  47.3 7.6 %collective-permute-start.10 = (f32[112,128]{1,0:T(8,128)S(1)}, f32[112,128]{1,0:T(8,128)S(1)}, u32[]{:S(2)}, u32[]{:S(2)}) collective-permute-start(f32[112,128]{1,0:T(8,128)S(1)} %add_add_fusion.1), channel_id=1, source_target_pairs={{0,96},{1,97},{2,98},{3,99},{4,100},{5,101},{6,102},{7,103},{8,104... | collective-permute-start | bytes 172040 | tf_op jit(solution)/shard_map/ppermute | solution.py:318
  54.9 0.1 collective-permute-start.9
  55.0 0.6 collective-permute-start.8
  55.6 0.0 copy-done.9
  55.6 0.6 reshape_tile.3.refs_4_.refs_3_
  56.2 0.0 copy-done.2
  56.2 0.0 copy-done.1
  56.2 4.8 %shard_map.87 = (bf16[2,16,12288]{2,1,0:T(8,128)(2,1)}, bf16[2,16,12288]{2,1,0:T(8,128)(2,1)}) custom-call(bf16[24,96,128]{2,1,0:T(8,128)(2,1)} %copy-done.1, bf16[12,96,128]{2,1,0:T(8,128)(2,1)} %copy-done.2, bf16[2,3,3,256,128]{4,3,2,1,0:T(8,128)(2,1)} %get-tuple-element.46.refs_2_.refs_1_, f32[2,2,16,96,128]{4,3,2,1,0:T(8,128)} %get-tuple-element.47.refs_3_.refs_2_, ...), custom_call_target="tpu_custom_call" | custom-call | tf_op jit(solution)/shard_map/pallas_call | solution.py:27
  61.0 0.0 collective-permute-done.10
  61.1 0.0 collective-permute-done.9
  61.1 1.3 %collective-permute-done.8 = f32[112,128]{1,0:T(8,128)S(1)} collective-permute-done((f32[112,128]{1,0:T(8,128)S(1)}, f32[112,128]{1,0:T(8,128)S(1)}, u32[]{:S(2)}, u32[]{:S(2)}) %collective-permute-start.8) | collective-permute-done | bytes 57376 | tf_op jit(solution)/shard_map/ppermute | solution.py:318
  62.4 0.8 %collective-permute-start.11 = (f32[112,128]{1,0:T(8,128)S(1)}, f32[112,128]{1,0:T(8,128)S(1)}, u32[]{:S(2)}, u32[]{:S(2)}) collective-permute-start(f32[112,128]{1,0:T(8,128)S(1)} %add_add_fusion.part), channel_id=1, source_target_pairs={{0,1},{1,0},{2,3},{3,2},{4,5},{5,4},{6,7},{7,6},{8,9},{9,8},{10,11... | collective-permute-start | bytes 172040 | tf_op jit(solution)/shard_map/ppermute | solution.py:318
  63.2 0.9 %collective-permute-done.11.other = f32[112,128]{1,0:T(8,128)S(1)} collective-permute-done((f32[112,128]{1,0:T(8,128)S(1)}, f32[112,128]{1,0:T(8,128)S(1)}, u32[]{:S(2)}, u32[]{:S(2)}) %collective-permute-start.11) | collective-permute-done | bytes 57376 | tf_op jit(solution)/shard_map/ppermute | solution.py:318
  64.2 0.0 collective-permute-done.12.refs_0_
  64.2 1.2 %collective-permute-start.15 = (f32[224,128]{1,0:T(8,128)S(1)}, f32[224,128]{1,0:T(8,128)S(1)}, u32[]{:S(2)}, u32[]{:S(2)}) collective-permute-start(f32[224,128]{1,0:T(8,128)S(1)} %shard_map.88.part), channel_id=1, source_target_pairs={{0,18},{1,19},{2,16},{3,17},{4,22},{5,23},{6,20},{7,21},{8,26},{9,... | collective-permute-start | bytes 344072 | tf_op jit(solution)/shard_map/ppermute | solution.py:318
  65.4 2.1 %collective-permute-start.14 = (f32[224,128]{1,0:T(8,128)S(1)}, f32[224,128]{1,0:T(8,128)S(1)}, u32[]{:S(2)}, u32[]{:S(2)}) collective-permute-start(f32[224,128]{1,0:T(8,128)S(1)} %shard_map.88.part), channel_id=1, source_target_pairs={{0,16},{1,17},{2,18},{3,19},{4,20},{5,21},{6,22},{7,23},{8,24},{9,... | collective-permute-start | bytes 344072 | tf_op jit(solution)/shard_map/ppermute | solution.py:318
  67.5 0.1 collective-permute-start.13
  67.5 4.8 %shard_map.89 = (bf16[2,16,12288]{2,1,0:T(8,128)(2,1)}, bf16[2,16,12288]{2,1,0:T(8,128)(2,1)}) custom-call(bf16[36,96,128]{2,1,0:T(8,128)(2,1)} %collective-permute-done.12.refs_0_, bf16[2,3,3,256,128]{4,3,2,1,0:T(8,128)(2,1)} %get-tuple-element.46.refs_2_.refs_1_, ...), custom_call_target="tpu_custom_call", output_to_operand_aliasing={{0}: (4, {}), {1}: (5, {})} | custom-call | tf_op jit(solution)/shard_map/pallas_call | solution.py:27
  72.3 0.0 collective-permute-done.15.three
  72.3 0.0 collective-permute-done.14.two
  72.3 0.3 collective-permute-done.13.one
  72.6 1.0 %shard_map.90 = (f32[864,32]{1,0:T(8,128)}, f32[1,32]{1,0:T(1,128)}) custom-call(f32[224,128]{1,0:T(8,128)S(1)} %shard_map.88.part, f32[224,128]{1,0:T(8,128)S(1)} %collective-permute-done.13.one, f32[224,128]{1,0:T(8,128)S(1)} %collective-permute-done.14.two, f32[224,128]{1,0:T(8,128)S(1)} %collective-permute-done.15.three), custom_call_target="tpu_custom_call" | custom-call | tf_op jit(solution)/shard_map/pallas_call | solution.py:18
  (8 shorter events, 0.1 us)
Async XLA Ops:
  3.7 26.7 %copy-start = (bf16[32,96,128]{2,1,0:T(8,128)(2,1)S(1)}, bf16[32,96,128]{2,1,0:T(8,128)(2,1)}, u32[]{:S(2)}) copy-start(bf16[32,96,128]{2,1,0:T(8,128)(2,1)} %get-tuple-element.33.low) | copy-start | bytes 2359300
  3.7 12.3 %collective-permute-start.1 = (bf16[4,96,128]{2,1,0:T(8,128)(2,1)}, bf16[4,96,128]{2,1,0:T(8,128)(2,1)S(1)}, u32[]{:S(2)}, u32[]{:S(2)}) collective-permute-start(bf16[4,96,128]{2,1,0:T(8,128)(2,1)} %get-tuple-element.34), channel_id=1, source_target_pairs={{0,1},{1,2},{2,3},{3,4},{4,5},{5,6},{6,7},{7,8},{8,9},{9,10},{10,1... | collective-permute-start | bytes 294920 | tf_op jit(solution)/shard_map/ppermute | solution.py:313
  8.8 7.2 %collective-permute-start.2 = (bf16[4,96,128]{2,1,0:T(8,128)(2,1)}, bf16[4,96,128]{2,1,0:T(8,128)(2,1)S(1)}, u32[]{:S(2)}, u32[]{:S(2)}) collective-permute-start(bf16[4,96,128]{2,1,0:T(8,128)(2,1)} %get-tuple-element.35), channel_id=1, source_target_pairs={{1,0},{2,1},{3,2},{4,3},{5,4},{6,5},{7,6},{8,7},{9,8},{10,9},{11,1... | collective-permute-start | bytes 294920 | tf_op jit(solution)/shard_map/ppermute | solution.py:313
  10.7 24.6 %collective-permute-start = (bf16[24,96,128]{2,1,0:T(8,128)(2,1)}, bf16[24,96,128]{2,1,0:T(8,128)(2,1)S(1)}, u32[]{:S(2)}, u32[]{:S(2)}) collective-permute-start(bf16[24,96,128]{2,1,0:T(8,128)(2,1)} %get-tuple-element.32.high_first), channel_id=1, source_target_pairs={{0,16},{16,32},{32,48},{48,64},{64,80},{80,96},{96,112},{1,17},{17... | collective-permute-start | bytes 1769480 | tf_op jit(solution)/shard_map/ppermute | solution.py:313
  16.0 5.2 %copy-start.3 = (bf16[4,96,128]{2,1,0:T(8,128)(2,1)}, bf16[4,96,128]{2,1,0:T(8,128)(2,1)S(1)}, u32[]{:S(2)}) copy-start(bf16[4,96,128]{2,1,0:T(8,128)(2,1)S(1)} %collective-permute-done.1.from_left) | copy-start | bytes 294916
  16.0 5.2 %copy-start.5 = (bf16[4,96,128]{2,1,0:T(8,128)(2,1)}, bf16[4,96,128]{2,1,0:T(8,128)(2,1)S(1)}, u32[]{:S(2)}) copy-start(bf16[4,96,128]{2,1,0:T(8,128)(2,1)S(1)} %collective-permute-done.2.from_right) | copy-start | bytes 294916
  17.0 17.0 %collective-permute-start.3 = (bf16[12,96,128]{2,1,0:T(8,128)(2,1)S(1)}, bf16[12,96,128]{2,1,0:T(8,128)(2,1)S(1)}, u32[]{:S(2)}, u32[]{:S(2)}) collective-permute-start(bf16[12,96,128]{2,1,0:T(8,128)(2,1)S(1)} %pad_maximum_fusion.1), channel_id=1, source_target_pairs={{0,16},{16,32},{32,48},{48,64},{64,80},{80,96},{96,112},{1,17},{17... | collective-permute-start | bytes 884744 | tf_op jit(solution)/shard_map/ppermute | solution.py:313
  30.4 5.0 %copy-start.4 = (bf16[4,96,128]{2,1,0:T(8,128)(2,1)S(1)}, bf16[4,96,128]{2,1,0:T(8,128)(2,1)}, u32[]{:S(2)}) copy-start(bf16[4,96,128]{2,1,0:T(8,128)(2,1)} %copy-done.3) | copy-start | bytes 294916
  30.4 5.0 %copy-start.6 = (bf16[4,96,128]{2,1,0:T(8,128)(2,1)S(1)}, bf16[4,96,128]{2,1,0:T(8,128)(2,1)}, u32[]{:S(2)}) copy-start(bf16[4,96,128]{2,1,0:T(8,128)(2,1)} %copy-done.5) | copy-start | bytes 294916
  30.4 5.0 %copy-start.7 = (f32[3,3,32,128]{3,2,1,0:T(8,128)S(1)}, f32[3,3,32,128]{3,2,1,0:T(8,128)}, u32[]{:S(2)}) copy-start(f32[3,3,32,128]{3,2,1,0:T(8,128)} %get-tuple-element.42.folded) | copy-start | bytes 442372
  30.4 5.0 %copy-start.8 = (f32[8,128]{1,0:T(8,128)S(1)}, f32[8,128]{1,0:T(8,128)}, u32[]{:S(2)}) copy-start(f32[8,128]{1,0:T(8,128)} %get-tuple-element.43.bias_terms) | copy-start | bytes 12292
  30.6 25.0 %copy-start.9 = (f32[32]{0:T(128)S(1)}, f32[32]{0:T(128)}, u32[]{:S(2)}) copy-start(f32[32]{0:T(128)} %param.9) | copy-start | bytes 388
  34.0 22.2 %copy-start.2 = (bf16[12,96,128]{2,1,0:T(8,128)(2,1)}, bf16[12,96,128]{2,1,0:T(8,128)(2,1)S(1)}, u32[]{:S(2)}) copy-start(bf16[12,96,128]{2,1,0:T(8,128)(2,1)S(1)} %collective-permute-done.3.below_rest.refs_1_) | copy-start | bytes 884740
  34.0 30.1 %collective-permute-start.12 = (bf16[36,96,128]{2,1,0:T(8,128)(2,1)S(1)}, bf16[36,96,128]{2,1,0:T(8,128)(2,1)}, u32[]{:S(2)}, u32[]{:S(2)}) collective-permute-start(bf16[36,96,128]{2,1,0:T(8,128)(2,1)S(1)} %pad_maximum_fusion), channel_id=1, source_target_pairs={{16,0},{32,16},{48,32},{64,48},{80,64},{96,80},{112,96},{17,1},{33... | collective-permute-start | bytes 2654216 | tf_op jit(solution)/shard_map/ppermute | solution.py:313
  35.3 20.9 %copy-start.1 = (bf16[24,96,128]{2,1,0:T(8,128)(2,1)}, bf16[24,96,128]{2,1,0:T(8,128)(2,1)S(1)}, u32[]{:S(2)}) copy-start(bf16[24,96,128]{2,1,0:T(8,128)(2,1)S(1)} %collective-permute-done.below_first.refs_0_) | copy-start | bytes 1769476
  36.9 1.3 %collective-permute-start.4 = (f32[112,128]{1,0:T(8,128)S(1)}, f32[112,128]{1,0:T(8,128)S(1)}, u32[]{:S(2)}, u32[]{:S(2)}) collective-permute-start(f32[112,128]{1,0:T(8,128)S(1)} %get-tuple-element.45), channel_id=1, source_target_pairs={{0,1},{1,0},{2,3},{3,2},{4,5},{5,4},{6,7},{7,6},{8,9},{9,8},{10,11... | collective-permute-start | bytes 172040 | tf_op jit(solution)/shard_map/ppermute | solution.py:318
  38.3 6.2 %collective-permute-start.7 = (f32[112,128]{1,0:T(8,128)S(1)}, f32[112,128]{1,0:T(8,128)S(1)}, u32[]{:S(2)}, u32[]{:S(2)}) collective-permute-start(f32[112,128]{1,0:T(8,128)S(1)} %add.26), channel_id=1, source_target_pairs={{0,12},{1,13},{2,14},{3,15},{4,8},{5,9},{6,10},{7,11},{8,4},{9,5},... | collective-permute-start | bytes 172040 | tf_op jit(solution)/shard_map/ppermute | solution.py:318
  42.4 4.9 %collective-permute-start.6 = (f32[112,128]{1,0:T(8,128)S(1)}, f32[112,128]{1,0:T(8,128)S(1)}, u32[]{:S(2)}, u32[]{:S(2)}) collective-permute-start(f32[112,128]{1,0:T(8,128)S(1)} %add.26), channel_id=1, source_target_pairs={{0,8},{1,9},{2,10},{3,11},{4,12},{5,13},{6,14},{7,15},{8,0},{9,1},... | collective-permute-start | bytes 172040 | tf_op jit(solution)/shard_map/ppermute | solution.py:318
  42.9 4.4 %collective-permute-start.5 = (f32[112,128]{1,0:T(8,128)S(1)}, f32[112,128]{1,0:T(8,128)S(1)}, u32[]{:S(2)}, u32[]{:S(2)}) collective-permute-start(f32[112,128]{1,0:T(8,128)S(1)} %add.26), channel_id=1, source_target_pairs={{0,4},{1,5},{2,6},{3,7},{4,0},{5,1},{6,2},{7,3},{8,12},{9,13},{10,... | collective-permute-start | bytes 172040 | tf_op jit(solution)/shard_map/ppermute | solution.py:318
  47.3 13.7 %collective-permute-start.10 = (f32[112,128]{1,0:T(8,128)S(1)}, f32[112,128]{1,0:T(8,128)S(1)}, u32[]{:S(2)}, u32[]{:S(2)}) collective-permute-start(f32[112,128]{1,0:T(8,128)S(1)} %add_add_fusion.1), channel_id=1, source_target_pairs={{0,96},{1,97},{2,98},{3,99},{4,100},{5,101},{6,102},{7,103},{8,104... | collective-permute-start | bytes 172040 | tf_op jit(solution)/shard_map/ppermute | solution.py:318
  54.9 6.1 %collective-permute-start.9 = (f32[112,128]{1,0:T(8,128)S(1)}, f32[112,128]{1,0:T(8,128)S(1)}, u32[]{:S(2)}, u32[]{:S(2)}) collective-permute-start(f32[112,128]{1,0:T(8,128)S(1)} %add_add_fusion.1), channel_id=1, source_target_pairs={{0,64},{1,65},{2,66},{3,67},{4,68},{5,69},{6,70},{7,71},{8,72},{9,... | collective-permute-start | bytes 172040 | tf_op jit(solution)/shard_map/ppermute | solution.py:318
  55.0 7.4 %collective-permute-start.8 = (f32[112,128]{1,0:T(8,128)S(1)}, f32[112,128]{1,0:T(8,128)S(1)}, u32[]{:S(2)}, u32[]{:S(2)}) collective-permute-start(f32[112,128]{1,0:T(8,128)S(1)} %add_add_fusion.1), channel_id=1, source_target_pairs={{0,32},{1,33},{2,34},{3,35},{4,36},{5,37},{6,38},{7,39},{8,40},{9,... | collective-permute-start | bytes 172040 | tf_op jit(solution)/shard_map/ppermute | solution.py:318
  62.4 1.7 %collective-permute-start.11 = (f32[112,128]{1,0:T(8,128)S(1)}, f32[112,128]{1,0:T(8,128)S(1)}, u32[]{:S(2)}, u32[]{:S(2)}) collective-permute-start(f32[112,128]{1,0:T(8,128)S(1)} %add_add_fusion.part), channel_id=1, source_target_pairs={{0,1},{1,0},{2,3},{3,2},{4,5},{5,4},{6,7},{7,6},{8,9},{9,8},{10,11... | collective-permute-start | bytes 172040 | tf_op jit(solution)/shard_map/ppermute | solution.py:318
  64.2 8.2 %collective-permute-start.15 = (f32[224,128]{1,0:T(8,128)S(1)}, f32[224,128]{1,0:T(8,128)S(1)}, u32[]{:S(2)}, u32[]{:S(2)}) collective-permute-start(f32[224,128]{1,0:T(8,128)S(1)} %shard_map.88.part), channel_id=1, source_target_pairs={{0,18},{1,19},{2,16},{3,17},{4,22},{5,23},{6,20},{7,21},{8,26},{9,... | collective-permute-start | bytes 344072 | tf_op jit(solution)/shard_map/ppermute | solution.py:318
  65.4 7.0 %collective-permute-start.14 = (f32[224,128]{1,0:T(8,128)S(1)}, f32[224,128]{1,0:T(8,128)S(1)}, u32[]{:S(2)}, u32[]{:S(2)}) collective-permute-start(f32[224,128]{1,0:T(8,128)S(1)} %shard_map.88.part), channel_id=1, source_target_pairs={{0,16},{1,17},{2,18},{3,19},{4,20},{5,21},{6,22},{7,23},{8,24},{9,... | collective-permute-start | bytes 344072 | tf_op jit(solution)/shard_map/ppermute | solution.py:318
  67.5 5.2 %collective-permute-start.13 = (f32[224,128]{1,0:T(8,128)S(1)}, f32[224,128]{1,0:T(8,128)S(1)}, u32[]{:S(2)}, u32[]{:S(2)}) collective-permute-start(f32[224,128]{1,0:T(8,128)S(1)} %shard_map.88.part), channel_id=1, source_target_pairs={{0,2},{1,3},{2,0},{3,1},{4,6},{5,7},{6,4},{7,5},{8,10},{9,11},{10,... | collective-permute-start | bytes 344072 | tf_op jit(solution)/shard_map/ppermute | solution.py:318

commit v7 on v6

--- a/solution.py
+++ b/solution.py
@@ -33,7 +33,7 @@
         scratch_shapes=scratch,
         input_output_aliases=aliases or {},
         cost_estimate=pl.CostEstimate(flops=flops, bytes_accessed=0, transcendentals=0),
-        compiler_params=pltpu.CompilerParams(vmem_limit_bytes=56 * MIB),
+        compiler_params=pltpu.CompilerParams(vmem_limit_bytes=20 * MIB),
     )(*args)
 
 
@@ -396,7 +396,6 @@
     ends = (from_left[:2], from_right[:2])
     ends, folded, partial = lax.optimization_barrier((ends, folded, partial))
     down = jnp.concatenate([low, *ends])
-    down, below_rest = lax.optimization_barrier((down, below_rest))
     above = shifted(down, "gz", -1)
 
     part, send = call(

time: 74.6 us -> 75.6 us (1.013)
  local copies, waits for them, and re-layouts: 0.66 us -> 7.53 us
  waiting for transfers between devices: 11.5 us -> 7.46 us
  Pallas kernels: 24.4 us -> 21.3 us
  other arithmetic: 1.15 us -> 3.83 us
  starting transfers between devices: 35 us -> 34 us
    unnamed x20 -> x26, local copies, waits for them, and re-layouts: 0.04 us -> 7.43 us
    pallas_call x3, Pallas kernels: 18.9 us -> 14.6 us  [blocked(): pl.pallas_call(body, grid=(grid,), out_shape=outs, in_specs=in_specs, out...]
    ppermute x5, waiting for transfers between devices: 3.46 us -> 0.11 us  [shifted(): return lax.ppermute(value, axis, pairs)]
    concatenate x1, other arithmetic: 0.11 us -> 1.2 us  [local(): down = jnp.concatenate([low, *ends])]
    pallas_call x3, Pallas kernels: 2.51 us -> 3.56 us  [call(): pl.pallas_call(body, out_shape=outs, scratch_shapes=scratch, compiler_par...]
    ppermute x11, starting transfers between devices: 17.3 us -> 16.3 us  [swapped(): lax.ppermute(value, ('gz', 'gy'), [(i, i ^ bit) for i in range(count)])]
    add x2, other arithmetic: 0.03 us -> 0.91 us  [sum_of_four(): return value + one + (two + three)]
  transfers between devices with their start and end apart: 16 -> 16, of which waited for: 7 -> 6; matrix products, arithmetic and copies ran while one was open for 2% -> 5% of each run, Pallas kernels for 28% -> 23%
where the time goes in v7:
time: 75.6 us; the launch traced here: 74.9 us
  starting transfers between devices  34 us (45%)
  Pallas kernels  21.3 us (28%)
  local copies, waits for them, and re-layouts  7.53 us (10%)
  waiting for transfers between devices  7.46 us (10%)
  other arithmetic  3.83 us (5%)
  between operations  0.83 us (1%)
    ppermute x5, starting transfers between devices, shifted(): return lax.ppermute(value, axis, pairs)  17.7 us
    ppermute x11, starting transfers between devices, swapped(): lax.ppermute(value, ('gz', 'gy'), [(i, i ^ bit) for i in range(count)])  16.3 us
    pallas_call x3, Pallas kernels, blocked(): pl.pallas_call(body, grid=(grid,), out_shape=outs, in_specs=in_specs, out...  14.6 us
    unnamed x26, local copies, waits for them, and re-layouts  7.43 us
    ppermute x11, waiting for transfers between devices, swapped(): lax.ppermute(value, ('gz', 'gy'), [(i, i ^ bit) for i in range(count)])  7.35 us
    pallas_call x3, Pallas kernels, call(): pl.pallas_call(body, out_shape=outs, scratch_shapes=scratch, compiler_par...  3.56 us
    pallas_call x1, Pallas kernels, local(): pl.pallas_call(group_body, in_specs=[pl.BlockSpec(memory_space=pl.ANY)] *...  3.11 us
    concatenate x1, other arithmetic, local(): jnp.concatenate([high_rest, from_left[2:], from_right[2:]])  1.71 us
  transfers between devices with their start and end apart: 16, of which 6 were waited for; matrix products, arithmetic and copies ran while one was open for 5% of the time, Pallas kernels for 23%

profile of v7, /device:TPU:1, one launch (start us, length us, event | category | flops | bytes accessed | tf_op | source)
XLA Modules:
  0.0 74.9 jit_solution(15762273063021046061)
XLA Ops:
  0.6 0.0 copy-start.9
  0.6 3.1 %shard_map.84 = (bf16[32,96,128]{2,1,0:T(8,128)(2,1)}, bf16[24,96,128]{2,1,0:T(8,128)(2,1)}, bf16[8,96,128]{2,1,0:T(8,128)(2,1)}, bf16[4,96,128]{2,1,0:T(8,128)(2,1)}, bf16[4,96,128]{2,1,0:T(8,128)(2,1)}) custom-call(bf16[2,16,12288]{2,1,0:T(8,128)(2,1)} %act_in.1, bf16[2,16,12288]{2,1,0:T(8,128)(2,1)} %grad_in.1, s32[2,16,12288]{2,1,0:T(8,128)} %mask_in.1), custom_call_target="tpu_custom_call" | custom-call | tf_op jit(solution)/shard_map/pallas_call | solution.py:340
  3.8 4.9 %collective-permute-start.1 = (bf16[4,96,128]{2,1,0:T(8,128)(2,1)}, bf16[4,96,128]{2,1,0:T(8,128)(2,1)S(1)}, u32[]{:S(2)}, u32[]{:S(2)}) collective-permute-start(bf16[4,96,128]{2,1,0:T(8,128)(2,1)} %get-tuple-element.32), channel_id=1, source_target_pairs={{0,1},{1,2},{2,3},{3,4},{4,5},{5,6},{6,7},{7,8},{8,9},{9,10},{10,1... | collective-permute-start | bytes 294920 | tf_op jit(solution)/shard_map/ppermute | solution.py:313
  8.7 1.9 %collective-permute-start.2 = (bf16[4,96,128]{2,1,0:T(8,128)(2,1)}, bf16[4,96,128]{2,1,0:T(8,128)(2,1)S(1)}, u32[]{:S(2)}, u32[]{:S(2)}) collective-permute-start(bf16[4,96,128]{2,1,0:T(8,128)(2,1)} %get-tuple-element.33), channel_id=1, source_target_pairs={{1,0},{2,1},{3,2},{4,3},{5,4},{6,5},{7,6},{8,7},{9,8},{10,9},{11,1... | collective-permute-start | bytes 294920 | tf_op jit(solution)/shard_map/ppermute | solution.py:313
  10.6 6.0 %collective-permute-start = (bf16[24,96,128]{2,1,0:T(8,128)(2,1)}, bf16[24,96,128]{2,1,0:T(8,128)(2,1)}, u32[]{:S(2)}, u32[]{:S(2)}) collective-permute-start(bf16[24,96,128]{2,1,0:T(8,128)(2,1)} %get-tuple-element.30.high_first), channel_id=1, source_target_pairs={{0,16},{16,32},{32,48},{48,64},{64,80},{80,96},{96,112},{1,17},{17... | collective-permute-start | bytes 1769480 | tf_op jit(solution)/shard_map/ppermute | solution.py:313
  16.7 0.0 collective-permute-done.1.from_left
  16.7 0.0 collective-permute-done.2.from_right
  16.7 0.0 copy-start.5
  16.7 1.7 %pad_maximum_fusion.1 = bf16[12,96,128]{2,1,0:T(8,128)(2,1)} fusion(bf16[2,96,128]{2,1,0:T(8,128)(2,1)S(1)} %get-tuple-element.57, bf16[2,96,128]{2,1,0:T(8,128)(2,1)S(1)} %get-tuple-element.59, bf16[8,96,128]{2,1,0:T(8,128)(2,1)} %get-tuple-element.31.high_rest), kind=kLoop, calls=%fused_computation.1 | loop fusion | flops 294912 | bytes 589824 | tf_op jit(solution)/shard_map/concatenate | solution.py:355
  18.4 3.4 %collective-permute-start.3 = (bf16[12,96,128]{2,1,0:T(8,128)(2,1)}, bf16[12,96,128]{2,1,0:T(8,128)(2,1)S(1)}, u32[]{:S(2)}, u32[]{:S(2)}) collective-permute-start(bf16[12,96,128]{2,1,0:T(8,128)(2,1)} %pad_maximum_fusion.1), channel_id=1, source_target_pairs={{0,16},{16,32},{32,48},{48,64},{64,80},{80,96},{96,112},{1,17},{17... | collective-permute-start | bytes 884744 | tf_op jit(solution)/shard_map/ppermute | solution.py:313
  21.8 0.0 copy-done.9
  21.8 0.0 copy-start
  21.8 1.1 %copy-done = bf16[32,96,128]{2,1,0:T(8,128)(2,1)S(1)} copy-done((bf16[32,96,128]{2,1,0:T(8,128)(2,1)S(1)}, bf16[32,96,128]{2,1,0:T(8,128)(2,1)}, u32[]{:S(2)}) %copy-start) | copy-done | bytes 786456
  22.9 0.0 copy-start.7
  22.9 0.9 %copy-done.7 = bf16[8,96,128]{2,1,0:T(8,128)(2,1)S(1)} copy-done((bf16[8,96,128]{2,1,0:T(8,128)(2,1)S(1)}, bf16[8,96,128]{2,1,0:T(8,128)(2,1)}, u32[]{:S(2)}) %copy-start.7) | copy-done | bytes 196632
  23.9 0.0 copy-start.8
  23.9 1.1 %copy-done.8 = bf16[24,96,128]{2,1,0:T(8,128)(2,1)S(1)} copy-done((bf16[24,96,128]{2,1,0:T(8,128)(2,1)S(1)}, bf16[24,96,128]{2,1,0:T(8,128)(2,1)}, u32[]{:S(2)}) %copy-start.8) | copy-done | bytes 589848
  24.9 6.3 %shard_map.85 = (f32[3,3,32,128]{3,2,1,0:T(8,128)S(1)}, f32[8,128]{1,0:T(8,128)S(1)}, f32[2,2,16,96,128]{4,3,2,1,0:T(8,128)S(1)}, bf16[2,3,3,256,128]{4,3,2,1,0:T(8,128)(2,1)S(1)}) custom-call(bf16[32,96,128]{2,1,0:T(8,128)(2,1)S(1)} %copy-done, bf16[24,96,128]{2,1,0:T(8,128)(2,1)S(1)} %copy-done.8, bf16[8,96,128]{2,1,0:T(8,128)(2,1)S(1)} %copy-done.7, ...), custom_call_target="tpu_custom_call" | custom-call | tf_op jit(solution)/shard_map/pallas_call | solution.py:27
  31.2 0.0 copy-start.2
  31.2 0.0 copy-start.10
  31.2 1.2 %pad_maximum_fusion = bf16[36,96,128]{2,1,0:T(8,128)(2,1)} fusion(bf16[2,96,128]{2,1,0:T(8,128)(2,1)S(1)} %get-tuple-element.47, bf16[2,96,128]{2,1,0:T(8,128)(2,1)S(1)} %get-tuple-element.46, bf16[32,96,128]{2,1,0:T(8,128)(2,1)S(1)} %copy-done), kind=kLoop, calls=%fused_computation | loop fusion | flops 884736 | bytes 1769472 | tf_op jit(solution)/shard_map/concatenate | solution.py:398
  32.4 0.0 copy-done.5
  32.4 0.1 copy-done.2
  32.5 0.0 copy-start.12
  32.5 1.4 %collective-permute-start.12 = (bf16[36,96,128]{2,1,0:T(8,128)(2,1)}, bf16[36,96,128]{2,1,0:T(8,128)(2,1)}, u32[]{:S(2)}, u32[]{:S(2)}) collective-permute-start(bf16[36,96,128]{2,1,0:T(8,128)(2,1)} %pad_maximum_fusion), channel_id=1, source_target_pairs={{16,0},{32,16},{48,32},{64,48},{80,64},{96,80},{112,96},{17,1},{33... | collective-permute-start | bytes 2654216 | tf_op jit(solution)/shard_map/ppermute | solution.py:313
  33.9 0.0 copy-done.10
  34.0 0.1 collective-permute-done.3.below_rest.refs_1_
  34.0 0.0 collective-permute-done.below_first.refs_0_
  34.1 0.0 copy-start.1
  34.1 1.1 %copy-done.1 = bf16[32,96,128]{2,1,0:T(8,128)(2,1)S(1)} copy-done((bf16[32,96,128]{2,1,0:T(8,128)(2,1)S(1)}, bf16[32,96,128]{2,1,0:T(8,128)(2,1)}, u32[]{:S(2)}) %copy-start.1) | copy-done | bytes 786456
  35.2 0.9 %copy-done.6 = bf16[4,96,128]{2,1,0:T(8,128)(2,1)S(1)} copy-done((bf16[4,96,128]{2,1,0:T(8,128)(2,1)S(1)}, bf16[4,96,128]{2,1,0:T(8,128)(2,1)}, u32[]{:S(2)}) %copy-start.6) | copy-done | bytes 98328
  36.1 0.9 %copy-done.11 = f32[3,3,32,128]{3,2,1,0:T(8,128)S(1)} copy-done((f32[3,3,32,128]{3,2,1,0:T(8,128)S(1)}, f32[3,3,32,128]{3,2,1,0:T(8,128)}, u32[]{:S(2)}) %copy-start.11) | copy-done | bytes 147480
  37.0 2.6 %shard_map.86 = (f32[112,128]{1,0:T(8,128)S(1)}, f32[112,128]{1,0:T(8,128)S(1)}) custom-call(bf16[24,96,128]{2,1,0:T(8,128)(2,1)} %collective-permute-done.below_first.refs_0_, bf16[12,96,128]{2,1,0:T(8,128)(2,1)S(1)} %collective-permute-done.3.below_rest.refs_1_, bf16[32,96,128]{2,1,0:T(8,128)(2,1)S(1)} %copy-done.1, ...), custom_call_target="tpu_custom_call" | custom-call | tf_op jit(solution)/shard_map/pallas_call | solution.py:18
  39.6 0.1 collective-permute-start.4
  39.7 1.2 %collective-permute-done.4 = f32[112,128]{1,0:T(8,128)S(1)} collective-permute-done((f32[112,128]{1,0:T(8,128)S(1)}, f32[112,128]{1,0:T(8,128)S(1)}, u32[]{:S(2)}, u32[]{:S(2)}) %collective-permute-start.4) | collective-permute-done | bytes 57376 | tf_op jit(solution)/shard_map/ppermute | solution.py:318
  40.9 4.1 %collective-permute-start.7 = (f32[112,128]{1,0:T(8,128)S(1)}, f32[112,128]{1,0:T(8,128)S(1)}, u32[]{:S(2)}, u32[]{:S(2)}) collective-permute-start(f32[112,128]{1,0:T(8,128)S(1)} %add.26), channel_id=1, source_target_pairs={{0,12},{1,13},{2,14},{3,15},{4,8},{5,9},{6,10},{7,11},{8,4},{9,5},... | collective-permute-start | bytes 172040 | tf_op jit(solution)/shard_map/ppermute | solution.py:318
  45.0 0.5 collective-permute-start.6
  45.6 0.2 collective-permute-start.5
  45.7 1.4 %collective-permute-done.7 = f32[112,128]{1,0:T(8,128)S(1)} collective-permute-done((f32[112,128]{1,0:T(8,128)S(1)}, f32[112,128]{1,0:T(8,128)S(1)}, u32[]{:S(2)}, u32[]{:S(2)}) %collective-permute-start.7) | collective-permute-done | bytes 57376 | tf_op jit(solution)/shard_map/ppermute | solution.py:318
  47.1 2.9 %collective-permute-done.6 = f32[112,128]{1,0:T(8,128)S(1)} collective-permute-done((f32[112,128]{1,0:T(8,128)S(1)}, f32[112,128]{1,0:T(8,128)S(1)}, u32[]{:S(2)}, u32[]{:S(2)}) %collective-permute-start.6) | collective-permute-done | bytes 57376 | tf_op jit(solution)/shard_map/ppermute | solution.py:318
  50.0 0.0 collective-permute-done.5
  50.0 5.2 %collective-permute-start.10 = (f32[112,128]{1,0:T(8,128)S(1)}, f32[112,128]{1,0:T(8,128)}, u32[]{:S(2)}, u32[]{:S(2)}) collective-permute-start(f32[112,128]{1,0:T(8,128)S(1)} %add_add_fusion.1), channel_id=1, source_target_pairs={{0,96},{1,97},{2,98},{3,99},{4,100},{5,101},{6,102},{7,103},{8,104... | collective-permute-start | bytes 172040 | tf_op jit(solution)/shard_map/ppermute | solution.py:318
  55.2 0.3 collective-permute-start.9
  55.6 0.3 collective-permute-start.8
  55.9 0.0 copy-done.12
  55.9 0.1 reshape_tile.3.refs_4_.refs_3_
  56.0 1.3 %copy-done.3 = bf16[2,3,3,256,128]{4,3,2,1,0:T(8,128)(2,1)S(1)} copy-done((bf16[2,3,3,256,128]{4,3,2,1,0:T(8,128)(2,1)S(1)}, bf16[2,3,3,256,128]{4,3,2,1,0:T(8,128)(2,1)}, u32[]{:S(2)}) %copy-start.3) | copy-done | bytes 1179672
  57.3 4.2 %shard_map.87 = (bf16[2,16,12288]{2,1,0:T(8,128)(2,1)}, bf16[2,16,12288]{2,1,0:T(8,128)(2,1)}) custom-call(bf16[24,96,128]{2,1,0:T(8,128)(2,1)} %collective-permute-done.below_first.refs_0_, bf16[12,96,128]{2,1,0:T(8,128)(2,1)S(1)} %collective-permute-done.3.below_rest.refs_1_, bf16[2,3,3,256,128]{4,3,2,1,0:T(8,128)(2,1)S(1)} %copy-done.3, ...), custom_call_target="tpu_custom_call" | custom-call | tf_op jit(solution)/shard_map/pallas_call | solution.py:27
  61.5 0.0 collective-permute-done.10
  61.5 0.0 collective-permute-done.9
  61.5 0.0 collective-permute-done.8
  61.5 0.9 %add_add_fusion.part = f32[112,128]{1,0:T(8,128)S(1)} fusion(f32[112,128]{1,0:T(8,128)} %collective-permute-done.9, f32[112,128]{1,0:T(8,128)} %collective-permute-done.10, f32[112,128]{1,0:T(8,128)S(1)} %add_add_fusion.1, f32[112,128]{1,0:T(8,128)} %collective-permute-done.8), kind=kLoop, calls=%fused_computation.2 | loop fusion | flops 43008 | bytes 286720 | tf_op jit(solution)/shard_map/add | solution.py:323
  62.4 2.2 %collective-permute-start.11 = (f32[112,128]{1,0:T(8,128)S(1)}, f32[112,128]{1,0:T(8,128)S(1)}, u32[]{:S(2)}, u32[]{:S(2)}) collective-permute-start(f32[112,128]{1,0:T(8,128)S(1)} %add_add_fusion.part), channel_id=1, source_target_pairs={{0,1},{1,0},{2,3},{3,2},{4,5},{5,4},{6,7},{7,6},{8,9},{9,8},{10,11... | collective-permute-start | bytes 172040 | tf_op jit(solution)/shard_map/ppermute | solution.py:318
  64.5 0.9 %collective-permute-done.11.other = f32[112,128]{1,0:T(8,128)S(1)} collective-permute-done((f32[112,128]{1,0:T(8,128)S(1)}, f32[112,128]{1,0:T(8,128)S(1)}, u32[]{:S(2)}, u32[]{:S(2)}) %collective-permute-start.11) | collective-permute-done | bytes 57376 | tf_op jit(solution)/shard_map/ppermute | solution.py:318
  65.4 0.0 collective-permute-done.12.refs_0_
  65.4 1.2 %collective-permute-start.15 = (f32[224,128]{1,0:T(8,128)S(1)}, f32[224,128]{1,0:T(8,128)S(1)}, u32[]{:S(2)}, u32[]{:S(2)}) collective-permute-start(f32[224,128]{1,0:T(8,128)S(1)} %shard_map.88.part), channel_id=1, source_target_pairs={{0,18},{1,19},{2,16},{3,17},{4,22},{5,23},{6,20},{7,21},{8,26},{9,... | collective-permute-start | bytes 344072 | tf_op jit(solution)/shard_map/ppermute | solution.py:318
  66.6 0.5 collective-permute-start.14
  67.1 1.6 %collective-permute-start.13 = (f32[224,128]{1,0:T(8,128)S(1)}, f32[224,128]{1,0:T(8,128)S(1)}, u32[]{:S(2)}, u32[]{:S(2)}) collective-permute-start(f32[224,128]{1,0:T(8,128)S(1)} %shard_map.88.part), channel_id=1, source_target_pairs={{0,2},{1,3},{2,0},{3,1},{4,6},{5,7},{6,4},{7,5},{8,10},{9,11},{10,... | collective-permute-start | bytes 344072 | tf_op jit(solution)/shard_map/ppermute | solution.py:318
  68.8 0.0 copy-done.4
  68.8 4.2 %shard_map.89 = (bf16[2,16,12288]{2,1,0:T(8,128)(2,1)}, bf16[2,16,12288]{2,1,0:T(8,128)(2,1)}) custom-call(bf16[36,96,128]{2,1,0:T(8,128)(2,1)} %collective-permute-done.12.refs_0_, bf16[2,3,3,256,128]{4,3,2,1,0:T(8,128)(2,1)S(1)} %copy-done.4, ...), custom_call_target="tpu_custom_call", output_to_operand_aliasing={{0}: (4, {}), {1}: (5, {})} | custom-call | tf_op jit(solution)/shard_map/pallas_call | solution.py:27
  73.0 0.0 collective-permute-done.15.three
  73.0 0.0 collective-permute-done.14.two
  73.0 1.0 %collective-permute-done.13.one = f32[224,128]{1,0:T(8,128)S(1)} collective-permute-done((f32[224,128]{1,0:T(8,128)S(1)}, f32[224,128]{1,0:T(8,128)S(1)}, u32[]{:S(2)}, u32[]{:S(2)}) %collective-permute-start.13) | collective-permute-done | bytes 114720 | tf_op jit(solution)/shard_map/ppermute | solution.py:318
  73.9 1.0 %shard_map.90 = (f32[864,32]{1,0:T(8,128)}, f32[1,32]{1,0:T(1,128)}) custom-call(f32[224,128]{1,0:T(8,128)S(1)} %shard_map.88.part, f32[224,128]{1,0:T(8,128)S(1)} %collective-permute-done.13.one, f32[224,128]{1,0:T(8,128)S(1)} %collective-permute-done.14.two, f32[224,128]{1,0:T(8,128)S(1)} %collective-permute-done.15.three), custom_call_target="tpu_custom_call" | custom-call | tf_op jit(solution)/shard_map/pallas_call | solution.py:18
  (11 shorter events, 0.1 us)
Async XLA Ops:
  0.6 21.2 %copy-start.9 = (bf16[3,3,3,32,32]{4,3,2,1,0:T(8,128)(2,1)S(1)}, bf16[3,3,3,32,32]{4,3,2,1,0:T(8,128)(2,1)}, u32[]{:S(2)}) copy-start(bf16[3,3,3,32,32]{4,3,2,1,0:T(8,128)(2,1)} %param.8) | copy-start | bytes 165892
  3.8 12.9 %collective-permute-start.1 = (bf16[4,96,128]{2,1,0:T(8,128)(2,1)}, bf16[4,96,128]{2,1,0:T(8,128)(2,1)S(1)}, u32[]{:S(2)}, u32[]{:S(2)}) collective-permute-start(bf16[4,96,128]{2,1,0:T(8,128)(2,1)} %get-tuple-element.32), channel_id=1, source_target_pairs={{0,1},{1,2},{2,3},{3,4},{4,5},{5,6},{6,7},{7,8},{8,9},{9,10},{10,1... | collective-permute-start | bytes 294920 | tf_op jit(solution)/shard_map/ppermute | solution.py:313
  8.7 8.0 %collective-permute-start.2 = (bf16[4,96,128]{2,1,0:T(8,128)(2,1)}, bf16[4,96,128]{2,1,0:T(8,128)(2,1)S(1)}, u32[]{:S(2)}, u32[]{:S(2)}) collective-permute-start(bf16[4,96,128]{2,1,0:T(8,128)(2,1)} %get-tuple-element.33), channel_id=1, source_target_pairs={{1,0},{2,1},{3,2},{4,3},{5,4},{6,5},{7,6},{8,7},{9,8},{10,9},{11,1... | collective-permute-start | bytes 294920 | tf_op jit(solution)/shard_map/ppermute | solution.py:313
  10.6 23.4 %collective-permute-start = (bf16[24,96,128]{2,1,0:T(8,128)(2,1)}, bf16[24,96,128]{2,1,0:T(8,128)(2,1)}, u32[]{:S(2)}, u32[]{:S(2)}) collective-permute-start(bf16[24,96,128]{2,1,0:T(8,128)(2,1)} %get-tuple-element.30.high_first), channel_id=1, source_target_pairs={{0,16},{16,32},{32,48},{48,64},{64,80},{80,96},{96,112},{1,17},{17... | collective-permute-start | bytes 1769480 | tf_op jit(solution)/shard_map/ppermute | solution.py:313
  16.7 15.7 %copy-start.5 = (bf16[4,96,128]{2,1,0:T(8,128)(2,1)}, bf16[4,96,128]{2,1,0:T(8,128)(2,1)S(1)}, u32[]{:S(2)}) copy-start(bf16[4,96,128]{2,1,0:T(8,128)(2,1)S(1)} %collective-permute-done.2.from_right) | copy-start | bytes 294916
  18.4 15.6 %collective-permute-start.3 = (bf16[12,96,128]{2,1,0:T(8,128)(2,1)}, bf16[12,96,128]{2,1,0:T(8,128)(2,1)S(1)}, u32[]{:S(2)}, u32[]{:S(2)}) collective-permute-start(bf16[12,96,128]{2,1,0:T(8,128)(2,1)} %pad_maximum_fusion.1), channel_id=1, source_target_pairs={{0,16},{16,32},{32,48},{48,64},{64,80},{80,96},{96,112},{1,17},{17... | collective-permute-start | bytes 884744 | tf_op jit(solution)/shard_map/ppermute | solution.py:313
  21.8 1.1 %copy-start = (bf16[32,96,128]{2,1,0:T(8,128)(2,1)S(1)}, bf16[32,96,128]{2,1,0:T(8,128)(2,1)}, u32[]{:S(2)}) copy-start(bf16[32,96,128]{2,1,0:T(8,128)(2,1)} %get-tuple-element.34.low) | copy-start | bytes 2359300
  22.9 0.9 %copy-start.7 = (bf16[8,96,128]{2,1,0:T(8,128)(2,1)S(1)}, bf16[8,96,128]{2,1,0:T(8,128)(2,1)}, u32[]{:S(2)}) copy-start(bf16[8,96,128]{2,1,0:T(8,128)(2,1)} %get-tuple-element.31.high_rest) | copy-start | bytes 589828
  23.9 1.1 %copy-start.8 = (bf16[24,96,128]{2,1,0:T(8,128)(2,1)S(1)}, bf16[24,96,128]{2,1,0:T(8,128)(2,1)}, u32[]{:S(2)}) copy-start(bf16[24,96,128]{2,1,0:T(8,128)(2,1)} %get-tuple-element.30.high_first) | copy-start | bytes 1769476
  31.2 1.3 %copy-start.2 = (bf16[2,3,3,256,128]{4,3,2,1,0:T(8,128)(2,1)}, bf16[2,3,3,256,128]{4,3,2,1,0:T(8,128)(2,1)S(1)}, u32[]{:S(2)}) copy-start(bf16[2,3,3,256,128]{4,3,2,1,0:T(8,128)(2,1)S(1)} %get-tuple-element.41.refs_2_.refs_1_) | copy-start | bytes 3538948
  31.2 2.7 %copy-start.10 = (f32[3,3,32,128]{3,2,1,0:T(8,128)}, f32[3,3,32,128]{3,2,1,0:T(8,128)S(1)}, u32[]{:S(2)}) copy-start(f32[3,3,32,128]{3,2,1,0:T(8,128)S(1)} %get-tuple-element.37.folded) | copy-start | bytes 442372
  32.5 23.4 %copy-start.12 = (f32[32]{0:T(128)S(1)}, f32[32]{0:T(128)}, u32[]{:S(2)}) copy-start(f32[32]{0:T(128)} %param.9) | copy-start | bytes 388
  32.5 32.9 %collective-permute-start.12 = (bf16[36,96,128]{2,1,0:T(8,128)(2,1)}, bf16[36,96,128]{2,1,0:T(8,128)(2,1)}, u32[]{:S(2)}, u32[]{:S(2)}) collective-permute-start(bf16[36,96,128]{2,1,0:T(8,128)(2,1)} %pad_maximum_fusion), channel_id=1, source_target_pairs={{16,0},{32,16},{48,32},{64,48},{80,64},{96,80},{112,96},{17,1},{33... | collective-permute-start | bytes 2654216 | tf_op jit(solution)/shard_map/ppermute | solution.py:313
  34.1 1.1 %copy-start.1 = (bf16[32,96,128]{2,1,0:T(8,128)(2,1)S(1)}, bf16[32,96,128]{2,1,0:T(8,128)(2,1)}, u32[]{:S(2)}) copy-start(bf16[32,96,128]{2,1,0:T(8,128)(2,1)} %get-tuple-element.34.low) | copy-start | bytes 2359300
  35.2 0.9 %copy-start.6 = (bf16[4,96,128]{2,1,0:T(8,128)(2,1)S(1)}, bf16[4,96,128]{2,1,0:T(8,128)(2,1)}, u32[]{:S(2)}) copy-start(bf16[4,96,128]{2,1,0:T(8,128)(2,1)} %copy-done.5) | copy-start | bytes 294916
  36.1 0.9 %copy-start.11 = (f32[3,3,32,128]{3,2,1,0:T(8,128)S(1)}, f32[3,3,32,128]{3,2,1,0:T(8,128)}, u32[]{:S(2)}) copy-start(f32[3,3,32,128]{3,2,1,0:T(8,128)} %copy-done.10) | copy-start | bytes 442372
  39.6 1.3 %collective-permute-start.4 = (f32[112,128]{1,0:T(8,128)S(1)}, f32[112,128]{1,0:T(8,128)S(1)}, u32[]{:S(2)}, u32[]{:S(2)}) collective-permute-start(f32[112,128]{1,0:T(8,128)S(1)} %get-tuple-element.40), channel_id=1, source_target_pairs={{0,1},{1,0},{2,3},{3,2},{4,5},{5,4},{6,7},{7,6},{8,9},{9,8},{10,11... | collective-permute-start | bytes 172040 | tf_op jit(solution)/shard_map/ppermute | solution.py:318
  40.9 6.2 %collective-permute-start.7 = (f32[112,128]{1,0:T(8,128)S(1)}, f32[112,128]{1,0:T(8,128)S(1)}, u32[]{:S(2)}, u32[]{:S(2)}) collective-permute-start(f32[112,128]{1,0:T(8,128)S(1)} %add.26), channel_id=1, source_target_pairs={{0,12},{1,13},{2,14},{3,15},{4,8},{5,9},{6,10},{7,11},{8,4},{9,5},... | collective-permute-start | bytes 172040 | tf_op jit(solution)/shard_map/ppermute | solution.py:318
  45.0 4.9 %collective-permute-start.6 = (f32[112,128]{1,0:T(8,128)S(1)}, f32[112,128]{1,0:T(8,128)S(1)}, u32[]{:S(2)}, u32[]{:S(2)}) collective-permute-start(f32[112,128]{1,0:T(8,128)S(1)} %add.26), channel_id=1, source_target_pairs={{0,8},{1,9},{2,10},{3,11},{4,12},{5,13},{6,14},{7,15},{8,0},{9,1},... | collective-permute-start | bytes 172040 | tf_op jit(solution)/shard_map/ppermute | solution.py:318
  45.6 4.4 %collective-permute-start.5 = (f32[112,128]{1,0:T(8,128)S(1)}, f32[112,128]{1,0:T(8,128)S(1)}, u32[]{:S(2)}, u32[]{:S(2)}) collective-permute-start(f32[112,128]{1,0:T(8,128)S(1)} %add.26), channel_id=1, source_target_pairs={{0,4},{1,5},{2,6},{3,7},{4,0},{5,1},{6,2},{7,3},{8,12},{9,13},{10,... | collective-permute-start | bytes 172040 | tf_op jit(solution)/shard_map/ppermute | solution.py:318
  50.0 11.5 %collective-permute-start.10 = (f32[112,128]{1,0:T(8,128)S(1)}, f32[112,128]{1,0:T(8,128)}, u32[]{:S(2)}, u32[]{:S(2)}) collective-permute-start(f32[112,128]{1,0:T(8,128)S(1)} %add_add_fusion.1), channel_id=1, source_target_pairs={{0,96},{1,97},{2,98},{3,99},{4,100},{5,101},{6,102},{7,103},{8,104... | collective-permute-start | bytes 172040 | tf_op jit(solution)/shard_map/ppermute | solution.py:318
  55.2 6.2 %collective-permute-start.9 = (f32[112,128]{1,0:T(8,128)S(1)}, f32[112,128]{1,0:T(8,128)}, u32[]{:S(2)}, u32[]{:S(2)}) collective-permute-start(f32[112,128]{1,0:T(8,128)S(1)} %add_add_fusion.1), channel_id=1, source_target_pairs={{0,64},{1,65},{2,66},{3,67},{4,68},{5,69},{6,70},{7,71},{8,72},{9,... | collective-permute-start | bytes 172040 | tf_op jit(solution)/shard_map/ppermute | solution.py:318
  55.6 5.9 %collective-permute-start.8 = (f32[112,128]{1,0:T(8,128)S(1)}, f32[112,128]{1,0:T(8,128)}, u32[]{:S(2)}, u32[]{:S(2)}) collective-permute-start(f32[112,128]{1,0:T(8,128)S(1)} %add_add_fusion.1), channel_id=1, source_target_pairs={{0,32},{1,33},{2,34},{3,35},{4,36},{5,37},{6,38},{7,39},{8,40},{9,... | collective-permute-start | bytes 172040 | tf_op jit(solution)/shard_map/ppermute | solution.py:318
  56.0 1.3 %copy-start.3 = (bf16[2,3,3,256,128]{4,3,2,1,0:T(8,128)(2,1)S(1)}, bf16[2,3,3,256,128]{4,3,2,1,0:T(8,128)(2,1)}, u32[]{:S(2)}) copy-start(bf16[2,3,3,256,128]{4,3,2,1,0:T(8,128)(2,1)} %copy-done.2) | copy-start | bytes 3538948
  57.3 11.5 %copy-start.4 = (bf16[2,3,3,256,128]{4,3,2,1,0:T(8,128)(2,1)S(1)}, bf16[2,3,3,256,128]{4,3,2,1,0:T(8,128)(2,1)}, u32[]{:S(2)}) copy-start(bf16[2,3,3,256,128]{4,3,2,1,0:T(8,128)(2,1)} %copy-done.2) | copy-start | bytes 3538948
  62.4 3.1 %collective-permute-start.11 = (f32[112,128]{1,0:T(8,128)S(1)}, f32[112,128]{1,0:T(8,128)S(1)}, u32[]{:S(2)}, u32[]{:S(2)}) collective-permute-start(f32[112,128]{1,0:T(8,128)S(1)} %add_add_fusion.part), channel_id=1, source_target_pairs={{0,1},{1,0},{2,3},{3,2},{4,5},{5,4},{6,7},{7,6},{8,9},{9,8},{10,11... | collective-permute-start | bytes 172040 | tf_op jit(solution)/shard_map/ppermute | solution.py:318
  65.4 7.5 %collective-permute-start.15 = (f32[224,128]{1,0:T(8,128)S(1)}, f32[224,128]{1,0:T(8,128)S(1)}, u32[]{:S(2)}, u32[]{:S(2)}) collective-permute-start(f32[224,128]{1,0:T(8,128)S(1)} %shard_map.88.part), channel_id=1, source_target_pairs={{0,18},{1,19},{2,16},{3,17},{4,22},{5,23},{6,20},{7,21},{8,26},{9,... | collective-permute-start | bytes 344072 | tf_op jit(solution)/shard_map/ppermute | solution.py:318
  66.6 6.3 %collective-permute-start.14 = (f32[224,128]{1,0:T(8,128)S(1)}, f32[224,128]{1,0:T(8,128)S(1)}, u32[]{:S(2)}, u32[]{:S(2)}) collective-permute-start(f32[224,128]{1,0:T(8,128)S(1)} %shard_map.88.part), channel_id=1, source_target_pairs={{0,16},{1,17},{2,18},{3,19},{4,20},{5,21},{6,22},{7,23},{8,24},{9,... | collective-permute-start | bytes 344072 | tf_op jit(solution)/shard_map/ppermute | solution.py:318
  67.1 6.8 %collective-permute-start.13 = (f32[224,128]{1,0:T(8,128)S(1)}, f32[224,128]{1,0:T(8,128)S(1)}, u32[]{:S(2)}, u32[]{:S(2)}) collective-permute-start(f32[224,128]{1,0:T(8,128)S(1)} %shard_map.88.part), channel_id=1, source_target_pairs={{0,2},{1,3},{2,0},{3,1},{4,6},{5,7},{6,4},{7,5},{8,10},{9,11},{10,... | collective-permute-start | bytes 344072 | tf_op jit(solution)/shard_map/ppermute | solution.py:318

commit v8 on v6

--- a/solution.py
+++ b/solution.py
@@ -248,6 +248,7 @@
     weights, partial, line = refs[count : count + 3]
     output, grad_input, taps, scratch, grad = refs[-5:]
     rows, groups = partial.shape[2:4]
+    repeated = jnp.concatenate([line[...]] * 4, axis=1)
     act, edge = first.at[:rows], rest.at[rest.shape[0] - 4 :]
     gather_grad(first, rest, grad)
     for kind, (source, out, turn) in enumerate(((act, output, rectified), (grad, grad_input, kept))):
@@ -259,12 +260,12 @@
                 at = start + tap_y
                 lhs = taps[kind, at : at + CHUNK].reshape(CHUNK * groups, 256)
                 total = total + jnp.dot(lhs, weights[kind, 0, tap_y], preferred_element_type=F32)
-            put_rows(scratch, turn(total, line), chunk, groups)
+            put_rows(scratch, turn(total, repeated), chunk, groups)
         lay_out(scratch, out, 0, rows, groups)
 
 
 def rectified(total, line):
-    return jnp.maximum(total + line[...], 0.0)
+    return jnp.maximum(total + line, 0.0)
 
 
 def kept(total, line):
@@ -354,7 +355,7 @@
     below_first = shifted(high_first, "gz", 1)
     below_rest = shifted(jnp.concatenate([high_rest, from_left[2:], from_right[2:]]), "gz", 1)
 
-    line = jnp.tile(bias, 4).reshape(1, LANES)
+    line = bias.reshape(1, 32)
     flat_kernel = kernel.reshape(27 * 32, 32)
     plane = (rows, groups, LANES)
     folded_shape, bias_shape, weights_shape = (3, 3, 32, LANES), (8, LANES), (3, 3, 256, LANES)
@@ -387,7 +388,7 @@
             [
                 *[part_of(array.shape, 0, 0, 0) for array in planes_beside],
                 part_of((2, 1, 3, 256, LANES), 0, 2 * side, 0, 0, 0), part_of((2, 1, *plane), 0, side, 0, 0, 0),
-                part_of((1, LANES), 0, 0),
+                part_of(line.shape, 0, 0),
                 *[pl.BlockSpec(memory_space=pl.ANY)] * len(done),
             ],
             {count + 3: 0, count + 4: 1} if done else None,
@@ -396,7 +397,6 @@
     ends = (from_left[:2], from_right[:2])
     ends, folded, partial = lax.optimization_barrier((ends, folded, partial))
     down = jnp.concatenate([low, *ends])
-    down, below_rest = lax.optimization_barrier((down, below_rest))
     above = shifted(down, "gz", -1)
 
     part, send = call(

time: 74.6 us -> 87.3 us (1.17)
  starting transfers between devices: 35 us -> 50.3 us
  waiting for transfers between devices: 11.5 us -> 8.86 us
    ppermute x11, starting transfers between devices: 17.3 us -> 32.7 us  [swapped(): lax.ppermute(value, ('gz', 'gy'), [(i, i ^ bit) for i in range(count)])]
    ppermute x11, waiting for transfers between devices: 8.04 us -> 6.7 us  [swapped(): lax.ppermute(value, ('gz', 'gy'), [(i, i ^ bit) for i in range(count)])]
    ppermute x5, waiting for transfers between devices: 3.46 us -> 2.16 us  [shifted(): return lax.ppermute(value, axis, pairs)]
  transfers between devices with their start and end apart: 16 -> 16, of which waited for: 7 -> 6; matrix products, arithmetic and copies ran while one was open for 2% -> 1% of each run, Pallas kernels for 28% -> 24%
where the time goes in v8:
time: 87.3 us; the launch traced here: 85.8 us
  starting transfers between devices  50.3 us (58%)
  Pallas kernels  24.4 us (28%)
  waiting for transfers between devices  8.86 us (10%)
  other arithmetic  1.15 us (1%)
  between operations  0.9 us (1%)
    ppermute x11, starting transfers between devices, swapped(): lax.ppermute(value, ('gz', 'gy'), [(i, i ^ bit) for i in range(count)])  32.7 us
    pallas_call x3, Pallas kernels, blocked(): pl.pallas_call(body, grid=(grid,), out_shape=outs, in_specs=in_specs, out...  18.9 us
    ppermute x5, starting transfers between devices, shifted(): return lax.ppermute(value, axis, pairs)  17.7 us
    ppermute x11, waiting for transfers between devices, swapped(): lax.ppermute(value, ('gz', 'gy'), [(i, i ^ bit) for i in range(count)])  6.7 us
    pallas_call x1, Pallas kernels, local(): pl.pallas_call(group_body, in_specs=[pl.BlockSpec(memory_space=pl.ANY)] *...  3.06 us
    pallas_call x3, Pallas kernels, call(): pl.pallas_call(body, out_shape=outs, scratch_shapes=scratch, compiler_par...  2.51 us
    ppermute x5, waiting for transfers between devices, shifted(): return lax.ppermute(value, axis, pairs)  2.16 us
  transfers between devices with their start and end apart: 16, of which 6 were waited for; matrix products, arithmetic and copies ran while one was open for 1% of the time, Pallas kernels for 24%

profile of v8, /device:TPU:1, one launch (start us, length us, event | category | flops | bytes accessed | tf_op | source)
XLA Modules:
  0.0 85.8 jit_solution(9253322935874547699)
XLA Ops:
  0.6 3.1 %shard_map.84 = (bf16[32,96,128]{2,1,0:T(8,128)(2,1)}, bf16[24,96,128]{2,1,0:T(8,128)(2,1)}, bf16[8,96,128]{2,1,0:T(8,128)(2,1)}, bf16[4,96,128]{2,1,0:T(8,128)(2,1)}, bf16[4,96,128]{2,1,0:T(8,128)(2,1)}) custom-call(bf16[2,16,12288]{2,1,0:T(8,128)(2,1)} %act_in.1, bf16[2,16,12288]{2,1,0:T(8,128)(2,1)} %grad_in.1, s32[2,16,12288]{2,1,0:T(8,128)} %mask_in.1), custom_call_target="tpu_custom_call" | custom-call | tf_op jit(solution)/shard_map/pallas_call | solution.py:341
  3.7 0.0 copy-start
  3.7 5.1 %collective-permute-start.1 = (bf16[4,96,128]{2,1,0:T(8,128)(2,1)}, bf16[4,96,128]{2,1,0:T(8,128)(2,1)S(1)}, u32[]{:S(2)}, u32[]{:S(2)}) collective-permute-start(bf16[4,96,128]{2,1,0:T(8,128)(2,1)} %get-tuple-element.32), channel_id=1, source_target_pairs={{0,1},{1,2},{2,3},{3,4},{4,5},{5,6},{6,7},{7,8},{8,9},{9,10},{10,1... | collective-permute-start | bytes 294920 | tf_op jit(solution)/shard_map/ppermute | solution.py:314
  8.8 1.9 %collective-permute-start.2 = (bf16[4,96,128]{2,1,0:T(8,128)(2,1)}, bf16[4,96,128]{2,1,0:T(8,128)(2,1)S(1)}, u32[]{:S(2)}, u32[]{:S(2)}) collective-permute-start(bf16[4,96,128]{2,1,0:T(8,128)(2,1)} %get-tuple-element.33), channel_id=1, source_target_pairs={{1,0},{2,1},{3,2},{4,3},{5,4},{6,5},{7,6},{8,7},{9,8},{10,9},{11,1... | collective-permute-start | bytes 294920 | tf_op jit(solution)/shard_map/ppermute | solution.py:314
  10.7 5.2 %collective-permute-start = (bf16[24,96,128]{2,1,0:T(8,128)(2,1)}, bf16[24,96,128]{2,1,0:T(8,128)(2,1)S(1)}, u32[]{:S(2)}, u32[]{:S(2)}) collective-permute-start(bf16[24,96,128]{2,1,0:T(8,128)(2,1)} %get-tuple-element.30.high_first), channel_id=1, source_target_pairs={{0,16},{16,32},{32,48},{48,64},{64,80},{80,96},{96,112},{1,17},{17... | collective-permute-start | bytes 1769480 | tf_op jit(solution)/shard_map/ppermute | solution.py:314
  16.0 0.0 collective-permute-done.1.from_left
  16.0 0.0 copy-start.3
  16.0 0.0 collective-permute-done.2.from_right
  16.0 0.0 copy-start.5
  16.0 1.0 %pad_maximum_fusion.1 = bf16[12,96,128]{2,1,0:T(8,128)(2,1)S(1)} fusion(bf16[2,96,128]{2,1,0:T(8,128)(2,1)S(1)} %get-tuple-element.57, bf16[2,96,128]{2,1,0:T(8,128)(2,1)S(1)} %get-tuple-element.59, bf16[8,96,128]{2,1,0:T(8,128)(2,1)} %get-tuple-element.31.high_rest), kind=kLoop, calls=%fused_computation.1 | loop fusion | flops 294912 | bytes 589824 | tf_op jit(solution)/shard_map/concatenate | solution.py:356
  17.0 4.1 %collective-permute-start.3 = (bf16[12,96,128]{2,1,0:T(8,128)(2,1)S(1)}, bf16[12,96,128]{2,1,0:T(8,128)(2,1)S(1)}, u32[]{:S(2)}, u32[]{:S(2)}) collective-permute-start(bf16[12,96,128]{2,1,0:T(8,128)(2,1)S(1)} %pad_maximum_fusion.1), channel_id=1, source_target_pairs={{0,16},{16,32},{32,48},{48,64},{64,80},{80,96},{96,112},{1,17},{17... | collective-permute-start | bytes 884744 | tf_op jit(solution)/shard_map/ppermute | solution.py:314
  21.2 0.0 copy-done.3
  21.2 0.0 copy-done.5
  21.2 9.2 %shard_map.85 = (f32[3,3,32,128]{3,2,1,0:T(8,128)}, f32[8,128]{1,0:T(8,128)}, f32[2,2,16,96,128]{4,3,2,1,0:T(8,128)}, bf16[2,3,3,256,128]{4,3,2,1,0:T(8,128)(2,1)}) custom-call(bf16[32,96,128]{2,1,0:T(8,128)(2,1)} %get-tuple-element.34.low, bf16[24,96,128]{2,1,0:T(8,128)(2,1)} %get-tuple-element.30.high_first, ...), custom_call_target="tpu_custom_call" | custom-call | tf_op jit(solution)/shard_map/pallas_call | solution.py:27
  30.4 0.0 copy-start.4
  30.4 0.0 copy-start.6
  30.4 0.0 copy-start.7
  30.4 0.0 copy-start.8
  30.4 0.0 copy-done
  30.4 0.1 pad_maximum_fusion
  30.6 1.3 %collective-permute-start.12 = (bf16[36,96,128]{2,1,0:T(8,128)(2,1)S(1)}, bf16[36,96,128]{2,1,0:T(8,128)(2,1)}, u32[]{:S(2)}, u32[]{:S(2)}) collective-permute-start(bf16[36,96,128]{2,1,0:T(8,128)(2,1)S(1)} %pad_maximum_fusion), channel_id=1, source_target_pairs={{16,0},{32,16},{48,32},{64,48},{80,64},{96,80},{112,96},{17,1},{33... | collective-permute-start | bytes 2654216 | tf_op jit(solution)/shard_map/ppermute | solution.py:314
  31.9 2.1 %collective-permute-done.3.below_rest.refs_1_ = bf16[12,96,128]{2,1,0:T(8,128)(2,1)S(1)} collective-permute-done((bf16[12,96,128]{2,1,0:T(8,128)(2,1)S(1)}, bf16[12,96,128]{2,1,0:T(8,128)(2,1)S(1)}, u32[]{:S(2)}, u32[]{:S(2)}) %collective-permute-start.3) | collective-permute-done | bytes 294944 | tf_op jit(solution)/shard_map/ppermute | solution.py:314
  34.0 0.0 copy-start.2
  34.0 0.0 collective-permute-done.below_first.refs_0_
  34.0 0.0 copy-start.1
  34.0 0.0 copy-done.4
  34.0 0.0 copy-done.6
  34.1 0.0 copy-done.7
  34.1 0.0 copy-done.8
  34.1 1.5 %shard_map.86 = (f32[112,128]{1,0:T(8,128)S(1)}, f32[112,128]{1,0:T(8,128)S(1)}) custom-call(bf16[24,96,128]{2,1,0:T(8,128)(2,1)S(1)} %collective-permute-done.below_first.refs_0_, bf16[12,96,128]{2,1,0:T(8,128)(2,1)S(1)} %collective-permute-done.3.below_rest.refs_1_, bf16[32,96,128]{2,1,0:T(8,128)(2,1)S(1)} %copy-done, bf16[4,96,128]{2,1,0:T(8,128)(2,1)S(1)} %copy-done.4, ...), custom_call_target="tpu_custom_call" | custom-call | tf_op jit(solution)/shard_map/pallas_call | solution.py:18
  35.6 0.1 collective-permute-start.4
  35.7 1.2 %collective-permute-done.4 = f32[112,128]{1,0:T(8,128)S(1)} collective-permute-done((f32[112,128]{1,0:T(8,128)S(1)}, f32[112,128]{1,0:T(8,128)S(1)}, u32[]{:S(2)}, u32[]{:S(2)}) %collective-permute-start.4) | collective-permute-done | bytes 57376 | tf_op jit(solution)/shard_map/ppermute | solution.py:319
  36.9 4.1 %collective-permute-start.7 = (f32[112,128]{1,0:T(8,128)S(1)}, f32[112,128]{1,0:T(8,128)S(1)}, u32[]{:S(2)}, u32[]{:S(2)}) collective-permute-start(f32[112,128]{1,0:T(8,128)S(1)} %add.26), channel_id=1, source_target_pairs={{0,12},{1,13},{2,14},{3,15},{4,8},{5,9},{6,10},{7,11},{8,4},{9,5},... | collective-permute-start | bytes 172040 | tf_op jit(solution)/shard_map/ppermute | solution.py:319
  41.1 0.5 collective-permute-start.6
  41.6 0.2 collective-permute-start.5
  41.7 1.4 %collective-permute-done.7 = f32[112,128]{1,0:T(8,128)S(1)} collective-permute-done((f32[112,128]{1,0:T(8,128)S(1)}, f32[112,128]{1,0:T(8,128)S(1)}, u32[]{:S(2)}, u32[]{:S(2)}) %collective-permute-start.7) | collective-permute-done | bytes 57376 | tf_op jit(solution)/shard_map/ppermute | solution.py:319
  43.1 2.9 %collective-permute-done.6 = f32[112,128]{1,0:T(8,128)S(1)} collective-permute-done((f32[112,128]{1,0:T(8,128)S(1)}, f32[112,128]{1,0:T(8,128)S(1)}, u32[]{:S(2)}, u32[]{:S(2)}) %collective-permute-start.6) | collective-permute-done | bytes 57376 | tf_op jit(solution)/shard_map/ppermute | solution.py:319
  46.0 0.0 collective-permute-done.5
  46.0 4.3 %collective-permute-start.10 = (f32[112,128]{1,0:T(8,128)S(1)}, f32[112,128]{1,0:T(8,128)S(1)}, u32[]{:S(2)}, u32[]{:S(2)}) collective-permute-start(f32[112,128]{1,0:T(8,128)S(1)} %add_add_fusion.1), channel_id=1, source_target_pairs={{0,96},{1,97},{2,98},{3,99},{4,100},{5,101},{6,102},{7,103},{8,104... | collective-permute-start | bytes 172040 | tf_op jit(solution)/shard_map/ppermute | solution.py:319
  50.3 17.4 %collective-permute-start.9 = (f32[112,128]{1,0:T(8,128)S(1)}, f32[112,128]{1,0:T(8,128)S(1)}, u32[]{:S(2)}, u32[]{:S(2)}) collective-permute-start(f32[112,128]{1,0:T(8,128)S(1)} %add_add_fusion.1), channel_id=1, source_target_pairs={{0,64},{1,65},{2,66},{3,67},{4,68},{5,69},{6,70},{7,71},{8,72},{9,... | collective-permute-start | bytes 172040 | tf_op jit(solution)/shard_map/ppermute | solution.py:319
  67.7 0.0 collective-permute-start.8
  67.7 0.0 copy-done.2
  67.7 0.0 copy-done.1
  67.7 4.8 %shard_map.87 = (bf16[2,16,12288]{2,1,0:T(8,128)(2,1)}, bf16[2,16,12288]{2,1,0:T(8,128)(2,1)}) custom-call(bf16[24,96,128]{2,1,0:T(8,128)(2,1)} %copy-done.1, bf16[12,96,128]{2,1,0:T(8,128)(2,1)} %copy-done.2, bf16[2,3,3,256,128]{4,3,2,1,0:T(8,128)(2,1)} %get-tuple-element.41.refs_2_.refs_1_, f32[2,2,16,96,128]{4,3,2,1,0:T(8,128)} %get-tuple-element.42.refs_3_.refs_2_, ...), custom_call_target="tpu_custom_call" | custom-call | tf_op jit(solution)/shard_map/pallas_call | solution.py:27
  72.5 0.0 collective-permute-done.10
  72.6 0.0 collective-permute-done.9
  72.6 0.0 collective-permute-done.8
  72.6 2.3 %collective-permute-start.11 = (f32[112,128]{1,0:T(8,128)S(1)}, f32[112,128]{1,0:T(8,128)S(1)}, u32[]{:S(2)}, u32[]{:S(2)}) collective-permute-start(f32[112,128]{1,0:T(8,128)S(1)} %add_add_fusion.part), channel_id=1, source_target_pairs={{0,1},{1,0},{2,3},{3,2},{4,5},{5,4},{6,7},{7,6},{8,9},{9,8},{10,11... | collective-permute-start | bytes 172040 | tf_op jit(solution)/shard_map/ppermute | solution.py:319
  74.9 0.9 %collective-permute-done.11.other = f32[112,128]{1,0:T(8,128)S(1)} collective-permute-done((f32[112,128]{1,0:T(8,128)S(1)}, f32[112,128]{1,0:T(8,128)S(1)}, u32[]{:S(2)}, u32[]{:S(2)}) %collective-permute-start.11) | collective-permute-done | bytes 57376 | tf_op jit(solution)/shard_map/ppermute | solution.py:319
  75.8 0.0 collective-permute-done.12.refs_0_
  75.8 2.7 %collective-permute-start.15 = (f32[224,128]{1,0:T(8,128)S(1)}, f32[224,128]{1,0:T(8,128)S(1)}, u32[]{:S(2)}, u32[]{:S(2)}) collective-permute-start(f32[224,128]{1,0:T(8,128)S(1)} %shard_map.88.part), channel_id=1, source_target_pairs={{0,18},{1,19},{2,16},{3,17},{4,22},{5,23},{6,20},{7,21},{8,26},{9,... | collective-permute-start | bytes 344072 | tf_op jit(solution)/shard_map/ppermute | solution.py:319
  78.5 1.2 %collective-permute-start.14 = (f32[224,128]{1,0:T(8,128)S(1)}, f32[224,128]{1,0:T(8,128)S(1)}, u32[]{:S(2)}, u32[]{:S(2)}) collective-permute-start(f32[224,128]{1,0:T(8,128)S(1)} %shard_map.88.part), channel_id=1, source_target_pairs={{0,16},{1,17},{2,18},{3,19},{4,20},{5,21},{6,22},{7,23},{8,24},{9,... | collective-permute-start | bytes 344072 | tf_op jit(solution)/shard_map/ppermute | solution.py:319
  79.6 0.0 collective-permute-start.13
  79.6 4.8 %shard_map.89 = (bf16[2,16,12288]{2,1,0:T(8,128)(2,1)}, bf16[2,16,12288]{2,1,0:T(8,128)(2,1)}) custom-call(bf16[36,96,128]{2,1,0:T(8,128)(2,1)} %collective-permute-done.12.refs_0_, bf16[2,3,3,256,128]{4,3,2,1,0:T(8,128)(2,1)} %get-tuple-element.41.refs_2_.refs_1_, ...), custom_call_target="tpu_custom_call", output_to_operand_aliasing={{0}: (4, {}), {1}: (5, {})} | custom-call | tf_op jit(solution)/shard_map/pallas_call | solution.py:27
  84.5 0.0 collective-permute-done.15.three
  84.5 0.0 collective-permute-done.14.two
  84.5 0.3 collective-permute-done.13.one
  84.8 1.0 %shard_map.90 = (f32[864,32]{1,0:T(8,128)}, f32[1,32]{1,0:T(1,128)}) custom-call(f32[224,128]{1,0:T(8,128)S(1)} %shard_map.88.part, f32[224,128]{1,0:T(8,128)S(1)} %collective-permute-done.13.one, f32[224,128]{1,0:T(8,128)S(1)} %collective-permute-done.14.two, f32[224,128]{1,0:T(8,128)S(1)} %collective-permute-done.15.three), custom_call_target="tpu_custom_call" | custom-call | tf_op jit(solution)/shard_map/pallas_call | solution.py:18
  (7 shorter events, 0.1 us)
Async XLA Ops:
  3.7 26.7 %copy-start = (bf16[32,96,128]{2,1,0:T(8,128)(2,1)S(1)}, bf16[32,96,128]{2,1,0:T(8,128)(2,1)}, u32[]{:S(2)}) copy-start(bf16[32,96,128]{2,1,0:T(8,128)(2,1)} %get-tuple-element.34.low) | copy-start | bytes 2359300
  3.7 12.3 %collective-permute-start.1 = (bf16[4,96,128]{2,1,0:T(8,128)(2,1)}, bf16[4,96,128]{2,1,0:T(8,128)(2,1)S(1)}, u32[]{:S(2)}, u32[]{:S(2)}) collective-permute-start(bf16[4,96,128]{2,1,0:T(8,128)(2,1)} %get-tuple-element.32), channel_id=1, source_target_pairs={{0,1},{1,2},{2,3},{3,4},{4,5},{5,6},{6,7},{7,8},{8,9},{9,10},{10,1... | collective-permute-start | bytes 294920 | tf_op jit(solution)/shard_map/ppermute | solution.py:314
  8.8 7.2 %collective-permute-start.2 = (bf16[4,96,128]{2,1,0:T(8,128)(2,1)}, bf16[4,96,128]{2,1,0:T(8,128)(2,1)S(1)}, u32[]{:S(2)}, u32[]{:S(2)}) collective-permute-start(bf16[4,96,128]{2,1,0:T(8,128)(2,1)} %get-tuple-element.33), channel_id=1, source_target_pairs={{1,0},{2,1},{3,2},{4,3},{5,4},{6,5},{7,6},{8,7},{9,8},{10,9},{11,1... | collective-permute-start | bytes 294920 | tf_op jit(solution)/shard_map/ppermute | solution.py:314
  10.7 23.3 %collective-permute-start = (bf16[24,96,128]{2,1,0:T(8,128)(2,1)}, bf16[24,96,128]{2,1,0:T(8,128)(2,1)S(1)}, u32[]{:S(2)}, u32[]{:S(2)}) collective-permute-start(bf16[24,96,128]{2,1,0:T(8,128)(2,1)} %get-tuple-element.30.high_first), channel_id=1, source_target_pairs={{0,16},{16,32},{32,48},{48,64},{64,80},{80,96},{96,112},{1,17},{17... | collective-permute-start | bytes 1769480 | tf_op jit(solution)/shard_map/ppermute | solution.py:314
  16.0 5.2 %copy-start.3 = (bf16[4,96,128]{2,1,0:T(8,128)(2,1)}, bf16[4,96,128]{2,1,0:T(8,128)(2,1)S(1)}, u32[]{:S(2)}) copy-start(bf16[4,96,128]{2,1,0:T(8,128)(2,1)S(1)} %collective-permute-done.1.from_left) | copy-start | bytes 294916
  16.0 5.2 %copy-start.5 = (bf16[4,96,128]{2,1,0:T(8,128)(2,1)}, bf16[4,96,128]{2,1,0:T(8,128)(2,1)S(1)}, u32[]{:S(2)}) copy-start(bf16[4,96,128]{2,1,0:T(8,128)(2,1)S(1)} %collective-permute-done.2.from_right) | copy-start | bytes 294916
  17.0 17.0 %collective-permute-start.3 = (bf16[12,96,128]{2,1,0:T(8,128)(2,1)S(1)}, bf16[12,96,128]{2,1,0:T(8,128)(2,1)S(1)}, u32[]{:S(2)}, u32[]{:S(2)}) collective-permute-start(bf16[12,96,128]{2,1,0:T(8,128)(2,1)S(1)} %pad_maximum_fusion.1), channel_id=1, source_target_pairs={{0,16},{16,32},{32,48},{48,64},{64,80},{80,96},{96,112},{1,17},{17... | collective-permute-start | bytes 884744 | tf_op jit(solution)/shard_map/ppermute | solution.py:314
  30.4 3.6 %copy-start.4 = (bf16[4,96,128]{2,1,0:T(8,128)(2,1)S(1)}, bf16[4,96,128]{2,1,0:T(8,128)(2,1)}, u32[]{:S(2)}) copy-start(bf16[4,96,128]{2,1,0:T(8,128)(2,1)} %copy-done.3) | copy-start | bytes 294916
  30.4 3.6 %copy-start.6 = (bf16[4,96,128]{2,1,0:T(8,128)(2,1)S(1)}, bf16[4,96,128]{2,1,0:T(8,128)(2,1)}, u32[]{:S(2)}) copy-start(bf16[4,96,128]{2,1,0:T(8,128)(2,1)} %copy-done.5) | copy-start | bytes 294916
  30.4 3.6 %copy-start.7 = (f32[3,3,32,128]{3,2,1,0:T(8,128)S(1)}, f32[3,3,32,128]{3,2,1,0:T(8,128)}, u32[]{:S(2)}) copy-start(f32[3,3,32,128]{3,2,1,0:T(8,128)} %get-tuple-element.37.folded) | copy-start | bytes 442372
  30.4 3.6 %copy-start.8 = (f32[8,128]{1,0:T(8,128)S(1)}, f32[8,128]{1,0:T(8,128)}, u32[]{:S(2)}) copy-start(f32[8,128]{1,0:T(8,128)} %get-tuple-element.38.bias_terms) | copy-start | bytes 12292
  30.6 45.2 %collective-permute-start.12 = (bf16[36,96,128]{2,1,0:T(8,128)(2,1)S(1)}, bf16[36,96,128]{2,1,0:T(8,128)(2,1)}, u32[]{:S(2)}, u32[]{:S(2)}) collective-permute-start(bf16[36,96,128]{2,1,0:T(8,128)(2,1)S(1)} %pad_maximum_fusion), channel_id=1, source_target_pairs={{16,0},{32,16},{48,32},{64,48},{80,64},{96,80},{112,96},{17,1},{33... | collective-permute-start | bytes 2654216 | tf_op jit(solution)/shard_map/ppermute | solution.py:314
  34.0 33.7 %copy-start.2 = (bf16[12,96,128]{2,1,0:T(8,128)(2,1)}, bf16[12,96,128]{2,1,0:T(8,128)(2,1)S(1)}, u32[]{:S(2)}) copy-start(bf16[12,96,128]{2,1,0:T(8,128)(2,1)S(1)} %collective-permute-done.3.below_rest.refs_1_) | copy-start | bytes 884740
  34.0 33.7 %copy-start.1 = (bf16[24,96,128]{2,1,0:T(8,128)(2,1)}, bf16[24,96,128]{2,1,0:T(8,128)(2,1)S(1)}, u32[]{:S(2)}) copy-start(bf16[24,96,128]{2,1,0:T(8,128)(2,1)S(1)} %collective-permute-done.below_first.refs_0_) | copy-start | bytes 1769476
  35.6 1.3 %collective-permute-start.4 = (f32[112,128]{1,0:T(8,128)S(1)}, f32[112,128]{1,0:T(8,128)S(1)}, u32[]{:S(2)}, u32[]{:S(2)}) collective-permute-start(f32[112,128]{1,0:T(8,128)S(1)} %get-tuple-element.40), channel_id=1, source_target_pairs={{0,1},{1,0},{2,3},{3,2},{4,5},{5,4},{6,7},{7,6},{8,9},{9,8},{10,11... | collective-permute-start | bytes 172040 | tf_op jit(solution)/shard_map/ppermute | solution.py:319
  36.9 6.2 %collective-permute-start.7 = (f32[112,128]{1,0:T(8,128)S(1)}, f32[112,128]{1,0:T(8,128)S(1)}, u32[]{:S(2)}, u32[]{:S(2)}) collective-permute-start(f32[112,128]{1,0:T(8,128)S(1)} %add.26), channel_id=1, source_target_pairs={{0,12},{1,13},{2,14},{3,15},{4,8},{5,9},{6,10},{7,11},{8,4},{9,5},... | collective-permute-start | bytes 172040 | tf_op jit(solution)/shard_map/ppermute | solution.py:319
  41.1 4.9 %collective-permute-start.6 = (f32[112,128]{1,0:T(8,128)S(1)}, f32[112,128]{1,0:T(8,128)S(1)}, u32[]{:S(2)}, u32[]{:S(2)}) collective-permute-start(f32[112,128]{1,0:T(8,128)S(1)} %add.26), channel_id=1, source_target_pairs={{0,8},{1,9},{2,10},{3,11},{4,12},{5,13},{6,14},{7,15},{8,0},{9,1},... | collective-permute-start | bytes 172040 | tf_op jit(solution)/shard_map/ppermute | solution.py:319
  41.6 4.4 %collective-permute-start.5 = (f32[112,128]{1,0:T(8,128)S(1)}, f32[112,128]{1,0:T(8,128)S(1)}, u32[]{:S(2)}, u32[]{:S(2)}) collective-permute-start(f32[112,128]{1,0:T(8,128)S(1)} %add.26), channel_id=1, source_target_pairs={{0,4},{1,5},{2,6},{3,7},{4,0},{5,1},{6,2},{7,3},{8,12},{9,13},{10,... | collective-permute-start | bytes 172040 | tf_op jit(solution)/shard_map/ppermute | solution.py:319
  46.0 26.5 %collective-permute-start.10 = (f32[112,128]{1,0:T(8,128)S(1)}, f32[112,128]{1,0:T(8,128)S(1)}, u32[]{:S(2)}, u32[]{:S(2)}) collective-permute-start(f32[112,128]{1,0:T(8,128)S(1)} %add_add_fusion.1), channel_id=1, source_target_pairs={{0,96},{1,97},{2,98},{3,99},{4,100},{5,101},{6,102},{7,103},{8,104... | collective-permute-start | bytes 172040 | tf_op jit(solution)/shard_map/ppermute | solution.py:319
  50.3 22.3 %collective-permute-start.9 = (f32[112,128]{1,0:T(8,128)S(1)}, f32[112,128]{1,0:T(8,128)S(1)}, u32[]{:S(2)}, u32[]{:S(2)}) collective-permute-start(f32[112,128]{1,0:T(8,128)S(1)} %add_add_fusion.1), channel_id=1, source_target_pairs={{0,64},{1,65},{2,66},{3,67},{4,68},{5,69},{6,70},{7,71},{8,72},{9,... | collective-permute-start | bytes 172040 | tf_op jit(solution)/shard_map/ppermute | solution.py:319
  67.7 4.9 %collective-permute-start.8 = (f32[112,128]{1,0:T(8,128)S(1)}, f32[112,128]{1,0:T(8,128)S(1)}, u32[]{:S(2)}, u32[]{:S(2)}) collective-permute-start(f32[112,128]{1,0:T(8,128)S(1)} %add_add_fusion.1), channel_id=1, source_target_pairs={{0,32},{1,33},{2,34},{3,35},{4,36},{5,37},{6,38},{7,39},{8,40},{9,... | collective-permute-start | bytes 172040 | tf_op jit(solution)/shard_map/ppermute | solution.py:319
  72.6 3.2 %collective-permute-start.11 = (f32[112,128]{1,0:T(8,128)S(1)}, f32[112,128]{1,0:T(8,128)S(1)}, u32[]{:S(2)}, u32[]{:S(2)}) collective-permute-start(f32[112,128]{1,0:T(8,128)S(1)} %add_add_fusion.part), channel_id=1, source_target_pairs={{0,1},{1,0},{2,3},{3,2},{4,5},{5,4},{6,7},{7,6},{8,9},{9,8},{10,11... | collective-permute-start | bytes 172040 | tf_op jit(solution)/shard_map/ppermute | solution.py:319
  75.8 8.7 %collective-permute-start.15 = (f32[224,128]{1,0:T(8,128)S(1)}, f32[224,128]{1,0:T(8,128)S(1)}, u32[]{:S(2)}, u32[]{:S(2)}) collective-permute-start(f32[224,128]{1,0:T(8,128)S(1)} %shard_map.88.part), channel_id=1, source_target_pairs={{0,18},{1,19},{2,16},{3,17},{4,22},{5,23},{6,20},{7,21},{8,26},{9,... | collective-permute-start | bytes 344072 | tf_op jit(solution)/shard_map/ppermute | solution.py:319
  78.5 6.0 %collective-permute-start.14 = (f32[224,128]{1,0:T(8,128)S(1)}, f32[224,128]{1,0:T(8,128)S(1)}, u32[]{:S(2)}, u32[]{:S(2)}) collective-permute-start(f32[224,128]{1,0:T(8,128)S(1)} %shard_map.88.part), channel_id=1, source_target_pairs={{0,16},{1,17},{2,18},{3,19},{4,20},{5,21},{6,22},{7,23},{8,24},{9,... | collective-permute-start | bytes 344072 | tf_op jit(solution)/shard_map/ppermute | solution.py:319
  79.6 5.1 %collective-permute-start.13 = (f32[224,128]{1,0:T(8,128)S(1)}, f32[224,128]{1,0:T(8,128)S(1)}, u32[]{:S(2)}, u32[]{:S(2)}) collective-permute-start(f32[224,128]{1,0:T(8,128)S(1)} %shard_map.88.part), channel_id=1, source_target_pairs={{0,2},{1,3},{2,0},{3,1},{4,6},{5,7},{6,4},{7,5},{8,10},{9,11},{10,... | collective-permute-start | bytes 344072 | tf_op jit(solution)/shard_map/ppermute | solution.py:319

commit v9 on v4

--- a/solution.py
+++ b/solution.py
@@ -251,9 +251,12 @@
     return total
 
 
-def outer_body(first, rest, weights_f, weights_g, partial_f, partial_g, line, *more):
-    output, grad_input, taps, scratch, grad = more[-5:]
+def outer_body(count, *refs):
+    first, rest = refs[0], refs[count - 1]
+    weights_f, weights_g, partial_f, partial_g, line = refs[count : count + 5]
+    output, grad_input, taps, scratch, grad = refs[-5:]
     rows, groups = partial_f.shape[1:3]
+    repeated = jnp.concatenate([line[...]] * 4, axis=1)
     act, edge = first.at[:rows], rest.at[rest.shape[0] - 4 :]
     gather_grad(first, rest, grad)
     for kind, (source, weights, partial, out, turn) in enumerate(
@@ -270,12 +273,12 @@
                 at = start + tap_y
                 lhs = taps[kind, at : at + CHUNK].reshape(CHUNK * groups, 256)
                 total = total + jnp.dot(lhs, weights[0, tap_y], preferred_element_type=F32)
-            put_rows(scratch, turn(total, line), chunk, groups)
+            put_rows(scratch, turn(total, repeated), chunk, groups)
         lay_out(scratch, out, 0, rows, groups)
 
 
 def rectified(total, line):
-    return jnp.maximum(total + line[...], 0.0)
+    return jnp.maximum(total + line, 0.0)
 
 
 def kept(total, line):
@@ -364,7 +367,7 @@
     below_first = shifted(high_first, "gz", 1)
     below_rest = shifted(jnp.concatenate([high_rest, from_left[2:], from_right[2:]]), "gz", 1)
 
-    line = jnp.tile(bias, 4).reshape(1, LANES)
+    line = bias.reshape(1, 32)
     flat_kernel = kernel.reshape(27 * 32, 32)
     chunks = rows // CHUNK
     plane = (rows, groups, LANES)
@@ -390,21 +393,21 @@
         [part_of(array.shape, 0, 0, 0) for array in (low, high_first, high_rest)] + [part_of(lines.shape, 0, 0, 0)] * 2 + [part_of(flat_kernel.shape, 0, 0)],
     )
 
-    def outer(side, first, rest, done=()):
+    def outer(side, beside, done=()):
         weights, partial = part_of((1, 3, 256, LANES), 2 * side, 0, 0, 0), part_of((1, *plane), side, 0, 0, 0)
         return blocked(
-            outer_body,
+            functools.partial(outer_body, len(beside)),
             1,
             (shape(block, BF16), shape(block, BF16)),
             (part_of((1, *block[1:]), side, 0, 0),) * 2,
             [two_taps, spread, one_plane],
-            (first, rest, weights_f, weights_g, partial_f, partial_g, line, *done),
+            (*beside, weights_f, weights_g, partial_f, partial_g, line, *done),
             [
-                part_of(first.shape, 0, 0, 0), part_of(rest.shape, 0, 0, 0),
-                weights, weights, partial, partial, part_of((1, LANES), 0, 0),
+                *[part_of(array.shape, 0, 0, 0) for array in beside],
+                weights, weights, partial, partial, part_of(line.shape, 0, 0),
                 *[pl.BlockSpec(memory_space=pl.ANY)] * len(done),
             ],
-            {7: 0, 8: 1} if done else None,
+            {len(beside) + 5: 0, len(beside) + 6: 1} if done else None,
         )
 
     ends = (from_left[:2], from_right[:2])
@@ -421,12 +424,12 @@
     part = part + swapped(send, 1)
     part = sum_of_four(part, 4, 8)
     part = sum_of_four(part, 32, 64)
-    results = outer(0, below_first, below_rest)
+    results = outer(0, (below_first, below_rest))
     part, results = lax.optimization_barrier((part, results))
     part = call(join_body, shape((2 * HALF, LANES), F32), [], (part, swapped(part, 1), flag))
     part, above = lax.optimization_barrier((part, above))
     others = [swapped(part, bit) for bit in (2, 16, 18)]
-    results = outer(1, above, above, results)
+    results = outer(1, (above,), results)
 
     voxels = planes * lax.axis_size("gz") * rows * lax.axis_size("gy") * (width // 32)
     grad_kernel, grad_bias = call(

time: 72.3 us -> 71.1 us (0.983)
  the two profiles are of different devices: /device:TPU:1 before, /device:TPU:10 now
where the time goes in v9:
time: 71.1 us; the launch traced here: 70.7 us
  starting transfers between devices  33.3 us (47%)
  Pallas kernels  26.1 us (37%)
  waiting for transfers between devices  9.21 us (13%)
  other arithmetic  1.15 us (2%)
  between operations  0.9 us (1%)
    ppermute x5, starting transfers between devices, shifted(): return lax.ppermute(value, axis, pairs)  20.6 us
    pallas_call x3, Pallas kernels, blocked(): pl.pallas_call(body, grid=(grid,), out_shape=outs, in_specs=in_specs, out...  20.5 us
    ppermute x11, starting transfers between devices, swapped(): lax.ppermute(value, ('gz', 'gy'), [(i, i ^ bit) for i in range(count)])  12.7 us
    ppermute x11, waiting for transfers between devices, swapped(): lax.ppermute(value, ('gz', 'gy'), [(i, i ^ bit) for i in range(count)])  9.02 us
    pallas_call x1, Pallas kernels, local(): pl.pallas_call(group_body, in_specs=[pl.BlockSpec(memory_space=pl.ANY)] *...  3.06 us
    pallas_call x3, Pallas kernels, call(): pl.pallas_call(body, out_shape=outs, scratch_shapes=scratch, compiler_par...  2.52 us
  transfers between devices with their start and end apart: 16, of which 8 were waited for; matrix products, arithmetic and copies ran while one was open for 2% of the time, Pallas kernels for 31%

profile of v9, /device:TPU:10, one launch (start us, length us, event | category | flops | bytes accessed | tf_op | source)
XLA Modules:
  0.0 70.7 jit_solution(7225739748036716647)
XLA Ops:
  0.6 3.1 %shard_map.84 = (bf16[32,96,128]{2,1,0:T(8,128)(2,1)}, bf16[24,96,128]{2,1,0:T(8,128)(2,1)}, bf16[8,96,128]{2,1,0:T(8,128)(2,1)}, bf16[4,96,128]{2,1,0:T(8,128)(2,1)}, bf16[4,96,128]{2,1,0:T(8,128)(2,1)}) custom-call(bf16[2,16,12288]{2,1,0:T(8,128)(2,1)} %act_in.1, bf16[2,16,12288]{2,1,0:T(8,128)(2,1)} %grad_in.1, s32[2,16,12288]{2,1,0:T(8,128)} %mask_in.1), custom_call_target="tpu_custom_call" | custom-call | tf_op jit(solution)/shard_map/pallas_call | solution.py:353
  3.7 0.0 copy-start
  3.7 2.1 %collective-permute-start.1 = (bf16[4,96,128]{2,1,0:T(8,128)(2,1)}, bf16[4,96,128]{2,1,0:T(8,128)(2,1)S(1)}, u32[]{:S(2)}, u32[]{:S(2)}) collective-permute-start(bf16[4,96,128]{2,1,0:T(8,128)(2,1)} %get-tuple-element.34), channel_id=1, source_target_pairs={{0,1},{1,2},{2,3},{3,4},{4,5},{5,6},{6,7},{7,8},{8,9},{9,10},{10,1... | collective-permute-start | bytes 294920 | tf_op jit(solution)/shard_map/ppermute | solution.py:326
  5.8 4.5 %collective-permute-start.2 = (bf16[4,96,128]{2,1,0:T(8,128)(2,1)}, bf16[4,96,128]{2,1,0:T(8,128)(2,1)S(1)}, u32[]{:S(2)}, u32[]{:S(2)}) collective-permute-start(bf16[4,96,128]{2,1,0:T(8,128)(2,1)} %get-tuple-element.35), channel_id=1, source_target_pairs={{1,0},{2,1},{3,2},{4,3},{5,4},{6,5},{7,6},{8,7},{9,8},{10,9},{11,1... | collective-permute-start | bytes 294920 | tf_op jit(solution)/shard_map/ppermute | solution.py:326
  10.3 5.8 %collective-permute-start = (bf16[24,96,128]{2,1,0:T(8,128)(2,1)}, bf16[24,96,128]{2,1,0:T(8,128)(2,1)S(1)}, u32[]{:S(2)}, u32[]{:S(2)}) collective-permute-start(bf16[24,96,128]{2,1,0:T(8,128)(2,1)} %get-tuple-element.32.high_first), channel_id=1, source_target_pairs={{0,16},{16,32},{32,48},{48,64},{64,80},{80,96},{96,112},{1,17},{17... | collective-permute-start | bytes 1769480 | tf_op jit(solution)/shard_map/ppermute | solution.py:326
  16.1 0.0 collective-permute-done.1.from_left
  16.1 0.0 copy-start.3
  16.1 0.0 collective-permute-done.2.from_right
  16.2 0.0 copy-start.5
  16.2 1.0 %pad_maximum_fusion.1 = bf16[12,96,128]{2,1,0:T(8,128)(2,1)S(1)} fusion(bf16[2,96,128]{2,1,0:T(8,128)(2,1)S(1)} %get-tuple-element.61, bf16[2,96,128]{2,1,0:T(8,128)(2,1)S(1)} %get-tuple-element.63, bf16[8,96,128]{2,1,0:T(8,128)(2,1)} %get-tuple-element.33.high_rest), kind=kLoop, calls=%fused_computation.1 | loop fusion | flops 294912 | bytes 589824 | tf_op jit(solution)/shard_map/concatenate | solution.py:368
  17.2 2.6 %collective-permute-start.3 = (bf16[12,96,128]{2,1,0:T(8,128)(2,1)S(1)}, bf16[12,96,128]{2,1,0:T(8,128)(2,1)S(1)}, u32[]{:S(2)}, u32[]{:S(2)}) collective-permute-start(bf16[12,96,128]{2,1,0:T(8,128)(2,1)S(1)} %pad_maximum_fusion.1), channel_id=1, source_target_pairs={{0,16},{16,32},{32,48},{48,64},{64,80},{80,96},{96,112},{1,17},{17... | collective-permute-start | bytes 884744 | tf_op jit(solution)/shard_map/ppermute | solution.py:326
  19.8 0.0 copy-done.3
  19.8 0.0 copy-done.5
  19.8 11.0 %shard_map.85 = (f32[3,3,32,128]{3,2,1,0:T(8,128)}, f32[8,128]{1,0:T(8,128)}, f32[2,16,96,128]{3,2,1,0:T(8,128)}, bf16[3,3,256,128]{3,2,1,0:T(8,128)(2,1)}, f32[...) custom-call(bf16[32,96,128]{2,1,0:T(8,128)(2,1)} %get-tuple-element.36.low, ...), custom_call_target="tpu_custom_call" | custom-call | tf_op jit(solution)/shard_map/pallas_call | solution.py:27
  30.8 0.0 copy-start.4
  30.8 0.0 copy-start.6
  30.8 0.0 copy-start.7
  30.8 0.0 copy-start.8
  30.8 0.0 copy-done
  30.8 0.1 pad_maximum_fusion
  31.0 5.7 %collective-permute-start.12 = (bf16[36,96,128]{2,1,0:T(8,128)(2,1)S(1)}, bf16[36,96,128]{2,1,0:T(8,128)(2,1)}, u32[]{:S(2)}, u32[]{:S(2)}) collective-permute-start(bf16[36,96,128]{2,1,0:T(8,128)(2,1)S(1)} %pad_maximum_fusion), channel_id=1, source_target_pairs={{16,0},{32,16},{48,32},{64,48},{80,64},{96,80},{112,96},{17,1},{33... | collective-permute-start | bytes 2654216 | tf_op jit(solution)/shard_map/ppermute | solution.py:326
  36.6 0.2 collective-permute-done.3.below_rest.refs_1_
  36.8 0.0 copy-start.2
  36.8 0.0 collective-permute-done.below_first.refs_0_
  36.8 0.0 copy-start.1
  36.8 0.0 copy-done.4
  36.9 0.0 copy-done.6
  36.9 0.0 copy-done.7
  36.9 0.0 copy-done.8
  36.9 1.5 %shard_map.86 = (f32[112,128]{1,0:T(8,128)S(1)}, f32[112,128]{1,0:T(8,128)S(1)}) custom-call(bf16[24,96,128]{2,1,0:T(8,128)(2,1)S(1)} %collective-permute-done.below_first.refs_0_, bf16[12,96,128]{2,1,0:T(8,128)(2,1)S(1)} %collective-permute-done.3.below_rest.refs_1_, bf16[32,96,128]{2,1,0:T(8,128)(2,1)S(1)} %copy-done, bf16[4,96,128]{2,1,0:T(8,128)(2,1)S(1)} %copy-done.4, ...), custom_call_target="tpu_custom_call" | custom-call | tf_op jit(solution)/shard_map/pallas_call | solution.py:18
  38.4 0.1 collective-permute-start.4
  38.5 1.2 %collective-permute-done.4 = f32[112,128]{1,0:T(8,128)S(1)} collective-permute-done((f32[112,128]{1,0:T(8,128)S(1)}, f32[112,128]{1,0:T(8,128)S(1)}, u32[]{:S(2)}, u32[]{:S(2)}) %collective-permute-start.4) | collective-permute-done | bytes 57376 | tf_op jit(solution)/shard_map/ppermute | solution.py:331
  39.8 1.4 %collective-permute-start.7 = (f32[112,128]{1,0:T(8,128)S(1)}, f32[112,128]{1,0:T(8,128)S(1)}, u32[]{:S(2)}, u32[]{:S(2)}) collective-permute-start(f32[112,128]{1,0:T(8,128)S(1)} %add.26), channel_id=1, source_target_pairs={{0,12},{1,13},{2,14},{3,15},{4,8},{5,9},{6,10},{7,11},{8,4},{9,5},... | collective-permute-start | bytes 172040 | tf_op jit(solution)/shard_map/ppermute | solution.py:331
  41.2 0.7 %collective-permute-start.6 = (f32[112,128]{1,0:T(8,128)S(1)}, f32[112,128]{1,0:T(8,128)S(1)}, u32[]{:S(2)}, u32[]{:S(2)}) collective-permute-start(f32[112,128]{1,0:T(8,128)S(1)} %add.26), channel_id=1, source_target_pairs={{0,8},{1,9},{2,10},{3,11},{4,12},{5,13},{6,14},{7,15},{8,0},{9,1},... | collective-permute-start | bytes 172040 | tf_op jit(solution)/shard_map/ppermute | solution.py:331
  41.9 2.0 %collective-permute-start.5 = (f32[112,128]{1,0:T(8,128)S(1)}, f32[112,128]{1,0:T(8,128)S(1)}, u32[]{:S(2)}, u32[]{:S(2)}) collective-permute-start(f32[112,128]{1,0:T(8,128)S(1)} %add.26), channel_id=1, source_target_pairs={{0,4},{1,5},{2,6},{3,7},{4,0},{5,1},{6,2},{7,3},{8,12},{9,13},{10,... | collective-permute-start | bytes 172040 | tf_op jit(solution)/shard_map/ppermute | solution.py:331
  43.9 0.1 collective-permute-done.7
  44.0 3.2 %collective-permute-done.6 = f32[112,128]{1,0:T(8,128)S(1)} collective-permute-done((f32[112,128]{1,0:T(8,128)S(1)}, f32[112,128]{1,0:T(8,128)S(1)}, u32[]{:S(2)}, u32[]{:S(2)}) %collective-permute-start.6) | collective-permute-done | bytes 57376 | tf_op jit(solution)/shard_map/ppermute | solution.py:331
  47.3 0.0 collective-permute-done.5
  47.3 1.7 %collective-permute-start.10 = (f32[112,128]{1,0:T(8,128)S(1)}, f32[112,128]{1,0:T(8,128)S(1)}, u32[]{:S(2)}, u32[]{:S(2)}) collective-permute-start(f32[112,128]{1,0:T(8,128)S(1)} %add_add_fusion.1), channel_id=1, source_target_pairs={{0,96},{1,97},{2,98},{3,99},{4,100},{5,101},{6,102},{7,103},{8,104... | collective-permute-start | bytes 172040 | tf_op jit(solution)/shard_map/ppermute | solution.py:331
  49.0 0.8 %collective-permute-start.9 = (f32[112,128]{1,0:T(8,128)S(1)}, f32[112,128]{1,0:T(8,128)S(1)}, u32[]{:S(2)}, u32[]{:S(2)}) collective-permute-start(f32[112,128]{1,0:T(8,128)S(1)} %add_add_fusion.1), channel_id=1, source_target_pairs={{0,64},{1,65},{2,66},{3,67},{4,68},{5,69},{6,70},{7,71},{8,72},{9,... | collective-permute-start | bytes 172040 | tf_op jit(solution)/shard_map/ppermute | solution.py:331
  49.8 1.7 %collective-permute-start.8 = (f32[112,128]{1,0:T(8,128)S(1)}, f32[112,128]{1,0:T(8,128)S(1)}, u32[]{:S(2)}, u32[]{:S(2)}) collective-permute-start(f32[112,128]{1,0:T(8,128)S(1)} %add_add_fusion.1), channel_id=1, source_target_pairs={{0,32},{1,33},{2,34},{3,35},{4,36},{5,37},{6,38},{7,39},{8,40},{9,... | collective-permute-start | bytes 172040 | tf_op jit(solution)/shard_map/ppermute | solution.py:331
  51.5 0.0 copy-done.2
  51.5 0.0 copy-done.1
  51.5 4.7 %shard_map.87 = (bf16[2,16,12288]{2,1,0:T(8,128)(2,1)}, bf16[2,16,12288]{2,1,0:T(8,128)(2,1)}) custom-call(bf16[24,96,128]{2,1,0:T(8,128)(2,1)} %copy-done.1, bf16[12,96,128]{2,1,0:T(8,128)(2,1)} %copy-done.2, bf16[3,3,256,128]{3,2,1,0:T(8,128)(2,1)} %get-tuple-element.43.refs_2_.refs_1_, bf16[3,3,256,128]{3,2,1,0:T(8,128)(2,1)} %get-tuple-element.44.refs_3_.refs_2_, ...), custom_call_target="tpu_custom_call" | custom-call | tf_op jit(solution)/shard_map/pallas_call | solution.py:27
  56.2 1.9 %collective-permute-done.10 = f32[112,128]{1,0:T(8,128)S(1)} collective-permute-done((f32[112,128]{1,0:T(8,128)S(1)}, f32[112,128]{1,0:T(8,128)S(1)}, u32[]{:S(2)}, u32[]{:S(2)}) %collective-permute-start.10) | collective-permute-done | bytes 57376 | tf_op jit(solution)/shard_map/ppermute | solution.py:331
  58.1 0.7 %collective-permute-done.9 = f32[112,128]{1,0:T(8,128)S(1)} collective-permute-done((f32[112,128]{1,0:T(8,128)S(1)}, f32[112,128]{1,0:T(8,128)S(1)}, u32[]{:S(2)}, u32[]{:S(2)}) %collective-permute-start.9) | collective-permute-done | bytes 57376 | tf_op jit(solution)/shard_map/ppermute | solution.py:331
  58.8 0.0 collective-permute-done.8
  58.8 0.1 collective-permute-start.11
  58.9 1.2 %collective-permute-done.11.other = f32[112,128]{1,0:T(8,128)S(1)} collective-permute-done((f32[112,128]{1,0:T(8,128)S(1)}, f32[112,128]{1,0:T(8,128)S(1)}, u32[]{:S(2)}, u32[]{:S(2)}) %collective-permute-start.11) | collective-permute-done | bytes 57376 | tf_op jit(solution)/shard_map/ppermute | solution.py:331
  60.2 0.0 collective-permute-done.12.refs_0_
  60.2 0.6 collective-permute-start.15
  60.8 2.8 %collective-permute-start.14 = (f32[224,128]{1,0:T(8,128)S(1)}, f32[224,128]{1,0:T(8,128)S(1)}, u32[]{:S(2)}, u32[]{:S(2)}) collective-permute-start(f32[224,128]{1,0:T(8,128)S(1)} %shard_map.88.part), channel_id=1, source_target_pairs={{0,16},{1,17},{2,18},{3,19},{4,20},{5,21},{6,22},{7,23},{8,24},{9,... | collective-permute-start | bytes 344072 | tf_op jit(solution)/shard_map/ppermute | solution.py:331
  63.6 0.8 %collective-permute-start.13 = (f32[224,128]{1,0:T(8,128)S(1)}, f32[224,128]{1,0:T(8,128)S(1)}, u32[]{:S(2)}, u32[]{:S(2)}) collective-permute-start(f32[224,128]{1,0:T(8,128)S(1)} %shard_map.88.part), channel_id=1, source_target_pairs={{0,2},{1,3},{2,0},{3,1},{4,6},{5,7},{6,4},{7,5},{8,10},{9,11},{10,... | collective-permute-start | bytes 344072 | tf_op jit(solution)/shard_map/ppermute | solution.py:331
  64.4 4.7 %shard_map.89 = (bf16[2,16,12288]{2,1,0:T(8,128)(2,1)}, bf16[2,16,12288]{2,1,0:T(8,128)(2,1)}) custom-call(bf16[36,96,128]{2,1,0:T(8,128)(2,1)} %collective-permute-done.12.refs_0_, bf16[3,3,256,128]{3,2,1,0:T(8,128)(2,1)} %get-tuple-element.43.refs_2_.refs_1_, ...), custom_call_target="tpu_custom_call", output_to_operand_aliasing={{0}: (6, {}), {1}: (7, {})} | custom-call | tf_op jit(solution)/shard_map/pallas_call | solution.py:27
  69.1 0.0 collective-permute-done.15.three
  69.2 0.0 collective-permute-done.14.two
  69.2 0.6 collective-permute-done.13.one
  69.7 1.0 %shard_map.90 = (f32[864,32]{1,0:T(8,128)}, f32[1,32]{1,0:T(1,128)}) custom-call(f32[224,128]{1,0:T(8,128)S(1)} %shard_map.88.part, f32[224,128]{1,0:T(8,128)S(1)} %collective-permute-done.13.one, f32[224,128]{1,0:T(8,128)S(1)} %collective-permute-done.14.two, f32[224,128]{1,0:T(8,128)S(1)} %collective-permute-done.15.three), custom_call_target="tpu_custom_call" | custom-call | tf_op jit(solution)/shard_map/pallas_call | solution.py:18
  (7 shorter events, 0.1 us)
Async XLA Ops:
  3.7 27.1 %copy-start = (bf16[32,96,128]{2,1,0:T(8,128)(2,1)S(1)}, bf16[32,96,128]{2,1,0:T(8,128)(2,1)}, u32[]{:S(2)}) copy-start(bf16[32,96,128]{2,1,0:T(8,128)(2,1)} %get-tuple-element.36.low) | copy-start | bytes 2359300
  3.7 12.4 %collective-permute-start.1 = (bf16[4,96,128]{2,1,0:T(8,128)(2,1)}, bf16[4,96,128]{2,1,0:T(8,128)(2,1)S(1)}, u32[]{:S(2)}, u32[]{:S(2)}) collective-permute-start(bf16[4,96,128]{2,1,0:T(8,128)(2,1)} %get-tuple-element.34), channel_id=1, source_target_pairs={{0,1},{1,2},{2,3},{3,4},{4,5},{5,6},{6,7},{7,8},{8,9},{9,10},{10,1... | collective-permute-start | bytes 294920 | tf_op jit(solution)/shard_map/ppermute | solution.py:326
  5.8 10.4 %collective-permute-start.2 = (bf16[4,96,128]{2,1,0:T(8,128)(2,1)}, bf16[4,96,128]{2,1,0:T(8,128)(2,1)S(1)}, u32[]{:S(2)}, u32[]{:S(2)}) collective-permute-start(bf16[4,96,128]{2,1,0:T(8,128)(2,1)} %get-tuple-element.35), channel_id=1, source_target_pairs={{1,0},{2,1},{3,2},{4,3},{5,4},{6,5},{7,6},{8,7},{9,8},{10,9},{11,1... | collective-permute-start | bytes 294920 | tf_op jit(solution)/shard_map/ppermute | solution.py:326
  10.3 26.5 %collective-permute-start = (bf16[24,96,128]{2,1,0:T(8,128)(2,1)}, bf16[24,96,128]{2,1,0:T(8,128)(2,1)S(1)}, u32[]{:S(2)}, u32[]{:S(2)}) collective-permute-start(bf16[24,96,128]{2,1,0:T(8,128)(2,1)} %get-tuple-element.32.high_first), channel_id=1, source_target_pairs={{0,16},{16,32},{32,48},{48,64},{64,80},{80,96},{96,112},{1,17},{17... | collective-permute-start | bytes 1769480 | tf_op jit(solution)/shard_map/ppermute | solution.py:326
  16.1 3.6 %copy-start.3 = (bf16[4,96,128]{2,1,0:T(8,128)(2,1)}, bf16[4,96,128]{2,1,0:T(8,128)(2,1)S(1)}, u32[]{:S(2)}) copy-start(bf16[4,96,128]{2,1,0:T(8,128)(2,1)S(1)} %collective-permute-done.1.from_left) | copy-start | bytes 294916
  16.2 3.6 %copy-start.5 = (bf16[4,96,128]{2,1,0:T(8,128)(2,1)}, bf16[4,96,128]{2,1,0:T(8,128)(2,1)S(1)}, u32[]{:S(2)}) copy-start(bf16[4,96,128]{2,1,0:T(8,128)(2,1)S(1)} %collective-permute-done.2.from_right) | copy-start | bytes 294916
  17.2 19.6 %collective-permute-start.3 = (bf16[12,96,128]{2,1,0:T(8,128)(2,1)S(1)}, bf16[12,96,128]{2,1,0:T(8,128)(2,1)S(1)}, u32[]{:S(2)}, u32[]{:S(2)}) collective-permute-start(bf16[12,96,128]{2,1,0:T(8,128)(2,1)S(1)} %pad_maximum_fusion.1), channel_id=1, source_target_pairs={{0,16},{16,32},{32,48},{48,64},{64,80},{80,96},{96,112},{1,17},{17... | collective-permute-start | bytes 884744 | tf_op jit(solution)/shard_map/ppermute | solution.py:326
  30.8 6.1 %copy-start.4 = (bf16[4,96,128]{2,1,0:T(8,128)(2,1)S(1)}, bf16[4,96,128]{2,1,0:T(8,128)(2,1)}, u32[]{:S(2)}) copy-start(bf16[4,96,128]{2,1,0:T(8,128)(2,1)} %copy-done.3) | copy-start | bytes 294916
  30.8 6.1 %copy-start.6 = (bf16[4,96,128]{2,1,0:T(8,128)(2,1)S(1)}, bf16[4,96,128]{2,1,0:T(8,128)(2,1)}, u32[]{:S(2)}) copy-start(bf16[4,96,128]{2,1,0:T(8,128)(2,1)} %copy-done.5) | copy-start | bytes 294916
  30.8 6.1 %copy-start.7 = (f32[3,3,32,128]{3,2,1,0:T(8,128)S(1)}, f32[3,3,32,128]{3,2,1,0:T(8,128)}, u32[]{:S(2)}) copy-start(f32[3,3,32,128]{3,2,1,0:T(8,128)} %get-tuple-element.39.folded) | copy-start | bytes 442372
  30.8 6.1 %copy-start.8 = (f32[8,128]{1,0:T(8,128)S(1)}, f32[8,128]{1,0:T(8,128)}, u32[]{:S(2)}) copy-start(f32[8,128]{1,0:T(8,128)} %get-tuple-element.40.bias_terms) | copy-start | bytes 12292
  31.0 29.2 %collective-permute-start.12 = (bf16[36,96,128]{2,1,0:T(8,128)(2,1)S(1)}, bf16[36,96,128]{2,1,0:T(8,128)(2,1)}, u32[]{:S(2)}, u32[]{:S(2)}) collective-permute-start(bf16[36,96,128]{2,1,0:T(8,128)(2,1)S(1)} %pad_maximum_fusion), channel_id=1, source_target_pairs={{16,0},{32,16},{48,32},{64,48},{80,64},{96,80},{112,96},{17,1},{33... | collective-permute-start | bytes 2654216 | tf_op jit(solution)/shard_map/ppermute | solution.py:326
  36.8 14.6 %copy-start.2 = (bf16[12,96,128]{2,1,0:T(8,128)(2,1)}, bf16[12,96,128]{2,1,0:T(8,128)(2,1)S(1)}, u32[]{:S(2)}) copy-start(bf16[12,96,128]{2,1,0:T(8,128)(2,1)S(1)} %collective-permute-done.3.below_rest.refs_1_) | copy-start | bytes 884740
  36.8 14.6 %copy-start.1 = (bf16[24,96,128]{2,1,0:T(8,128)(2,1)}, bf16[24,96,128]{2,1,0:T(8,128)(2,1)S(1)}, u32[]{:S(2)}) copy-start(bf16[24,96,128]{2,1,0:T(8,128)(2,1)S(1)} %collective-permute-done.below_first.refs_0_) | copy-start | bytes 1769476
  38.4 1.3 %collective-permute-start.4 = (f32[112,128]{1,0:T(8,128)S(1)}, f32[112,128]{1,0:T(8,128)S(1)}, u32[]{:S(2)}, u32[]{:S(2)}) collective-permute-start(f32[112,128]{1,0:T(8,128)S(1)} %get-tuple-element.42), channel_id=1, source_target_pairs={{0,1},{1,0},{2,3},{3,2},{4,5},{5,4},{6,7},{7,6},{8,9},{9,8},{10,11... | collective-permute-start | bytes 172040 | tf_op jit(solution)/shard_map/ppermute | solution.py:331
  39.8 4.3 %collective-permute-start.7 = (f32[112,128]{1,0:T(8,128)S(1)}, f32[112,128]{1,0:T(8,128)S(1)}, u32[]{:S(2)}, u32[]{:S(2)}) collective-permute-start(f32[112,128]{1,0:T(8,128)S(1)} %add.26), channel_id=1, source_target_pairs={{0,12},{1,13},{2,14},{3,15},{4,8},{5,9},{6,10},{7,11},{8,4},{9,5},... | collective-permute-start | bytes 172040 | tf_op jit(solution)/shard_map/ppermute | solution.py:331
  41.2 6.1 %collective-permute-start.6 = (f32[112,128]{1,0:T(8,128)S(1)}, f32[112,128]{1,0:T(8,128)S(1)}, u32[]{:S(2)}, u32[]{:S(2)}) collective-permute-start(f32[112,128]{1,0:T(8,128)S(1)} %add.26), channel_id=1, source_target_pairs={{0,8},{1,9},{2,10},{3,11},{4,12},{5,13},{6,14},{7,15},{8,0},{9,1},... | collective-permute-start | bytes 172040 | tf_op jit(solution)/shard_map/ppermute | solution.py:331
  41.9 5.4 %collective-permute-start.5 = (f32[112,128]{1,0:T(8,128)S(1)}, f32[112,128]{1,0:T(8,128)S(1)}, u32[]{:S(2)}, u32[]{:S(2)}) collective-permute-start(f32[112,128]{1,0:T(8,128)S(1)} %add.26), channel_id=1, source_target_pairs={{0,4},{1,5},{2,6},{3,7},{4,0},{5,1},{6,2},{7,3},{8,12},{9,13},{10,... | collective-permute-start | bytes 172040 | tf_op jit(solution)/shard_map/ppermute | solution.py:331
  47.3 10.8 %collective-permute-start.10 = (f32[112,128]{1,0:T(8,128)S(1)}, f32[112,128]{1,0:T(8,128)S(1)}, u32[]{:S(2)}, u32[]{:S(2)}) collective-permute-start(f32[112,128]{1,0:T(8,128)S(1)} %add_add_fusion.1), channel_id=1, source_target_pairs={{0,96},{1,97},{2,98},{3,99},{4,100},{5,101},{6,102},{7,103},{8,104... | collective-permute-start | bytes 172040 | tf_op jit(solution)/shard_map/ppermute | solution.py:331
  49.0 9.9 %collective-permute-start.9 = (f32[112,128]{1,0:T(8,128)S(1)}, f32[112,128]{1,0:T(8,128)S(1)}, u32[]{:S(2)}, u32[]{:S(2)}) collective-permute-start(f32[112,128]{1,0:T(8,128)S(1)} %add_add_fusion.1), channel_id=1, source_target_pairs={{0,64},{1,65},{2,66},{3,67},{4,68},{5,69},{6,70},{7,71},{8,72},{9,... | collective-permute-start | bytes 172040 | tf_op jit(solution)/shard_map/ppermute | solution.py:331
  49.8 9.1 %collective-permute-start.8 = (f32[112,128]{1,0:T(8,128)S(1)}, f32[112,128]{1,0:T(8,128)S(1)}, u32[]{:S(2)}, u32[]{:S(2)}) collective-permute-start(f32[112,128]{1,0:T(8,128)S(1)} %add_add_fusion.1), channel_id=1, source_target_pairs={{0,32},{1,33},{2,34},{3,35},{4,36},{5,37},{6,38},{7,39},{8,40},{9,... | collective-permute-start | bytes 172040 | tf_op jit(solution)/shard_map/ppermute | solution.py:331
  58.8 1.3 %collective-permute-start.11 = (f32[112,128]{1,0:T(8,128)S(1)}, f32[112,128]{1,0:T(8,128)S(1)}, u32[]{:S(2)}, u32[]{:S(2)}) collective-permute-start(f32[112,128]{1,0:T(8,128)S(1)} %add_add_fusion.part), channel_id=1, source_target_pairs={{0,1},{1,0},{2,3},{3,2},{4,5},{5,4},{6,7},{7,6},{8,9},{9,8},{10,11... | collective-permute-start | bytes 172040 | tf_op jit(solution)/shard_map/ppermute | solution.py:331
  60.2 9.0 %collective-permute-start.15 = (f32[224,128]{1,0:T(8,128)S(1)}, f32[224,128]{1,0:T(8,128)S(1)}, u32[]{:S(2)}, u32[]{:S(2)}) collective-permute-start(f32[224,128]{1,0:T(8,128)S(1)} %shard_map.88.part), channel_id=1, source_target_pairs={{0,18},{1,19},{2,16},{3,17},{4,22},{5,23},{6,20},{7,21},{8,26},{9,... | collective-permute-start | bytes 344072 | tf_op jit(solution)/shard_map/ppermute | solution.py:331
  60.8 8.4 %collective-permute-start.14 = (f32[224,128]{1,0:T(8,128)S(1)}, f32[224,128]{1,0:T(8,128)S(1)}, u32[]{:S(2)}, u32[]{:S(2)}) collective-permute-start(f32[224,128]{1,0:T(8,128)S(1)} %shard_map.88.part), channel_id=1, source_target_pairs={{0,16},{1,17},{2,18},{3,19},{4,20},{5,21},{6,22},{7,23},{8,24},{9,... | collective-permute-start | bytes 344072 | tf_op jit(solution)/shard_map/ppermute | solution.py:331
  63.6 6.1 %collective-permute-start.13 = (f32[224,128]{1,0:T(8,128)S(1)}, f32[224,128]{1,0:T(8,128)S(1)}, u32[]{:S(2)}, u32[]{:S(2)}) collective-permute-start(f32[224,128]{1,0:T(8,128)S(1)} %shard_map.88.part), channel_id=1, source_target_pairs={{0,2},{1,3},{2,0},{3,1},{4,6},{5,7},{6,4},{7,5},{8,10},{9,11},{10,... | collective-permute-start | bytes 344072 | tf_op jit(solution)/shard_map/ppermute | solution.py:331

commit v10 on v9

--- a/solution.py
+++ b/solution.py
@@ -203,7 +203,7 @@
 
 
 def kernel_grad_body(
-    below_first, below_rest, low, from_left, from_right, folded, bias_terms, flag,
+    below_first, below_rest, low, from_left, from_right, folded, bias_terms,
     keep, send, packed, taps, sums, below_grad,
 ):
     rows, groups = low.shape[0] // 2, low.shape[1]
@@ -235,7 +235,7 @@
         else:
             extra = jnp.where(first, jnp.broadcast_to(row, (32, LANES)), 0.0)
         packed[place * 32 : place * 32 + 32, :] = jnp.where(lane < 96, parts[place], extra)
-    upper = flag[...] > 0.5
+    upper = lax.rem(lax.axis_index("gy"), 2) == 1
     keep[...] = jnp.where(upper, packed[HALF : 2 * HALF], packed[:HALF])
     send[...] = jnp.where(upper, packed[:HALF], packed[HALF : 2 * HALF])
 
@@ -302,8 +302,8 @@
 HALF = 112
 
 
-def join_body(part, other, flag, packed):
-    upper = flag[...] > 0.5
+def join_body(part, other, packed):
+    upper = lax.rem(lax.axis_index("gy"), 2) == 1
     packed[:HALF] = jnp.where(upper, other[...], part[...])
     packed[HALF : 2 * HALF] = jnp.where(upper, part[...], other[...])
 
@@ -348,7 +348,6 @@
     two_taps = pltpu.VMEM((2, rows + 2, groups, 2 * LANES), BF16)
     half = shape((HALF, LANES), F32)
     packed = pltpu.VMEM((2 * HALF, LANES), F32)
-    flag = jnp.full((1, LANES), lax.axis_index("gy") % 2, F32)
 
     low, high_first, high_rest, firsts, lasts = pl.pallas_call(
         group_body,
@@ -419,14 +418,14 @@
         kernel_grad_body,
         (half, half),
         [packed, two_taps, pltpu.VMEM((2, 3, LANES, 256), F32), one_plane],
-        (below_first, below_rest, low, from_left, from_right, folded, bias_terms, flag),
+        (below_first, below_rest, low, from_left, from_right, folded, bias_terms),
     )
     part = part + swapped(send, 1)
     part = sum_of_four(part, 4, 8)
     part = sum_of_four(part, 32, 64)
     results = outer(0, (below_first, below_rest))
     part, results = lax.optimization_barrier((part, results))
-    part = call(join_body, shape((2 * HALF, LANES), F32), [], (part, swapped(part, 1), flag))
+    part = call(join_body, shape((2 * HALF, LANES), F32), [], (part, swapped(part, 1)))
     part, above = lax.optimization_barrier((part, above))
     others = [swapped(part, bit) for bit in (2, 16, 18)]
     results = outer(1, (above,), results)

time: 71.1 us -> 71.1 us (level)
  the two profiles are of different devices: /device:TPU:10 before, /device:TPU:14 now
where the time goes in v10:
time: 71.1 us; the launch traced here: 70.7 us
  starting transfers between devices  33.3 us (47%)
  Pallas kernels  26.1 us (37%)
  waiting for transfers between devices  9.2 us (13%)
  other arithmetic  1.15 us (2%)
  between operations  0.94 us (1%)
    ppermute x5, starting transfers between devices, shifted(): return lax.ppermute(value, axis, pairs)  20.6 us
    pallas_call x3, Pallas kernels, blocked(): pl.pallas_call(body, grid=(grid,), out_shape=outs, in_specs=in_specs, out...  20.5 us
    ppermute x11, starting transfers between devices, swapped(): lax.ppermute(value, ('gz', 'gy'), [(i, i ^ bit) for i in range(count)])  12.7 us
    ppermute x11, waiting for transfers between devices, swapped(): lax.ppermute(value, ('gz', 'gy'), [(i, i ^ bit) for i in range(count)])  9.19 us
    pallas_call x1, Pallas kernels, local(): pl.pallas_call(group_body, in_specs=[pl.BlockSpec(memory_space=pl.ANY)] *...  3.06 us
    pallas_call x3, Pallas kernels, call(): pl.pallas_call(body, out_shape=outs, scratch_shapes=scratch, compiler_par...  2.53 us
  transfers between devices with their start and end apart: 16, of which 7 were waited for; matrix products, arithmetic and copies ran while one was open for 2% of the time, Pallas kernels for 31%

profile of v10, /device:TPU:14, one launch (start us, length us, event | category | flops | bytes accessed | tf_op | source)
XLA Modules:
  0.0 70.7 jit_solution(14243516253862842533)
XLA Ops:
  0.6 3.1 %shard_map.84 = (bf16[32,96,128]{2,1,0:T(8,128)(2,1)}, bf16[24,96,128]{2,1,0:T(8,128)(2,1)}, bf16[8,96,128]{2,1,0:T(8,128)(2,1)}, bf16[4,96,128]{2,1,0:T(8,128)(2,1)}, bf16[4,96,128]{2,1,0:T(8,128)(2,1)}) custom-call(bf16[2,16,12288]{2,1,0:T(8,128)(2,1)} %act_in.1, bf16[2,16,12288]{2,1,0:T(8,128)(2,1)} %grad_in.1, s32[2,16,12288]{2,1,0:T(8,128)} %mask_in.1), custom_call_target="tpu_custom_call" | custom-call | tf_op jit(solution)/shard_map/pallas_call | solution.py:352
  3.7 0.0 copy-start
  3.7 2.1 %collective-permute-start.1 = (bf16[4,96,128]{2,1,0:T(8,128)(2,1)}, bf16[4,96,128]{2,1,0:T(8,128)(2,1)S(1)}, u32[]{:S(2)}, u32[]{:S(2)}) collective-permute-start(bf16[4,96,128]{2,1,0:T(8,128)(2,1)} %get-tuple-element.34), channel_id=1, source_target_pairs={{0,1},{1,2},{2,3},{3,4},{4,5},{5,6},{6,7},{7,8},{8,9},{9,10},{10,1... | collective-permute-start | bytes 294920 | tf_op jit(solution)/shard_map/ppermute | solution.py:326
  5.8 4.5 %collective-permute-start.2 = (bf16[4,96,128]{2,1,0:T(8,128)(2,1)}, bf16[4,96,128]{2,1,0:T(8,128)(2,1)S(1)}, u32[]{:S(2)}, u32[]{:S(2)}) collective-permute-start(bf16[4,96,128]{2,1,0:T(8,128)(2,1)} %get-tuple-element.35), channel_id=1, source_target_pairs={{1,0},{2,1},{3,2},{4,3},{5,4},{6,5},{7,6},{8,7},{9,8},{10,9},{11,1... | collective-permute-start | bytes 294920 | tf_op jit(solution)/shard_map/ppermute | solution.py:326
  10.3 5.8 %collective-permute-start = (bf16[24,96,128]{2,1,0:T(8,128)(2,1)}, bf16[24,96,128]{2,1,0:T(8,128)(2,1)S(1)}, u32[]{:S(2)}, u32[]{:S(2)}) collective-permute-start(bf16[24,96,128]{2,1,0:T(8,128)(2,1)} %get-tuple-element.32.high_first), channel_id=1, source_target_pairs={{0,16},{16,32},{32,48},{48,64},{64,80},{80,96},{96,112},{1,17},{17... | collective-permute-start | bytes 1769480 | tf_op jit(solution)/shard_map/ppermute | solution.py:326
  16.1 0.0 collective-permute-done.1.from_left
  16.1 0.0 copy-start.3
  16.2 0.0 collective-permute-done.2.from_right
  16.2 0.0 copy-start.5
  16.2 1.0 %pad_maximum_fusion.1 = bf16[12,96,128]{2,1,0:T(8,128)(2,1)S(1)} fusion(bf16[2,96,128]{2,1,0:T(8,128)(2,1)S(1)} %get-tuple-element.61, bf16[2,96,128]{2,1,0:T(8,128)(2,1)S(1)} %get-tuple-element.63, bf16[8,96,128]{2,1,0:T(8,128)(2,1)} %get-tuple-element.33.high_rest), kind=kLoop, calls=%fused_computation.1 | loop fusion | flops 294912 | bytes 589824 | tf_op jit(solution)/shard_map/concatenate | solution.py:367
  17.2 2.6 %collective-permute-start.3 = (bf16[12,96,128]{2,1,0:T(8,128)(2,1)S(1)}, bf16[12,96,128]{2,1,0:T(8,128)(2,1)S(1)}, u32[]{:S(2)}, u32[]{:S(2)}) collective-permute-start(bf16[12,96,128]{2,1,0:T(8,128)(2,1)S(1)} %pad_maximum_fusion.1), channel_id=1, source_target_pairs={{0,16},{16,32},{32,48},{48,64},{64,80},{80,96},{96,112},{1,17},{17... | collective-permute-start | bytes 884744 | tf_op jit(solution)/shard_map/ppermute | solution.py:326
  19.8 0.0 copy-done.3
  19.8 0.0 copy-done.5
  19.8 11.0 %shard_map.85 = (f32[3,3,32,128]{3,2,1,0:T(8,128)}, f32[8,128]{1,0:T(8,128)}, f32[2,16,96,128]{3,2,1,0:T(8,128)}, bf16[3,3,256,128]{3,2,1,0:T(8,128)(2,1)}, f32[...) custom-call(bf16[32,96,128]{2,1,0:T(8,128)(2,1)} %get-tuple-element.36.low, ...), custom_call_target="tpu_custom_call" | custom-call | tf_op jit(solution)/shard_map/pallas_call | solution.py:27
  30.8 0.0 copy-start.4
  30.8 0.0 copy-start.6
  30.8 0.0 copy-start.7
  30.8 0.0 copy-start.8
  30.8 0.0 copy-done
  30.8 0.1 pad_maximum_fusion
  31.0 5.7 %collective-permute-start.12 = (bf16[36,96,128]{2,1,0:T(8,128)(2,1)S(1)}, bf16[36,96,128]{2,1,0:T(8,128)(2,1)S(1)}, u32[]{:S(2)}, u32[]{:S(2)}) collective-permute-start(bf16[36,96,128]{2,1,0:T(8,128)(2,1)S(1)} %pad_maximum_fusion), channel_id=1, source_target_pairs={{16,0},{32,16},{48,32},{64,48},{80,64},{96,80},{112,96},{17,1},{33... | collective-permute-start | bytes 2654216 | tf_op jit(solution)/shard_map/ppermute | solution.py:326
  36.6 0.0 collective-permute-done.3.below_rest.refs_1_
  36.7 0.0 copy-start.2
  36.7 0.0 collective-permute-done.below_first.refs_0_
  36.7 0.0 copy-start.1
  36.7 0.0 copy-done.4
  36.7 0.0 copy-done.6
  36.7 0.0 copy-done.7
  36.7 0.0 copy-done.8
  36.7 1.5 %shard_map.86 = (f32[112,128]{1,0:T(8,128)S(1)}, f32[112,128]{1,0:T(8,128)S(1)}) custom-call(bf16[24,96,128]{2,1,0:T(8,128)(2,1)S(1)} %collective-permute-done.below_first.refs_0_, bf16[12,96,128]{2,1,0:T(8,128)(2,1)S(1)} %collective-permute-done.3.below_rest.refs_1_, bf16[32,96,128]{2,1,0:T(8,128)(2,1)S(1)} %copy-done, bf16[4,96,128]{2,1,0:T(8,128)(2,1)S(1)} %copy-done.4, ...), custom_call_target="tpu_custom_call" | custom-call | tf_op jit(solution)/shard_map/pallas_call | solution.py:18
  38.3 0.1 collective-permute-start.4
  38.4 1.2 %collective-permute-done.4 = f32[112,128]{1,0:T(8,128)S(1)} collective-permute-done((f32[112,128]{1,0:T(8,128)S(1)}, f32[112,128]{1,0:T(8,128)S(1)}, u32[]{:S(2)}, u32[]{:S(2)}) %collective-permute-start.4) | collective-permute-done | bytes 57376 | tf_op jit(solution)/shard_map/ppermute | solution.py:331
  39.6 0.1 collective-permute-start.7
  39.7 2.9 %collective-permute-start.6 = (f32[112,128]{1,0:T(8,128)S(1)}, f32[112,128]{1,0:T(8,128)S(1)}, u32[]{:S(2)}, u32[]{:S(2)}) collective-permute-start(f32[112,128]{1,0:T(8,128)S(1)} %add.21), channel_id=1, source_target_pairs={{0,8},{1,9},{2,10},{3,11},{4,12},{5,13},{6,14},{7,15},{8,0},{9,1},... | collective-permute-start | bytes 172040 | tf_op jit(solution)/shard_map/ppermute | solution.py:331
  42.6 1.2 %collective-permute-start.5 = (f32[112,128]{1,0:T(8,128)S(1)}, f32[112,128]{1,0:T(8,128)S(1)}, u32[]{:S(2)}, u32[]{:S(2)}) collective-permute-start(f32[112,128]{1,0:T(8,128)S(1)} %add.21), channel_id=1, source_target_pairs={{0,4},{1,5},{2,6},{3,7},{4,0},{5,1},{6,2},{7,3},{8,12},{9,13},{10,... | collective-permute-start | bytes 172040 | tf_op jit(solution)/shard_map/ppermute | solution.py:331
  43.8 2.3 %collective-permute-done.7 = f32[112,128]{1,0:T(8,128)S(1)} collective-permute-done((f32[112,128]{1,0:T(8,128)S(1)}, f32[112,128]{1,0:T(8,128)S(1)}, u32[]{:S(2)}, u32[]{:S(2)}) %collective-permute-start.7) | collective-permute-done | bytes 57376 | tf_op jit(solution)/shard_map/ppermute | solution.py:331
  46.1 0.0 collective-permute-done.6
  46.1 0.7 collective-permute-done.5
  46.8 1.7 %collective-permute-start.10 = (f32[112,128]{1,0:T(8,128)S(1)}, f32[112,128]{1,0:T(8,128)S(1)}, u32[]{:S(2)}, u32[]{:S(2)}) collective-permute-start(f32[112,128]{1,0:T(8,128)S(1)} %add_add_fusion.1), channel_id=1, source_target_pairs={{0,96},{1,97},{2,98},{3,99},{4,100},{5,101},{6,102},{7,103},{8,104... | collective-permute-start | bytes 172040 | tf_op jit(solution)/shard_map/ppermute | solution.py:331
  48.4 0.8 %collective-permute-start.9 = (f32[112,128]{1,0:T(8,128)S(1)}, f32[112,128]{1,0:T(8,128)S(1)}, u32[]{:S(2)}, u32[]{:S(2)}) collective-permute-start(f32[112,128]{1,0:T(8,128)S(1)} %add_add_fusion.1), channel_id=1, source_target_pairs={{0,64},{1,65},{2,66},{3,67},{4,68},{5,69},{6,70},{7,71},{8,72},{9,... | collective-permute-start | bytes 172040 | tf_op jit(solution)/shard_map/ppermute | solution.py:331
  49.3 1.7 %collective-permute-start.8 = (f32[112,128]{1,0:T(8,128)S(1)}, f32[112,128]{1,0:T(8,128)S(1)}, u32[]{:S(2)}, u32[]{:S(2)}) collective-permute-start(f32[112,128]{1,0:T(8,128)S(1)} %add_add_fusion.1), channel_id=1, source_target_pairs={{0,32},{1,33},{2,34},{3,35},{4,36},{5,37},{6,38},{7,39},{8,40},{9,... | collective-permute-start | bytes 172040 | tf_op jit(solution)/shard_map/ppermute | solution.py:331
  51.0 0.0 copy-done.2
  51.0 0.0 copy-done.1
  51.0 4.7 %shard_map.87 = (bf16[2,16,12288]{2,1,0:T(8,128)(2,1)}, bf16[2,16,12288]{2,1,0:T(8,128)(2,1)}) custom-call(bf16[24,96,128]{2,1,0:T(8,128)(2,1)} %copy-done.1, bf16[12,96,128]{2,1,0:T(8,128)(2,1)} %copy-done.2, bf16[3,3,256,128]{3,2,1,0:T(8,128)(2,1)} %get-tuple-element.43.refs_2_.refs_1_, bf16[3,3,256,128]{3,2,1,0:T(8,128)(2,1)} %get-tuple-element.44.refs_3_.refs_2_, ...), custom_call_target="tpu_custom_call" | custom-call | tf_op jit(solution)/shard_map/pallas_call | solution.py:27
  55.7 2.4 %collective-permute-done.10 = f32[112,128]{1,0:T(8,128)S(1)} collective-permute-done((f32[112,128]{1,0:T(8,128)S(1)}, f32[112,128]{1,0:T(8,128)S(1)}, u32[]{:S(2)}, u32[]{:S(2)}) %collective-permute-start.10) | collective-permute-done | bytes 57376 | tf_op jit(solution)/shard_map/ppermute | solution.py:331
  58.1 0.7 %collective-permute-done.9 = f32[112,128]{1,0:T(8,128)S(1)} collective-permute-done((f32[112,128]{1,0:T(8,128)S(1)}, f32[112,128]{1,0:T(8,128)S(1)}, u32[]{:S(2)}, u32[]{:S(2)}) %collective-permute-start.9) | collective-permute-done | bytes 57376 | tf_op jit(solution)/shard_map/ppermute | solution.py:331
  58.8 0.0 collective-permute-done.8
  58.9 0.1 collective-permute-start.11
  58.9 1.2 %collective-permute-done.11.other = f32[112,128]{1,0:T(8,128)S(1)} collective-permute-done((f32[112,128]{1,0:T(8,128)S(1)}, f32[112,128]{1,0:T(8,128)S(1)}, u32[]{:S(2)}, u32[]{:S(2)}) %collective-permute-start.11) | collective-permute-done | bytes 57376 | tf_op jit(solution)/shard_map/ppermute | solution.py:331
  60.2 0.0 collective-permute-done.12.refs_0_
  60.2 0.0 copy-start.9
  60.2 0.1 collective-permute-start.15
  60.3 1.8 %collective-permute-start.14 = (f32[224,128]{1,0:T(8,128)S(1)}, f32[224,128]{1,0:T(8,128)S(1)}, u32[]{:S(2)}, u32[]{:S(2)}) collective-permute-start(f32[224,128]{1,0:T(8,128)S(1)} %shard_map.88.part), channel_id=1, source_target_pairs={{0,16},{1,17},{2,18},{3,19},{4,20},{5,21},{6,22},{7,23},{8,24},{9,... | collective-permute-start | bytes 344072 | tf_op jit(solution)/shard_map/ppermute | solution.py:331
  62.2 2.2 %collective-permute-start.13 = (f32[224,128]{1,0:T(8,128)S(1)}, f32[224,128]{1,0:T(8,128)S(1)}, u32[]{:S(2)}, u32[]{:S(2)}) collective-permute-start(f32[224,128]{1,0:T(8,128)S(1)} %shard_map.88.part), channel_id=1, source_target_pairs={{0,2},{1,3},{2,0},{3,1},{4,6},{5,7},{6,4},{7,5},{8,10},{9,11},{10,... | collective-permute-start | bytes 344072 | tf_op jit(solution)/shard_map/ppermute | solution.py:331
  64.4 0.0 copy-done.9
  64.4 4.7 %shard_map.89 = (bf16[2,16,12288]{2,1,0:T(8,128)(2,1)}, bf16[2,16,12288]{2,1,0:T(8,128)(2,1)}) custom-call(bf16[36,96,128]{2,1,0:T(8,128)(2,1)} %copy-done.9, bf16[3,3,256,128]{3,2,1,0:T(8,128)(2,1)} %get-tuple-element.43.refs_2_.refs_1_, bf16[3,3,256,128]{3,2,1,0:T(8,128)(2,1)} %get-tuple-element.44.refs_3_.refs_2_, ...), custom_call_target="tpu_custom_call", output_to_operand_aliasing={{0}: (6, {}), {1}: (7, {})} | custom-call | tf_op jit(solution)/shard_map/pallas_call | solution.py:27
  69.1 0.0 collective-permute-done.15.three
  69.2 0.0 collective-permute-done.14.two
  69.2 0.6 collective-permute-done.13.one
  69.8 1.0 %shard_map.90 = (f32[864,32]{1,0:T(8,128)}, f32[1,32]{1,0:T(1,128)}) custom-call(f32[224,128]{1,0:T(8,128)S(1)} %shard_map.88.part, f32[224,128]{1,0:T(8,128)S(1)} %collective-permute-done.13.one, f32[224,128]{1,0:T(8,128)S(1)} %collective-permute-done.14.two, f32[224,128]{1,0:T(8,128)S(1)} %collective-permute-done.15.three), custom_call_target="tpu_custom_call" | custom-call | tf_op jit(solution)/shard_map/pallas_call | solution.py:18
  (6 shorter events, 0.1 us)
Async XLA Ops:
  3.7 27.1 %copy-start = (bf16[32,96,128]{2,1,0:T(8,128)(2,1)S(1)}, bf16[32,96,128]{2,1,0:T(8,128)(2,1)}, u32[]{:S(2)}) copy-start(bf16[32,96,128]{2,1,0:T(8,128)(2,1)} %get-tuple-element.36.low) | copy-start | bytes 2359300
  3.7 12.4 %collective-permute-start.1 = (bf16[4,96,128]{2,1,0:T(8,128)(2,1)}, bf16[4,96,128]{2,1,0:T(8,128)(2,1)S(1)}, u32[]{:S(2)}, u32[]{:S(2)}) collective-permute-start(bf16[4,96,128]{2,1,0:T(8,128)(2,1)} %get-tuple-element.34), channel_id=1, source_target_pairs={{0,1},{1,2},{2,3},{3,4},{4,5},{5,6},{6,7},{7,8},{8,9},{9,10},{10,1... | collective-permute-start | bytes 294920 | tf_op jit(solution)/shard_map/ppermute | solution.py:326
  5.8 10.4 %collective-permute-start.2 = (bf16[4,96,128]{2,1,0:T(8,128)(2,1)}, bf16[4,96,128]{2,1,0:T(8,128)(2,1)S(1)}, u32[]{:S(2)}, u32[]{:S(2)}) collective-permute-start(bf16[4,96,128]{2,1,0:T(8,128)(2,1)} %get-tuple-element.35), channel_id=1, source_target_pairs={{1,0},{2,1},{3,2},{4,3},{5,4},{6,5},{7,6},{8,7},{9,8},{10,9},{11,1... | collective-permute-start | bytes 294920 | tf_op jit(solution)/shard_map/ppermute | solution.py:326
  10.3 26.3 %collective-permute-start = (bf16[24,96,128]{2,1,0:T(8,128)(2,1)}, bf16[24,96,128]{2,1,0:T(8,128)(2,1)S(1)}, u32[]{:S(2)}, u32[]{:S(2)}) collective-permute-start(bf16[24,96,128]{2,1,0:T(8,128)(2,1)} %get-tuple-element.32.high_first), channel_id=1, source_target_pairs={{0,16},{16,32},{32,48},{48,64},{64,80},{80,96},{96,112},{1,17},{17... | collective-permute-start | bytes 1769480 | tf_op jit(solution)/shard_map/ppermute | solution.py:326
  16.1 3.6 %copy-start.3 = (bf16[4,96,128]{2,1,0:T(8,128)(2,1)}, bf16[4,96,128]{2,1,0:T(8,128)(2,1)S(1)}, u32[]{:S(2)}) copy-start(bf16[4,96,128]{2,1,0:T(8,128)(2,1)S(1)} %collective-permute-done.1.from_left) | copy-start | bytes 294916
  16.2 3.6 %copy-start.5 = (bf16[4,96,128]{2,1,0:T(8,128)(2,1)}, bf16[4,96,128]{2,1,0:T(8,128)(2,1)S(1)}, u32[]{:S(2)}) copy-start(bf16[4,96,128]{2,1,0:T(8,128)(2,1)S(1)} %collective-permute-done.2.from_right) | copy-start | bytes 294916
  17.2 19.5 %collective-permute-start.3 = (bf16[12,96,128]{2,1,0:T(8,128)(2,1)S(1)}, bf16[12,96,128]{2,1,0:T(8,128)(2,1)S(1)}, u32[]{:S(2)}, u32[]{:S(2)}) collective-permute-start(bf16[12,96,128]{2,1,0:T(8,128)(2,1)S(1)} %pad_maximum_fusion.1), channel_id=1, source_target_pairs={{0,16},{16,32},{32,48},{48,64},{64,80},{80,96},{96,112},{1,17},{17... | collective-permute-start | bytes 884744 | tf_op jit(solution)/shard_map/ppermute | solution.py:326
  30.8 5.9 %copy-start.4 = (bf16[4,96,128]{2,1,0:T(8,128)(2,1)S(1)}, bf16[4,96,128]{2,1,0:T(8,128)(2,1)}, u32[]{:S(2)}) copy-start(bf16[4,96,128]{2,1,0:T(8,128)(2,1)} %copy-done.3) | copy-start | bytes 294916
  30.8 5.9 %copy-start.6 = (bf16[4,96,128]{2,1,0:T(8,128)(2,1)S(1)}, bf16[4,96,128]{2,1,0:T(8,128)(2,1)}, u32[]{:S(2)}) copy-start(bf16[4,96,128]{2,1,0:T(8,128)(2,1)} %copy-done.5) | copy-start | bytes 294916
  30.8 5.9 %copy-start.7 = (f32[3,3,32,128]{3,2,1,0:T(8,128)S(1)}, f32[3,3,32,128]{3,2,1,0:T(8,128)}, u32[]{:S(2)}) copy-start(f32[3,3,32,128]{3,2,1,0:T(8,128)} %get-tuple-element.39.folded) | copy-start | bytes 442372
  30.8 5.9 %copy-start.8 = (f32[8,128]{1,0:T(8,128)S(1)}, f32[8,128]{1,0:T(8,128)}, u32[]{:S(2)}) copy-start(f32[8,128]{1,0:T(8,128)} %get-tuple-element.40.bias_terms) | copy-start | bytes 12292
  31.0 29.2 %collective-permute-start.12 = (bf16[36,96,128]{2,1,0:T(8,128)(2,1)S(1)}, bf16[36,96,128]{2,1,0:T(8,128)(2,1)S(1)}, u32[]{:S(2)}, u32[]{:S(2)}) collective-permute-start(bf16[36,96,128]{2,1,0:T(8,128)(2,1)S(1)} %pad_maximum_fusion), channel_id=1, source_target_pairs={{16,0},{32,16},{48,32},{64,48},{80,64},{96,80},{112,96},{17,1},{33... | collective-permute-start | bytes 2654216 | tf_op jit(solution)/shard_map/ppermute | solution.py:326
  36.7 14.3 %copy-start.2 = (bf16[12,96,128]{2,1,0:T(8,128)(2,1)}, bf16[12,96,128]{2,1,0:T(8,128)(2,1)S(1)}, u32[]{:S(2)}) copy-start(bf16[12,96,128]{2,1,0:T(8,128)(2,1)S(1)} %collective-permute-done.3.below_rest.refs_1_) | copy-start | bytes 884740
  36.7 14.3 %copy-start.1 = (bf16[24,96,128]{2,1,0:T(8,128)(2,1)}, bf16[24,96,128]{2,1,0:T(8,128)(2,1)S(1)}, u32[]{:S(2)}) copy-start(bf16[24,96,128]{2,1,0:T(8,128)(2,1)S(1)} %collective-permute-done.below_first.refs_0_) | copy-start | bytes 1769476
  38.3 1.3 %collective-permute-start.4 = (f32[112,128]{1,0:T(8,128)S(1)}, f32[112,128]{1,0:T(8,128)S(1)}, u32[]{:S(2)}, u32[]{:S(2)}) collective-permute-start(f32[112,128]{1,0:T(8,128)S(1)} %get-tuple-element.42), channel_id=1, source_target_pairs={{0,1},{1,0},{2,3},{3,2},{4,5},{5,4},{6,7},{7,6},{8,9},{9,8},{10,11... | collective-permute-start | bytes 172040 | tf_op jit(solution)/shard_map/ppermute | solution.py:331
  39.6 6.5 %collective-permute-start.7 = (f32[112,128]{1,0:T(8,128)S(1)}, f32[112,128]{1,0:T(8,128)S(1)}, u32[]{:S(2)}, u32[]{:S(2)}) collective-permute-start(f32[112,128]{1,0:T(8,128)S(1)} %add.21), channel_id=1, source_target_pairs={{0,12},{1,13},{2,14},{3,15},{4,8},{5,9},{6,10},{7,11},{8,4},{9,5},... | collective-permute-start | bytes 172040 | tf_op jit(solution)/shard_map/ppermute | solution.py:331
  39.7 6.4 %collective-permute-start.6 = (f32[112,128]{1,0:T(8,128)S(1)}, f32[112,128]{1,0:T(8,128)S(1)}, u32[]{:S(2)}, u32[]{:S(2)}) collective-permute-start(f32[112,128]{1,0:T(8,128)S(1)} %add.21), channel_id=1, source_target_pairs={{0,8},{1,9},{2,10},{3,11},{4,12},{5,13},{6,14},{7,15},{8,0},{9,1},... | collective-permute-start | bytes 172040 | tf_op jit(solution)/shard_map/ppermute | solution.py:331
  42.6 4.2 %collective-permute-start.5 = (f32[112,128]{1,0:T(8,128)S(1)}, f32[112,128]{1,0:T(8,128)S(1)}, u32[]{:S(2)}, u32[]{:S(2)}) collective-permute-start(f32[112,128]{1,0:T(8,128)S(1)} %add.21), channel_id=1, source_target_pairs={{0,4},{1,5},{2,6},{3,7},{4,0},{5,1},{6,2},{7,3},{8,12},{9,13},{10,... | collective-permute-start | bytes 172040 | tf_op jit(solution)/shard_map/ppermute | solution.py:331
  46.8 11.3 %collective-permute-start.10 = (f32[112,128]{1,0:T(8,128)S(1)}, f32[112,128]{1,0:T(8,128)S(1)}, u32[]{:S(2)}, u32[]{:S(2)}) collective-permute-start(f32[112,128]{1,0:T(8,128)S(1)} %add_add_fusion.1), channel_id=1, source_target_pairs={{0,96},{1,97},{2,98},{3,99},{4,100},{5,101},{6,102},{7,103},{8,104... | collective-permute-start | bytes 172040 | tf_op jit(solution)/shard_map/ppermute | solution.py:331
  48.4 10.4 %collective-permute-start.9 = (f32[112,128]{1,0:T(8,128)S(1)}, f32[112,128]{1,0:T(8,128)S(1)}, u32[]{:S(2)}, u32[]{:S(2)}) collective-permute-start(f32[112,128]{1,0:T(8,128)S(1)} %add_add_fusion.1), channel_id=1, source_target_pairs={{0,64},{1,65},{2,66},{3,67},{4,68},{5,69},{6,70},{7,71},{8,72},{9,... | collective-permute-start | bytes 172040 | tf_op jit(solution)/shard_map/ppermute | solution.py:331
  49.3 9.6 %collective-permute-start.8 = (f32[112,128]{1,0:T(8,128)S(1)}, f32[112,128]{1,0:T(8,128)S(1)}, u32[]{:S(2)}, u32[]{:S(2)}) collective-permute-start(f32[112,128]{1,0:T(8,128)S(1)} %add_add_fusion.1), channel_id=1, source_target_pairs={{0,32},{1,33},{2,34},{3,35},{4,36},{5,37},{6,38},{7,39},{8,40},{9,... | collective-permute-start | bytes 172040 | tf_op jit(solution)/shard_map/ppermute | solution.py:331
  58.9 1.3 %collective-permute-start.11 = (f32[112,128]{1,0:T(8,128)S(1)}, f32[112,128]{1,0:T(8,128)S(1)}, u32[]{:S(2)}, u32[]{:S(2)}) collective-permute-start(f32[112,128]{1,0:T(8,128)S(1)} %add_add_fusion.part), channel_id=1, source_target_pairs={{0,1},{1,0},{2,3},{3,2},{4,5},{5,4},{6,7},{7,6},{8,9},{9,8},{10,11... | collective-permute-start | bytes 172040 | tf_op jit(solution)/shard_map/ppermute | solution.py:331
  60.2 4.2 %copy-start.9 = (bf16[36,96,128]{2,1,0:T(8,128)(2,1)}, bf16[36,96,128]{2,1,0:T(8,128)(2,1)S(1)}, u32[]{:S(2)}) copy-start(bf16[36,96,128]{2,1,0:T(8,128)(2,1)S(1)} %collective-permute-done.12.refs_0_) | copy-start | bytes 2654212
  60.2 9.0 %collective-permute-start.15 = (f32[224,128]{1,0:T(8,128)S(1)}, f32[224,128]{1,0:T(8,128)S(1)}, u32[]{:S(2)}, u32[]{:S(2)}) collective-permute-start(f32[224,128]{1,0:T(8,128)S(1)} %shard_map.88.part), channel_id=1, source_target_pairs={{0,18},{1,19},{2,16},{3,17},{4,22},{5,23},{6,20},{7,21},{8,26},{9,... | collective-permute-start | bytes 344072 | tf_op jit(solution)/shard_map/ppermute | solution.py:331
  60.3 8.9 %collective-permute-start.14 = (f32[224,128]{1,0:T(8,128)S(1)}, f32[224,128]{1,0:T(8,128)S(1)}, u32[]{:S(2)}, u32[]{:S(2)}) collective-permute-start(f32[224,128]{1,0:T(8,128)S(1)} %shard_map.88.part), channel_id=1, source_target_pairs={{0,16},{1,17},{2,18},{3,19},{4,20},{5,21},{6,22},{7,23},{8,24},{9,... | collective-permute-start | bytes 344072 | tf_op jit(solution)/shard_map/ppermute | solution.py:331
  62.2 7.6 %collective-permute-start.13 = (f32[224,128]{1,0:T(8,128)S(1)}, f32[224,128]{1,0:T(8,128)S(1)}, u32[]{:S(2)}, u32[]{:S(2)}) collective-permute-start(f32[224,128]{1,0:T(8,128)S(1)} %shard_map.88.part), channel_id=1, source_target_pairs={{0,2},{1,3},{2,0},{3,1},{4,6},{5,7},{6,4},{7,5},{8,10},{9,11},{10,... | collective-permute-start | bytes 344072 | tf_op jit(solution)/shard_map/ppermute | solution.py:331

commit v11 on v10

--- a/solution.py
+++ b/solution.py
@@ -126,7 +126,7 @@
 
 
 CHUNK = 4
-EARLY = 8
+EARLY = 12
 
 
 def fold(term):

time: 71.1 us -> 71.1 us (level)
  the two profiles are of different devices: /device:TPU:14 before, /device:TPU:10 now
where the time goes in v11:
time: 71.1 us; the launch traced here: 70.7 us
  starting transfers between devices  33.3 us (47%)
  Pallas kernels  26.1 us (37%)
  waiting for transfers between devices  9.19 us (13%)
  other arithmetic  1.1 us (2%)
  between operations  0.89 us (1%)
    ppermute x5, starting transfers between devices, shifted(): return lax.ppermute(value, axis, pairs)  20.6 us
    pallas_call x3, Pallas kernels, blocked(): pl.pallas_call(body, grid=(grid,), out_shape=outs, in_specs=in_specs, out...  20.5 us
    ppermute x11, starting transfers between devices, swapped(): lax.ppermute(value, ('gz', 'gy'), [(i, i ^ bit) for i in range(count)])  12.7 us
    ppermute x11, waiting for transfers between devices, swapped(): lax.ppermute(value, ('gz', 'gy'), [(i, i ^ bit) for i in range(count)])  8.94 us
    pallas_call x1, Pallas kernels, local(): pl.pallas_call(group_body, in_specs=[pl.BlockSpec(memory_space=pl.ANY)] *...  3.06 us
    pallas_call x3, Pallas kernels, call(): pl.pallas_call(body, out_shape=outs, scratch_shapes=scratch, compiler_par...  2.53 us
  transfers between devices with their start and end apart: 16, of which 8 were waited for; matrix products, arithmetic and copies ran while one was open for 2% of the time, Pallas kernels for 31%

profile of v11, /device:TPU:10, one launch (start us, length us, event | category | flops | bytes accessed | tf_op | source)
XLA Modules:
  0.0 70.7 jit_solution(13817337209004582512)
XLA Ops:
  0.6 3.1 %shard_map.84 = (bf16[32,96,128]{2,1,0:T(8,128)(2,1)}, bf16[28,96,128]{2,1,0:T(8,128)(2,1)}, bf16[4,96,128]{2,1,0:T(8,128)(2,1)}, bf16[4,96,128]{2,1,0:T(8,128)(2,1)}, bf16[4,96,128]{2,1,0:T(8,128)(2,1)}) custom-call(bf16[2,16,12288]{2,1,0:T(8,128)(2,1)} %act_in.1, bf16[2,16,12288]{2,1,0:T(8,128)(2,1)} %grad_in.1, s32[2,16,12288]{2,1,0:T(8,128)} %mask_in.1), custom_call_target="tpu_custom_call" | custom-call | tf_op jit(solution)/shard_map/pallas_call | solution.py:352
  3.7 0.0 copy-start
  3.7 2.1 %collective-permute-start.1 = (bf16[4,96,128]{2,1,0:T(8,128)(2,1)}, bf16[4,96,128]{2,1,0:T(8,128)(2,1)S(1)}, u32[]{:S(2)}, u32[]{:S(2)}) collective-permute-start(bf16[4,96,128]{2,1,0:T(8,128)(2,1)} %get-tuple-element.34), channel_id=1, source_target_pairs={{0,1},{1,2},{2,3},{3,4},{4,5},{5,6},{6,7},{7,8},{8,9},{9,10},{10,1... | collective-permute-start | bytes 294920 | tf_op jit(solution)/shard_map/ppermute | solution.py:326
  5.8 4.5 %collective-permute-start.2 = (bf16[4,96,128]{2,1,0:T(8,128)(2,1)}, bf16[4,96,128]{2,1,0:T(8,128)(2,1)S(1)}, u32[]{:S(2)}, u32[]{:S(2)}) collective-permute-start(bf16[4,96,128]{2,1,0:T(8,128)(2,1)} %get-tuple-element.35), channel_id=1, source_target_pairs={{1,0},{2,1},{3,2},{4,3},{5,4},{6,5},{7,6},{8,7},{9,8},{10,9},{11,1... | collective-permute-start | bytes 294920 | tf_op jit(solution)/shard_map/ppermute | solution.py:326
  10.3 5.8 %collective-permute-start = (bf16[28,96,128]{2,1,0:T(8,128)(2,1)}, bf16[28,96,128]{2,1,0:T(8,128)(2,1)S(1)}, u32[]{:S(2)}, u32[]{:S(2)}) collective-permute-start(bf16[28,96,128]{2,1,0:T(8,128)(2,1)} %get-tuple-element.32.high_first), channel_id=1, source_target_pairs={{0,16},{16,32},{32,48},{48,64},{64,80},{80,96},{96,112},{1,17},{17... | collective-permute-start | bytes 2064392 | tf_op jit(solution)/shard_map/ppermute | solution.py:326
  16.1 0.0 collective-permute-done.1.from_left
  16.1 0.0 copy-start.2
  16.2 0.0 collective-permute-done.2.from_right
  16.2 0.0 copy-start.4
  16.2 0.9 %pad_maximum_fusion.1 = bf16[8,96,128]{2,1,0:T(8,128)(2,1)S(1)} fusion(bf16[2,96,128]{2,1,0:T(8,128)(2,1)S(1)} %get-tuple-element.61, bf16[2,96,128]{2,1,0:T(8,128)(2,1)S(1)} %get-tuple-element.63, bf16[4,96,128]{2,1,0:T(8,128)(2,1)} %get-tuple-element.33.high_rest), kind=kLoop, calls=%fused_computation.1 | loop fusion | flops 196608 | bytes 393216 | tf_op jit(solution)/shard_map/concatenate | solution.py:367
  17.1 2.6 %collective-permute-start.3 = (bf16[8,96,128]{2,1,0:T(8,128)(2,1)S(1)}, bf16[8,96,128]{2,1,0:T(8,128)(2,1)S(1)}, u32[]{:S(2)}, u32[]{:S(2)}) collective-permute-start(bf16[8,96,128]{2,1,0:T(8,128)(2,1)S(1)} %pad_maximum_fusion.1), channel_id=1, source_target_pairs={{0,16},{16,32},{32,48},{48,64},{64,80},{80,96},{96,112},{1,17},{17... | collective-permute-start | bytes 589832 | tf_op jit(solution)/shard_map/ppermute | solution.py:326
  19.7 0.0 copy-done.2
  19.7 0.0 copy-done.4
  19.7 11.0 %shard_map.85 = (f32[3,3,32,128]{3,2,1,0:T(8,128)}, f32[8,128]{1,0:T(8,128)}, f32[2,16,96,128]{3,2,1,0:T(8,128)}, bf16[3,3,256,128]{3,2,1,0:T(8,128)(2,1)}, f32[...) custom-call(bf16[32,96,128]{2,1,0:T(8,128)(2,1)} %get-tuple-element.36.low, ...), custom_call_target="tpu_custom_call" | custom-call | tf_op jit(solution)/shard_map/pallas_call | solution.py:27
  30.7 0.0 copy-start.3
  30.8 0.0 copy-start.5
  30.8 0.0 copy-start.7
  30.8 0.0 copy-start.8
  30.8 0.0 copy-done
  30.8 0.1 pad_maximum_fusion
  30.9 5.7 %collective-permute-start.12 = (bf16[36,96,128]{2,1,0:T(8,128)(2,1)S(1)}, bf16[36,96,128]{2,1,0:T(8,128)(2,1)S(1)}, u32[]{:S(2)}, u32[]{:S(2)}) collective-permute-start(bf16[36,96,128]{2,1,0:T(8,128)(2,1)S(1)} %pad_maximum_fusion), channel_id=1, source_target_pairs={{16,0},{32,16},{48,32},{64,48},{80,64},{96,80},{112,96},{17,1},{33... | collective-permute-start | bytes 2654216 | tf_op jit(solution)/shard_map/ppermute | solution.py:326
  36.6 0.2 collective-permute-done.3.below_rest.refs_1_
  36.8 0.0 copy-start.6
  36.8 0.0 collective-permute-done.below_first.refs_0_
  36.8 0.0 copy-start.1
  36.8 0.0 copy-done.3
  36.8 0.0 copy-done.5
  36.9 0.0 copy-done.7
  36.9 0.0 copy-done.8
  36.9 1.5 %shard_map.86 = (f32[112,128]{1,0:T(8,128)S(1)}, f32[112,128]{1,0:T(8,128)S(1)}) custom-call(bf16[28,96,128]{2,1,0:T(8,128)(2,1)S(1)} %collective-permute-done.below_first.refs_0_, bf16[8,96,128]{2,1,0:T(8,128)(2,1)S(1)} %collective-permute-done.3.below_rest.refs_1_, bf16[32,96,128]{2,1,0:T(8,128)(2,1)S(1)} %copy-done, bf16[4,96,128]{2,1,0:T(8,128)(2,1)S(1)} %copy-done.3, ...), custom_call_target="tpu_custom_call" | custom-call | tf_op jit(solution)/shard_map/pallas_call | solution.py:18
  38.4 0.1 collective-permute-start.4
  38.5 1.2 %collective-permute-done.4 = f32[112,128]{1,0:T(8,128)S(1)} collective-permute-done((f32[112,128]{1,0:T(8,128)S(1)}, f32[112,128]{1,0:T(8,128)S(1)}, u32[]{:S(2)}, u32[]{:S(2)}) %collective-permute-start.4) | collective-permute-done | bytes 57376 | tf_op jit(solution)/shard_map/ppermute | solution.py:331
  39.8 1.4 %collective-permute-start.7 = (f32[112,128]{1,0:T(8,128)S(1)}, f32[112,128]{1,0:T(8,128)S(1)}, u32[]{:S(2)}, u32[]{:S(2)}) collective-permute-start(f32[112,128]{1,0:T(8,128)S(1)} %add.21), channel_id=1, source_target_pairs={{0,12},{1,13},{2,14},{3,15},{4,8},{5,9},{6,10},{7,11},{8,4},{9,5},... | collective-permute-start | bytes 172040 | tf_op jit(solution)/shard_map/ppermute | solution.py:331
  41.1 0.7 %collective-permute-start.6 = (f32[112,128]{1,0:T(8,128)S(1)}, f32[112,128]{1,0:T(8,128)S(1)}, u32[]{:S(2)}, u32[]{:S(2)}) collective-permute-start(f32[112,128]{1,0:T(8,128)S(1)} %add.21), channel_id=1, source_target_pairs={{0,8},{1,9},{2,10},{3,11},{4,12},{5,13},{6,14},{7,15},{8,0},{9,1},... | collective-permute-start | bytes 172040 | tf_op jit(solution)/shard_map/ppermute | solution.py:331
  41.9 2.1 %collective-permute-start.5 = (f32[112,128]{1,0:T(8,128)S(1)}, f32[112,128]{1,0:T(8,128)S(1)}, u32[]{:S(2)}, u32[]{:S(2)}) collective-permute-start(f32[112,128]{1,0:T(8,128)S(1)} %add.21), channel_id=1, source_target_pairs={{0,4},{1,5},{2,6},{3,7},{4,0},{5,1},{6,2},{7,3},{8,12},{9,13},{10,... | collective-permute-start | bytes 172040 | tf_op jit(solution)/shard_map/ppermute | solution.py:331
  43.9 0.1 collective-permute-done.7
  44.0 3.2 %collective-permute-done.6 = f32[112,128]{1,0:T(8,128)S(1)} collective-permute-done((f32[112,128]{1,0:T(8,128)S(1)}, f32[112,128]{1,0:T(8,128)S(1)}, u32[]{:S(2)}, u32[]{:S(2)}) %collective-permute-start.6) | collective-permute-done | bytes 57376 | tf_op jit(solution)/shard_map/ppermute | solution.py:331
  47.2 0.0 collective-permute-done.5
  47.2 1.7 %collective-permute-start.10 = (f32[112,128]{1,0:T(8,128)S(1)}, f32[112,128]{1,0:T(8,128)S(1)}, u32[]{:S(2)}, u32[]{:S(2)}) collective-permute-start(f32[112,128]{1,0:T(8,128)S(1)} %add_add_fusion.1), channel_id=1, source_target_pairs={{0,96},{1,97},{2,98},{3,99},{4,100},{5,101},{6,102},{7,103},{8,104... | collective-permute-start | bytes 172040 | tf_op jit(solution)/shard_map/ppermute | solution.py:331
  48.9 0.8 %collective-permute-start.9 = (f32[112,128]{1,0:T(8,128)S(1)}, f32[112,128]{1,0:T(8,128)S(1)}, u32[]{:S(2)}, u32[]{:S(2)}) collective-permute-start(f32[112,128]{1,0:T(8,128)S(1)} %add_add_fusion.1), channel_id=1, source_target_pairs={{0,64},{1,65},{2,66},{3,67},{4,68},{5,69},{6,70},{7,71},{8,72},{9,... | collective-permute-start | bytes 172040 | tf_op jit(solution)/shard_map/ppermute | solution.py:331
  49.7 1.7 %collective-permute-start.8 = (f32[112,128]{1,0:T(8,128)S(1)}, f32[112,128]{1,0:T(8,128)S(1)}, u32[]{:S(2)}, u32[]{:S(2)}) collective-permute-start(f32[112,128]{1,0:T(8,128)S(1)} %add_add_fusion.1), channel_id=1, source_target_pairs={{0,32},{1,33},{2,34},{3,35},{4,36},{5,37},{6,38},{7,39},{8,40},{9,... | collective-permute-start | bytes 172040 | tf_op jit(solution)/shard_map/ppermute | solution.py:331
  51.4 0.0 copy-done.6
  51.4 0.0 copy-done.1
  51.4 4.8 %shard_map.87 = (bf16[2,16,12288]{2,1,0:T(8,128)(2,1)}, bf16[2,16,12288]{2,1,0:T(8,128)(2,1)}) custom-call(bf16[28,96,128]{2,1,0:T(8,128)(2,1)} %copy-done.1, bf16[8,96,128]{2,1,0:T(8,128)(2,1)} %copy-done.6, bf16[3,3,256,128]{3,2,1,0:T(8,128)(2,1)} %get-tuple-element.43.refs_2_.refs_1_, bf16[3,3,256,128]{3,2,1,0:T(8,128)(2,1)} %get-tuple-element.44.refs_3_.refs_2_, ...), custom_call_target="tpu_custom_call" | custom-call | tf_op jit(solution)/shard_map/pallas_call | solution.py:27
  56.2 1.9 %collective-permute-done.10 = f32[112,128]{1,0:T(8,128)S(1)} collective-permute-done((f32[112,128]{1,0:T(8,128)S(1)}, f32[112,128]{1,0:T(8,128)S(1)}, u32[]{:S(2)}, u32[]{:S(2)}) %collective-permute-start.10) | collective-permute-done | bytes 57376 | tf_op jit(solution)/shard_map/ppermute | solution.py:331
  58.1 0.7 %collective-permute-done.9 = f32[112,128]{1,0:T(8,128)S(1)} collective-permute-done((f32[112,128]{1,0:T(8,128)S(1)}, f32[112,128]{1,0:T(8,128)S(1)}, u32[]{:S(2)}, u32[]{:S(2)}) %collective-permute-start.9) | collective-permute-done | bytes 57376 | tf_op jit(solution)/shard_map/ppermute | solution.py:331
  58.8 0.0 collective-permute-done.8
  58.8 0.1 collective-permute-start.11
  58.9 1.2 %collective-permute-done.11.other = f32[112,128]{1,0:T(8,128)S(1)} collective-permute-done((f32[112,128]{1,0:T(8,128)S(1)}, f32[112,128]{1,0:T(8,128)S(1)}, u32[]{:S(2)}, u32[]{:S(2)}) %collective-permute-start.11) | collective-permute-done | bytes 57376 | tf_op jit(solution)/shard_map/ppermute | solution.py:331
  60.2 0.0 collective-permute-done.12.refs_0_
  60.2 0.0 copy-start.9
  60.2 0.5 collective-permute-start.15
  60.6 2.9 %collective-permute-start.14 = (f32[224,128]{1,0:T(8,128)S(1)}, f32[224,128]{1,0:T(8,128)S(1)}, u32[]{:S(2)}, u32[]{:S(2)}) collective-permute-start(f32[224,128]{1,0:T(8,128)S(1)} %shard_map.88.part), channel_id=1, source_target_pairs={{0,16},{1,17},{2,18},{3,19},{4,20},{5,21},{6,22},{7,23},{8,24},{9,... | collective-permute-start | bytes 344072 | tf_op jit(solution)/shard_map/ppermute | solution.py:331
  63.6 0.8 %collective-permute-start.13 = (f32[224,128]{1,0:T(8,128)S(1)}, f32[224,128]{1,0:T(8,128)S(1)}, u32[]{:S(2)}, u32[]{:S(2)}) collective-permute-start(f32[224,128]{1,0:T(8,128)S(1)} %shard_map.88.part), channel_id=1, source_target_pairs={{0,2},{1,3},{2,0},{3,1},{4,6},{5,7},{6,4},{7,5},{8,10},{9,11},{10,... | collective-permute-start | bytes 344072 | tf_op jit(solution)/shard_map/ppermute | solution.py:331
  64.3 0.0 copy-done.9
  64.3 4.7 %shard_map.89 = (bf16[2,16,12288]{2,1,0:T(8,128)(2,1)}, bf16[2,16,12288]{2,1,0:T(8,128)(2,1)}) custom-call(bf16[36,96,128]{2,1,0:T(8,128)(2,1)} %copy-done.9, bf16[3,3,256,128]{3,2,1,0:T(8,128)(2,1)} %get-tuple-element.43.refs_2_.refs_1_, bf16[3,3,256,128]{3,2,1,0:T(8,128)(2,1)} %get-tuple-element.44.refs_3_.refs_2_, ...), custom_call_target="tpu_custom_call", output_to_operand_aliasing={{0}: (6, {}), {1}: (7, {})} | custom-call | tf_op jit(solution)/shard_map/pallas_call | solution.py:27
  69.1 0.0 collective-permute-done.15.three
  69.1 0.0 collective-permute-done.14.two
  69.1 0.6 collective-permute-done.13.one
  69.7 1.0 %shard_map.90 = (f32[864,32]{1,0:T(8,128)}, f32[1,32]{1,0:T(1,128)}) custom-call(f32[224,128]{1,0:T(8,128)S(1)} %shard_map.88.part, f32[224,128]{1,0:T(8,128)S(1)} %collective-permute-done.13.one, f32[224,128]{1,0:T(8,128)S(1)} %collective-permute-done.14.two, f32[224,128]{1,0:T(8,128)S(1)} %collective-permute-done.15.three), custom_call_target="tpu_custom_call" | custom-call | tf_op jit(solution)/shard_map/pallas_call | solution.py:18
  (6 shorter events, 0.1 us)
Async XLA Ops:
  3.7 27.1 %copy-start = (bf16[32,96,128]{2,1,0:T(8,128)(2,1)S(1)}, bf16[32,96,128]{2,1,0:T(8,128)(2,1)}, u32[]{:S(2)}) copy-start(bf16[32,96,128]{2,1,0:T(8,128)(2,1)} %get-tuple-element.36.low) | copy-start | bytes 2359300
  3.7 12.4 %collective-permute-start.1 = (bf16[4,96,128]{2,1,0:T(8,128)(2,1)}, bf16[4,96,128]{2,1,0:T(8,128)(2,1)S(1)}, u32[]{:S(2)}, u32[]{:S(2)}) collective-permute-start(bf16[4,96,128]{2,1,0:T(8,128)(2,1)} %get-tuple-element.34), channel_id=1, source_target_pairs={{0,1},{1,2},{2,3},{3,4},{4,5},{5,6},{6,7},{7,8},{8,9},{9,10},{10,1... | collective-permute-start | bytes 294920 | tf_op jit(solution)/shard_map/ppermute | solution.py:326
  5.8 10.4 %collective-permute-start.2 = (bf16[4,96,128]{2,1,0:T(8,128)(2,1)}, bf16[4,96,128]{2,1,0:T(8,128)(2,1)S(1)}, u32[]{:S(2)}, u32[]{:S(2)}) collective-permute-start(bf16[4,96,128]{2,1,0:T(8,128)(2,1)} %get-tuple-element.35), channel_id=1, source_target_pairs={{1,0},{2,1},{3,2},{4,3},{5,4},{6,5},{7,6},{8,7},{9,8},{10,9},{11,1... | collective-permute-start | bytes 294920 | tf_op jit(solution)/shard_map/ppermute | solution.py:326
  10.3 26.5 %collective-permute-start = (bf16[28,96,128]{2,1,0:T(8,128)(2,1)}, bf16[28,96,128]{2,1,0:T(8,128)(2,1)S(1)}, u32[]{:S(2)}, u32[]{:S(2)}) collective-permute-start(bf16[28,96,128]{2,1,0:T(8,128)(2,1)} %get-tuple-element.32.high_first), channel_id=1, source_target_pairs={{0,16},{16,32},{32,48},{48,64},{64,80},{80,96},{96,112},{1,17},{17... | collective-permute-start | bytes 2064392 | tf_op jit(solution)/shard_map/ppermute | solution.py:326
  16.1 3.6 %copy-start.2 = (bf16[4,96,128]{2,1,0:T(8,128)(2,1)}, bf16[4,96,128]{2,1,0:T(8,128)(2,1)S(1)}, u32[]{:S(2)}) copy-start(bf16[4,96,128]{2,1,0:T(8,128)(2,1)S(1)} %collective-permute-done.1.from_left) | copy-start | bytes 294916
  16.2 3.6 %copy-start.4 = (bf16[4,96,128]{2,1,0:T(8,128)(2,1)}, bf16[4,96,128]{2,1,0:T(8,128)(2,1)S(1)}, u32[]{:S(2)}) copy-start(bf16[4,96,128]{2,1,0:T(8,128)(2,1)S(1)} %collective-permute-done.2.from_right) | copy-start | bytes 294916
  17.1 19.7 %collective-permute-start.3 = (bf16[8,96,128]{2,1,0:T(8,128)(2,1)S(1)}, bf16[8,96,128]{2,1,0:T(8,128)(2,1)S(1)}, u32[]{:S(2)}, u32[]{:S(2)}) collective-permute-start(bf16[8,96,128]{2,1,0:T(8,128)(2,1)S(1)} %pad_maximum_fusion.1), channel_id=1, source_target_pairs={{0,16},{16,32},{32,48},{48,64},{64,80},{80,96},{96,112},{1,17},{17... | collective-permute-start | bytes 589832 | tf_op jit(solution)/shard_map/ppermute | solution.py:326
  30.7 6.1 %copy-start.3 = (bf16[4,96,128]{2,1,0:T(8,128)(2,1)S(1)}, bf16[4,96,128]{2,1,0:T(8,128)(2,1)}, u32[]{:S(2)}) copy-start(bf16[4,96,128]{2,1,0:T(8,128)(2,1)} %copy-done.2) | copy-start | bytes 294916
  30.8 6.1 %copy-start.5 = (bf16[4,96,128]{2,1,0:T(8,128)(2,1)S(1)}, bf16[4,96,128]{2,1,0:T(8,128)(2,1)}, u32[]{:S(2)}) copy-start(bf16[4,96,128]{2,1,0:T(8,128)(2,1)} %copy-done.4) | copy-start | bytes 294916
  30.8 6.1 %copy-start.7 = (f32[3,3,32,128]{3,2,1,0:T(8,128)S(1)}, f32[3,3,32,128]{3,2,1,0:T(8,128)}, u32[]{:S(2)}) copy-start(f32[3,3,32,128]{3,2,1,0:T(8,128)} %get-tuple-element.39.folded) | copy-start | bytes 442372
  30.8 6.1 %copy-start.8 = (f32[8,128]{1,0:T(8,128)S(1)}, f32[8,128]{1,0:T(8,128)}, u32[]{:S(2)}) copy-start(f32[8,128]{1,0:T(8,128)} %get-tuple-element.40.bias_terms) | copy-start | bytes 12292
  30.9 29.2 %collective-permute-start.12 = (bf16[36,96,128]{2,1,0:T(8,128)(2,1)S(1)}, bf16[36,96,128]{2,1,0:T(8,128)(2,1)S(1)}, u32[]{:S(2)}, u32[]{:S(2)}) collective-permute-start(bf16[36,96,128]{2,1,0:T(8,128)(2,1)S(1)} %pad_maximum_fusion), channel_id=1, source_target_pairs={{16,0},{32,16},{48,32},{64,48},{80,64},{96,80},{112,96},{17,1},{33... | collective-permute-start | bytes 2654216 | tf_op jit(solution)/shard_map/ppermute | solution.py:326
  36.8 14.6 %copy-start.6 = (bf16[8,96,128]{2,1,0:T(8,128)(2,1)}, bf16[8,96,128]{2,1,0:T(8,128)(2,1)S(1)}, u32[]{:S(2)}) copy-start(bf16[8,96,128]{2,1,0:T(8,128)(2,1)S(1)} %collective-permute-done.3.below_rest.refs_1_) | copy-start | bytes 589828
  36.8 14.6 %copy-start.1 = (bf16[28,96,128]{2,1,0:T(8,128)(2,1)}, bf16[28,96,128]{2,1,0:T(8,128)(2,1)S(1)}, u32[]{:S(2)}) copy-start(bf16[28,96,128]{2,1,0:T(8,128)(2,1)S(1)} %collective-permute-done.below_first.refs_0_) | copy-start | bytes 2064388
  38.4 1.3 %collective-permute-start.4 = (f32[112,128]{1,0:T(8,128)S(1)}, f32[112,128]{1,0:T(8,128)S(1)}, u32[]{:S(2)}, u32[]{:S(2)}) collective-permute-start(f32[112,128]{1,0:T(8,128)S(1)} %get-tuple-element.42), channel_id=1, source_target_pairs={{0,1},{1,0},{2,3},{3,2},{4,5},{5,4},{6,7},{7,6},{8,9},{9,8},{10,11... | collective-permute-start | bytes 172040 | tf_op jit(solution)/shard_map/ppermute | solution.py:331
  39.8 4.3 %collective-permute-start.7 = (f32[112,128]{1,0:T(8,128)S(1)}, f32[112,128]{1,0:T(8,128)S(1)}, u32[]{:S(2)}, u32[]{:S(2)}) collective-permute-start(f32[112,128]{1,0:T(8,128)S(1)} %add.21), channel_id=1, source_target_pairs={{0,12},{1,13},{2,14},{3,15},{4,8},{5,9},{6,10},{7,11},{8,4},{9,5},... | collective-permute-start | bytes 172040 | tf_op jit(solution)/shard_map/ppermute | solution.py:331
  41.1 6.1 %collective-permute-start.6 = (f32[112,128]{1,0:T(8,128)S(1)}, f32[112,128]{1,0:T(8,128)S(1)}, u32[]{:S(2)}, u32[]{:S(2)}) collective-permute-start(f32[112,128]{1,0:T(8,128)S(1)} %add.21), channel_id=1, source_target_pairs={{0,8},{1,9},{2,10},{3,11},{4,12},{5,13},{6,14},{7,15},{8,0},{9,1},... | collective-permute-start | bytes 172040 | tf_op jit(solution)/shard_map/ppermute | solution.py:331
  41.9 5.4 %collective-permute-start.5 = (f32[112,128]{1,0:T(8,128)S(1)}, f32[112,128]{1,0:T(8,128)S(1)}, u32[]{:S(2)}, u32[]{:S(2)}) collective-permute-start(f32[112,128]{1,0:T(8,128)S(1)} %add.21), channel_id=1, source_target_pairs={{0,4},{1,5},{2,6},{3,7},{4,0},{5,1},{6,2},{7,3},{8,12},{9,13},{10,... | collective-permute-start | bytes 172040 | tf_op jit(solution)/shard_map/ppermute | solution.py:331
  47.2 10.8 %collective-permute-start.10 = (f32[112,128]{1,0:T(8,128)S(1)}, f32[112,128]{1,0:T(8,128)S(1)}, u32[]{:S(2)}, u32[]{:S(2)}) collective-permute-start(f32[112,128]{1,0:T(8,128)S(1)} %add_add_fusion.1), channel_id=1, source_target_pairs={{0,96},{1,97},{2,98},{3,99},{4,100},{5,101},{6,102},{7,103},{8,104... | collective-permute-start | bytes 172040 | tf_op jit(solution)/shard_map/ppermute | solution.py:331
  48.9 9.9 %collective-permute-start.9 = (f32[112,128]{1,0:T(8,128)S(1)}, f32[112,128]{1,0:T(8,128)S(1)}, u32[]{:S(2)}, u32[]{:S(2)}) collective-permute-start(f32[112,128]{1,0:T(8,128)S(1)} %add_add_fusion.1), channel_id=1, source_target_pairs={{0,64},{1,65},{2,66},{3,67},{4,68},{5,69},{6,70},{7,71},{8,72},{9,... | collective-permute-start | bytes 172040 | tf_op jit(solution)/shard_map/ppermute | solution.py:331
  49.7 9.1 %collective-permute-start.8 = (f32[112,128]{1,0:T(8,128)S(1)}, f32[112,128]{1,0:T(8,128)S(1)}, u32[]{:S(2)}, u32[]{:S(2)}) collective-permute-start(f32[112,128]{1,0:T(8,128)S(1)} %add_add_fusion.1), channel_id=1, source_target_pairs={{0,32},{1,33},{2,34},{3,35},{4,36},{5,37},{6,38},{7,39},{8,40},{9,... | collective-permute-start | bytes 172040 | tf_op jit(solution)/shard_map/ppermute | solution.py:331
  58.8 1.3 %collective-permute-start.11 = (f32[112,128]{1,0:T(8,128)S(1)}, f32[112,128]{1,0:T(8,128)S(1)}, u32[]{:S(2)}, u32[]{:S(2)}) collective-permute-start(f32[112,128]{1,0:T(8,128)S(1)} %add_add_fusion.part), channel_id=1, source_target_pairs={{0,1},{1,0},{2,3},{3,2},{4,5},{5,4},{6,7},{7,6},{8,9},{9,8},{10,11... | collective-permute-start | bytes 172040 | tf_op jit(solution)/shard_map/ppermute | solution.py:331
  60.2 4.2 %copy-start.9 = (bf16[36,96,128]{2,1,0:T(8,128)(2,1)}, bf16[36,96,128]{2,1,0:T(8,128)(2,1)S(1)}, u32[]{:S(2)}) copy-start(bf16[36,96,128]{2,1,0:T(8,128)(2,1)S(1)} %collective-permute-done.12.refs_0_) | copy-start | bytes 2654212
  60.2 9.0 %collective-permute-start.15 = (f32[224,128]{1,0:T(8,128)S(1)}, f32[224,128]{1,0:T(8,128)S(1)}, u32[]{:S(2)}, u32[]{:S(2)}) collective-permute-start(f32[224,128]{1,0:T(8,128)S(1)} %shard_map.88.part), channel_id=1, source_target_pairs={{0,18},{1,19},{2,16},{3,17},{4,22},{5,23},{6,20},{7,21},{8,26},{9,... | collective-permute-start | bytes 344072 | tf_op jit(solution)/shard_map/ppermute | solution.py:331
  60.6 8.5 %collective-permute-start.14 = (f32[224,128]{1,0:T(8,128)S(1)}, f32[224,128]{1,0:T(8,128)S(1)}, u32[]{:S(2)}, u32[]{:S(2)}) collective-permute-start(f32[224,128]{1,0:T(8,128)S(1)} %shard_map.88.part), channel_id=1, source_target_pairs={{0,16},{1,17},{2,18},{3,19},{4,20},{5,21},{6,22},{7,23},{8,24},{9,... | collective-permute-start | bytes 344072 | tf_op jit(solution)/shard_map/ppermute | solution.py:331
  63.6 6.1 %collective-permute-start.13 = (f32[224,128]{1,0:T(8,128)S(1)}, f32[224,128]{1,0:T(8,128)S(1)}, u32[]{:S(2)}, u32[]{:S(2)}) collective-permute-start(f32[224,128]{1,0:T(8,128)S(1)} %shard_map.88.part), channel_id=1, source_target_pairs={{0,2},{1,3},{2,0},{3,1},{4,6},{5,7},{6,4},{7,5},{8,10},{9,11},{10,... | collective-permute-start | bytes 344072 | tf_op jit(solution)/shard_map/ppermute | solution.py:331
